TPU v7x, 32 devices: a whole 2x2x4 slice. The times are simulated.
32 devices in a mesh: row: 4 (over z), col: 8 (over y, x, core).
Axes of the slice: x: 2, y: 2, z: 4, core: 2. Of those that a mesh axis runs over, the one named last changes fastest.
Arguments:
- tile_values: bfloat16 [4, 8, 256, 128, 128], P('row', 'col'), may hold values from -0.125 to 0.125
- tile_rows: int32 [4, 8, 256], P('row', 'col'), may hold values from 0 to 127
- tile_cols: int32 [4, 8, 256], P('row', 'col'), may hold values from 0 to 255
- increments: float32 [16, 128, 2048], P('row', None, 'col'), may hold values from 0 to 0.1
- dual_vars: float32 [16, 65536], P(None, 'row'), may hold values from 0 to 1
- flight_cost: float32 [128, 2048], P(None, 'col'), may hold values from -0.5 to 0.5
- win_start: int32 [2048], P('col'), may hold values from 0 to 63
- win_len: int32 [2048], P('col'), may hold values from 32 to 64
- capacity: int32 [16, 65536], P(None, 'row'), may hold values from 0 to 3
Outputs:
- primal: float32 [16, 128, 2048], P('row', None, 'col')
- duals_out: float32 [16, 65536], P(None, 'row')
Inputs may be any that keep to these rules, and one draw needn't show every extreme that they name: `tile_rows`: a block position may occur more than once in a device's list; such blocks add.
All inputs are finite; a program needn't handle non-finite values.
Results may differ from a plain program's by a relative error of at most 0.0056.
Values may be sent and summed in bfloat16 or wider, within the bound.
No kernel may reach another device: no remote copies, remote signals or barrier semaphores. Data moves between devices by JAX's collectives and lax.ppermute only.
A program may use at most 64 MiB of HBM per device.

v0:
```python
import math

import jax
import jax.numpy as jnp
from jax import lax
from jax.sharding import PartitionSpec as P

ITERS = 2


SIGMA_STEP = 0.2


def running_total(values):
    length = values.shape[1]
    row_iota = lax.broadcasted_iota(jnp.int32, (length, length), 0)
    col_iota = lax.broadcasted_iota(jnp.int32, (length, length), 1)
    triangle = (row_iota >= col_iota).astype(jnp.float32)
    return jnp.einsum("kj,sjf->skf", triangle, values, precision=lax.Precision.HIGHEST)


def trailing_total(values):
    length = values.shape[1]
    row_iota = lax.broadcasted_iota(jnp.int32, (length, length), 0)
    col_iota = lax.broadcasted_iota(jnp.int32, (length, length), 1)
    triangle = (row_iota >= col_iota).astype(jnp.float32)
    return jnp.einsum("jk,sjf->skf", triangle, values, precision=lax.Precision.HIGHEST)


def per_device(
    tile_values,
    tile_rows,
    tile_cols,
    increments,
    dual_vars,
    flight_cost,
    win_start,
    win_len,
    capacity,
):
    n_col = lax.axis_size("col")
    tile_count = tile_values.shape[2]
    tile_side = tile_values.shape[3]
    blocks = tile_values.reshape(tile_count, tile_side, tile_side)
    row_index = tile_rows.reshape(tile_count)
    col_index = tile_cols.reshape(tile_count)
    scen_local, window, flight_local = increments.shape
    tau_step = 0.6 / math.sqrt(window)
    scenarios, row_length = dual_vars.shape
    row_tiles = row_length // tile_side
    time_block = window // n_col
    flights = flight_local * n_col
    col_tiles = time_block * flights // tile_side
    hot_rows = (
        row_index[None, :] == lax.broadcasted_iota(jnp.int32, (row_tiles, tile_count), 0)
    ).astype(jnp.float32)
    hot_cols = (
        col_index[None, :] == lax.broadcasted_iota(jnp.int32, (col_tiles, tile_count), 0)
    ).astype(jnp.float32)
    minutes = lax.broadcasted_iota(jnp.int32, (window, flight_local), 0)
    upper_bound = (
        (minutes >= win_start[None, :]) & (minutes < (win_start + win_len)[None, :])
    ).astype(jnp.float32)
    capacity_f = capacity.astype(jnp.float32)
    current = dual_vars
    primal = increments
    cumulative = running_total(primal)
    for sweep_index in range(ITERS):
        dual_blocks = current.astype(jnp.bfloat16).reshape(scenarios, row_tiles, tile_side)
        picked = jnp.take(dual_blocks, row_index, axis=1)
        products = jnp.einsum("nij,sni->snj", blocks, picked, preferred_element_type=jnp.float32)
        summed = lax.psum_scatter(
            jnp.einsum("cn,snj->scj", hot_cols, products, precision=lax.Precision.HIGHEST),
            "row",
            scatter_dimension=0,
            tiled=True,
        )
        slope_tb = summed.reshape(scen_local, time_block, flights)
        flight_slope = lax.all_to_all(slope_tb, "col", split_axis=2, concat_axis=1, tiled=True)
        gradient = trailing_total(flight_slope + flight_cost[None])
        primal = jnp.clip(primal - tau_step * gradient, 0.0, upper_bound[None])
        fresh_sum = running_total(primal)
        probe_fc = (2.0 * fresh_sum - cumulative).astype(jnp.bfloat16)
        probe_vec = lax.all_to_all(probe_fc, "col", split_axis=1, concat_axis=2, tiled=True)
        gathered_part = lax.all_gather(probe_vec, "row", axis=0, tiled=True)
        probe_blocks = gathered_part.reshape(gathered_part.shape[0], col_tiles, tile_side)
        image_picked = jnp.take(probe_blocks, col_index, axis=1)
        image_products = jnp.einsum(
            "nij,snj->sni", blocks, image_picked, preferred_element_type=jnp.float32
        )
        partial_value = jnp.einsum(
            "rn,sni->sri", hot_rows, image_products, precision=lax.Precision.HIGHEST
        )
        flattened = partial_value.reshape(scenarios, row_length)
        col_total = lax.psum(flattened, "col")
        current = jnp.maximum(current + SIGMA_STEP * (col_total - capacity_f), 0.0)
        cumulative = fresh_sum
    return (primal, current)


def solution(mesh):
    placed = (
        P("row", "col", None, None, None),
        P("row", "col", None),
        P("row", "col", None),
        P("row", None, "col"),
        P(None, "row"),
        P(None, "col"),
        P("col"),
        P("col"),
        P(None, "row"),
    )
    return jax.shard_map(
        per_device,
        mesh=mesh,
        in_specs=placed,
        out_specs=(P("row", None, "col"), P(None, "row")),
        check_vma=False,
    )
```

profile of v0, /device:TPU:0, one launch (start us, length us, event | category | flops | bytes accessed | tf_op | source)
XLA Modules:
  0.0 418.2 jit_solution(5962648822199088613)
XLA Ops:
  7.2 0.7 compare_and_fusion.1
  8.6 1.3 copy_bitcast_fusion.3
  9.9 0.8 gather_fusion
  10.7 4.7 %fusion.22 = f32[16,256,128]{2,0,1:T(8,128)S(1)} fusion(bf16[1,1,256,128,128]{4,3,2,1,0:T(8,128)(2,1)} %param.13, bf16[256,16,128]{2,1,0:T(8,128)(2,1)S(1)} %gather_fusion, pred[256]{0:T(512)(128)(4,1)S(1)} %compare_and_fusion.1), kind=kOutput, calls=%fused_computation.22 | convolution fusion | flops 134742016 | bytes 11534592 | tf_op jit(solution)/shard_map/nij,sni->snj/dot_general | solution.py:71
  15.5 3.4 fusion.16
  19.0 46.7 %reduce-scatter.3.cloned.1.call-done = f32[4,256,128]{1,2,0:T(8,128)} async-done(((f32[16,256,128]{1,2,0:T(8,128)}), f32[4,256,128]{1,2,0:T(8,128)}) %reduce-scatter.3.cloned.1.call-update) | async-done | bytes 524304 | tf_op jit(solution)/shard_map/reduce_scatter | solution.py:72
  65.7 1.2 copy.55
  67.0 3.1 copy.56
  70.1 5.5 %reshape.143 = f32[8,1,16384]{2,1,0:T(1,128)} reshape(f32[2048,4,16]{2,1,0:T(4,128)} %bitcast.137) | data formatting | bytes 1048576
  75.6 3.8 all-to-all-start
  80.3 8.8 %all-to-all-done = f32[8,1,16384]{2,1,0:T(1,128)S(1)} async-done(((f32[8,1,16384]{2,1,0:T(1,128)}), f32[8,1,16384]{2,1,0:T(1,128)S(1)}, u32[]{:S(2)}, u32[]{:S(2)}) %all-to-all-start) | async-done | bytes 524320 | tf_op jit(solution)/shard_map/all_to_all | solution.py:79
  89.7 1.9 reduce
  91.6 4.9 %reshape.144 = f32[2048,4,16]{2,1,0:T(4,128)} reshape(f32[8,16384]{1,0:T(8,128)S(1)} %reduce) | data formatting | bytes 1048576
  96.5 3.5 copy.86
  101.8 9.3 %all_to_all.72 = bf16[4,128,256]{2,0,1:T(4,128)(2,1)S(1)} all-to-all(bf16[4,128,256]{2,0,1:T(4,128)(2,1)S(1)} %copy.62), channel_id=1, replica_groups=mesh['row'=4,'col'=8] {'col'}, dimensions={1} | all-to-all | bytes 524288 | tf_op jit(solution)/shard_map/all_to_all | solution.py:84
  111.2 0.7 copy.91
  112.2 25.3 %all-gather.3.cloned.1.call-done = bf16[16,16,2048]{2,1,0:T(8,128)(2,1)} async-done(((bf16[4,16,2048]{2,1,0:T(8,128)(2,1)}), bf16[16,16,2048]{2,1,0:T(8,128)(2,1)}) %all-gather.3.cloned.1.call-update) | async-done | bytes 1048592 | tf_op jit(solution)/shard_map/all_gather | solution.py:85
  137.5 1.6 reshape.90
  139.8 0.8 gather_fusion.1
  140.7 6.9 %fusion.25 = f32[16,256,128]{2,0,1:T(8,128)S(1)} fusion(bf16[1,1,256,128,128]{4,3,2,1,0:T(8,128)(2,1)} %param.13, bf16[256,16,128]{2,1,0:T(8,128)(2,1)S(1)} %gather_fusion.1, pred[256]{0:T(512)(128)(4,1)S(1)} %compare_and_fusion), kind=kOutput, calls=%fused_computation.23 | convolution fusion | flops 134742016 | bytes 11534592 | tf_op jit(solution)/shard_map/nij,snj->sni/dot_general | solution.py:88
  147.5 2.1 fusion.34
  150.0 1.6 copy.116
  151.6 56.2 %all-reduce.3.cloned.1.call-done = f32[16,16384]{1,0:T(8,128)} async-done(((f32[16,16384]{1,0:T(8,128)}), f32[16,16384]{1,0:T(8,128)}) %all-reduce.3.cloned.1.call-update) | async-done | bytes 1048592 | tf_op jit(solution)/shard_map/psum | solution.py:95
  207.9 1.7 copy_bitcast_fusion.2
  209.6 1.8 gather_fusion.2
  211.4 6.1 %fusion.28 = f32[16,256,128]{2,0,1:T(8,128)S(1)} fusion(bf16[1,1,256,128,128]{4,3,2,1,0:T(8,128)(2,1)} %param.13, bf16[256,16,128]{2,1,0:T(8,128)(2,1)} %gather_fusion.2, pred[256]{0:T(512)(128)(4,1)S(1)} %compare_and_fusion.1), kind=kOutput, calls=%fused_computation.24 | convolution fusion | flops 134742016 | bytes 11534592 | tf_op jit(solution)/shard_map/nij,sni->snj/dot_general | solution.py:71
  217.4 3.5 fusion.19
  221.2 42.8 %reduce-scatter.5.cloned.1.call-done = f32[4,256,128]{1,2,0:T(8,128)} async-done(((f32[16,256,128]{1,2,0:T(8,128)}), f32[4,256,128]{1,2,0:T(8,128)}) %reduce-scatter.5.cloned.1.call-update) | async-done | bytes 524304 | tf_op jit(solution)/shard_map/reduce_scatter | solution.py:72
  264.0 1.2 copy.70
  265.3 3.1 copy.71
  268.4 4.7 %reshape.145 = f32[8,1,16384]{2,1,0:T(1,128)S(1)} reshape(f32[2048,4,16]{2,1,0:T(4,128)} %bitcast.139) | data formatting | bytes 1048576
  273.1 13.2 %all_to_all.73 = f32[8,1,16384]{2,1,0:T(1,128)S(1)} all-to-all(f32[8,1,16384]{2,1,0:T(1,128)S(1)} %reshape.145), channel_id=1, replica_groups=mesh['row'=4,'col'=8] {'col'}, dimensions={0} | all-to-all | bytes 1048576 | tf_op jit(solution)/shard_map/all_to_all | solution.py:79
  286.3 1.9 reduce.1
  288.2 4.9 %reshape.146 = f32[2048,4,16]{2,1,0:T(4,128)} reshape(f32[8,16384]{1,0:T(8,128)S(1)} %reduce.1) | data formatting | bytes 1048576
  293.1 3.4 copy.88
  297.8 9.3 %all_to_all.74 = bf16[4,128,256]{2,0,1:T(4,128)(2,1)S(1)} all-to-all(bf16[4,128,256]{2,0,1:T(4,128)(2,1)S(1)} %copy.75), channel_id=1, replica_groups=mesh['row'=4,'col'=8] {'col'}, dimensions={1} | all-to-all | bytes 524288 | tf_op jit(solution)/shard_map/all_to_all | solution.py:84
  307.2 0.7 copy.92
  308.2 25.3 %all-gather.5.cloned.1.call-done = bf16[16,16,2048]{2,1,0:T(8,128)(2,1)} async-done(((bf16[4,16,2048]{2,1,0:T(8,128)(2,1)}), bf16[16,16,2048]{2,1,0:T(8,128)(2,1)}) %all-gather.5.cloned.1.call-update) | async-done | bytes 1048592 | tf_op jit(solution)/shard_map/all_gather | solution.py:85
  333.5 1.6 reshape.94
  335.1 1.6 copy.78
  336.7 2.1 gather_fusion.3
  338.8 6.9 %fusion.31 = f32[16,256,128]{2,0,1:T(8,128)S(1)} fusion(bf16[1,1,256,128,128]{4,3,2,1,0:T(8,128)(2,1)} %param.13, bf16[256,16,128]{2,1,0:T(8,128)(2,1)S(1)} %gather_fusion.3, pred[256]{0:T(512)(128)(4,1)S(1)} %compare_and_fusion), kind=kOutput, calls=%fused_computation.25 | convolution fusion | flops 134742016 | bytes 11534592 | tf_op jit(solution)/shard_map/nij,snj->sni/dot_general | solution.py:88
  345.7 2.1 fusion.37
  347.8 1.3 copy.80
  349.1 2.9 copy.115
  352.1 1.0 copy.81
  353.1 55.3 %all-reduce.5.cloned.1.call-done = f32[16,16384]{1,0:T(8,128)} async-done(((f32[16,16384]{1,0:T(8,128)}), f32[16,16384]{1,0:T(8,128)}) %all-reduce.5.cloned.1.call-update) | async-done | bytes 1048592 | tf_op jit(solution)/shard_map/psum | solution.py:95
  408.3 2.8 add_maximum_fusion
  (52 shorter events, 7.4 us)
Async XLA Ops:
  7.2 58.5 %reduce-scatter.3.cloned.1.call-start = ((), (), s32[]{:S(2)}) async-start(), calls=%async_computation.6 | async-start | bytes 2621440 | tf_op jit(solution)/shard_map/reduce_scatter | solution.py:72
  10.7 4.8 %copy-start.4 = (s32[1,1,256]{2,1,0:T(1,128)S(1)}, s32[1,1,256]{2,1,0:T(1,128)}, u32[]{:S(2)}) copy-start(s32[1,1,256]{2,1,0:T(1,128)} %param.15) | copy-start | bytes 3076
  70.1 9.8 %copy-start.2 = (f32[4,128,256]{2,1,0:T(8,128)S(1)}, f32[4,128,256]{2,1,0:T(8,128)}, u32[]{:S(2)}) copy-start(f32[4,128,256]{2,1,0:T(8,128)} %param.16) | copy-start | bytes 1572868
  75.6 4.6 %copy-start.6 = (s32[256]{0:T(256)S(1)}, s32[256]{0:T(256)}, u32[]{:S(2)}) copy-start(s32[256]{0:T(256)} %param.19) | copy-start | bytes 3076
  75.6 4.6 %copy-start.7 = (s32[256]{0:T(256)S(1)}, s32[256]{0:T(256)}, u32[]{:S(2)}) copy-start(s32[256]{0:T(256)} %param.20) | copy-start | bytes 3076
  75.6 13.5 %all-to-all-start = ((f32[8,1,16384]{2,1,0:T(1,128)}), f32[8,1,16384]{2,1,0:T(1,128)S(1)}, u32[]{:S(2)}, u32[]{:S(2)}) async-start(f32[8,1,16384]{2,1,0:T(1,128)} %reshape.143), calls=%async_computation.1 | async-start | bytes 1048576 | tf_op jit(solution)/shard_map/all_to_all | solution.py:79
  79.4 58.2 %all-gather.3.cloned.1.call-start = ((), (), s32[]{:S(2)}) async-start(), calls=%async_computation.7 | async-start | bytes 1310720 | tf_op jit(solution)/shard_map/all_gather | solution.py:85
  96.5 3.5 copy-start.3
  112.0 95.9 %all-reduce.3.cloned.1.call-start = ((), (), s32[]{:S(2)}) async-start(), calls=%async_computation.8 | async-start | bytes 2097152 | tf_op jit(solution)/shard_map/psum | solution.py:95
  140.6 6.9 %copy-start.5 = (s32[1,1,256]{2,1,0:T(1,128)S(1)}, s32[1,1,256]{2,1,0:T(1,128)}, u32[]{:S(2)}) copy-start(s32[1,1,256]{2,1,0:T(1,128)} %param.14) | copy-start | bytes 3076
  150.0 57.9 %copy-start = (f32[16,16384]{1,0:T(8,128)S(1)}, f32[16,16384]{1,0:T(8,128)}, u32[]{:S(2)}) copy-start(f32[16,16384]{1,0:T(8,128)} %param.17) | copy-start | bytes 3145732
  151.6 112.4 %reduce-scatter.5.cloned.1.call-start = ((), (), s32[]{:S(2)}) async-start(), calls=%async_computation.9 | async-start | bytes 2621440 | tf_op jit(solution)/shard_map/reduce_scatter | solution.py:72
  220.9 112.6 %all-gather.5.cloned.1.call-start = ((), (), s32[]{:S(2)}) async-start(), calls=%async_computation.10 | async-start | bytes 1310720 | tf_op jit(solution)/shard_map/all_gather | solution.py:85
  307.9 100.4 %all-reduce.5.cloned.1.call-start = ((), (), s32[]{:S(2)}) async-start(), calls=%async_computation.11 | async-start | bytes 2097152 | tf_op jit(solution)/shard_map/psum | solution.py:95
  349.1 59.2 %copy-start.1 = (s32[16,16384]{1,0:T(8,128)S(1)}, s32[16,16384]{1,0:T(8,128)}, u32[]{:S(2)}) copy-start(s32[16,16384]{1,0:T(8,128)} %param.21) | copy-start | bytes 3145732
Sparse Core Ops, SparseCore 0:
  19.1 46.5 reduce-scatter.2
  112.1 25.4 all-gather.2
  151.7 56.0 all-reduce.2
  221.0 42.9 reduce-scatter.4
  308.0 25.4 all-gather.4
  352.2 56.0 all-reduce.4
where the time goes:
time: 424 us; the launch traced here: 418 us
  waiting for transfers between devices  261 us (62%)
  local copies, waits for them, and re-layouts  56.4 us (13%)
  matrix products  38.2 us (9%)
  blocking collectives  31.9 us (8%)
  between operations  14.7 us (3%)
  other arithmetic  11.3 us (3%)
  starting transfers between devices  5.19 us (1%)
    psum x2, waiting for transfers between devices, per_device(): col_total = lax.psum(flattened, 'col')  111 us
    reduce_scatter x2, waiting for transfers between devices, per_device(): lax.psum_scatter(jnp.einsum('cn,snj->scj', hot_cols, products, precision=...  89.5 us
    all_gather x2, waiting for transfers between devices, per_device(): gathered_part = lax.all_gather(probe_vec, 'row', axis=0, tiled=True)  50.6 us
    unnamed x24, local copies, waits for them, and re-layouts  25.7 us
    all_to_all x2, blocking collectives, per_device(): lax.all_to_all(probe_fc, 'col', split_axis=1, concat_axis=2, tiled=True)  18.7 us
    dot_general x2, matrix products, per_device(): jnp.einsum('nij,snj->sni', blocks, image_picked, preferred_element_type=j...  13.7 us
    all_to_all x1, blocking collectives, per_device(): lax.all_to_all(slope_tb, 'col', split_axis=2, concat_axis=1, tiled=True)  13.2 us
    dot_general x2, matrix products, per_device(): jnp.einsum('nij,sni->snj', blocks, picked, preferred_element_type=jnp.flo...  10.8 us
  transfers between devices with their start and end apart: 7, of which 7 were waited for; matrix products, arithmetic and copies ran while one was open for 0% of the time, Pallas kernels for 0%

commit v1 on v0

v1 whole, which is shorter than its diff:
```python
import functools
import math

import jax
import jax.numpy as jnp
from jax import lax
from jax.experimental import pallas as pl
from jax.experimental.pallas import tpu as pltpu
from jax.sharding import PartitionSpec as P

ITERS = 2
SIGMA_STEP = 0.2
UNROLL = 16
VMEM_BYTES = 40 * 1024 * 1024


def params():
    return pltpu.CompilerParams(vmem_limit_bytes=VMEM_BYTES)


def whole_vmem():
    return pl.BlockSpec(memory_space=pltpu.VMEM)


def backward_kernel(dims, rows_ref, cols_ref, duals_ref, tiles_ref, out_ref, acc_ref):
    n_row, n_col, scen_local, time_block, flight_tiles, own_tiles = dims
    scen = n_row * scen_local
    step = pl.program_id(0)
    chunk = tiles_ref.shape[0]

    @pl.when(step == 0)
    def _():
        acc_ref[...] = jnp.zeros_like(acc_ref)

    def body(index, _):
        start = index * UNROLL
        products = [
            jnp.dot(
                duals_ref[rows_ref[step * chunk + start + u]],
                tiles_ref[start + u],
                preferred_element_type=jnp.float32,
            )
            for u in range(UNROLL)
        ]
        for u in range(UNROLL):
            place = pl.multiple_of(cols_ref[step * chunk + start + u] * scen, scen)
            acc_ref[pl.ds(place, scen), :] += products[u]
        return 0

    lax.fori_loop(0, chunk // UNROLL, body, 0)

    @pl.when(step == pl.num_programs(0) - 1)
    def _():
        piece = own_tiles * time_block
        for group in range(n_row):
            for column in range(n_col):
                for j in range(scen_local):
                    s = group * scen_local + j
                    parts = [
                        acc_ref[
                            pl.ds((column * own_tiles + f) * scen + s, time_block, stride=flight_tiles * scen), :
                        ]
                        for f in range(own_tiles)
                    ]
                    out_ref[group * n_col + column, pl.ds(j * piece, piece), :] = jnp.concatenate(
                        parts, axis=0
                    ).astype(jnp.bfloat16)


def forward_kernel(dims, rows_ref, cols_ref, probe_ref, tiles_ref, out_ref, flat_ref, acc_ref):
    n_row, n_col, scen_local, time_block, flight_tiles, own_tiles = dims
    scen = n_row * scen_local
    step = pl.program_id(0)
    chunk = tiles_ref.shape[0]

    @pl.when(step == 0)
    def _():
        acc_ref[...] = jnp.zeros_like(acc_ref)
        piece = own_tiles * time_block
        for group in range(n_row):
            for column in range(n_col):
                for j in range(scen_local):
                    s = group * scen_local + j
                    block = probe_ref[group * n_col + column, pl.ds(j * piece, piece), :].astype(jnp.float32)
                    for f in range(own_tiles):
                        flat_ref[
                            pl.ds((column * own_tiles + f) * scen + s, time_block, stride=flight_tiles * scen), :
                        ] = block[f * time_block : (f + 1) * time_block]

    def body(index, _):
        start = index * UNROLL
        products = []
        for u in range(UNROLL):
            place = pl.multiple_of(cols_ref[step * chunk + start + u] * scen, scen)
            products.append(
                lax.dot_general(
                    flat_ref[pl.ds(place, scen), :].astype(jnp.bfloat16),
                    tiles_ref[start + u],
                    (((1,), (1,)), ((), ())),
                    preferred_element_type=jnp.float32,
                )
            )
        for u in range(UNROLL):
            place = pl.multiple_of(rows_ref[step * chunk + start + u] * scen, scen)
            acc_ref[pl.ds(place, scen), :] += products[u]
        return 0

    lax.fori_loop(0, chunk // UNROLL, body, 0)

    @pl.when(step == pl.num_programs(0) - 1)
    def _():
        out_ref[...] = acc_ref[...].astype(jnp.bfloat16)


def running(values, trailing):
    length = values.shape[0]
    row_iota = lax.broadcasted_iota(jnp.int32, (length, length), 0)
    col_iota = lax.broadcasted_iota(jnp.int32, (length, length), 1)
    keep = (col_iota >= row_iota) if trailing else (row_iota >= col_iota)
    return jnp.dot(
        keep.astype(jnp.float32), values, precision=lax.Precision.HIGHEST, preferred_element_type=jnp.float32
    )


def primal_kernel(dims, first, *refs):
    n_row, n_col, scen_local, time_block, flight_tiles, own_tiles = dims
    if first:
        recv_ref, inc_ref, cost_ref, start_ref, len_ref, inc_out, cum_out, send_ref = refs
    else:
        recv_ref, inc_ref, cum_ref, cost_ref, start_ref, len_ref, inc_out, cum_out, send_ref = refs
    window, flight_local = cost_ref.shape
    side = flight_local // own_tiles
    piece = own_tiles * time_block
    tau_step = 0.6 / math.sqrt(window)
    minutes = lax.broadcasted_iota(jnp.int32, (window, flight_local), 0)
    begin = start_ref[...]
    upper = ((minutes >= begin) & (minutes < begin + len_ref[...])).astype(jnp.float32)
    for j in range(scen_local):
        bands = []
        for h in range(n_col):
            total = recv_ref[h, pl.ds(j * piece, piece), :].astype(jnp.float32)
            for g in range(1, n_row):
                total = total + recv_ref[g * n_col + h, pl.ds(j * piece, piece), :].astype(jnp.float32)
            bands.append(
                jnp.concatenate([total[f * time_block : (f + 1) * time_block] for f in range(own_tiles)], axis=1)
            )
        slope = jnp.concatenate(bands, axis=0) + cost_ref[...]
        gradient = running(slope, True)
        old = inc_ref[j]
        old_sum = running(old, False) if first else cum_ref[j]
        fresh = jnp.clip(old - tau_step * gradient, 0.0, upper)
        inc_out[j] = fresh
        fresh_sum = running(fresh, False)
        cum_out[j] = fresh_sum
        probe = (2.0 * fresh_sum - old_sum).astype(jnp.bfloat16)
        for h in range(n_col):
            band = probe[h * time_block : (h + 1) * time_block]
            block = jnp.concatenate([band[:, f * side : (f + 1) * side] for f in range(own_tiles)], axis=0)
            for g in range(n_row):
                send_ref[g * n_col + h, pl.ds(j * piece, piece), :] = block


def pair_kernel(own_ref, other_ref, out_ref):
    out_ref[...] = (own_ref[...].astype(jnp.float32) + other_ref[...].astype(jnp.float32)).astype(jnp.bfloat16)


def dual_kernel(count, *refs):
    parts, (dual_ref, cap_ref, dual_out, round_out) = refs[:count], refs[count:]
    total = parts[0][...].astype(jnp.float32)
    for part in parts[1:]:
        total = total + part[...].astype(jnp.float32)
    fresh = jnp.maximum(dual_ref[...] + SIGMA_STEP * (total - cap_ref[...].astype(jnp.float32)), 0.0)
    dual_out[...] = fresh
    round_out[...] = fresh.astype(jnp.bfloat16)


def per_device(
    tile_values, tile_rows, tile_cols, increments, dual_vars, flight_cost, win_start, win_len, capacity
):
    n_row, n_col = lax.axis_size("row"), lax.axis_size("col")
    count, side = tile_values.shape[2], tile_values.shape[3]
    scen_local, window, flight_local = increments.shape
    scen, row_length = dual_vars.shape
    row_tiles = row_length // side
    time_block = window // n_col
    flight_tiles = flight_local * n_col // side
    own_tiles = flight_local // side
    col_tiles = time_block * flight_tiles
    dims = (n_row, n_col, scen_local, time_block, flight_tiles, own_tiles)
    devices = n_row * n_col
    message = (devices, scen_local * own_tiles * time_block, side)
    half = row_tiles * scen // 2

    blocks = tile_values.reshape(count, side, side)
    rows, cols = tile_rows.reshape(count), tile_cols.reshape(count)
    core = lax.axis_index("col") % 2
    chunk = min(count, 64)
    flops = 2 * count * scen * side * side

    tile_spec = pl.BlockSpec((chunk, side, side), lambda i, *_: (i, 0, 0))
    cost = pl.CostEstimate(flops=flops, bytes_accessed=2 * count * side * side, transcendentals=0)

    def backward(duals):
        return pl.pallas_call(
            functools.partial(backward_kernel, dims),
            grid_spec=pltpu.PrefetchScalarGridSpec(
                num_scalar_prefetch=2,
                grid=(count // chunk,),
                in_specs=[pl.BlockSpec((row_tiles, scen, side), lambda i, *_: (0, 0, 0)), tile_spec],
                out_specs=pl.BlockSpec(message, lambda i, *_: (0, 0, 0)),
                scratch_shapes=[pltpu.VMEM((col_tiles * scen, side), jnp.float32)],
            ),
            out_shape=jax.ShapeDtypeStruct(message, jnp.bfloat16),
            compiler_params=params(),
            cost_estimate=cost,
            name="backward_products",
        )(rows, cols, duals, blocks)

    def forward(probe):
        return pl.pallas_call(
            functools.partial(forward_kernel, dims),
            grid_spec=pltpu.PrefetchScalarGridSpec(
                num_scalar_prefetch=2,
                grid=(count // chunk,),
                in_specs=[pl.BlockSpec(message, lambda i, *_: (0, 0, 0)), tile_spec],
                out_specs=pl.BlockSpec((row_tiles * scen, side), lambda i, *_: (0, 0)),
                scratch_shapes=[
                    pltpu.VMEM((col_tiles * scen, side), jnp.float32),
                    pltpu.VMEM((row_tiles * scen, side), jnp.float32),
                ],
            ),
            out_shape=jax.ShapeDtypeStruct((row_tiles * scen, side), jnp.bfloat16),
            compiler_params=params(),
            cost_estimate=cost,
            name="forward_products",
        )(rows, cols, probe, blocks)

    def primal_step(recv, primal, cumulative):
        first = cumulative is None
        state = (primal,) if first else (primal, cumulative)
        shape = jax.ShapeDtypeStruct(primal.shape, jnp.float32)
        return pl.pallas_call(
            functools.partial(primal_kernel, dims, first),
            in_specs=[whole_vmem()] * (4 + len(state)),
            out_specs=[whole_vmem()] * 3,
            out_shape=[shape, shape, jax.ShapeDtypeStruct(message, jnp.bfloat16)],
            compiler_params=params(),
            name="primal_update",
        )(recv, *state, flight_cost, win_start.reshape(1, -1), win_len.reshape(1, -1))

    def swap_core(value):
        return lax.ppermute(value, "col", [(i, i ^ 1) for i in range(n_col)])

    def all_chips(value):
        return [
            lax.ppermute(value, "col", [(i, i ^ (2 * d)) for i in range(n_col)]) for d in range(1, n_col // 2)
        ]

    def dual_step(partial, dual, cap):
        own = lax.dynamic_slice_in_dim(partial, core * half, half, 0)
        away = lax.dynamic_slice_in_dim(partial, (1 - core) * half, half, 0)
        pair = pl.pallas_call(
            pair_kernel,
            in_specs=[whole_vmem()] * 2,
            out_specs=whole_vmem(),
            out_shape=jax.ShapeDtypeStruct(own.shape, jnp.bfloat16),
            compiler_params=params(),
            name="core_pair_sum",
        )(own, swap_core(away))
        parts = [pair, *all_chips(pair)]
        return pl.pallas_call(
            functools.partial(dual_kernel, len(parts)),
            in_specs=[whole_vmem()] * (len(parts) + 2),
            out_specs=[whole_vmem()] * 2,
            out_shape=[
                jax.ShapeDtypeStruct(own.shape, jnp.float32),
                jax.ShapeDtypeStruct(own.shape, jnp.bfloat16),
            ],
            compiler_params=params(),
            name="dual_update",
        )(*parts, dual, cap)

    def by_row_block(array):
        return array.reshape(scen, row_tiles, side).transpose(1, 0, 2)

    def both_halves(own):
        other = swap_core(own)
        pieces = jnp.concatenate([jnp.where(core == 0, own, other), jnp.where(core == 0, other, own)], axis=0)
        return pieces.reshape(row_tiles, scen, side)

    rounded = by_row_block(dual_vars.astype(jnp.bfloat16))
    start = core * (row_tiles // 2)
    dual = lax.dynamic_slice_in_dim(by_row_block(dual_vars), start, row_tiles // 2, 0).reshape(half, side)
    cap = lax.dynamic_slice_in_dim(by_row_block(capacity), start, row_tiles // 2, 0).reshape(half, side)
    primal, cumulative = increments, None
    for sweep in range(ITERS):
        recv = lax.all_to_all(backward(rounded), ("row", "col"), 0, 0, tiled=True)
        primal, cumulative, send = primal_step(recv, primal, cumulative)
        probe = lax.all_to_all(send, ("row", "col"), 0, 0, tiled=True)
        dual, half_round = dual_step(forward(probe), dual, cap)
        if sweep + 1 < ITERS:
            rounded = both_halves(half_round)
    duals_out = both_halves(dual).transpose(1, 0, 2).reshape(scen, row_length)
    return (primal, duals_out)


def solution(mesh):
    placed = (
        P("row", "col", None, None, None),
        P("row", "col", None),
        P("row", "col", None),
        P("row", None, "col"),
        P(None, "row"),
        P(None, "col"),
        P("col"),
        P("col"),
        P(None, "row"),
    )
    return jax.shard_map(
        per_device,
        mesh=mesh,
        in_specs=placed,
        out_specs=(P("row", None, "col"), P(None, "row")),
        check_vma=False,
    )
```

time: 424 us -> 213 us (0.50); the launches traced: 418 us -> 212 us
  waiting for transfers between devices: 261 us -> 51.9 us
  blocking collectives: 31.9 us -> 91.8 us
  matrix products: 38.2 us -> 0 us
  local copies, waits for them, and re-layouts: 56.4 us -> 19.6 us
  Pallas kernels: 0 us -> 35.4 us
  between operations: 14.7 us -> 0.91 us
  other arithmetic: 11.3 us -> 1.59 us
  starting transfers between devices: 5.19 us -> 10.9 us
    psum x2 -> x0, waiting for transfers between devices: 111 us -> none  [per_device(): col_total = lax.psum(flattened, 'col')]
    reduce_scatter x2 -> x0, waiting for transfers between devices: 89.5 us -> none  [per_device(): lax.psum_scatter(jnp.einsum('cn,snj->scj', hot_cols, products, precision=...]
    all_to_all x3, blocking collectives: 31.9 us -> 91.8 us  [the longest x2 62.2 us: per_device(): recv = lax.all_to_all(backward(rounded), ('row', 'col'), 0, 0, tiled=True)]
    all_gather x2 -> x0, waiting for transfers between devices: 50.6 us -> none  [per_device(): gathered_part = lax.all_gather(probe_vec, 'row', axis=0, tiled=True)]
    dot_general x13 -> x0, matrix products: 38.2 us -> none  [the longest x2 13.7 us: per_device(): jnp.einsum('nij,snj->sni', blocks, image_picked, preferred_element_type=j...]
    pallas_call x0 -> x10, Pallas kernels: none -> 35.4 us  [the longest x2 17.4 us: forward(): pl.pallas_call(functools.partial(forward_kernel, dims), grid_spec=pltpu.P...]
    ppermute x0 -> x10, waiting for transfers between devices: none -> 25.7 us  [the longest x6 19.2 us: all_chips(): lax.ppermute(value, 'col', [(i, i ^ 2 * d) for i in range(n_col)])]
    all_to_all x1, waiting for transfers between devices: 8.79 us -> 26.2 us  [per_device(): probe = lax.all_to_all(send, ('row', 'col'), 0, 0, tiled=True)]
  transfers between devices with their start and end apart: 7 -> 11, of which waited for: 7 -> 11; matrix products, arithmetic and copies ran while one was open for 0% -> 2% of each run, Pallas kernels for 0% -> 0%
where the time goes in v1:
time: 213 us; the launch traced here: 212 us
  blocking collectives  91.8 us (43%)
  waiting for transfers between devices  51.9 us (24%)
  Pallas kernels  35.4 us (17%)
  local copies, waits for them, and re-layouts  19.6 us (9%)
  starting transfers between devices  10.9 us (5%)
    all_to_all x2, blocking collectives, per_device(): recv = lax.all_to_all(backward(rounded), ('row', 'col'), 0, 0, tiled=True)  62.2 us
    all_to_all x1, blocking collectives, per_device(): probe = lax.all_to_all(send, ('row', 'col'), 0, 0, tiled=True)  29.7 us
    all_to_all x1, waiting for transfers between devices, per_device(): probe = lax.all_to_all(send, ('row', 'col'), 0, 0, tiled=True)  26.2 us
    ppermute x6, waiting for transfers between devices, all_chips(): lax.ppermute(value, 'col', [(i, i ^ 2 * d) for i in range(n_col)])  19.2 us
    unnamed x28, local copies, waits for them, and re-layouts  18.4 us
    pallas_call x2, Pallas kernels, forward(): pl.pallas_call(functools.partial(forward_kernel, dims), grid_spec=pltpu.P...  17.4 us
    pallas_call x2, Pallas kernels, backward(): pl.pallas_call(functools.partial(backward_kernel, dims), grid_spec=pltpu....  12 us
    ppermute x6, starting transfers between devices, all_chips(): lax.ppermute(value, 'col', [(i, i ^ 2 * d) for i in range(n_col)])  7.11 us
  transfers between devices with their start and end apart: 11, of which 11 were waited for; matrix products, arithmetic and copies ran while one was open for 2% of the time, Pallas kernels for 0%

profile of v1, /device:TPU:0, one launch (start us, length us, event | category | flops | bytes accessed | tf_op | source)
XLA Modules:
  0.0 212.2 jit_solution(17510681935894178055)
XLA Ops:
  0.7 1.4 bitcast_bitcast_fusion.duals_ref
  2.1 3.4 %copy-done = bf16[1,1,256,128,128]{4,3,2,1,0:T(8,128)(2,1)S(1)} copy-done((bf16[1,1,256,128,128]{4,3,2,1,0:T(8,128)(2,1)S(1)}, bf16[1,1,256,128,128]{4,3,2,1,0:T(8,128)(2,1)}, u32[]{:S(2)}) %copy-start) | copy-done | bytes 8388632
  5.5 0.7 copy-done.6
  6.1 0.7 copy-done.8
  6.8 6.0 %backward_products.2 = bf16[32,128,128]{2,1,0:T(8,128)(2,1)S(1)} custom-call(s32[256]{0:T(256)S(1)} %bitcast.38, s32[256]{0:T(256)S(1)} %bitcast.42, bf16[128,16,128]{2,1,0:T(8,128)(2,1)S(1)} %bitcast_bitcast_fusion.duals_ref, bf16[256,128,128]{2,1,0:T(8,128)(2,1)S(1)} %bitcast.30), custom_call_target="tpu_custom_call" | custom-call | flops 134217728 | bytes 8388608 | tf_op jit(solution)/shard_map/backward_products/pallas_call | solution.py:204
  12.8 33.3 %all_to_all.20.refs_0_ = bf16[32,128,128]{2,1,0:T(8,128)(2,1)S(1)} all-to-all(bf16[32,128,128]{2,1,0:T(8,128)(2,1)S(1)} %backward_products.2), channel_id=1, replica_groups=mesh['row'=4,'col'=8] {'row','col'}, dimensions={0} | all-to-all | bytes 2097152 | tf_op jit(solution)/shard_map/all_to_all | solution.py:297
  46.2 2.7 %primal_update.2 = (f32[4,128,256]{2,1,0:T(8,128)S(1)}, f32[4,128,256]{2,1,0:T(8,128)S(1)}, bf16[32,128,128]{2,1,0:T(8,128)(2,1)}) custom-call(bf16[32,128,128]{2,1,0:T(8,128)(2,1)S(1)} %all_to_all.20.refs_0_, f32[4,128,256]{2,1,0:T(8,128)S(1)} %copy-done.4, f32[128,256]{1,0:T(8,128)S(1)} %copy-done.5, s32[1,256]{1,0:T(1,128)S(1)} %bitcast.46, ...), custom_call_target="tpu_custom_call" | custom-call | tf_op jit(solution)/shard_map/primal_update/pallas_call | solution.py:242
  48.9 3.6 %all-to-all-start.1 = ((bf16[32,128,128]{2,1,0:T(8,128)(2,1)}), bf16[32,128,128]{2,1,0:T(8,128)(2,1)S(1)}, u32[]{:S(2)}, u32[]{:S(2)}) async-start(bf16[32,128,128]{2,1,0:T(8,128)(2,1)} %get-tuple-element.10), calls=%async_computation.1 | async-start | bytes 2097152 | tf_op jit(solution)/shard_map/all_to_all | solution.py:299
  52.5 26.2 %all-to-all-done.1.probe_ref = bf16[32,128,128]{2,1,0:T(8,128)(2,1)S(1)} async-done(((bf16[32,128,128]{2,1,0:T(8,128)(2,1)}), bf16[32,128,128]{2,1,0:T(8,128)(2,1)S(1)}, u32[]{:S(2)}, u32[]{:S(2)}) %all-to-all-start.1) | async-done | bytes 1048608 | tf_op jit(solution)/shard_map/all_to_all | solution.py:299
  78.7 3.4 %copy-done.1 = bf16[1,1,256,128,128]{4,3,2,1,0:T(8,128)(2,1)S(1)} copy-done((bf16[1,1,256,128,128]{4,3,2,1,0:T(8,128)(2,1)S(1)}, bf16[1,1,256,128,128]{4,3,2,1,0:T(8,128)(2,1)}, u32[]{:S(2)}) %copy-start.1) | copy-done | bytes 8388632
  82.1 8.7 %forward_products.2 = bf16[2048,128]{1,0:T(8,128)(2,1)S(1)} custom-call(s32[256]{0:T(256)S(1)} %bitcast.39, s32[256]{0:T(256)S(1)} %bitcast.43, bf16[32,128,128]{2,1,0:T(8,128)(2,1)S(1)} %all-to-all-done.1.probe_ref, bf16[256,128,128]{2,1,0:T(8,128)(2,1)S(1)} %bitcast.31), custom_call_target="tpu_custom_call" | custom-call | flops 134217728 | bytes 8388608 | tf_op jit(solution)/shard_map/forward_products/pallas_call | solution.py:220
  90.9 0.1 collective-permute-start
  90.9 1.5 collective-permute-done.other_ref
  92.5 0.1 core_pair_sum.2.refs_0_
  92.5 2.5 %collective-permute-start.3 = (bf16[1024,128]{1,0:T(8,128)(2,1)S(1)}, bf16[1024,128]{1,0:T(8,128)(2,1)S(1)}, u32[]{:S(2)}, u32[]{:S(2)}) collective-permute-start(bf16[1024,128]{1,0:T(8,128)(2,1)S(1)} %core_pair_sum.2.refs_0_), channel_id=1, source_target_pairs={{0,6},{1,7},{2,4},{3,5},{4,2},{5,3},{6,0},{7,1},{8,14},{9,15},{10,... | collective-permute-start | bytes 786440 | tf_op jit(solution)/shard_map/ppermute | solution.py:256
  95.0 0.5 collective-permute-start.2
  95.5 0.6 collective-permute-start.1
  96.1 1.4 copy.23
  97.6 0.3 copy.19
  97.9 1.4 copy.22
  99.4 0.3 copy.18
  99.7 3.0 %collective-permute-done.3.refs_3_ = bf16[1024,128]{1,0:T(8,128)(2,1)S(1)} collective-permute-done((bf16[1024,128]{1,0:T(8,128)(2,1)S(1)}, bf16[1024,128]{1,0:T(8,128)(2,1)S(1)}, u32[]{:S(2)}, u32[]{:S(2)}) %collective-permute-start.3) | collective-permute-done | bytes 262176 | tf_op jit(solution)/shard_map/ppermute | solution.py:256
  102.7 4.8 %collective-permute-done.2.refs_2_ = bf16[1024,128]{1,0:T(8,128)(2,1)S(1)} collective-permute-done((bf16[1024,128]{1,0:T(8,128)(2,1)S(1)}, bf16[1024,128]{1,0:T(8,128)(2,1)S(1)}, u32[]{:S(2)}, u32[]{:S(2)}) %collective-permute-start.2) | collective-permute-done | bytes 262176 | tf_op jit(solution)/shard_map/ppermute | solution.py:256
  107.5 0.1 collective-permute-done.1.refs_1_
  107.5 0.2 dual_update.2
  107.7 0.1 collective-permute-start.4
  107.8 1.5 collective-permute-done.4
  109.4 3.4 %copy-done.2 = bf16[1,1,256,128,128]{4,3,2,1,0:T(8,128)(2,1)S(1)} copy-done((bf16[1,1,256,128,128]{4,3,2,1,0:T(8,128)(2,1)S(1)}, bf16[1,1,256,128,128]{4,3,2,1,0:T(8,128)(2,1)}, u32[]{:S(2)}) %copy-start.2) | copy-done | bytes 8388632
  112.8 6.0 %backward_products.3 = bf16[32,128,128]{2,1,0:T(8,128)(2,1)S(1)} custom-call(s32[256]{0:T(256)S(1)} %bitcast.40, s32[256]{0:T(256)S(1)} %bitcast.44, bf16[128,16,128]{2,1,0:T(8,128)(2,1)S(1)} %bitcast.37, bf16[256,128,128]{2,1,0:T(8,128)(2,1)S(1)} %bitcast.32), custom_call_target="tpu_custom_call" | custom-call | flops 134217728 | bytes 8388608 | tf_op jit(solution)/shard_map/backward_products/pallas_call | solution.py:204
  118.8 28.8 %all_to_all.21.refs_0_ = bf16[32,128,128]{2,1,0:T(8,128)(2,1)S(1)} all-to-all(bf16[32,128,128]{2,1,0:T(8,128)(2,1)S(1)} %backward_products.3), channel_id=1, replica_groups=mesh['row'=4,'col'=8] {'row','col'}, dimensions={0} | all-to-all | bytes 2097152 | tf_op jit(solution)/shard_map/all_to_all | solution.py:297
  147.6 2.1 %primal_update.3 = (f32[4,128,256]{2,1,0:T(8,128)}, f32[4,128,256]{2,1,0:T(8,128)}, bf16[32,128,128]{2,1,0:T(8,128)(2,1)S(1)}) custom-call(bf16[32,128,128]{2,1,0:T(8,128)(2,1)S(1)} %all_to_all.21.refs_0_, f32[4,128,256]{2,1,0:T(8,128)S(1)} %get-tuple-element.12.refs_1_, f32[4,128,256]{2,1,0:T(8,128)S(1)} %get-tuple-element.13.refs_2_, ...), custom_call_target="tpu_custom_call" | custom-call | tf_op jit(solution)/shard_map/primal_update/pallas_call | solution.py:242
  149.8 29.7 %all_to_all.22.probe_ref = bf16[32,128,128]{2,1,0:T(8,128)(2,1)S(1)} all-to-all(bf16[32,128,128]{2,1,0:T(8,128)(2,1)S(1)} %get-tuple-element.15), channel_id=1, replica_groups=mesh['row'=4,'col'=8] {'row','col'}, dimensions={0} | all-to-all | bytes 2097152 | tf_op jit(solution)/shard_map/all_to_all | solution.py:299
  179.4 3.4 %copy-done.3 = bf16[1,1,256,128,128]{4,3,2,1,0:T(8,128)(2,1)S(1)} copy-done((bf16[1,1,256,128,128]{4,3,2,1,0:T(8,128)(2,1)S(1)}, bf16[1,1,256,128,128]{4,3,2,1,0:T(8,128)(2,1)}, u32[]{:S(2)}) %copy-start.3) | copy-done | bytes 8388632
  182.8 8.7 %forward_products.3 = bf16[2048,128]{1,0:T(8,128)(2,1)S(1)} custom-call(s32[256]{0:T(256)S(1)} %bitcast.41, s32[256]{0:T(256)S(1)} %bitcast.45, bf16[32,128,128]{2,1,0:T(8,128)(2,1)S(1)} %all_to_all.22.probe_ref, bf16[256,128,128]{2,1,0:T(8,128)(2,1)S(1)} %bitcast.33), custom_call_target="tpu_custom_call" | custom-call | flops 134217728 | bytes 8388608 | tf_op jit(solution)/shard_map/forward_products/pallas_call | solution.py:220
  191.6 0.1 collective-permute-start.5
  191.6 1.5 collective-permute-done.5.other_ref
  193.2 0.1 core_pair_sum.3.refs_0_
  193.2 2.5 %collective-permute-start.8 = (bf16[1024,128]{1,0:T(8,128)(2,1)S(1)}, bf16[1024,128]{1,0:T(8,128)(2,1)S(1)}, u32[]{:S(2)}, u32[]{:S(2)}) collective-permute-start(bf16[1024,128]{1,0:T(8,128)(2,1)S(1)} %core_pair_sum.3.refs_0_), channel_id=1, source_target_pairs={{0,6},{1,7},{2,4},{3,5},{4,2},{5,3},{6,0},{7,1},{8,14},{9,15},{10,... | collective-permute-start | bytes 786440 | tf_op jit(solution)/shard_map/ppermute | solution.py:256
  195.7 0.5 collective-permute-start.7
  196.2 0.6 collective-permute-start.6
  196.8 6.6 %collective-permute-done.8.refs_3_ = bf16[1024,128]{1,0:T(8,128)(2,1)S(1)} collective-permute-done((bf16[1024,128]{1,0:T(8,128)(2,1)S(1)}, bf16[1024,128]{1,0:T(8,128)(2,1)S(1)}, u32[]{:S(2)}, u32[]{:S(2)}) %collective-permute-start.8) | collective-permute-done | bytes 262176 | tf_op jit(solution)/shard_map/ppermute | solution.py:256
  203.4 4.8 %collective-permute-done.7.refs_2_ = bf16[1024,128]{1,0:T(8,128)(2,1)S(1)} collective-permute-done((bf16[1024,128]{1,0:T(8,128)(2,1)S(1)}, bf16[1024,128]{1,0:T(8,128)(2,1)S(1)}, u32[]{:S(2)}, u32[]{:S(2)}) %collective-permute-start.7) | collective-permute-done | bytes 262176 | tf_op jit(solution)/shard_map/ppermute | solution.py:256
  208.2 0.1 collective-permute-done.6.refs_1_
  208.2 0.9 dual_update.3
  209.1 1.9 collective-permute-done.9
  211.0 0.1 broadcast_select_fusion.1
  211.1 0.1 pad_maximum_fusion
  211.2 1.0 copy.26
  (25 shorter events, 0.3 us)
Async XLA Ops:
  0.6 78.1 %copy-start.9 = (s32[1,1,256]{2,1,0:T(1,128)S(1)}, s32[1,1,256]{2,1,0:T(1,128)}, u32[]{:S(2)}) copy-start(s32[1,1,256]{2,1,0:T(1,128)} %param.11) | copy-start | bytes 3076
  0.6 78.1 %copy-start.7 = (s32[1,1,256]{2,1,0:T(1,128)S(1)}, s32[1,1,256]{2,1,0:T(1,128)}, u32[]{:S(2)}) copy-start(s32[1,1,256]{2,1,0:T(1,128)} %param.10) | copy-start | bytes 3076
  0.7 45.5 %copy-start.5 = (f32[128,256]{1,0:T(8,128)S(1)}, f32[128,256]{1,0:T(8,128)}, u32[]{:S(2)}) copy-start(f32[128,256]{1,0:T(8,128)} %refs_3_.1) | copy-start | bytes 393220
  0.7 45.5 %copy-start.11 = (s32[256]{0:T(256)S(1)}, s32[256]{0:T(256)}, u32[]{:S(2)}) copy-start(s32[256]{0:T(256)} %param.16) | copy-start | bytes 3076
  0.7 45.5 %copy-start.10 = (s32[256]{0:T(256)S(1)}, s32[256]{0:T(256)}, u32[]{:S(2)}) copy-start(s32[256]{0:T(256)} %param.15) | copy-start | bytes 3076
  0.7 45.5 %copy-start.4 = (f32[4,128,256]{2,1,0:T(8,128)S(1)}, f32[4,128,256]{2,1,0:T(8,128)}, u32[]{:S(2)}) copy-start(f32[4,128,256]{2,1,0:T(8,128)} %refs_1_.1) | copy-start | bytes 1572868
  2.1 3.4 %copy-start = (bf16[1,1,256,128,128]{4,3,2,1,0:T(8,128)(2,1)S(1)}, bf16[1,1,256,128,128]{4,3,2,1,0:T(8,128)(2,1)}, u32[]{:S(2)}) copy-start(bf16[1,1,256,128,128]{4,3,2,1,0:T(8,128)(2,1)} %param.9) | copy-start | bytes 25165828
  5.5 0.7 copy-start.6
  6.1 0.7 copy-start.8
  48.9 29.9 %all-to-all-start.1 = ((bf16[32,128,128]{2,1,0:T(8,128)(2,1)}), bf16[32,128,128]{2,1,0:T(8,128)(2,1)S(1)}, u32[]{:S(2)}, u32[]{:S(2)}) async-start(bf16[32,128,128]{2,1,0:T(8,128)(2,1)} %get-tuple-element.10), calls=%async_computation.1 | async-start | bytes 2097152 | tf_op jit(solution)/shard_map/all_to_all | solution.py:299
  78.7 3.4 %copy-start.1 = (bf16[1,1,256,128,128]{4,3,2,1,0:T(8,128)(2,1)S(1)}, bf16[1,1,256,128,128]{4,3,2,1,0:T(8,128)(2,1)}, u32[]{:S(2)}) copy-start(bf16[1,1,256,128,128]{4,3,2,1,0:T(8,128)(2,1)} %param.9) | copy-start | bytes 25165828
  90.9 1.6 collective-permute-start
  92.5 10.2 %collective-permute-start.3 = (bf16[1024,128]{1,0:T(8,128)(2,1)S(1)}, bf16[1024,128]{1,0:T(8,128)(2,1)S(1)}, u32[]{:S(2)}, u32[]{:S(2)}) collective-permute-start(bf16[1024,128]{1,0:T(8,128)(2,1)S(1)} %core_pair_sum.2.refs_0_), channel_id=1, source_target_pairs={{0,6},{1,7},{2,4},{3,5},{4,2},{5,3},{6,0},{7,1},{8,14},{9,15},{10,... | collective-permute-start | bytes 786440 | tf_op jit(solution)/shard_map/ppermute | solution.py:256
  95.0 12.5 %collective-permute-start.2 = (bf16[1024,128]{1,0:T(8,128)(2,1)S(1)}, bf16[1024,128]{1,0:T(8,128)(2,1)S(1)}, u32[]{:S(2)}, u32[]{:S(2)}) collective-permute-start(bf16[1024,128]{1,0:T(8,128)(2,1)S(1)} %core_pair_sum.2.refs_0_), channel_id=1, source_target_pairs={{0,4},{1,5},{2,6},{3,7},{4,0},{5,1},{6,2},{7,3},{8,12},{9,13},{10,... | collective-permute-start | bytes 786440 | tf_op jit(solution)/shard_map/ppermute | solution.py:256
  95.5 12.0 %collective-permute-start.1 = (bf16[1024,128]{1,0:T(8,128)(2,1)S(1)}, bf16[1024,128]{1,0:T(8,128)(2,1)S(1)}, u32[]{:S(2)}, u32[]{:S(2)}) collective-permute-start(bf16[1024,128]{1,0:T(8,128)(2,1)S(1)} %core_pair_sum.2.refs_0_), channel_id=1, source_target_pairs={{0,2},{1,3},{2,0},{3,1},{4,6},{5,7},{6,4},{7,5},{8,10},{9,11},{10,... | collective-permute-start | bytes 786440 | tf_op jit(solution)/shard_map/ppermute | solution.py:256
  107.7 1.6 collective-permute-start.4
  109.4 3.4 %copy-start.2 = (bf16[1,1,256,128,128]{4,3,2,1,0:T(8,128)(2,1)S(1)}, bf16[1,1,256,128,128]{4,3,2,1,0:T(8,128)(2,1)}, u32[]{:S(2)}) copy-start(bf16[1,1,256,128,128]{4,3,2,1,0:T(8,128)(2,1)} %param.9) | copy-start | bytes 25165828
  179.4 3.4 %copy-start.3 = (bf16[1,1,256,128,128]{4,3,2,1,0:T(8,128)(2,1)S(1)}, bf16[1,1,256,128,128]{4,3,2,1,0:T(8,128)(2,1)}, u32[]{:S(2)}) copy-start(bf16[1,1,256,128,128]{4,3,2,1,0:T(8,128)(2,1)} %param.9) | copy-start | bytes 25165828
  191.6 1.6 collective-permute-start.5
  193.2 10.2 %collective-permute-start.8 = (bf16[1024,128]{1,0:T(8,128)(2,1)S(1)}, bf16[1024,128]{1,0:T(8,128)(2,1)S(1)}, u32[]{:S(2)}, u32[]{:S(2)}) collective-permute-start(bf16[1024,128]{1,0:T(8,128)(2,1)S(1)} %core_pair_sum.3.refs_0_), channel_id=1, source_target_pairs={{0,6},{1,7},{2,4},{3,5},{4,2},{5,3},{6,0},{7,1},{8,14},{9,15},{10,... | collective-permute-start | bytes 786440 | tf_op jit(solution)/shard_map/ppermute | solution.py:256
  195.7 12.5 %collective-permute-start.7 = (bf16[1024,128]{1,0:T(8,128)(2,1)S(1)}, bf16[1024,128]{1,0:T(8,128)(2,1)S(1)}, u32[]{:S(2)}, u32[]{:S(2)}) collective-permute-start(bf16[1024,128]{1,0:T(8,128)(2,1)S(1)} %core_pair_sum.3.refs_0_), channel_id=1, source_target_pairs={{0,4},{1,5},{2,6},{3,7},{4,0},{5,1},{6,2},{7,3},{8,12},{9,13},{10,... | collective-permute-start | bytes 786440 | tf_op jit(solution)/shard_map/ppermute | solution.py:256
  196.2 12.0 %collective-permute-start.6 = (bf16[1024,128]{1,0:T(8,128)(2,1)S(1)}, bf16[1024,128]{1,0:T(8,128)(2,1)S(1)}, u32[]{:S(2)}, u32[]{:S(2)}) collective-permute-start(bf16[1024,128]{1,0:T(8,128)(2,1)S(1)} %core_pair_sum.3.refs_0_), channel_id=1, source_target_pairs={{0,2},{1,3},{2,0},{3,1},{4,6},{5,7},{6,4},{7,5},{8,10},{9,11},{10,... | collective-permute-start | bytes 786440 | tf_op jit(solution)/shard_map/ppermute | solution.py:256
  209.1 1.9 collective-permute-start.9

commit v2 on v1

v2 whole, which is shorter than its diff:
```python
import functools
import math

import jax
import jax.numpy as jnp
from jax import lax
from jax.experimental import pallas as pl
from jax.experimental.pallas import tpu as pltpu
from jax.sharding import PartitionSpec as P

ITERS = 2
SIGMA_STEP = 0.2
UNROLL = 32
PITCH_PAD = 8
VMEM_BYTES = 24 * 1024 * 1024
TRANSPOSED = (((1,), (1,)), ((), ()))


def params():
    return pltpu.CompilerParams(vmem_limit_bytes=VMEM_BYTES)


def whole():
    return pl.BlockSpec(memory_space=pltpu.VMEM)


def scalars():
    return pl.BlockSpec(memory_space=pltpu.SMEM)


def stacked_pair(first, second):
    zero = jnp.zeros_like(first)
    return jnp.concatenate(
        [jnp.concatenate([first, zero], axis=1), jnp.concatenate([zero, second], axis=1)], axis=0
    )


def column_place(dims, column, pitch):
    time_block, flight_tiles = dims[3], dims[4]
    return pl.multiple_of((column % flight_tiles * time_block + column // flight_tiles) * pitch, 8)


def backward_blocks(dims, pitch, rows_ref, cols_ref, duals_ref, tiles_ref, acc_ref, start):
    scen = dims[0] * dims[2]
    products = []
    for u in range(0, UNROLL, 2):
        pair = stacked_pair(duals_ref[rows_ref[start + u]], duals_ref[rows_ref[start + u + 1]])
        both = tiles_ref[pl.ds(start + u, 2)]
        result = jnp.dot(pair, both.reshape(-1, both.shape[2]), preferred_element_type=jnp.float32)
        products += [result[:scen], result[scen:]]
    for u in range(UNROLL):
        place = column_place(dims, cols_ref[start + u], pitch)
        acc_ref[pl.ds(place, scen), :] += products[u]


def write_messages(dims, pitch, acc_ref, out_ref):
    n_row, n_col, scen_local, time_block, _, own_tiles = dims
    piece = own_tiles * time_block
    for group in range(n_row):
        for column in range(n_col):
            for j in range(scen_local):
                base = column * own_tiles * time_block * pitch + group * scen_local + j
                parts = [
                    acc_ref[pl.ds(base + f * time_block * pitch, time_block, stride=pitch), :]
                    for f in range(own_tiles)
                ]
                out_ref[group * n_col + column, pl.ds(j * piece, piece), :] = jnp.concatenate(
                    parts, axis=0
                ).astype(jnp.bfloat16)


def first_backward_kernel(dims, pitch, rows_ref, cols_ref, dual_ref, source_ref, out_ref, tiles_ref, duals_ref, acc_ref, sems):
    count, parts = tiles_ref.shape[0], sems.shape[0]
    chunk = count // parts
    copies = [
        pltpu.make_async_copy(source_ref.at[pl.ds(i * chunk, chunk)], tiles_ref.at[pl.ds(i * chunk, chunk)], sems.at[i])
        for i in range(parts)
    ]
    for copy in copies:
        copy.start()
    bands = [dual_ref[a].astype(jnp.bfloat16) for a in range(dual_ref.shape[0])]
    duals_ref[...] = jnp.concatenate(bands, axis=1)
    acc_ref[...] = jnp.zeros_like(acc_ref)

    def body(index, _):
        backward_blocks(dims, pitch, rows_ref, cols_ref, duals_ref, tiles_ref, acc_ref, index * UNROLL)
        return 0

    for i, copy in enumerate(copies):
        copy.wait()
        lax.fori_loop(i * chunk // UNROLL, (i + 1) * chunk // UNROLL, body, 0)
    write_messages(dims, pitch, acc_ref, out_ref)


def backward_kernel(dims, pitch, core_ref, rows_ref, cols_ref, own_ref, other_ref, tiles_ref, out_ref, duals_ref, acc_ref):
    core = core_ref[0]
    half, scen, side = duals_ref.shape[0] // 2, duals_ref.shape[1], duals_ref.shape[2]
    duals_ref[pl.ds(core * half, half)] = own_ref[...].reshape(half, scen, side)
    duals_ref[pl.ds((1 - core) * half, half)] = other_ref[...].reshape(half, scen, side)
    acc_ref[...] = jnp.zeros_like(acc_ref)

    def body(index, _):
        backward_blocks(dims, pitch, rows_ref, cols_ref, duals_ref, tiles_ref, acc_ref, index * UNROLL)
        return 0

    lax.fori_loop(0, tiles_ref.shape[0] // UNROLL, body, 0)
    write_messages(dims, pitch, acc_ref, out_ref)


def forward_kernel(dims, pitch, core_ref, rows_ref, cols_ref, probe_ref, tiles_ref, own_ref, away_ref, flat_ref, acc_ref):
    n_row, n_col, scen_local, time_block, _, own_tiles = dims
    scen = n_row * scen_local
    piece = own_tiles * time_block
    core = core_ref[0]
    acc_ref[...] = jnp.zeros_like(acc_ref)
    for group in range(n_row):
        for column in range(n_col):
            for j in range(scen_local):
                base = column * own_tiles * time_block * pitch + group * scen_local + j
                block = probe_ref[group * n_col + column, pl.ds(j * piece, piece), :].astype(jnp.float32)
                for f in range(own_tiles):
                    flat_ref[pl.ds(base + f * time_block * pitch, time_block, stride=pitch), :] = block[
                        f * time_block : (f + 1) * time_block
                    ]

    def picked(index):
        return flat_ref[pl.ds(column_place(dims, cols_ref[index], pitch), scen), :].astype(jnp.bfloat16)

    def body(index, _):
        start = index * UNROLL
        products = []
        for u in range(0, UNROLL, 2):
            both = jnp.concatenate([tiles_ref[start + u], tiles_ref[start + u + 1]], axis=1)
            result = lax.dot_general(
                stacked_pair(picked(start + u), picked(start + u + 1)),
                both,
                TRANSPOSED,
                preferred_element_type=jnp.float32,
            )
            products += [result[:scen], result[scen:]]
        for u in range(UNROLL):
            place = pl.multiple_of(rows_ref[start + u] * scen, scen)
            acc_ref[pl.ds(place, scen), :] += products[u]
        return 0

    lax.fori_loop(0, tiles_ref.shape[0] // UNROLL, body, 0)
    half = acc_ref.shape[0] // 2
    own_ref[...] = acc_ref[pl.ds(pl.multiple_of(core * half, half), half), :]
    away_ref[...] = acc_ref[pl.ds(pl.multiple_of((1 - core) * half, half), half), :]


def running(values, trailing):
    length = values.shape[0]
    row_iota = lax.broadcasted_iota(jnp.int32, (length, length), 0)
    col_iota = lax.broadcasted_iota(jnp.int32, (length, length), 1)
    keep = (col_iota >= row_iota) if trailing else (row_iota >= col_iota)
    return jnp.dot(
        keep.astype(jnp.float32), values, precision=lax.Precision.HIGHEST, preferred_element_type=jnp.float32
    )


def primal_kernel(dims, first, *refs):
    n_row, n_col, scen_local, time_block, _, own_tiles = dims
    if first:
        recv_ref, inc_ref, cost_ref, start_ref, len_ref, inc_out, cum_out, send_ref = refs
    else:
        recv_ref, inc_ref, cum_ref, cost_ref, start_ref, len_ref, inc_out, cum_out, send_ref = refs
    window, flight_local = cost_ref.shape
    side = flight_local // own_tiles
    piece = own_tiles * time_block
    tau_step = 0.6 / math.sqrt(window)
    minutes = lax.broadcasted_iota(jnp.int32, (window, flight_local), 0)
    begin = start_ref[...]
    upper = ((minutes >= begin) & (minutes < begin + len_ref[...])).astype(jnp.float32)
    for j in range(scen_local):
        bands = []
        for h in range(n_col):
            total = recv_ref[h, pl.ds(j * piece, piece), :].astype(jnp.float32)
            for g in range(1, n_row):
                total = total + recv_ref[g * n_col + h, pl.ds(j * piece, piece), :].astype(jnp.float32)
            bands.append(
                jnp.concatenate([total[f * time_block : (f + 1) * time_block] for f in range(own_tiles)], axis=1)
            )
        slope = jnp.concatenate(bands, axis=0) + cost_ref[...]
        gradient = running(slope, True)
        old = inc_ref[j]
        old_sum = running(old, False) if first else cum_ref[j]
        fresh = jnp.clip(old - tau_step * gradient, 0.0, upper)
        inc_out[j] = fresh
        fresh_sum = running(fresh, False)
        cum_out[j] = fresh_sum
        probe = (2.0 * fresh_sum - old_sum).astype(jnp.bfloat16)
        for h in range(n_col):
            band = probe[h * time_block : (h + 1) * time_block]
            block = jnp.concatenate([band[:, f * side : (f + 1) * side] for f in range(own_tiles)], axis=0)
            for g in range(n_row):
                send_ref[g * n_col + h, pl.ds(j * piece, piece), :] = block


def pair_kernel(own_ref, other_ref, out_ref):
    out_ref[...] = (own_ref[...] + other_ref[...]).astype(jnp.bfloat16)


def dual_kernel(remote, first, core_ref, own_ref, other_ref, *refs):
    parts, (dual_ref, cap_ref, dual_out, round_out) = refs[:remote], refs[remote:]
    total = own_ref[...] + other_ref[...]
    for part in parts:
        total = total + part[...].astype(jnp.float32)
    bands, row_tiles, band, side = cap_ref.shape
    half = row_tiles // 2
    begin = core_ref[0] * half

    def own_half(ref):
        return jnp.concatenate([ref[a, pl.ds(begin, half)] for a in range(bands)], axis=1).reshape(-1, side)

    old = own_half(dual_ref) if first else dual_ref[...]
    fresh = jnp.maximum(old + SIGMA_STEP * (total - own_half(cap_ref).astype(jnp.float32)), 0.0)
    dual_out[...] = fresh
    round_out[...] = fresh.astype(jnp.bfloat16)


def assemble_kernel(core_ref, own_ref, other_ref, out_ref):
    bands, row_tiles, band, side = out_ref.shape
    half = row_tiles // 2
    for ref, begin in ((own_ref, core_ref[0] * half), (other_ref, (1 - core_ref[0]) * half)):
        value = ref[...].reshape(half, bands * band, side)
        for a in range(bands):
            out_ref[a, pl.ds(begin, half)] = value[:, a * band : (a + 1) * band]


def per_device(
    tile_values, tile_rows, tile_cols, increments, dual_vars, flight_cost, win_start, win_len, capacity
):
    n_row, n_col = lax.axis_size("row"), lax.axis_size("col")
    count, side = tile_values.shape[2], tile_values.shape[3]
    scen_local, window, flight_local = increments.shape
    scen, row_length = dual_vars.shape
    row_tiles = row_length // side
    time_block = window // n_col
    flight_tiles = flight_local * n_col // side
    own_tiles = flight_local // side
    col_tiles = time_block * flight_tiles
    dims = (n_row, n_col, scen_local, time_block, flight_tiles, own_tiles)
    message = (n_row * n_col, scen_local * own_tiles * time_block, side)
    half = row_tiles * scen // 2
    pitch = scen + PITCH_PAD
    band = 8

    rows, cols = tile_rows.reshape(count), tile_cols.reshape(count)
    core = (lax.axis_index("col") % 2).reshape(1)
    cost = pl.CostEstimate(flops=2 * count * scen * side * side, bytes_accessed=count * side * side, transcendentals=0)
    acc_cols = pltpu.VMEM((col_tiles * pitch, side), jnp.float32)
    picked_duals = pltpu.VMEM((row_tiles, scen, side), jnp.bfloat16)
    messages = jax.ShapeDtypeStruct(message, jnp.bfloat16)
    half_f32 = jax.ShapeDtypeStruct((half, side), jnp.float32)
    half_bf16 = jax.ShapeDtypeStruct((half, side), jnp.bfloat16)

    def banded(array):
        return array.reshape(scen // band, band, row_tiles, side).transpose(0, 2, 1, 3)

    def first_backward(duals):
        return pl.pallas_call(
            functools.partial(first_backward_kernel, dims, pitch),
            in_specs=[scalars(), scalars(), whole(), pl.BlockSpec(memory_space=pltpu.HBM)],
            out_specs=[whole(), whole()],
            out_shape=[messages, pltpu.VMEM((count, side, side), jnp.bfloat16)],
            scratch_shapes=[picked_duals, acc_cols, pltpu.SemaphoreType.DMA((8,))],
            compiler_params=params(),
            cost_estimate=cost,
            name="first_backward_products",
        )(rows, cols, duals, pltpu.with_memory_space_constraint(tile_values.reshape(count, side, side), pltpu.HBM))

    def backward(own, other, tiles):
        return pl.pallas_call(
            functools.partial(backward_kernel, dims, pitch),
            in_specs=[scalars()] * 3 + [whole()] * 3,
            out_specs=whole(),
            out_shape=messages,
            scratch_shapes=[picked_duals, acc_cols],
            compiler_params=params(),
            cost_estimate=cost,
            name="backward_products",
        )(core, rows, cols, own, other, pltpu.with_memory_space_constraint(tiles, pltpu.VMEM))

    def forward(probe, tiles):
        return pl.pallas_call(
            functools.partial(forward_kernel, dims, pitch),
            in_specs=[scalars()] * 3 + [whole()] * 2,
            out_specs=[whole()] * 2,
            out_shape=[half_f32] * 2,
            scratch_shapes=[acc_cols, pltpu.VMEM((row_tiles * scen, side), jnp.float32)],
            compiler_params=params(),
            cost_estimate=cost,
            name="forward_products",
        )(core, rows, cols, probe, pltpu.with_memory_space_constraint(tiles, pltpu.VMEM))

    def primal_step(recv, primal, cumulative):
        first = cumulative is None
        state = (primal,) if first else (primal, cumulative)
        shape = jax.ShapeDtypeStruct(primal.shape, jnp.float32)
        return pl.pallas_call(
            functools.partial(primal_kernel, dims, first),
            in_specs=[whole()] * (4 + len(state)),
            out_specs=[whole()] * 3,
            out_shape=[shape, shape, messages],
            compiler_params=params(),
            name="primal_update",
        )(recv, *state, flight_cost, win_start.reshape(1, -1), win_len.reshape(1, -1))

    def swap_core(value):
        return lax.ppermute(value, "col", [(i, i ^ 1) for i in range(n_col)])

    def all_chips(value):
        return [
            lax.ppermute(value, "col", [(i, i ^ (2 * d)) for i in range(n_col)]) for d in range(1, n_col // 2)
        ]

    def dual_step(own, away, dual, first):
        other = swap_core(away)
        pair = pl.pallas_call(
            pair_kernel,
            in_specs=[whole()] * 2,
            out_specs=whole(),
            out_shape=half_bf16,
            compiler_params=params(),
            name="core_pair_sum",
        )(own, other)
        parts = all_chips(pair)
        return pl.pallas_call(
            functools.partial(dual_kernel, len(parts), first),
            in_specs=[scalars()] + [whole()] * (len(parts) + 4),
            out_specs=[whole()] * 2,
            out_shape=[half_f32, half_bf16],
            compiler_params=params(),
            name="dual_update",
        )(core, own, other, *parts, dual, banded(capacity))

    def assemble(own):
        return pl.pallas_call(
            assemble_kernel,
            in_specs=[scalars()] + [whole()] * 2,
            out_specs=whole(),
            out_shape=jax.ShapeDtypeStruct((scen // band, row_tiles, band, side), jnp.float32),
            compiler_params=params(),
            name="assemble_duals",
        )(core, own, swap_core(own))

    send, tiles = first_backward(banded(dual_vars))
    dual, primal, cumulative = banded(dual_vars), increments, None
    for sweep in range(ITERS):
        if sweep:
            send = backward(half_round, swap_core(half_round), tiles)
        recv = lax.all_to_all(send, ("row", "col"), 0, 0, tiled=True)
        primal, cumulative, send = primal_step(recv, primal, cumulative)
        probe = lax.all_to_all(send, ("row", "col"), 0, 0, tiled=True)
        own, away = forward(probe, tiles)
        dual, half_round = dual_step(own, away, dual, sweep == 0)
    duals_out = assemble(dual).transpose(0, 2, 1, 3).reshape(scen, row_length)
    return (primal, duals_out)


def solution(mesh):
    placed = (
        P("row", "col", None, None, None),
        P("row", "col", None),
        P("row", "col", None),
        P("row", None, "col"),
        P(None, "row"),
        P(None, "col"),
        P("col"),
        P("col"),
        P(None, "row"),
    )
    return jax.shard_map(
        per_device,
        mesh=mesh,
        in_specs=placed,
        out_specs=(P("row", None, "col"), P(None, "row")),
        check_vma=False,
    )
```

time: 213 us -> 196 us (0.920)
  Pallas kernels: 35.4 us -> 24.3 us
  local copies, waits for them, and re-layouts: 19.6 us -> 11.9 us
  waiting for transfers between devices: 51.9 us -> 56.3 us
    pallas_call x8 -> x9, Pallas kernels: 30.6 us -> 20.5 us  [the longest x2 9.5 us: forward(): pl.pallas_call(functools.partial(forward_kernel, dims, pitch), in_specs=[...]
    unnamed x28 -> x38, local copies, waits for them, and re-layouts: 18.4 us -> 11.9 us
    ppermute x6, waiting for transfers between devices: 19.2 us -> 22.9 us  [all_chips(): lax.ppermute(value, 'col', [(i, i ^ 2 * d) for i in range(n_col)])]
  transfers between devices with their start and end apart: 11 -> 11, of which waited for: 11 -> 11; matrix products, arithmetic and copies ran while one was open for 2% -> 0% of each run, Pallas kernels for 0% -> 0%
where the time goes in v2:
time: 196 us
  blocking collectives  91.8 us (47%)
  waiting for transfers between devices  56.3 us (29%)
  Pallas kernels  24.3 us (12%)
  local copies, waits for them, and re-layouts  11.9 us (6%)
  starting transfers between devices  10.9 us (6%)
    all_to_all x2, blocking collectives, per_device(): recv = lax.all_to_all(send, ('row', 'col'), 0, 0, tiled=True)  62.2 us
    all_to_all x1, blocking collectives, per_device(): probe = lax.all_to_all(send, ('row', 'col'), 0, 0, tiled=True)  29.7 us
    all_to_all x1, waiting for transfers between devices, per_device(): probe = lax.all_to_all(send, ('row', 'col'), 0, 0, tiled=True)  26.2 us
    ppermute x6, waiting for transfers between devices, all_chips(): lax.ppermute(value, 'col', [(i, i ^ 2 * d) for i in range(n_col)])  22.9 us
    unnamed x38, local copies, waits for them, and re-layouts  11.9 us
    pallas_call x2, Pallas kernels, forward(): pl.pallas_call(functools.partial(forward_kernel, dims, pitch), in_specs=[...  9.5 us
    ppermute x4, waiting for transfers between devices, swap_core(): return lax.ppermute(value, 'col', [(i, i ^ 1) for i in range(n_col)])  7.22 us
    ppermute x6, starting transfers between devices, all_chips(): lax.ppermute(value, 'col', [(i, i ^ 2 * d) for i in range(n_col)])  7.11 us
  transfers between devices with their start and end apart: 11, of which 11 were waited for; matrix products, arithmetic and copies ran while one was open for 0% of the time, Pallas kernels for 0%

profile of v2, /device:TPU:0, one launch (start us, length us, event | category | flops | bytes accessed | tf_op | source)
XLA Modules:
  0.0 196.1 jit_solution(6665124611628111533)
XLA Ops:
  0.7 0.0 copy-start.3
  0.7 1.2 copy-done.3
  1.9 0.7 copy-done.13
  2.6 0.7 copy-done.15
  3.3 4.7 %first_backward_products.1 = (bf16[32,128,128]{2,1,0:T(8,128)(2,1)S(1)}, bf16[256,128,128]{2,1,0:T(8,128)(2,1)S(1)}) custom-call(s32[256]{0:T(256)S(1)} %bitcast.19, s32[256]{0:T(256)S(1)} %bitcast.23, f32[2,128,8,128]{3,2,1,0:T(8,128)S(1)} %bitcast.15, bf16[256,128,128]{2,1,0:T(8,128)(2,1)} %bitcast.31), custom_call_target="tpu_custom_call" | custom-call | flops 134217728 | bytes 4194304 | tf_op jit(solution)/shard_map/first_backward_products/pallas_call | solution.py:262
  8.0 3.3 %copy-done = bf16[256,128,128]{2,1,0:T(8,128)(2,1)} copy-done((bf16[256,128,128]{2,1,0:T(8,128)(2,1)}, bf16[256,128,128]{2,1,0:T(8,128)(2,1)S(1)}, u32[]{:S(2)}) %copy-start) | copy-done | bytes 8388632
  11.2 33.3 %all_to_all.20.refs_0_ = bf16[32,128,128]{2,1,0:T(8,128)(2,1)S(1)} all-to-all(bf16[32,128,128]{2,1,0:T(8,128)(2,1)S(1)} %get-tuple-element.16), channel_id=1, replica_groups=mesh['row'=4,'col'=8] {'row','col'}, dimensions={0} | all-to-all | bytes 2097152 | tf_op jit(solution)/shard_map/all_to_all | solution.py:353
  44.6 0.0 copy-done.11
  44.6 0.0 copy-done.12
  44.6 1.7 primal_update.2
  46.3 0.0 copy-start.6
  46.3 1.0 copy-done.6
  47.3 0.8 copy-done.7
  48.1 0.8 copy-done.9
  48.9 3.6 %all-to-all-start.1 = ((bf16[32,128,128]{2,1,0:T(8,128)(2,1)}), bf16[32,128,128]{2,1,0:T(8,128)(2,1)S(1)}, u32[]{:S(2)}, u32[]{:S(2)}) async-start(bf16[32,128,128]{2,1,0:T(8,128)(2,1)} %copy-done.6), calls=%async_computation.1 | async-start | bytes 2097152 | tf_op jit(solution)/shard_map/all_to_all | solution.py:355
  52.6 26.2 %all-to-all-done.1.probe_ref = bf16[32,128,128]{2,1,0:T(8,128)(2,1)S(1)} async-done(((bf16[32,128,128]{2,1,0:T(8,128)(2,1)}), bf16[32,128,128]{2,1,0:T(8,128)(2,1)S(1)}, u32[]{:S(2)}, u32[]{:S(2)}) %all-to-all-start.1) | async-done | bytes 1048608 | tf_op jit(solution)/shard_map/all_to_all | solution.py:355
  78.8 0.0 copy-done.16
  78.8 3.4 %copy-done.1 = bf16[256,128,128]{2,1,0:T(8,128)(2,1)S(1)} copy-done((bf16[256,128,128]{2,1,0:T(8,128)(2,1)S(1)}, bf16[256,128,128]{2,1,0:T(8,128)(2,1)}, u32[]{:S(2)}) %copy-start.1) | copy-done | bytes 8388632
  82.2 4.8 %forward_products.2 = (f32[1024,128]{1,0:T(8,128)S(1)}, f32[1024,128]{1,0:T(8,128)S(1)}) custom-call(s32[1]{0:T(128)} %bitcast.core_ref, s32[256]{0:T(256)S(1)} %bitcast.20, s32[256]{0:T(256)S(1)} %bitcast.24, bf16[32,128,128]{2,1,0:T(8,128)(2,1)S(1)} %all-to-all-done.1.probe_ref, bf16[256,128,128]{2,1,0:T(8,128)(2,1)S(1)} %copy-done.1), custom_call_target="tpu_custom_call" | custom-call | flops 134217728 | bytes 4194304 | tf_op jit(solution)/shard_map/forward_products/pallas_call | solution.py:286
  86.9 0.1 collective-permute-start
  87.0 1.9 collective-permute-done.other_ref
  89.0 2.5 %collective-permute-start.3 = (bf16[1024,128]{1,0:T(8,128)(2,1)S(1)}, bf16[1024,128]{1,0:T(8,128)(2,1)S(1)}, u32[]{:S(2)}, u32[]{:S(2)}) collective-permute-start(bf16[1024,128]{1,0:T(8,128)(2,1)S(1)} %core_pair_sum.2), channel_id=1, source_target_pairs={{0,6},{1,7},{2,4},{3,5},{4,2},{5,3},{6,0},{7,1},{8,14},{9,15},{10,... | collective-permute-start | bytes 786440 | tf_op jit(solution)/shard_map/ppermute | solution.py:315
  91.4 0.5 collective-permute-start.2
  92.0 0.6 collective-permute-start.1
  92.5 6.6 %collective-permute-done.3.refs_2_ = bf16[1024,128]{1,0:T(8,128)(2,1)S(1)} collective-permute-done((bf16[1024,128]{1,0:T(8,128)(2,1)S(1)}, bf16[1024,128]{1,0:T(8,128)(2,1)S(1)}, u32[]{:S(2)}, u32[]{:S(2)}) %collective-permute-start.3) | collective-permute-done | bytes 262176 | tf_op jit(solution)/shard_map/ppermute | solution.py:315
  99.1 4.8 %collective-permute-done.2.refs_1_ = bf16[1024,128]{1,0:T(8,128)(2,1)S(1)} collective-permute-done((bf16[1024,128]{1,0:T(8,128)(2,1)S(1)}, bf16[1024,128]{1,0:T(8,128)(2,1)S(1)}, u32[]{:S(2)}, u32[]{:S(2)}) %collective-permute-start.2) | collective-permute-done | bytes 262176 | tf_op jit(solution)/shard_map/ppermute | solution.py:315
  103.9 0.1 collective-permute-done.1.refs_0_
  104.0 0.0 copy-done.5
  104.0 0.2 dual_update.2
  104.2 0.1 collective-permute-start.4
  104.3 1.5 collective-permute-done.4.other_ref
  105.8 4.0 %backward_products.1 = bf16[32,128,128]{2,1,0:T(8,128)(2,1)S(1)} custom-call(s32[1]{0:T(128)} %bitcast.core_ref, s32[256]{0:T(256)S(1)} %bitcast.21, s32[256]{0:T(256)S(1)} %bitcast.25, bf16[1024,128]{1,0:T(8,128)(2,1)S(1)} %get-tuple-element.21.own_ref, bf16[1024,128]{1,0:T(8,128)(2,1)S(1)} %collective-permute-done.4.other_ref, ...), custom_call_target="tpu_custom_call" | custom-call | flops 134217728 | bytes 4194304 | tf_op jit(solution)/shard_map/backward_products/pallas_call | solution.py:274
  109.8 28.8 %all_to_all.21.refs_0_ = bf16[32,128,128]{2,1,0:T(8,128)(2,1)S(1)} all-to-all(bf16[32,128,128]{2,1,0:T(8,128)(2,1)S(1)} %backward_products.1), channel_id=1, replica_groups=mesh['row'=4,'col'=8] {'row','col'}, dimensions={0} | all-to-all | bytes 2097152 | tf_op jit(solution)/shard_map/all_to_all | solution.py:353
  138.7 2.1 %primal_update.3 = (f32[4,128,256]{2,1,0:T(8,128)}, f32[4,128,256]{2,1,0:T(8,128)}, bf16[32,128,128]{2,1,0:T(8,128)(2,1)S(1)}) custom-call(bf16[32,128,128]{2,1,0:T(8,128)(2,1)S(1)} %all_to_all.21.refs_0_, f32[4,128,256]{2,1,0:T(8,128)S(1)} %copy-done.8, f32[4,128,256]{2,1,0:T(8,128)S(1)} %copy-done.10, f32[128,256]{1,0:T(8,128)S(1)} %copy-done.12, ...), custom_call_target="tpu_custom_call" | custom-call | tf_op jit(solution)/shard_map/primal_update/pallas_call | solution.py:301
  140.8 29.7 %all_to_all.22.probe_ref = bf16[32,128,128]{2,1,0:T(8,128)(2,1)S(1)} all-to-all(bf16[32,128,128]{2,1,0:T(8,128)(2,1)S(1)} %get-tuple-element.25), channel_id=1, replica_groups=mesh['row'=4,'col'=8] {'row','col'}, dimensions={0} | all-to-all | bytes 2097152 | tf_op jit(solution)/shard_map/all_to_all | solution.py:355
  170.5 4.8 %forward_products.3 = (f32[1024,128]{1,0:T(8,128)S(1)}, f32[1024,128]{1,0:T(8,128)S(1)}) custom-call(s32[1]{0:T(128)} %bitcast.core_ref, s32[256]{0:T(256)S(1)} %bitcast.22, s32[256]{0:T(256)S(1)} %bitcast.26, bf16[32,128,128]{2,1,0:T(8,128)(2,1)S(1)} %all_to_all.22.probe_ref, bf16[256,128,128]{2,1,0:T(8,128)(2,1)S(1)} %copy-done.2), custom_call_target="tpu_custom_call" | custom-call | flops 134217728 | bytes 4194304 | tf_op jit(solution)/shard_map/forward_products/pallas_call | solution.py:286
  175.2 0.1 collective-permute-start.5
  175.3 1.9 collective-permute-done.5.other_ref
  177.2 2.5 %collective-permute-start.8 = (bf16[1024,128]{1,0:T(8,128)(2,1)S(1)}, bf16[1024,128]{1,0:T(8,128)(2,1)S(1)}, u32[]{:S(2)}, u32[]{:S(2)}) collective-permute-start(bf16[1024,128]{1,0:T(8,128)(2,1)S(1)} %core_pair_sum.3), channel_id=1, source_target_pairs={{0,6},{1,7},{2,4},{3,5},{4,2},{5,3},{6,0},{7,1},{8,14},{9,15},{10,... | collective-permute-start | bytes 786440 | tf_op jit(solution)/shard_map/ppermute | solution.py:315
  179.7 0.5 collective-permute-start.7
  180.2 0.6 collective-permute-start.6
  180.8 6.6 %collective-permute-done.8.refs_2_ = bf16[1024,128]{1,0:T(8,128)(2,1)S(1)} collective-permute-done((bf16[1024,128]{1,0:T(8,128)(2,1)S(1)}, bf16[1024,128]{1,0:T(8,128)(2,1)S(1)}, u32[]{:S(2)}, u32[]{:S(2)}) %collective-permute-start.8) | collective-permute-done | bytes 262176 | tf_op jit(solution)/shard_map/ppermute | solution.py:315
  187.4 4.8 %collective-permute-done.7.refs_1_ = bf16[1024,128]{1,0:T(8,128)(2,1)S(1)} collective-permute-done((bf16[1024,128]{1,0:T(8,128)(2,1)S(1)}, bf16[1024,128]{1,0:T(8,128)(2,1)S(1)}, u32[]{:S(2)}, u32[]{:S(2)}) %collective-permute-start.7) | collective-permute-done | bytes 262176 | tf_op jit(solution)/shard_map/ppermute | solution.py:315
  192.2 0.1 collective-permute-done.6.refs_0_
  192.2 0.9 dual_update.3
  193.2 0.0 collective-permute-start.9
  193.2 1.9 collective-permute-done.9.other_ref
  195.1 1.0 assemble_duals.1
  (26 shorter events, 0.1 us)
Async XLA Ops:
  0.6 78.2 %copy-start.16 = (s32[1,1,256]{2,1,0:T(1,128)S(1)}, s32[1,1,256]{2,1,0:T(1,128)}, u32[]{:S(2)}) copy-start(s32[1,1,256]{2,1,0:T(1,128)} %param.11) | copy-start | bytes 3076
  0.6 78.1 %copy-start.14 = (s32[1,1,256]{2,1,0:T(1,128)S(1)}, s32[1,1,256]{2,1,0:T(1,128)}, u32[]{:S(2)}) copy-start(s32[1,1,256]{2,1,0:T(1,128)} %param.10) | copy-start | bytes 3076
  0.7 43.9 %copy-start.18 = (s32[256]{0:T(256)S(1)}, s32[256]{0:T(256)}, u32[]{:S(2)}) copy-start(s32[256]{0:T(256)} %param.16) | copy-start | bytes 3076
  0.7 43.9 %copy-start.17 = (s32[256]{0:T(256)S(1)}, s32[256]{0:T(256)}, u32[]{:S(2)}) copy-start(s32[256]{0:T(256)} %param.15) | copy-start | bytes 3076
  0.7 1.2 copy-start.3
  1.9 0.7 copy-start.13
  2.6 0.7 copy-start.15
  3.3 41.3 %copy-start.11 = (f32[4,128,256]{2,1,0:T(8,128)S(1)}, f32[4,128,256]{2,1,0:T(8,128)}, u32[]{:S(2)}) copy-start(f32[4,128,256]{2,1,0:T(8,128)} %refs_1_.1) | copy-start | bytes 1572868
  3.3 41.3 %copy-start.12 = (f32[128,256]{1,0:T(8,128)S(1)}, f32[128,256]{1,0:T(8,128)}, u32[]{:S(2)}) copy-start(f32[128,256]{1,0:T(8,128)} %refs_3_.1) | copy-start | bytes 393220
  8.0 3.3 %copy-start = (bf16[256,128,128]{2,1,0:T(8,128)(2,1)}, bf16[256,128,128]{2,1,0:T(8,128)(2,1)S(1)}, u32[]{:S(2)}) copy-start(bf16[256,128,128]{2,1,0:T(8,128)(2,1)S(1)} %get-tuple-element.18.tiles_ref) | copy-start | bytes 25165828
  11.2 92.7 %copy-start.4 = (f32[16,16384]{1,0:T(8,128)S(1)}, f32[16,16384]{1,0:T(8,128)}, u32[]{:S(2)}) copy-start(f32[16,16384]{1,0:T(8,128)} %param.13) | copy-start | bytes 3145732
  11.2 92.7 %copy-start.5 = (s32[16,16384]{1,0:T(8,128)S(1)}, s32[16,16384]{1,0:T(8,128)}, u32[]{:S(2)}) copy-start(s32[16,16384]{1,0:T(8,128)} %param.17) | copy-start | bytes 3145732
  46.3 1.0 copy-start.6
  47.3 0.8 copy-start.7
  48.1 0.8 copy-start.9
  48.9 29.9 %all-to-all-start.1 = ((bf16[32,128,128]{2,1,0:T(8,128)(2,1)}), bf16[32,128,128]{2,1,0:T(8,128)(2,1)S(1)}, u32[]{:S(2)}, u32[]{:S(2)}) async-start(bf16[32,128,128]{2,1,0:T(8,128)(2,1)} %copy-done.6), calls=%async_computation.1 | async-start | bytes 2097152 | tf_op jit(solution)/shard_map/all_to_all | solution.py:355
  78.8 3.4 %copy-start.1 = (bf16[256,128,128]{2,1,0:T(8,128)(2,1)S(1)}, bf16[256,128,128]{2,1,0:T(8,128)(2,1)}, u32[]{:S(2)}) copy-start(bf16[256,128,128]{2,1,0:T(8,128)(2,1)} %copy-done) | copy-start | bytes 25165828
  82.2 23.6 %copy-start.2 = (bf16[256,128,128]{2,1,0:T(8,128)(2,1)S(1)}, bf16[256,128,128]{2,1,0:T(8,128)(2,1)}, u32[]{:S(2)}) copy-start(bf16[256,128,128]{2,1,0:T(8,128)(2,1)} %copy-done) | copy-start | bytes 25165828
  86.9 2.0 %collective-permute-start = (f32[1024,128]{1,0:T(8,128)S(1)}, f32[1024,128]{1,0:T(8,128)S(1)}, u32[]{:S(2)}, u32[]{:S(2)}) collective-permute-start(f32[1024,128]{1,0:T(8,128)S(1)} %get-tuple-element.20), channel_id=1, source_target_pairs={{0,1},{1,0},{2,3},{3,2},{4,5},{5,4},{6,7},{7,6},{8,9},{9,8},{10,11... | collective-permute-start | bytes 1572872 | tf_op jit(solution)/shard_map/ppermute | solution.py:311
  88.9 49.7 %copy-start.8 = (f32[4,128,256]{2,1,0:T(8,128)S(1)}, f32[4,128,256]{2,1,0:T(8,128)}, u32[]{:S(2)}) copy-start(f32[4,128,256]{2,1,0:T(8,128)} %copy-done.7) | copy-start | bytes 1572868
  88.9 49.7 %copy-start.10 = (f32[4,128,256]{2,1,0:T(8,128)S(1)}, f32[4,128,256]{2,1,0:T(8,128)}, u32[]{:S(2)}) copy-start(f32[4,128,256]{2,1,0:T(8,128)} %copy-done.9) | copy-start | bytes 1572868
  89.0 10.2 %collective-permute-start.3 = (bf16[1024,128]{1,0:T(8,128)(2,1)S(1)}, bf16[1024,128]{1,0:T(8,128)(2,1)S(1)}, u32[]{:S(2)}, u32[]{:S(2)}) collective-permute-start(bf16[1024,128]{1,0:T(8,128)(2,1)S(1)} %core_pair_sum.2), channel_id=1, source_target_pairs={{0,6},{1,7},{2,4},{3,5},{4,2},{5,3},{6,0},{7,1},{8,14},{9,15},{10,... | collective-permute-start | bytes 786440 | tf_op jit(solution)/shard_map/ppermute | solution.py:315
  91.4 12.5 %collective-permute-start.2 = (bf16[1024,128]{1,0:T(8,128)(2,1)S(1)}, bf16[1024,128]{1,0:T(8,128)(2,1)S(1)}, u32[]{:S(2)}, u32[]{:S(2)}) collective-permute-start(bf16[1024,128]{1,0:T(8,128)(2,1)S(1)} %core_pair_sum.2), channel_id=1, source_target_pairs={{0,4},{1,5},{2,6},{3,7},{4,0},{5,1},{6,2},{7,3},{8,12},{9,13},{10,... | collective-permute-start | bytes 786440 | tf_op jit(solution)/shard_map/ppermute | solution.py:315
  92.0 12.0 %collective-permute-start.1 = (bf16[1024,128]{1,0:T(8,128)(2,1)S(1)}, bf16[1024,128]{1,0:T(8,128)(2,1)S(1)}, u32[]{:S(2)}, u32[]{:S(2)}) collective-permute-start(bf16[1024,128]{1,0:T(8,128)(2,1)S(1)} %core_pair_sum.2), channel_id=1, source_target_pairs={{0,2},{1,3},{2,0},{3,1},{4,6},{5,7},{6,4},{7,5},{8,10},{9,11},{10,... | collective-permute-start | bytes 786440 | tf_op jit(solution)/shard_map/ppermute | solution.py:315
  104.2 1.6 collective-permute-start.4
  175.2 2.0 %collective-permute-start.5 = (f32[1024,128]{1,0:T(8,128)S(1)}, f32[1024,128]{1,0:T(8,128)S(1)}, u32[]{:S(2)}, u32[]{:S(2)}) collective-permute-start(f32[1024,128]{1,0:T(8,128)S(1)} %get-tuple-element.27), channel_id=1, source_target_pairs={{0,1},{1,0},{2,3},{3,2},{4,5},{5,4},{6,7},{7,6},{8,9},{9,8},{10,11... | collective-permute-start | bytes 1572872 | tf_op jit(solution)/shard_map/ppermute | solution.py:311
  177.2 10.2 %collective-permute-start.8 = (bf16[1024,128]{1,0:T(8,128)(2,1)S(1)}, bf16[1024,128]{1,0:T(8,128)(2,1)S(1)}, u32[]{:S(2)}, u32[]{:S(2)}) collective-permute-start(bf16[1024,128]{1,0:T(8,128)(2,1)S(1)} %core_pair_sum.3), channel_id=1, source_target_pairs={{0,6},{1,7},{2,4},{3,5},{4,2},{5,3},{6,0},{7,1},{8,14},{9,15},{10,... | collective-permute-start | bytes 786440 | tf_op jit(solution)/shard_map/ppermute | solution.py:315
  179.7 12.5 %collective-permute-start.7 = (bf16[1024,128]{1,0:T(8,128)(2,1)S(1)}, bf16[1024,128]{1,0:T(8,128)(2,1)S(1)}, u32[]{:S(2)}, u32[]{:S(2)}) collective-permute-start(bf16[1024,128]{1,0:T(8,128)(2,1)S(1)} %core_pair_sum.3), channel_id=1, source_target_pairs={{0,4},{1,5},{2,6},{3,7},{4,0},{5,1},{6,2},{7,3},{8,12},{9,13},{10,... | collective-permute-start | bytes 786440 | tf_op jit(solution)/shard_map/ppermute | solution.py:315
  180.2 12.0 %collective-permute-start.6 = (bf16[1024,128]{1,0:T(8,128)(2,1)S(1)}, bf16[1024,128]{1,0:T(8,128)(2,1)S(1)}, u32[]{:S(2)}, u32[]{:S(2)}) collective-permute-start(bf16[1024,128]{1,0:T(8,128)(2,1)S(1)} %core_pair_sum.3), channel_id=1, source_target_pairs={{0,2},{1,3},{2,0},{3,1},{4,6},{5,7},{6,4},{7,5},{8,10},{9,11},{10,... | collective-permute-start | bytes 786440 | tf_op jit(solution)/shard_map/ppermute | solution.py:315
  193.2 1.9 collective-permute-start.9

commit v3 on v2

--- a/solution.py
+++ b/solution.py
@@ -69,18 +69,28 @@
                 ).astype(jnp.bfloat16)
 
 
-def first_backward_kernel(dims, pitch, rows_ref, cols_ref, dual_ref, source_ref, out_ref, tiles_ref, duals_ref, acc_ref, sems):
-    count, parts = tiles_ref.shape[0], sems.shape[0]
+def first_backward_kernel(
+    dims, pitch, core_ref, row_source, col_source, dual_source, source_ref, out_ref, tiles_ref,
+    rows_ref, cols_ref, bands_ref, duals_ref, acc_ref, sems
+):
+    count, parts = tiles_ref.shape[0], sems.shape[0] - 3
     chunk = count // parts
+    lists = [
+        pltpu.make_async_copy(row_source, rows_ref, sems.at[parts]),
+        pltpu.make_async_copy(col_source, cols_ref, sems.at[parts + 1]),
+        pltpu.make_async_copy(dual_source, bands_ref, sems.at[parts + 2]),
+    ]
     copies = [
         pltpu.make_async_copy(source_ref.at[pl.ds(i * chunk, chunk)], tiles_ref.at[pl.ds(i * chunk, chunk)], sems.at[i])
         for i in range(parts)
     ]
-    for copy in copies:
+    for copy in lists + copies:
         copy.start()
-    bands = [dual_ref[a].astype(jnp.bfloat16) for a in range(dual_ref.shape[0])]
+    acc_ref[...] = jnp.zeros_like(acc_ref)
+    for copy in lists:
+        copy.wait()
+    bands = [bands_ref[a].astype(jnp.bfloat16) for a in range(bands_ref.shape[0])]
     duals_ref[...] = jnp.concatenate(bands, axis=1)
-    acc_ref[...] = jnp.zeros_like(acc_ref)
 
     def body(index, _):
         backward_blocks(dims, pitch, rows_ref, cols_ref, duals_ref, tiles_ref, acc_ref, index * UNROLL)
@@ -197,15 +207,26 @@
                 send_ref[g * n_col + h, pl.ds(j * piece, piece), :] = block
 
 
-def pair_kernel(own_ref, other_ref, out_ref):
-    out_ref[...] = (own_ref[...] + other_ref[...]).astype(jnp.bfloat16)
-
-
-def dual_kernel(remote, first, core_ref, own_ref, other_ref, *refs):
-    parts, (dual_ref, cap_ref, dual_out, round_out) = refs[:remote], refs[remote:]
+def sum_kernel(*refs):
+    total = refs[0][...].astype(jnp.float32)
+    for ref in refs[1:-1]:
+        total = total + ref[...].astype(jnp.float32)
+    refs[-1][...] = total.astype(jnp.bfloat16)
+
+
+def pair_kernel(own_ref, other_ref, *outs):
+    rows = outs[0].shape[0]
+    for i, out_ref in enumerate(outs):
+        piece = pl.ds(i * rows, rows)
+        out_ref[...] = (own_ref[piece, :] + other_ref[piece, :]).astype(jnp.bfloat16)
+
+
+def dual_kernel(split, remote, first, core_ref, own_ref, other_ref, *refs):
+    parts, (dual_ref, cap_ref, dual_out, round_out) = refs[: split * remote], refs[split * remote :]
     total = own_ref[...] + other_ref[...]
-    for part in parts:
-        total = total + part[...].astype(jnp.float32)
+    for r in range(remote):
+        piece = [part[...].astype(jnp.float32) for part in parts[r * split : (r + 1) * split]]
+        total = total + jnp.concatenate(piece, axis=0)
     bands, row_tiles, band, side = cap_ref.shape
     half = row_tiles // 2
     begin = core_ref[0] * half
@@ -258,17 +279,27 @@
     def banded(array):
         return array.reshape(scen // band, band, row_tiles, side).transpose(0, 2, 1, 3)
 
+    def in_hbm(array):
+        return pltpu.with_memory_space_constraint(array, pltpu.HBM)
+
     def first_backward(duals):
         return pl.pallas_call(
             functools.partial(first_backward_kernel, dims, pitch),
-            in_specs=[scalars(), scalars(), whole(), pl.BlockSpec(memory_space=pltpu.HBM)],
+            in_specs=[scalars()] + [pl.BlockSpec(memory_space=pltpu.HBM)] * 4,
             out_specs=[whole(), whole()],
             out_shape=[messages, pltpu.VMEM((count, side, side), jnp.bfloat16)],
-            scratch_shapes=[picked_duals, acc_cols, pltpu.SemaphoreType.DMA((8,))],
+            scratch_shapes=[
+                pltpu.SMEM((count,), jnp.int32),
+                pltpu.SMEM((count,), jnp.int32),
+                pltpu.VMEM(duals.shape, jnp.float32),
+                picked_duals,
+                acc_cols,
+                pltpu.SemaphoreType.DMA((8 + 3,)),
+            ],
             compiler_params=params(),
             cost_estimate=cost,
             name="first_backward_products",
-        )(rows, cols, duals, pltpu.with_memory_space_constraint(tile_values.reshape(count, side, side), pltpu.HBM))
+        )(core, in_hbm(rows), in_hbm(cols), in_hbm(duals), in_hbm(tile_values.reshape(count, side, side)))
 
     def backward(own, other, tiles):
         return pl.pallas_call(
@@ -310,24 +341,40 @@
     def swap_core(value):
         return lax.ppermute(value, "col", [(i, i ^ 1) for i in range(n_col)])
 
-    def all_chips(value):
-        return [
-            lax.ppermute(value, "col", [(i, i ^ (2 * d)) for i in range(n_col)]) for d in range(1, n_col // 2)
-        ]
+    def swap_chip(value, bit):
+        return lax.ppermute(value, "col", [(i, i ^ (2 << bit)) for i in range(n_col)])
 
     def dual_step(own, away, dual, first):
+        bits = (n_col // 2).bit_length() - 1
+        split = min(bits, 2)
+        piece = jax.ShapeDtypeStruct((half // split, side), jnp.bfloat16)
         other = swap_core(away)
-        pair = pl.pallas_call(
+        sums = pl.pallas_call(
             pair_kernel,
             in_specs=[whole()] * 2,
-            out_specs=whole(),
-            out_shape=half_bf16,
+            out_specs=[whole()] * split,
+            out_shape=[piece] * split,
             compiler_params=params(),
             name="core_pair_sum",
         )(own, other)
-        parts = all_chips(pair)
-        return pl.pallas_call(
-            functools.partial(dual_kernel, len(parts), first),
+        parts = []
+        for step in range(bits):
+            got = [swap_chip(sums[i], (step + i) % bits) for i in range(split)]
+            parts += got
+            if step + 1 < bits:
+                sums = [
+                    pl.pallas_call(
+                        sum_kernel,
+                        in_specs=[whole()] * 2,
+                        out_specs=whole(),
+                        out_shape=piece,
+                        compiler_params=params(),
+                        name="chip_sum",
+                    )(sums[i], got[i])
+                    for i in range(split)
+                ]
+        return pl.pallas_call(
+            functools.partial(dual_kernel, split, bits, first),
             in_specs=[scalars()] + [whole()] * (len(parts) + 4),
             out_specs=[whole()] * 2,
             out_shape=[half_f32, half_bf16],

time: 196 us -> 179 us (0.913)
  waiting for transfers between devices: 56.3 us -> 19.4 us
  blocking collectives: 91.8 us -> 121 us
  local copies, waits for them, and re-layouts: 11.9 us -> 0.04 us
    all_to_all x1 -> x2, blocking collectives: 29.7 us -> 59.3 us  [per_device(): probe = lax.all_to_all(send, ('row', 'col'), 0, 0, tiled=True)]
    all_to_all x1 -> x0, waiting for transfers between devices: 26.2 us -> none  [per_device(): probe = lax.all_to_all(send, ('row', 'col'), 0, 0, tiled=True)]
    unnamed x38 -> x16, local copies, waits for them, and re-layouts: 11.9 us -> 0.04 us
    ppermute x6 -> x8, waiting for transfers between devices: 22.9 us -> 12.2 us  [swap_chip(): return lax.ppermute(value, 'col', [(i, i ^ 2 << bit) for i in range(n_col)])]
    ppermute x6 -> x8, starting transfers between devices: 7.11 us -> 12.2 us  [swap_chip(): return lax.ppermute(value, 'col', [(i, i ^ 2 << bit) for i in range(n_col)])]
    all_to_all x1 -> x0, starting transfers between devices: 3.62 us -> none  [per_device(): probe = lax.all_to_all(send, ('row', 'col'), 0, 0, tiled=True)]
  transfers between devices with their start and end apart: 11 -> 12, of which waited for: 11 -> 10; matrix products, arithmetic and copies ran while one was open for 0% -> 0% of each run, Pallas kernels for 0% -> 0%
where the time goes in v3:
time: 179 us; the launch traced here: 178 us
  blocking collectives  121 us (68%)
  Pallas kernels  24.3 us (14%)
  waiting for transfers between devices  19.4 us (11%)
  starting transfers between devices  12.4 us (7%)
    all_to_all x2, blocking collectives, per_device(): recv = lax.all_to_all(send, ('row', 'col'), 0, 0, tiled=True)  62.1 us
    all_to_all x2, blocking collectives, per_device(): probe = lax.all_to_all(send, ('row', 'col'), 0, 0, tiled=True)  59.3 us
    ppermute x8, starting transfers between devices, swap_chip(): return lax.ppermute(value, 'col', [(i, i ^ 2 << bit) for i in range(n_col)])  12.2 us
    ppermute x8, waiting for transfers between devices, swap_chip(): return lax.ppermute(value, 'col', [(i, i ^ 2 << bit) for i in range(n_col)])  12.2 us
    pallas_call x2, Pallas kernels, forward(): pl.pallas_call(functools.partial(forward_kernel, dims, pitch), in_specs=[...  9.51 us
    ppermute x4, waiting for transfers between devices, swap_core(): return lax.ppermute(value, 'col', [(i, i ^ 1) for i in range(n_col)])  7.22 us
    pallas_call x1, Pallas kernels, first_backward(): pl.pallas_call(functools.partial(first_backward_kernel, dims, pitch), in_...  4.52 us
    pallas_call x1, Pallas kernels, backward(): pl.pallas_call(functools.partial(backward_kernel, dims, pitch), in_specs=...  4 us
  transfers between devices with their start and end apart: 12, of which 10 were waited for; matrix products, arithmetic and copies ran while one was open for 0% of the time, Pallas kernels for 0%

profile of v3, /device:TPU:0, one launch (start us, length us, event | category | flops | bytes accessed | tf_op | source)
XLA Modules:
  0.0 178.4 jit_solution(7387572432170412519)
XLA Ops:
  0.6 0.0 copy-start.5
  0.6 0.0 copy-start.4
  0.7 0.0 copy-start.3
  0.7 0.0 copy-start.7
  0.7 0.0 copy-start.6
  0.7 0.0 copy-start.2
  0.7 4.5 %first_backward_products.1 = (bf16[32,128,128]{2,1,0:T(8,128)(2,1)S(1)}, bf16[256,128,128]{2,1,0:T(8,128)(2,1)S(1)}) custom-call(s32[1]{0:T(128)} %bitcast.core_ref, s32[256]{0:T(256)} %bitcast.19, s32[256]{0:T(256)} %bitcast.23, f32[2,128,8,128]{3,2,1,0:T(8,128)} %bitcast.17, bf16[256,128,128]{2,1,0:T(8,128)(2,1)} %bitcast.31), custom_call_target="tpu_custom_call" | custom-call | flops 134217728 | bytes 4194304 | tf_op jit(solution)/shard_map/first_backward_products/pallas_call | solution.py:286
  5.2 0.0 copy-start
  5.2 0.0 copy-start.1
  5.3 33.3 %all_to_all.20.refs_0_ = bf16[32,128,128]{2,1,0:T(8,128)(2,1)S(1)} all-to-all(bf16[32,128,128]{2,1,0:T(8,128)(2,1)S(1)} %get-tuple-element.20), channel_id=1, replica_groups=mesh['row'=4,'col'=8] {'row','col'}, dimensions={0} | all-to-all | bytes 2097152 | tf_op jit(solution)/shard_map/all_to_all | solution.py:400
  38.6 0.0 copy-done.3
  38.6 1.7 primal_update.2
  40.3 29.7 %all_to_all.21.probe_ref = bf16[32,128,128]{2,1,0:T(8,128)(2,1)S(1)} all-to-all(bf16[32,128,128]{2,1,0:T(8,128)(2,1)S(1)} %get-tuple-element.21), channel_id=1, replica_groups=mesh['row'=4,'col'=8] {'row','col'}, dimensions={0} | all-to-all | bytes 2097152 | tf_op jit(solution)/shard_map/all_to_all | solution.py:402
  70.0 0.0 copy-done.5
  70.0 4.8 %forward_products.2 = (f32[1024,128]{1,0:T(8,128)S(1)}, f32[1024,128]{1,0:T(8,128)S(1)}) custom-call(s32[1]{0:T(128)} %bitcast.core_ref, s32[256]{0:T(256)S(1)} %bitcast.20, s32[256]{0:T(256)S(1)} %bitcast.24, bf16[32,128,128]{2,1,0:T(8,128)(2,1)S(1)} %all_to_all.21.probe_ref, bf16[256,128,128]{2,1,0:T(8,128)(2,1)S(1)} %get-tuple-element.22.tiles_ref), custom_call_target="tpu_custom_call" | custom-call | flops 134217728 | bytes 4194304 | tf_op jit(solution)/shard_map/forward_products/pallas_call | solution.py:317
  74.8 0.1 collective-permute-start
  74.8 1.9 %collective-permute-done.other_ref = f32[1024,128]{1,0:T(8,128)S(1)} collective-permute-done((f32[1024,128]{1,0:T(8,128)S(1)}, f32[1024,128]{1,0:T(8,128)S(1)}, u32[]{:S(2)}, u32[]{:S(2)}) %collective-permute-start) | collective-permute-done | bytes 524320 | tf_op jit(solution)/shard_map/ppermute | solution.py:342
  76.8 1.5 collective-permute-start.1
  78.3 1.5 collective-permute-start.2
  79.8 2.6 %collective-permute-done.1.refs_1_.refs_0_ = bf16[512,128]{1,0:T(8,128)(2,1)S(1)} collective-permute-done((bf16[512,128]{1,0:T(8,128)(2,1)S(1)}, bf16[512,128]{1,0:T(8,128)(2,1)S(1)}, u32[]{:S(2)}, u32[]{:S(2)}) %collective-permute-start.1) | collective-permute-done | bytes 131104 | tf_op jit(solution)/shard_map/ppermute | solution.py:345
  82.4 1.6 collective-permute-start.3
  84.0 0.0 collective-permute-done.2.refs_1_
  84.0 1.5 collective-permute-start.4
  85.6 1.9 %collective-permute-done.3.refs_2_ = bf16[512,128]{1,0:T(8,128)(2,1)S(1)} collective-permute-done((bf16[512,128]{1,0:T(8,128)(2,1)S(1)}, bf16[512,128]{1,0:T(8,128)(2,1)S(1)}, u32[]{:S(2)}, u32[]{:S(2)}) %collective-permute-start.3) | collective-permute-done | bytes 131104 | tf_op jit(solution)/shard_map/ppermute | solution.py:345
  87.5 1.6 collective-permute-done.4.refs_3_
  89.1 0.0 copy-done.1
  89.1 0.2 dual_update.2
  89.3 0.1 collective-permute-start.5
  89.4 1.5 collective-permute-done.5.other_ref
  90.9 4.0 %backward_products.1 = bf16[32,128,128]{2,1,0:T(8,128)(2,1)S(1)} custom-call(s32[1]{0:T(128)} %bitcast.core_ref, s32[256]{0:T(256)S(1)} %bitcast.21, s32[256]{0:T(256)S(1)} %bitcast.25, bf16[1024,128]{1,0:T(8,128)(2,1)S(1)} %get-tuple-element.27.own_ref, bf16[1024,128]{1,0:T(8,128)(2,1)S(1)} %collective-permute-done.5.other_ref, ...), custom_call_target="tpu_custom_call" | custom-call | flops 134217728 | bytes 4194304 | tf_op jit(solution)/shard_map/backward_products/pallas_call | solution.py:305
  94.9 28.7 %all_to_all.22.refs_0_ = bf16[32,128,128]{2,1,0:T(8,128)(2,1)S(1)} all-to-all(bf16[32,128,128]{2,1,0:T(8,128)(2,1)S(1)} %backward_products.1), channel_id=1, replica_groups=mesh['row'=4,'col'=8] {'row','col'}, dimensions={0} | all-to-all | bytes 2097152 | tf_op jit(solution)/shard_map/all_to_all | solution.py:400
  123.6 2.1 %primal_update.3 = (f32[4,128,256]{2,1,0:T(8,128)}, f32[4,128,256]{2,1,0:T(8,128)}, bf16[32,128,128]{2,1,0:T(8,128)(2,1)S(1)}) custom-call(bf16[32,128,128]{2,1,0:T(8,128)(2,1)S(1)} %all_to_all.22.refs_0_, f32[4,128,256]{2,1,0:T(8,128)S(1)} %get-tuple-element.28.refs_1_, f32[4,128,256]{2,1,0:T(8,128)S(1)} %get-tuple-element.29.refs_2_, ...), custom_call_target="tpu_custom_call" | custom-call | tf_op jit(solution)/shard_map/primal_update/pallas_call | solution.py:332
  125.8 29.7 %all_to_all.23.probe_ref = bf16[32,128,128]{2,1,0:T(8,128)(2,1)S(1)} all-to-all(bf16[32,128,128]{2,1,0:T(8,128)(2,1)S(1)} %get-tuple-element.31), channel_id=1, replica_groups=mesh['row'=4,'col'=8] {'row','col'}, dimensions={0} | all-to-all | bytes 2097152 | tf_op jit(solution)/shard_map/all_to_all | solution.py:402
  155.4 4.8 %forward_products.3 = (f32[1024,128]{1,0:T(8,128)S(1)}, f32[1024,128]{1,0:T(8,128)S(1)}) custom-call(s32[1]{0:T(128)} %bitcast.core_ref, s32[256]{0:T(256)S(1)} %bitcast.22, s32[256]{0:T(256)S(1)} %bitcast.26, bf16[32,128,128]{2,1,0:T(8,128)(2,1)S(1)} %all_to_all.23.probe_ref, bf16[256,128,128]{2,1,0:T(8,128)(2,1)S(1)} %get-tuple-element.22.tiles_ref), custom_call_target="tpu_custom_call" | custom-call | flops 134217728 | bytes 4194304 | tf_op jit(solution)/shard_map/forward_products/pallas_call | solution.py:317
  160.2 0.1 collective-permute-start.6
  160.3 1.9 %collective-permute-done.6.other_ref = f32[1024,128]{1,0:T(8,128)S(1)} collective-permute-done((f32[1024,128]{1,0:T(8,128)S(1)}, f32[1024,128]{1,0:T(8,128)S(1)}, u32[]{:S(2)}, u32[]{:S(2)}) %collective-permute-start.6) | collective-permute-done | bytes 524320 | tf_op jit(solution)/shard_map/ppermute | solution.py:342
  162.2 1.5 collective-permute-start.7
  163.7 1.5 collective-permute-start.8
  165.2 2.6 %collective-permute-done.7.refs_1_.refs_0_ = bf16[512,128]{1,0:T(8,128)(2,1)S(1)} collective-permute-done((bf16[512,128]{1,0:T(8,128)(2,1)S(1)}, bf16[512,128]{1,0:T(8,128)(2,1)S(1)}, u32[]{:S(2)}, u32[]{:S(2)}) %collective-permute-start.7) | collective-permute-done | bytes 131104 | tf_op jit(solution)/shard_map/ppermute | solution.py:345
  167.9 1.5 collective-permute-start.9
  169.4 0.0 collective-permute-done.8.refs_1_
  169.5 1.5 collective-permute-start.10
  171.0 1.9 %collective-permute-done.9.refs_2_ = bf16[512,128]{1,0:T(8,128)(2,1)S(1)} collective-permute-done((bf16[512,128]{1,0:T(8,128)(2,1)S(1)}, bf16[512,128]{1,0:T(8,128)(2,1)S(1)}, u32[]{:S(2)}, u32[]{:S(2)}) %collective-permute-start.9) | collective-permute-done | bytes 131104 | tf_op jit(solution)/shard_map/ppermute | solution.py:345
  172.9 1.6 collective-permute-done.10.refs_3_
  174.5 0.9 dual_update.3
  175.4 0.0 collective-permute-start.11
  175.4 1.9 %collective-permute-done.11.other_ref = f32[1024,128]{1,0:T(8,128)S(1)} collective-permute-done((f32[1024,128]{1,0:T(8,128)S(1)}, f32[1024,128]{1,0:T(8,128)S(1)}, u32[]{:S(2)}, u32[]{:S(2)}) %collective-permute-start.11) | collective-permute-done | bytes 524320 | tf_op jit(solution)/shard_map/ppermute | solution.py:342
  177.3 1.0 assemble_duals.1
  (11 shorter events, 0.2 us)
Async XLA Ops:
  0.6 69.4 %copy-start.5 = (s32[1,1,256]{2,1,0:T(1,128)S(1)}, s32[1,1,256]{2,1,0:T(1,128)}, u32[]{:S(2)}) copy-start(s32[1,1,256]{2,1,0:T(1,128)} %param.11) | copy-start | bytes 3076
  0.6 69.4 %copy-start.4 = (s32[1,1,256]{2,1,0:T(1,128)S(1)}, s32[1,1,256]{2,1,0:T(1,128)}, u32[]{:S(2)}) copy-start(s32[1,1,256]{2,1,0:T(1,128)} %param.10) | copy-start | bytes 3076
  0.7 37.9 %copy-start.3 = (f32[128,256]{1,0:T(8,128)S(1)}, f32[128,256]{1,0:T(8,128)}, u32[]{:S(2)}) copy-start(f32[128,256]{1,0:T(8,128)} %refs_3_.1) | copy-start | bytes 393220
  0.7 37.9 %copy-start.7 = (s32[256]{0:T(256)S(1)}, s32[256]{0:T(256)}, u32[]{:S(2)}) copy-start(s32[256]{0:T(256)} %param.16) | copy-start | bytes 3076
  0.7 37.9 %copy-start.6 = (s32[256]{0:T(256)S(1)}, s32[256]{0:T(256)}, u32[]{:S(2)}) copy-start(s32[256]{0:T(256)} %param.15) | copy-start | bytes 3076
  0.7 37.9 %copy-start.2 = (f32[4,128,256]{2,1,0:T(8,128)S(1)}, f32[4,128,256]{2,1,0:T(8,128)}, u32[]{:S(2)}) copy-start(f32[4,128,256]{2,1,0:T(8,128)} %refs_1_.1) | copy-start | bytes 1572868
  5.2 83.8 %copy-start = (s32[16,16384]{1,0:T(8,128)S(1)}, s32[16,16384]{1,0:T(8,128)}, u32[]{:S(2)}) copy-start(s32[16,16384]{1,0:T(8,128)} %param.17) | copy-start | bytes 3145732
  5.2 83.8 %copy-start.1 = (f32[16,16384]{1,0:T(8,128)S(1)}, f32[16,16384]{1,0:T(8,128)}, u32[]{:S(2)}) copy-start(f32[16,16384]{1,0:T(8,128)} %param.13) | copy-start | bytes 3145732
  74.8 2.0 %collective-permute-start = (f32[1024,128]{1,0:T(8,128)S(1)}, f32[1024,128]{1,0:T(8,128)S(1)}, u32[]{:S(2)}, u32[]{:S(2)}) collective-permute-start(f32[1024,128]{1,0:T(8,128)S(1)} %get-tuple-element.24), channel_id=1, source_target_pairs={{0,1},{1,0},{2,3},{3,2},{4,5},{5,4},{6,7},{7,6},{8,9},{9,8},{10,11... | collective-permute-start | bytes 1572872 | tf_op jit(solution)/shard_map/ppermute | solution.py:342
  76.8 5.6 %collective-permute-start.1 = (bf16[512,128]{1,0:T(8,128)(2,1)S(1)}, bf16[512,128]{1,0:T(8,128)(2,1)S(1)}, u32[]{:S(2)}, u32[]{:S(2)}) collective-permute-start(bf16[512,128]{1,0:T(8,128)(2,1)S(1)} %get-tuple-element.25.refs_0_), channel_id=1, source_target_pairs={{0,2},{1,3},{2,0},{3,1},{4,6},{5,7},{6,4},{7,5},{8,10},{9,11},{10,... | collective-permute-start | bytes 393224 | tf_op jit(solution)/shard_map/ppermute | solution.py:345
  78.3 5.7 %collective-permute-start.2 = (bf16[512,128]{1,0:T(8,128)(2,1)S(1)}, bf16[512,128]{1,0:T(8,128)(2,1)S(1)}, u32[]{:S(2)}, u32[]{:S(2)}) collective-permute-start(bf16[512,128]{1,0:T(8,128)(2,1)S(1)} %get-tuple-element.26.refs_0_), channel_id=1, source_target_pairs={{0,4},{1,5},{2,6},{3,7},{4,0},{5,1},{6,2},{7,3},{8,12},{9,13},{10,... | collective-permute-start | bytes 393224 | tf_op jit(solution)/shard_map/ppermute | solution.py:345
  82.4 5.0 %collective-permute-start.3 = (bf16[512,128]{1,0:T(8,128)(2,1)S(1)}, bf16[512,128]{1,0:T(8,128)(2,1)S(1)}, u32[]{:S(2)}, u32[]{:S(2)}) collective-permute-start(bf16[512,128]{1,0:T(8,128)(2,1)S(1)} %chip_sum.4), channel_id=1, source_target_pairs={{0,4},{1,5},{2,6},{3,7},{4,0},{5,1},{6,2},{7,3},{8,12},{9,13},{10,... | collective-permute-start | bytes 393224 | tf_op jit(solution)/shard_map/ppermute | solution.py:345
  84.0 5.0 %collective-permute-start.4 = (bf16[512,128]{1,0:T(8,128)(2,1)S(1)}, bf16[512,128]{1,0:T(8,128)(2,1)S(1)}, u32[]{:S(2)}, u32[]{:S(2)}) collective-permute-start(bf16[512,128]{1,0:T(8,128)(2,1)S(1)} %chip_sum.5), channel_id=1, source_target_pairs={{0,2},{1,3},{2,0},{3,1},{4,6},{5,7},{6,4},{7,5},{8,10},{9,11},{10,... | collective-permute-start | bytes 393224 | tf_op jit(solution)/shard_map/ppermute | solution.py:345
  89.3 1.6 collective-permute-start.5
  160.2 2.0 %collective-permute-start.6 = (f32[1024,128]{1,0:T(8,128)S(1)}, f32[1024,128]{1,0:T(8,128)S(1)}, u32[]{:S(2)}, u32[]{:S(2)}) collective-permute-start(f32[1024,128]{1,0:T(8,128)S(1)} %get-tuple-element.33), channel_id=1, source_target_pairs={{0,1},{1,0},{2,3},{3,2},{4,5},{5,4},{6,7},{7,6},{8,9},{9,8},{10,11... | collective-permute-start | bytes 1572872 | tf_op jit(solution)/shard_map/ppermute | solution.py:342
  162.2 5.6 %collective-permute-start.7 = (bf16[512,128]{1,0:T(8,128)(2,1)S(1)}, bf16[512,128]{1,0:T(8,128)(2,1)S(1)}, u32[]{:S(2)}, u32[]{:S(2)}) collective-permute-start(bf16[512,128]{1,0:T(8,128)(2,1)S(1)} %get-tuple-element.34.refs_0_), channel_id=1, source_target_pairs={{0,2},{1,3},{2,0},{3,1},{4,6},{5,7},{6,4},{7,5},{8,10},{9,11},{10,... | collective-permute-start | bytes 393224 | tf_op jit(solution)/shard_map/ppermute | solution.py:345
  163.7 5.7 %collective-permute-start.8 = (bf16[512,128]{1,0:T(8,128)(2,1)S(1)}, bf16[512,128]{1,0:T(8,128)(2,1)S(1)}, u32[]{:S(2)}, u32[]{:S(2)}) collective-permute-start(bf16[512,128]{1,0:T(8,128)(2,1)S(1)} %get-tuple-element.35.refs_0_), channel_id=1, source_target_pairs={{0,4},{1,5},{2,6},{3,7},{4,0},{5,1},{6,2},{7,3},{8,12},{9,13},{10,... | collective-permute-start | bytes 393224 | tf_op jit(solution)/shard_map/ppermute | solution.py:345
  167.9 5.0 %collective-permute-start.9 = (bf16[512,128]{1,0:T(8,128)(2,1)S(1)}, bf16[512,128]{1,0:T(8,128)(2,1)S(1)}, u32[]{:S(2)}, u32[]{:S(2)}) collective-permute-start(bf16[512,128]{1,0:T(8,128)(2,1)S(1)} %chip_sum.6), channel_id=1, source_target_pairs={{0,4},{1,5},{2,6},{3,7},{4,0},{5,1},{6,2},{7,3},{8,12},{9,13},{10,... | collective-permute-start | bytes 393224 | tf_op jit(solution)/shard_map/ppermute | solution.py:345
  169.5 5.0 %collective-permute-start.10 = (bf16[512,128]{1,0:T(8,128)(2,1)S(1)}, bf16[512,128]{1,0:T(8,128)(2,1)S(1)}, u32[]{:S(2)}, u32[]{:S(2)}) collective-permute-start(bf16[512,128]{1,0:T(8,128)(2,1)S(1)} %chip_sum.7), channel_id=1, source_target_pairs={{0,2},{1,3},{2,0},{3,1},{4,6},{5,7},{6,4},{7,5},{8,10},{9,11},{10,... | collective-permute-start | bytes 393224 | tf_op jit(solution)/shard_map/ppermute | solution.py:345
  175.4 1.9 %collective-permute-start.11 = (f32[1024,128]{1,0:T(8,128)S(1)}, f32[1024,128]{1,0:T(8,128)S(1)}, u32[]{:S(2)}, u32[]{:S(2)}) collective-permute-start(f32[1024,128]{1,0:T(8,128)S(1)} %get-tuple-element.37.own_ref), channel_id=1, source_target_pairs={{0,1},{1,0},{2,3},{3,2},{4,5},{5,4},{6,7},{7,6},{8,9},{9,8},{10,11... | collective-permute-start | bytes 1572872 | tf_op jit(solution)/shard_map/ppermute | solution.py:342

commit v4 on v3

--- a/solution.py
+++ b/solution.py
@@ -10,7 +10,7 @@
 
 ITERS = 2
 SIGMA_STEP = 0.2
-UNROLL = 32
+UNROLL = 64
 PITCH_PAD = 8
 VMEM_BYTES = 24 * 1024 * 1024
 TRANSPOSED = (((1,), (1,)), ((), ()))
@@ -159,22 +159,27 @@
     away_ref[...] = acc_ref[pl.ds(pl.multiple_of((1 - core) * half, half), half), :]
 
 
-def running(values, trailing):
+def running(values, trailing, terms):
     length = values.shape[0]
     row_iota = lax.broadcasted_iota(jnp.int32, (length, length), 0)
     col_iota = lax.broadcasted_iota(jnp.int32, (length, length), 1)
-    keep = (col_iota >= row_iota) if trailing else (row_iota >= col_iota)
-    return jnp.dot(
-        keep.astype(jnp.float32), values, precision=lax.Precision.HIGHEST, preferred_element_type=jnp.float32
-    )
-
-
-def primal_kernel(dims, first, *refs):
+    keep = ((col_iota >= row_iota) if trailing else (row_iota >= col_iota)).astype(jnp.float32).astype(jnp.bfloat16)
+    total = None
+    for _ in range(terms):
+        term = values.astype(jnp.bfloat16)
+        values = values - term.astype(jnp.float32)
+        part = jnp.dot(keep, term, preferred_element_type=jnp.float32)
+        total = part if total is None else total + part
+    return total
+
+
+def primal_kernel(dims, first, last, *refs):
     n_row, n_col, scen_local, time_block, _, own_tiles = dims
-    if first:
-        recv_ref, inc_ref, cost_ref, start_ref, len_ref, inc_out, cum_out, send_ref = refs
-    else:
-        recv_ref, inc_ref, cum_ref, cost_ref, start_ref, len_ref, inc_out, cum_out, send_ref = refs
+    refs = list(refs)
+    recv_ref, inc_ref = refs[:2]
+    cum_ref = None if first else refs[2]
+    cost_ref, start_ref, len_ref, inc_out, send_ref = refs[2 + (not first) :][:5]
+    cum_out = None if last else refs[-1]
     window, flight_local = cost_ref.shape
     side = flight_local // own_tiles
     piece = own_tiles * time_block
@@ -182,6 +187,7 @@
     minutes = lax.broadcasted_iota(jnp.int32, (window, flight_local), 0)
     begin = start_ref[...]
     upper = ((minutes >= begin) & (minutes < begin + len_ref[...])).astype(jnp.float32)
+    slopes = []
     for j in range(scen_local):
         bands = []
         for h in range(n_col):
@@ -191,42 +197,37 @@
             bands.append(
                 jnp.concatenate([total[f * time_block : (f + 1) * time_block] for f in range(own_tiles)], axis=1)
             )
-        slope = jnp.concatenate(bands, axis=0) + cost_ref[...]
-        gradient = running(slope, True)
-        old = inc_ref[j]
-        old_sum = running(old, False) if first else cum_ref[j]
-        fresh = jnp.clip(old - tau_step * gradient, 0.0, upper)
-        inc_out[j] = fresh
-        fresh_sum = running(fresh, False)
-        cum_out[j] = fresh_sum
-        probe = (2.0 * fresh_sum - old_sum).astype(jnp.bfloat16)
+        slopes.append(jnp.concatenate(bands, axis=0) + cost_ref[...])
+    gradient = running(jnp.concatenate(slopes, axis=1), True, 2)
+    old = jnp.concatenate([inc_ref[j] for j in range(scen_local)], axis=1)
+    if first:
+        old_sum = running(old, False, 3)
+    else:
+        old_sum = jnp.concatenate([cum_ref[j] for j in range(scen_local)], axis=1)
+    fresh = jnp.clip(old - tau_step * gradient, 0.0, jnp.concatenate([upper] * scen_local, axis=1))
+    fresh_sum = running(fresh, False, 3)
+    probe = (2.0 * fresh_sum - old_sum).astype(jnp.bfloat16)
+    for j in range(scen_local):
+        lanes = slice(j * flight_local, (j + 1) * flight_local)
+        inc_out[j] = fresh[:, lanes]
+        if not last:
+            cum_out[j] = fresh_sum[:, lanes]
         for h in range(n_col):
-            band = probe[h * time_block : (h + 1) * time_block]
+            band = probe[h * time_block : (h + 1) * time_block, lanes]
             block = jnp.concatenate([band[:, f * side : (f + 1) * side] for f in range(own_tiles)], axis=0)
             for g in range(n_row):
                 send_ref[g * n_col + h, pl.ds(j * piece, piece), :] = block
 
 
-def sum_kernel(*refs):
-    total = refs[0][...].astype(jnp.float32)
-    for ref in refs[1:-1]:
-        total = total + ref[...].astype(jnp.float32)
-    refs[-1][...] = total.astype(jnp.bfloat16)
-
-
-def pair_kernel(own_ref, other_ref, *outs):
-    rows = outs[0].shape[0]
-    for i, out_ref in enumerate(outs):
-        piece = pl.ds(i * rows, rows)
-        out_ref[...] = (own_ref[piece, :] + other_ref[piece, :]).astype(jnp.bfloat16)
-
-
-def dual_kernel(split, remote, first, core_ref, own_ref, other_ref, *refs):
-    parts, (dual_ref, cap_ref, dual_out, round_out) = refs[: split * remote], refs[split * remote :]
+def sum_kernel(first_ref, second_ref, out_ref):
+    out_ref[...] = (first_ref[...].astype(jnp.float32) + second_ref[...].astype(jnp.float32)).astype(jnp.bfloat16)
+
+
+def dual_kernel(remote, first, last, core_ref, own_ref, other_ref, *refs):
+    parts, (dual_ref, cap_ref, dual_out) = refs[:remote], refs[remote : remote + 3]
     total = own_ref[...] + other_ref[...]
-    for r in range(remote):
-        piece = [part[...].astype(jnp.float32) for part in parts[r * split : (r + 1) * split]]
-        total = total + jnp.concatenate(piece, axis=0)
+    for part in parts:
+        total = total + part[...].astype(jnp.float32)
     bands, row_tiles, band, side = cap_ref.shape
     half = row_tiles // 2
     begin = core_ref[0] * half
@@ -237,7 +238,8 @@
     old = own_half(dual_ref) if first else dual_ref[...]
     fresh = jnp.maximum(old + SIGMA_STEP * (total - own_half(cap_ref).astype(jnp.float32)), 0.0)
     dual_out[...] = fresh
-    round_out[...] = fresh.astype(jnp.bfloat16)
+    if not last:
+        refs[-1][...] = fresh.astype(jnp.bfloat16)
 
 
 def assemble_kernel(core_ref, own_ref, other_ref, out_ref):
@@ -294,7 +296,7 @@
                 pltpu.VMEM(duals.shape, jnp.float32),
                 picked_duals,
                 acc_cols,
-                pltpu.SemaphoreType.DMA((8 + 3,)),
+                pltpu.SemaphoreType.DMA((count // UNROLL + 3,)),
             ],
             compiler_params=params(),
             cost_estimate=cost,
@@ -325,15 +327,16 @@
             name="forward_products",
         )(core, rows, cols, probe, pltpu.with_memory_space_constraint(tiles, pltpu.VMEM))
 
-    def primal_step(recv, primal, cumulative):
+    def primal_step(recv, primal, cumulative, last):
         first = cumulative is None
         state = (primal,) if first else (primal, cumulative)
         shape = jax.ShapeDtypeStruct(primal.shape, jnp.float32)
-        return pl.pallas_call(
-            functools.partial(primal_kernel, dims, first),
+        out_shape = [shape, messages] if last else [shape, messages, shape]
+        return pl.pallas_call(
+            functools.partial(primal_kernel, dims, first, last),
             in_specs=[whole()] * (4 + len(state)),
-            out_specs=[whole()] * 3,
-            out_shape=[shape, shape, messages],
+            out_specs=[whole()] * len(out_shape),
+            out_shape=out_shape,
             compiler_params=params(),
             name="primal_update",
         )(recv, *state, flight_cost, win_start.reshape(1, -1), win_len.reshape(1, -1))
@@ -341,43 +344,35 @@
     def swap_core(value):
         return lax.ppermute(value, "col", [(i, i ^ 1) for i in range(n_col)])
 
-    def swap_chip(value, bit):
-        return lax.ppermute(value, "col", [(i, i ^ (2 << bit)) for i in range(n_col)])
-
-    def dual_step(own, away, dual, first):
-        bits = (n_col // 2).bit_length() - 1
-        split = min(bits, 2)
-        piece = jax.ShapeDtypeStruct((half // split, side), jnp.bfloat16)
+    bits = (n_col // 2).bit_length() - 1
+
+    def swap_chip(value, step):
+        return lax.ppermute(value, "col", [(i, i ^ (2 << (step + i % 2) % bits)) for i in range(n_col)])
+
+    def bf16_sum(first, second, name):
+        return pl.pallas_call(
+            sum_kernel,
+            in_specs=[whole()] * 2,
+            out_specs=whole(),
+            out_shape=half_bf16,
+            compiler_params=params(),
+            name=name,
+        )(first, second)
+
+    def dual_step(own, away, dual, first, last):
         other = swap_core(away)
-        sums = pl.pallas_call(
-            pair_kernel,
-            in_specs=[whole()] * 2,
-            out_specs=[whole()] * split,
-            out_shape=[piece] * split,
-            compiler_params=params(),
-            name="core_pair_sum",
-        )(own, other)
+        partial = bf16_sum(own, other, "core_pair_sum")
         parts = []
         for step in range(bits):
-            got = [swap_chip(sums[i], (step + i) % bits) for i in range(split)]
-            parts += got
+            parts.append(swap_chip(partial, step))
             if step + 1 < bits:
-                sums = [
-                    pl.pallas_call(
-                        sum_kernel,
-                        in_specs=[whole()] * 2,
-                        out_specs=whole(),
-                        out_shape=piece,
-                        compiler_params=params(),
-                        name="chip_sum",
-                    )(sums[i], got[i])
-                    for i in range(split)
-                ]
-        return pl.pallas_call(
-            functools.partial(dual_kernel, split, bits, first),
-            in_specs=[scalars()] + [whole()] * (len(parts) + 4),
-            out_specs=[whole()] * 2,
-            out_shape=[half_f32, half_bf16],
+                partial = bf16_sum(partial, parts[-1], "chip_sum")
+        out_shape = [half_f32] if last else [half_f32, half_bf16]
+        return pl.pallas_call(
+            functools.partial(dual_kernel, bits, first, last),
+            in_specs=[scalars()] + [whole()] * (bits + 4),
+            out_specs=[whole()] * len(out_shape),
+            out_shape=out_shape,
             compiler_params=params(),
             name="dual_update",
         )(core, own, other, *parts, dual, banded(capacity))
@@ -395,13 +390,16 @@
     send, tiles = first_backward(banded(dual_vars))
     dual, primal, cumulative = banded(dual_vars), increments, None
     for sweep in range(ITERS):
+        last = sweep + 1 == ITERS
         if sweep:
             send = backward(half_round, swap_core(half_round), tiles)
         recv = lax.all_to_all(send, ("row", "col"), 0, 0, tiled=True)
-        primal, cumulative, send = primal_step(recv, primal, cumulative)
+        primal, send, *cumulative = primal_step(recv, primal, cumulative, last)
+        cumulative = None if last else cumulative[0]
         probe = lax.all_to_all(send, ("row", "col"), 0, 0, tiled=True)
         own, away = forward(probe, tiles)
-        dual, half_round = dual_step(own, away, dual, sweep == 0)
+        dual, *rounded = dual_step(own, away, dual, sweep == 0, last)
+        half_round = None if last else rounded[0]
     duals_out = assemble(dual).transpose(0, 2, 1, 3).reshape(scen, row_length)
     return (primal, duals_out)
 

time: 179 us -> 178 us (level)
  waiting for transfers between devices: 19.4 us -> 26.8 us
  starting transfers between devices: 12.4 us -> 6.42 us
  Pallas kernels: 24.3 us -> 20.9 us
    ppermute x8 -> x4, waiting for transfers between devices: 12.2 us -> 19.6 us  [swap_chip(): lax.ppermute(value, 'col', [(i, i ^ 2 << (step + i % 2) % bits) for i in...]
    ppermute x8 -> x4, starting transfers between devices: 12.2 us -> 6.14 us  [swap_chip(): lax.ppermute(value, 'col', [(i, i ^ 2 << (step + i % 2) % bits) for i in...]
    pallas_call x10 -> x8, Pallas kernels: 5.22 us -> 2.85 us  [the longest x2 2.23 us: primal_step(): pl.pallas_call(functools.partial(primal_kernel, dims, first, last), in_sp...]
  transfers between devices with their start and end apart: 12 -> 8, of which waited for: 10 -> 8; matrix products, arithmetic and copies ran while one was open for 0% -> 0% of each run, Pallas kernels for 0% -> 0%
where the time goes in v4:
time: 178 us; the launch traced here: 177 us
  blocking collectives  122 us (69%)
  waiting for transfers between devices  26.8 us (15%)
  Pallas kernels  20.9 us (12%)
  starting transfers between devices  6.42 us (4%)
    all_to_all x2, blocking collectives, per_device(): recv = lax.all_to_all(send, ('row', 'col'), 0, 0, tiled=True)  63 us
    all_to_all x2, blocking collectives, per_device(): probe = lax.all_to_all(send, ('row', 'col'), 0, 0, tiled=True)  59.3 us
    ppermute x4, waiting for transfers between devices, swap_chip(): lax.ppermute(value, 'col', [(i, i ^ 2 << (step + i % 2) % bits) for i in...  19.6 us
    pallas_call x2, Pallas kernels, forward(): pl.pallas_call(functools.partial(forward_kernel, dims, pitch), in_specs=[...  8.63 us
    ppermute x4, waiting for transfers between devices, swap_core(): return lax.ppermute(value, 'col', [(i, i ^ 1) for i in range(n_col)])  7.21 us
    ppermute x4, starting transfers between devices, swap_chip(): lax.ppermute(value, 'col', [(i, i ^ 2 << (step + i % 2) % bits) for i in...  6.14 us
    pallas_call x1, Pallas kernels, first_backward(): pl.pallas_call(functools.partial(first_backward_kernel, dims, pitch), in_...  4.76 us
    pallas_call x1, Pallas kernels, backward(): pl.pallas_call(functools.partial(backward_kernel, dims, pitch), in_specs=...  3.58 us
  transfers between devices with their start and end apart: 8, of which 8 were waited for; matrix products, arithmetic and copies ran while one was open for 0% of the time, Pallas kernels for 0%

profile of v4, /device:TPU:0, one launch (start us, length us, event | category | flops | bytes accessed | tf_op | source)
XLA Modules:
  0.0 177.3 jit_solution(9943813808250536112)
XLA Ops:
  0.6 0.0 copy-start.5
  0.6 0.0 copy-start.4
  0.7 0.0 copy-start.3
  0.7 0.0 copy-start.7
  0.7 0.0 copy-start.6
  0.7 0.0 copy-start.2
  0.7 4.8 %first_backward_products.1 = (bf16[32,128,128]{2,1,0:T(8,128)(2,1)S(1)}, bf16[256,128,128]{2,1,0:T(8,128)(2,1)S(1)}) custom-call(s32[1]{0:T(128)} %bitcast.core_ref, s32[256]{0:T(256)} %bitcast.19, s32[256]{0:T(256)} %bitcast.23, f32[2,128,8,128]{3,2,1,0:T(8,128)} %bitcast.17, bf16[256,128,128]{2,1,0:T(8,128)(2,1)} %bitcast.31), custom_call_target="tpu_custom_call" | custom-call | flops 134217728 | bytes 4194304 | tf_op jit(solution)/shard_map/first_backward_products/pallas_call | solution.py:288
  5.5 0.0 copy-start
  5.5 0.0 copy-start.1
  5.5 33.3 %all_to_all.20.refs_0_ = bf16[32,128,128]{2,1,0:T(8,128)(2,1)S(1)} all-to-all(bf16[32,128,128]{2,1,0:T(8,128)(2,1)S(1)} %get-tuple-element.15), channel_id=1, replica_groups=mesh['row'=4,'col'=8] {'row','col'}, dimensions={0} | all-to-all | bytes 2097152 | tf_op jit(solution)/shard_map/all_to_all | solution.py:396
  38.8 0.0 copy-done.3
  38.8 0.0 copy-done.7
  38.8 0.0 copy-done.6
  38.9 0.0 copy-done.2
  38.9 0.9 primal_update.2
  39.8 29.7 %all_to_all.21.probe_ref = bf16[32,128,128]{2,1,0:T(8,128)(2,1)S(1)} all-to-all(bf16[32,128,128]{2,1,0:T(8,128)(2,1)S(1)} %get-tuple-element.16), channel_id=1, replica_groups=mesh['row'=4,'col'=8] {'row','col'}, dimensions={0} | all-to-all | bytes 2097152 | tf_op jit(solution)/shard_map/all_to_all | solution.py:399
  69.5 0.0 copy-done.5
  69.5 0.0 copy-done.4
  69.5 4.3 %forward_products.2 = (f32[1024,128]{1,0:T(8,128)S(1)}, f32[1024,128]{1,0:T(8,128)S(1)}) custom-call(s32[1]{0:T(128)} %bitcast.core_ref, s32[256]{0:T(256)S(1)} %bitcast.20, s32[256]{0:T(256)S(1)} %bitcast.24, bf16[32,128,128]{2,1,0:T(8,128)(2,1)S(1)} %all_to_all.21.probe_ref, bf16[256,128,128]{2,1,0:T(8,128)(2,1)S(1)} %get-tuple-element.17.tiles_ref), custom_call_target="tpu_custom_call" | custom-call | flops 134217728 | bytes 4194304 | tf_op jit(solution)/shard_map/forward_products/pallas_call | solution.py:319
  73.8 0.1 collective-permute-start
  73.9 1.9 %collective-permute-done.second_ref.other_ref = f32[1024,128]{1,0:T(8,128)S(1)} collective-permute-done((f32[1024,128]{1,0:T(8,128)S(1)}, f32[1024,128]{1,0:T(8,128)S(1)}, u32[]{:S(2)}, u32[]{:S(2)}) %collective-permute-start) | collective-permute-done | bytes 524320 | tf_op jit(solution)/shard_map/ppermute | solution.py:345
  75.8 1.5 collective-permute-start.1
  77.4 4.9 %collective-permute-done.1.second_ref.refs_0_ = bf16[1024,128]{1,0:T(8,128)(2,1)S(1)} collective-permute-done((bf16[1024,128]{1,0:T(8,128)(2,1)S(1)}, bf16[1024,128]{1,0:T(8,128)(2,1)S(1)}, u32[]{:S(2)}, u32[]{:S(2)}) %collective-permute-start.1) | collective-permute-done | bytes 262176 | tf_op jit(solution)/shard_map/ppermute | solution.py:350
  82.3 0.1 chip_sum.2
  82.3 1.5 collective-permute-start.2
  83.9 4.9 %collective-permute-done.2.refs_1_ = bf16[1024,128]{1,0:T(8,128)(2,1)S(1)} collective-permute-done((bf16[1024,128]{1,0:T(8,128)(2,1)S(1)}, bf16[1024,128]{1,0:T(8,128)(2,1)S(1)}, u32[]{:S(2)}, u32[]{:S(2)}) %collective-permute-start.2) | collective-permute-done | bytes 262176 | tf_op jit(solution)/shard_map/ppermute | solution.py:350
  88.8 0.0 copy-done
  88.8 0.0 copy-done.1
  88.8 0.2 dual_update.2
  89.0 0.1 collective-permute-start.3
  89.0 1.5 collective-permute-done.3.other_ref
  90.6 3.6 %backward_products.1 = bf16[32,128,128]{2,1,0:T(8,128)(2,1)S(1)} custom-call(s32[1]{0:T(128)} %bitcast.core_ref, s32[256]{0:T(256)S(1)} %bitcast.21, s32[256]{0:T(256)S(1)} %bitcast.25, bf16[1024,128]{1,0:T(8,128)(2,1)S(1)} %get-tuple-element.20.own_ref, bf16[1024,128]{1,0:T(8,128)(2,1)S(1)} %collective-permute-done.3.other_ref, ...), custom_call_target="tpu_custom_call" | custom-call | flops 134217728 | bytes 4194304 | tf_op jit(solution)/shard_map/backward_products/pallas_call | solution.py:307
  94.2 29.7 %all_to_all.22.refs_0_ = bf16[32,128,128]{2,1,0:T(8,128)(2,1)S(1)} all-to-all(bf16[32,128,128]{2,1,0:T(8,128)(2,1)S(1)} %backward_products.1), channel_id=1, replica_groups=mesh['row'=4,'col'=8] {'row','col'}, dimensions={0} | all-to-all | bytes 2097152 | tf_op jit(solution)/shard_map/all_to_all | solution.py:396
  123.8 1.3 primal_update.3
  125.1 29.7 %all_to_all.23.probe_ref = bf16[32,128,128]{2,1,0:T(8,128)(2,1)S(1)} all-to-all(bf16[32,128,128]{2,1,0:T(8,128)(2,1)S(1)} %get-tuple-element.24), channel_id=1, replica_groups=mesh['row'=4,'col'=8] {'row','col'}, dimensions={0} | all-to-all | bytes 2097152 | tf_op jit(solution)/shard_map/all_to_all | solution.py:399
  154.8 4.3 %forward_products.3 = (f32[1024,128]{1,0:T(8,128)S(1)}, f32[1024,128]{1,0:T(8,128)S(1)}) custom-call(s32[1]{0:T(128)} %bitcast.core_ref, s32[256]{0:T(256)S(1)} %bitcast.22, s32[256]{0:T(256)S(1)} %bitcast.26, bf16[32,128,128]{2,1,0:T(8,128)(2,1)S(1)} %all_to_all.23.probe_ref, bf16[256,128,128]{2,1,0:T(8,128)(2,1)S(1)} %get-tuple-element.17.tiles_ref), custom_call_target="tpu_custom_call" | custom-call | flops 134217728 | bytes 4194304 | tf_op jit(solution)/shard_map/forward_products/pallas_call | solution.py:319
  159.1 0.1 collective-permute-start.4
  159.2 1.9 %collective-permute-done.4.second_ref.other_ref = f32[1024,128]{1,0:T(8,128)S(1)} collective-permute-done((f32[1024,128]{1,0:T(8,128)S(1)}, f32[1024,128]{1,0:T(8,128)S(1)}, u32[]{:S(2)}, u32[]{:S(2)}) %collective-permute-start.4) | collective-permute-done | bytes 524320 | tf_op jit(solution)/shard_map/ppermute | solution.py:345
  161.1 1.5 collective-permute-start.5
  162.7 4.9 %collective-permute-done.5.second_ref.refs_0_ = bf16[1024,128]{1,0:T(8,128)(2,1)S(1)} collective-permute-done((bf16[1024,128]{1,0:T(8,128)(2,1)S(1)}, bf16[1024,128]{1,0:T(8,128)(2,1)S(1)}, u32[]{:S(2)}, u32[]{:S(2)}) %collective-permute-start.5) | collective-permute-done | bytes 262176 | tf_op jit(solution)/shard_map/ppermute | solution.py:350
  167.6 0.1 chip_sum.3
  167.6 1.5 collective-permute-start.6
  169.2 4.9 %collective-permute-done.6.refs_1_ = bf16[1024,128]{1,0:T(8,128)(2,1)S(1)} collective-permute-done((bf16[1024,128]{1,0:T(8,128)(2,1)S(1)}, bf16[1024,128]{1,0:T(8,128)(2,1)S(1)}, u32[]{:S(2)}, u32[]{:S(2)}) %collective-permute-start.6) | collective-permute-done | bytes 262176 | tf_op jit(solution)/shard_map/ppermute | solution.py:350
  174.1 0.2 dual_update.3.own_ref
  174.3 0.1 collective-permute-start.7
  174.4 1.9 %collective-permute-done.7.other_ref = f32[1024,128]{1,0:T(8,128)S(1)} collective-permute-done((f32[1024,128]{1,0:T(8,128)S(1)}, f32[1024,128]{1,0:T(8,128)S(1)}, u32[]{:S(2)}, u32[]{:S(2)}) %collective-permute-start.7) | collective-permute-done | bytes 524320 | tf_op jit(solution)/shard_map/ppermute | solution.py:345
  176.3 1.0 assemble_duals.1
  (2 shorter events, 0.1 us)
Async XLA Ops:
  0.6 68.8 %copy-start.5 = (s32[1,1,256]{2,1,0:T(1,128)S(1)}, s32[1,1,256]{2,1,0:T(1,128)}, u32[]{:S(2)}) copy-start(s32[1,1,256]{2,1,0:T(1,128)} %param.11) | copy-start | bytes 3076
  0.6 68.8 %copy-start.4 = (s32[1,1,256]{2,1,0:T(1,128)S(1)}, s32[1,1,256]{2,1,0:T(1,128)}, u32[]{:S(2)}) copy-start(s32[1,1,256]{2,1,0:T(1,128)} %param.10) | copy-start | bytes 3076
  0.7 38.2 %copy-start.3 = (f32[128,256]{1,0:T(8,128)S(1)}, f32[128,256]{1,0:T(8,128)}, u32[]{:S(2)}) copy-start(f32[128,256]{1,0:T(8,128)} %refs_3_.1) | copy-start | bytes 393220
  0.7 38.2 %copy-start.7 = (s32[256]{0:T(256)S(1)}, s32[256]{0:T(256)}, u32[]{:S(2)}) copy-start(s32[256]{0:T(256)} %param.16) | copy-start | bytes 3076
  0.7 38.2 %copy-start.6 = (s32[256]{0:T(256)S(1)}, s32[256]{0:T(256)}, u32[]{:S(2)}) copy-start(s32[256]{0:T(256)} %param.15) | copy-start | bytes 3076
  0.7 38.2 %copy-start.2 = (f32[4,128,256]{2,1,0:T(8,128)S(1)}, f32[4,128,256]{2,1,0:T(8,128)}, u32[]{:S(2)}) copy-start(f32[4,128,256]{2,1,0:T(8,128)} %refs_1_.1) | copy-start | bytes 1572868
  5.5 83.3 %copy-start = (s32[16,16384]{1,0:T(8,128)S(1)}, s32[16,16384]{1,0:T(8,128)}, u32[]{:S(2)}) copy-start(s32[16,16384]{1,0:T(8,128)} %param.17) | copy-start | bytes 3145732
  5.5 83.3 %copy-start.1 = (f32[16,16384]{1,0:T(8,128)S(1)}, f32[16,16384]{1,0:T(8,128)}, u32[]{:S(2)}) copy-start(f32[16,16384]{1,0:T(8,128)} %param.13) | copy-start | bytes 3145732
  73.8 2.0 %collective-permute-start = (f32[1024,128]{1,0:T(8,128)S(1)}, f32[1024,128]{1,0:T(8,128)S(1)}, u32[]{:S(2)}, u32[]{:S(2)}) collective-permute-start(f32[1024,128]{1,0:T(8,128)S(1)} %get-tuple-element.19), channel_id=1, source_target_pairs={{0,1},{1,0},{2,3},{3,2},{4,5},{5,4},{6,7},{7,6},{8,9},{9,8},{10,11... | collective-permute-start | bytes 1572872 | tf_op jit(solution)/shard_map/ppermute | solution.py:345
  75.8 6.4 %collective-permute-start.1 = (bf16[1024,128]{1,0:T(8,128)(2,1)S(1)}, bf16[1024,128]{1,0:T(8,128)(2,1)S(1)}, u32[]{:S(2)}, u32[]{:S(2)}) collective-permute-start(bf16[1024,128]{1,0:T(8,128)(2,1)S(1)} %core_pair_sum.2.first_ref), channel_id=1, source_target_pairs={{0,2},{1,5},{2,0},{3,7},{4,6},{5,1},{6,4},{7,3},{8,10},{9,13},{10,... | collective-permute-start | bytes 786440 | tf_op jit(solution)/shard_map/ppermute | solution.py:350
  82.3 6.4 %collective-permute-start.2 = (bf16[1024,128]{1,0:T(8,128)(2,1)S(1)}, bf16[1024,128]{1,0:T(8,128)(2,1)S(1)}, u32[]{:S(2)}, u32[]{:S(2)}) collective-permute-start(bf16[1024,128]{1,0:T(8,128)(2,1)S(1)} %chip_sum.2), channel_id=1, source_target_pairs={{0,4},{1,3},{2,6},{3,1},{4,0},{5,7},{6,2},{7,5},{8,12},{9,11},{10,... | collective-permute-start | bytes 786440 | tf_op jit(solution)/shard_map/ppermute | solution.py:350
  89.0 1.6 collective-permute-start.3
  159.1 2.0 %collective-permute-start.4 = (f32[1024,128]{1,0:T(8,128)S(1)}, f32[1024,128]{1,0:T(8,128)S(1)}, u32[]{:S(2)}, u32[]{:S(2)}) collective-permute-start(f32[1024,128]{1,0:T(8,128)S(1)} %get-tuple-element.26), channel_id=1, source_target_pairs={{0,1},{1,0},{2,3},{3,2},{4,5},{5,4},{6,7},{7,6},{8,9},{9,8},{10,11... | collective-permute-start | bytes 1572872 | tf_op jit(solution)/shard_map/ppermute | solution.py:345
  161.1 6.4 %collective-permute-start.5 = (bf16[1024,128]{1,0:T(8,128)(2,1)S(1)}, bf16[1024,128]{1,0:T(8,128)(2,1)S(1)}, u32[]{:S(2)}, u32[]{:S(2)}) collective-permute-start(bf16[1024,128]{1,0:T(8,128)(2,1)S(1)} %core_pair_sum.3.first_ref), channel_id=1, source_target_pairs={{0,2},{1,5},{2,0},{3,7},{4,6},{5,1},{6,4},{7,3},{8,10},{9,13},{10,... | collective-permute-start | bytes 786440 | tf_op jit(solution)/shard_map/ppermute | solution.py:350
  167.6 6.4 %collective-permute-start.6 = (bf16[1024,128]{1,0:T(8,128)(2,1)S(1)}, bf16[1024,128]{1,0:T(8,128)(2,1)S(1)}, u32[]{:S(2)}, u32[]{:S(2)}) collective-permute-start(bf16[1024,128]{1,0:T(8,128)(2,1)S(1)} %chip_sum.3), channel_id=1, source_target_pairs={{0,4},{1,3},{2,6},{3,1},{4,0},{5,7},{6,2},{7,5},{8,12},{9,11},{10,... | collective-permute-start | bytes 786440 | tf_op jit(solution)/shard_map/ppermute | solution.py:350
  174.3 2.0 %collective-permute-start.7 = (f32[1024,128]{1,0:T(8,128)S(1)}, f32[1024,128]{1,0:T(8,128)S(1)}, u32[]{:S(2)}, u32[]{:S(2)}) collective-permute-start(f32[1024,128]{1,0:T(8,128)S(1)} %dual_update.3.own_ref), channel_id=1, source_target_pairs={{0,1},{1,0},{2,3},{3,2},{4,5},{5,4},{6,7},{7,6},{8,9},{9,8},{10,11... | collective-permute-start | bytes 1572872 | tf_op jit(solution)/shard_map/ppermute | solution.py:345

commit v5 on v4

v5 whole, which is shorter than its diff:
```python
import functools
import math

import jax
import jax.numpy as jnp
from jax import lax
from jax.experimental import pallas as pl
from jax.experimental.pallas import tpu as pltpu
from jax.sharding import PartitionSpec as P

ITERS = 2
SIGMA_STEP = 0.2
PARTS = 2
WIDE = 64
NARROW = 16
FIRST = 32
PITCH_PAD = 8
VMEM_BYTES = 24 * 1024 * 1024
TRANSPOSED = (((1,), (1,)), ((), ()))


def params():
    return pltpu.CompilerParams(vmem_limit_bytes=VMEM_BYTES)


def whole():
    return pl.BlockSpec(memory_space=pltpu.VMEM)


def scalars():
    return pl.BlockSpec(memory_space=pltpu.SMEM)


def stacked_pair(first, second):
    zero = jnp.zeros_like(first)
    return jnp.concatenate(
        [jnp.concatenate([first, zero], axis=1), jnp.concatenate([zero, second], axis=1)], axis=0
    )


def column_place(dims, column):
    time_block, flight_tiles = dims[3], dims[4]
    return column % flight_tiles * time_block + column // flight_tiles


def list_size(count):
    return PARTS * 3 * (count + NARROW) + PARTS


def list_base(count, part, field):
    return (part * 3 + field) * (count + NARROW)


def over_list(count, part, lists_ref, body):
    def entry(field, index):
        return lists_ref[list_base(count, part, field) + index]

    total = lists_ref[list_base(count, PARTS, 0) + part]
    wide = total // WIDE

    def wide_body(index, _):
        body(entry, index * WIDE, WIDE)
        return 0

    def narrow_body(index, _):
        body(entry, wide * WIDE + index * NARROW, NARROW)
        return 0

    lax.fori_loop(0, wide, wide_body, 0)
    lax.fori_loop(0, (total - wide * WIDE + NARROW - 1) // NARROW, narrow_body, 0)


def row_part(core, part, quarter):
    return (core * PARTS + part) * quarter


def backward_blocks(scen, pitch, width, entry, start, duals_ref, tiles_ref, acc_ref):
    products = []
    for u in range(0, width, 2):
        block, row, _ = entry(start + u)
        next_block, next_row, _ = entry(start + u + 1)
        result = jnp.dot(
            stacked_pair(duals_ref[row], duals_ref[next_row]),
            jnp.concatenate([tiles_ref[block], tiles_ref[next_block]], axis=0),
            preferred_element_type=jnp.float32,
        )
        products += [result[:scen], result[scen:]]
    for u in range(width):
        place = pl.multiple_of(entry(start + u)[2] * pitch, 8)
        acc_ref[pl.ds(place, scen), :] += products[u]


def write_messages(dims, pitch, acc_ref, out_ref):
    n_row, n_col, scen_local, time_block, _, own_tiles = dims
    piece = own_tiles * time_block
    for group in range(n_row):
        for column in range(n_col):
            for j in range(scen_local):
                base = column * own_tiles * time_block * pitch + group * scen_local + j
                parts = [
                    acc_ref[pl.ds(base + f * time_block * pitch, time_block, stride=pitch), :]
                    for f in range(own_tiles)
                ]
                out_ref[group * n_col + column, pl.ds(j * piece, piece), :] = jnp.concatenate(
                    parts, axis=0
                ).astype(jnp.bfloat16)


def first_backward_kernel(
    dims, pitch, core_ref, row_source, col_source, dual_source, source_ref, out_ref, tiles_ref, lists_ref,
    rows_ref, cols_ref, bands_ref, duals_ref, acc_ref, sems
):
    scen = dims[0] * dims[2]
    count, pieces = tiles_ref.shape[0], sems.shape[0] - 3
    chunk = count // pieces
    quarter = duals_ref.shape[0] // (2 * PARTS)
    lists = [
        pltpu.make_async_copy(row_source, rows_ref, sems.at[pieces]),
        pltpu.make_async_copy(col_source, cols_ref, sems.at[pieces + 1]),
        pltpu.make_async_copy(dual_source, bands_ref, sems.at[pieces + 2]),
    ]
    copies = [
        pltpu.make_async_copy(source_ref.at[pl.ds(i * chunk, chunk)], tiles_ref.at[pl.ds(i * chunk, chunk)], sems.at[i])
        for i in range(pieces)
    ]
    for copy in lists + copies:
        copy.start()
    acc_ref[...] = jnp.zeros_like(acc_ref)
    for copy in lists:
        copy.wait()
    bands = [bands_ref[a].astype(jnp.bfloat16) for a in range(bands_ref.shape[0])]
    duals_ref[...] = jnp.concatenate(bands, axis=1)

    def put(part, index, block, row, place):
        base = part * 3 * (count + NARROW) + index
        lists_ref[base] = block
        lists_ref[base + count + NARROW] = row
        lists_ref[base + 2 * (count + NARROW)] = place

    def body(index, totals):
        start = index * FIRST

        def entry(block):
            return block, rows_ref[block], column_place(dims, cols_ref[block])

        backward_blocks(scen, pitch, FIRST, entry, start, duals_ref, tiles_ref, acc_ref)
        zero, one = totals
        for u in range(FIRST):
            block, row, place = entry(start + u)
            part = row // quarter % PARTS
            put(part, jnp.where(part == 0, zero, one), block, row, place)
            zero, one = zero + 1 - part, one + part
        return zero, one

    totals = (jnp.int32(0), jnp.int32(0))
    for i, copy in enumerate(copies):
        copy.wait()
        totals = lax.fori_loop(i * chunk // FIRST, (i + 1) * chunk // FIRST, body, totals)
    for part in range(PARTS):
        lists_ref[list_base(count, PARTS, 0) + part] = totals[part]
        for extra in range(NARROW):
            put(part, totals[part] + extra, 0, duals_ref.shape[0], dims[3] * dims[4])
    write_messages(dims, pitch, acc_ref, out_ref)


def backward_kernel(dims, pitch, part, core_ref, lists_ref, own_ref, other_ref, tiles_ref, *refs):
    scen = dims[0] * dims[2]
    duals_ref = refs[-1] if part == 0 else refs[-2]
    acc_ref = refs[0] if part == 0 else refs[-1]
    quarter, side = own_ref.shape[0] // scen, own_ref.shape[1]
    core = core_ref[0]
    duals_ref[pl.ds(row_part(core, part, quarter), quarter)] = own_ref[...].reshape(quarter, scen, side)
    duals_ref[pl.ds(row_part(1 - core, part, quarter), quarter)] = other_ref[...].reshape(quarter, scen, side)
    duals_ref[duals_ref.shape[0] - 1] = jnp.zeros((scen, side), jnp.bfloat16)
    acc_ref[...] = jnp.zeros_like(acc_ref) if part == 0 else refs[0][...]

    def body(entry, start, width):
        def fields(index):
            return entry(0, index), entry(1, index), entry(2, index)

        backward_blocks(scen, pitch, width, fields, start, duals_ref, tiles_ref, acc_ref)

    over_list(tiles_ref.shape[0], part, lists_ref, body)
    if part == PARTS - 1:
        write_messages(dims, pitch, acc_ref, refs[1])


def forward_kernel(dims, pitch, part, core_ref, lists_ref, probe_ref, tiles_ref, own_ref, away_ref, *refs):
    n_row, n_col, scen_local, time_block, _, own_tiles = dims
    scen = n_row * scen_local
    piece = own_tiles * time_block
    core = core_ref[0]
    acc_ref = refs[-1]
    acc_ref[...] = jnp.zeros_like(acc_ref)
    if part == 0:
        flat_ref = refs[0]
        for group in range(n_row):
            for column in range(n_col):
                for j in range(scen_local):
                    base = column * own_tiles * time_block * pitch + group * scen_local + j
                    block = probe_ref[group * n_col + column, pl.ds(j * piece, piece), :].astype(jnp.float32)
                    for f in range(own_tiles):
                        flat_ref[pl.ds(base + f * time_block * pitch, time_block, stride=pitch), :] = block[
                            f * time_block : (f + 1) * time_block
                        ]
        null = flat_ref.shape[0] - pitch
        flat_ref[pl.ds(null, pitch), :] = jnp.zeros((pitch, flat_ref.shape[1]), jnp.float32)
    else:
        flat_ref = probe_ref

    def body(entry, start, width):
        def picked(index):
            return flat_ref[pl.ds(pl.multiple_of(entry(2, index) * pitch, 8), scen), :].astype(jnp.bfloat16)

        products = []
        for u in [start + v for v in range(0, width, 2)]:
            both = jnp.concatenate([tiles_ref[entry(0, u)], tiles_ref[entry(0, u + 1)]], axis=1)
            result = lax.dot_general(
                stacked_pair(picked(u), picked(u + 1)), both, TRANSPOSED, preferred_element_type=jnp.float32
            )
            products += [result[:scen], result[scen:]]
        for u in range(width):
            place = pl.multiple_of(entry(1, start + u) * scen, scen)
            acc_ref[pl.ds(place, scen), :] += products[u]

    over_list(tiles_ref.shape[0], part, lists_ref, body)
    size = own_ref.shape[0]
    own_ref[...] = acc_ref[pl.ds(pl.multiple_of(row_part(core, part, size), scen), size), :]
    away_ref[...] = acc_ref[pl.ds(pl.multiple_of(row_part(1 - core, part, size), scen), size), :]


def running(values, trailing, terms):
    length = values.shape[0]
    row_iota = lax.broadcasted_iota(jnp.int32, (length, length), 0)
    col_iota = lax.broadcasted_iota(jnp.int32, (length, length), 1)
    keep = ((col_iota >= row_iota) if trailing else (row_iota >= col_iota)).astype(jnp.float32).astype(jnp.bfloat16)
    total = None
    for _ in range(terms):
        term = values.astype(jnp.bfloat16)
        values = values - term.astype(jnp.float32)
        part = jnp.dot(keep, term, preferred_element_type=jnp.float32)
        total = part if total is None else total + part
    return total


def primal_kernel(dims, first, last, *refs):
    n_row, n_col, scen_local, time_block, _, own_tiles = dims
    refs = list(refs)
    recv_ref, inc_ref = refs[:2]
    cum_ref = None if first else refs[2]
    cost_ref, start_ref, len_ref, inc_out, send_ref = refs[2 + (not first) :][:5]
    cum_out = None if last else refs[-1]
    window, flight_local = cost_ref.shape
    side = flight_local // own_tiles
    piece = own_tiles * time_block
    tau_step = 0.6 / math.sqrt(window)
    minutes = lax.broadcasted_iota(jnp.int32, (window, flight_local), 0)
    begin = start_ref[...]
    upper = ((minutes >= begin) & (minutes < begin + len_ref[...])).astype(jnp.float32)
    slopes = []
    for j in range(scen_local):
        bands = []
        for h in range(n_col):
            total = recv_ref[h, pl.ds(j * piece, piece), :].astype(jnp.float32)
            for g in range(1, n_row):
                total = total + recv_ref[g * n_col + h, pl.ds(j * piece, piece), :].astype(jnp.float32)
            bands.append(
                jnp.concatenate([total[f * time_block : (f + 1) * time_block] for f in range(own_tiles)], axis=1)
            )
        slopes.append(jnp.concatenate(bands, axis=0) + cost_ref[...])
    gradient = running(jnp.concatenate(slopes, axis=1), True, 2)
    old = jnp.concatenate([inc_ref[j] for j in range(scen_local)], axis=1)
    if first:
        old_sum = running(old, False, 3)
    else:
        old_sum = jnp.concatenate([cum_ref[j] for j in range(scen_local)], axis=1)
    fresh = jnp.clip(old - tau_step * gradient, 0.0, jnp.concatenate([upper] * scen_local, axis=1))
    fresh_sum = running(fresh, False, 3)
    probe = (2.0 * fresh_sum - old_sum).astype(jnp.bfloat16)
    for j in range(scen_local):
        lanes = slice(j * flight_local, (j + 1) * flight_local)
        inc_out[j] = fresh[:, lanes]
        if not last:
            cum_out[j] = fresh_sum[:, lanes]
        for h in range(n_col):
            band = probe[h * time_block : (h + 1) * time_block, lanes]
            block = jnp.concatenate([band[:, f * side : (f + 1) * side] for f in range(own_tiles)], axis=0)
            for g in range(n_row):
                send_ref[g * n_col + h, pl.ds(j * piece, piece), :] = block


def sum_kernel(first_ref, second_ref, out_ref):
    out_ref[...] = (first_ref[...].astype(jnp.float32) + second_ref[...].astype(jnp.float32)).astype(jnp.bfloat16)


def dual_kernel(remote, part, first, last, core_ref, own_ref, other_ref, *refs):
    parts, (dual_ref, cap_ref, dual_out) = refs[:remote], refs[remote : remote + 3]
    total = own_ref[...] + other_ref[...]
    for received in parts:
        total = total + received[...].astype(jnp.float32)
    bands, row_tiles, band, side = cap_ref.shape
    quarter = row_tiles // (2 * PARTS)
    begin = row_part(core_ref[0], part, quarter)

    def own_rows(ref):
        return jnp.concatenate([ref[a, pl.ds(begin, quarter)] for a in range(bands)], axis=1).reshape(-1, side)

    old = own_rows(dual_ref) if first else dual_ref[...]
    fresh = jnp.maximum(old + SIGMA_STEP * (total - own_rows(cap_ref).astype(jnp.float32)), 0.0)
    dual_out[...] = fresh
    if not last:
        refs[-1][...] = fresh.astype(jnp.bfloat16)


def assemble_kernel(core_ref, *refs):
    out_ref = refs[-1]
    bands, row_tiles, band, side = out_ref.shape
    quarter = row_tiles // (2 * PARTS)
    for i, ref in enumerate(refs[:-1]):
        core = core_ref[0] if i < PARTS else 1 - core_ref[0]
        value = ref[...].reshape(quarter, bands * band, side)
        for a in range(bands):
            out_ref[a, pl.ds(row_part(core, i % PARTS, quarter), quarter)] = value[:, a * band : (a + 1) * band]


def per_device(
    tile_values, tile_rows, tile_cols, increments, dual_vars, flight_cost, win_start, win_len, capacity
):
    n_row, n_col = lax.axis_size("row"), lax.axis_size("col")
    count, side = tile_values.shape[2], tile_values.shape[3]
    scen_local, window, flight_local = increments.shape
    scen, row_length = dual_vars.shape
    row_tiles = row_length // side
    time_block = window // n_col
    flight_tiles = flight_local * n_col // side
    own_tiles = flight_local // side
    col_tiles = time_block * flight_tiles
    dims = (n_row, n_col, scen_local, time_block, flight_tiles, own_tiles)
    message = (n_row * n_col, scen_local * own_tiles * time_block, side)
    part_rows = row_tiles * scen // (2 * PARTS)
    pitch = scen + PITCH_PAD
    band = 8

    rows, cols = tile_rows.reshape(count), tile_cols.reshape(count)
    core = (lax.axis_index("col") % 2).reshape(1)
    cost = pl.CostEstimate(flops=2 * count * scen * side * side, bytes_accessed=count * side * side, transcendentals=0)
    acc_cols = pltpu.VMEM(((col_tiles + 1) * pitch, side), jnp.float32)
    picked_duals = pltpu.VMEM((row_tiles + 1, scen, side), jnp.bfloat16)
    messages = jax.ShapeDtypeStruct(message, jnp.bfloat16)
    part_f32 = jax.ShapeDtypeStruct((part_rows, side), jnp.float32)
    part_bf16 = jax.ShapeDtypeStruct((part_rows, side), jnp.bfloat16)

    def banded(array):
        return array.reshape(scen // band, band, row_tiles, side).transpose(0, 2, 1, 3)

    def in_hbm(array):
        return pltpu.with_memory_space_constraint(array, pltpu.HBM)

    def first_backward(duals):
        return pl.pallas_call(
            functools.partial(first_backward_kernel, dims, pitch),
            in_specs=[scalars()] + [pl.BlockSpec(memory_space=pltpu.HBM)] * 4,
            out_specs=[whole(), whole(), scalars()],
            out_shape=[
                messages,
                pltpu.VMEM((count, side, side), jnp.bfloat16),
                jax.ShapeDtypeStruct((list_size(count),), jnp.int32),
            ],
            scratch_shapes=[
                pltpu.SMEM((count,), jnp.int32),
                pltpu.SMEM((count,), jnp.int32),
                pltpu.VMEM(duals.shape, jnp.float32),
                pltpu.VMEM((row_tiles, scen, side), jnp.bfloat16),
                acc_cols,
                pltpu.SemaphoreType.DMA((count // FIRST + 3,)),
            ],
            compiler_params=params(),
            cost_estimate=cost,
            name="first_backward_products",
        )(core, in_hbm(rows), in_hbm(cols), in_hbm(duals), in_hbm(tile_values.reshape(count, side, side)))

    def in_vmem(array):
        return pltpu.with_memory_space_constraint(array, pltpu.VMEM)

    def backward(part, own, other, tiles, lists, *sums):
        first = part == 0
        return pl.pallas_call(
            functools.partial(backward_kernel, dims, pitch, part),
            in_specs=[scalars()] * 2 + [whole()] * (3 if first else 4),
            out_specs=whole(),
            out_shape=acc_cols if first else messages,
            scratch_shapes=[picked_duals] if first else [picked_duals, acc_cols],
            compiler_params=params(),
            cost_estimate=cost,
            name="backward_products",
        )(core, lists, own, other, in_vmem(tiles), *map(in_vmem, sums))

    def forward(part, probe, tiles, lists):
        first = part == 0
        return pl.pallas_call(
            functools.partial(forward_kernel, dims, pitch, part),
            in_specs=[scalars()] * 2 + [whole()] * 2,
            out_specs=[whole()] * (3 if first else 2),
            out_shape=[part_f32] * 2 + ([acc_cols] if first else []),
            scratch_shapes=[pltpu.VMEM(((row_tiles + 1) * scen, side), jnp.float32)],
            compiler_params=params(),
            cost_estimate=cost,
            name="forward_products",
        )(core, lists, probe if first else in_vmem(probe), in_vmem(tiles))

    def primal_step(recv, primal, cumulative, last):
        first = cumulative is None
        state = (primal,) if first else (primal, cumulative)
        shape = jax.ShapeDtypeStruct(primal.shape, jnp.float32)
        out_shape = [shape, messages] if last else [shape, messages, shape]
        return pl.pallas_call(
            functools.partial(primal_kernel, dims, first, last),
            in_specs=[whole()] * (4 + len(state)),
            out_specs=[whole()] * len(out_shape),
            out_shape=out_shape,
            compiler_params=params(),
            name="primal_update",
        )(recv, *state, flight_cost, win_start.reshape(1, -1), win_len.reshape(1, -1))

    def swap_core(value):
        return lax.ppermute(value, "col", [(i, i ^ 1) for i in range(n_col)])

    bits = (n_col // 2).bit_length() - 1

    def swap_chip(value, step):
        return lax.ppermute(value, "col", [(i, i ^ (2 << (step + i % 2) % bits)) for i in range(n_col)])

    def bf16_sum(first, second, name):
        return pl.pallas_call(
            sum_kernel,
            in_specs=[whole()] * 2,
            out_specs=whole(),
            out_shape=part_bf16,
            compiler_params=params(),
            name=name,
        )(first, second)

    def dual_step(part, own, away, dual, first, last):
        other = swap_core(away)
        partial = bf16_sum(own, other, "core_pair_sum")
        parts = []
        for step in range(bits):
            parts.append(swap_chip(partial, step))
            if step + 1 < bits:
                partial = bf16_sum(partial, parts[-1], "chip_sum")
        out_shape = [part_f32] if last else [part_f32, part_bf16]
        return pl.pallas_call(
            functools.partial(dual_kernel, bits, part, first, last),
            in_specs=[scalars()] + [whole()] * (bits + 4),
            out_specs=[whole()] * len(out_shape),
            out_shape=out_shape,
            compiler_params=params(),
            name="dual_update",
        )(core, own, other, *parts, dual, banded(capacity))

    def assemble(owned):
        pieces = [*owned, *map(swap_core, owned)]
        return pl.pallas_call(
            assemble_kernel,
            in_specs=[scalars()] + [whole()] * len(pieces),
            out_specs=whole(),
            out_shape=jax.ShapeDtypeStruct((scen // band, row_tiles, band, side), jnp.float32),
            compiler_params=params(),
            name="assemble_duals",
        )(core, *pieces)

    send, tiles, lists = first_backward(banded(dual_vars))
    duals, primal, cumulative = [banded(dual_vars)] * PARTS, increments, None
    for sweep in range(ITERS):
        last = sweep + 1 == ITERS
        if sweep:
            sums = backward(0, rounded[0], swap_core(rounded[0]), tiles, lists)
            send = backward(1, rounded[1], swap_core(rounded[1]), tiles, lists, sums)
        recv = lax.all_to_all(send, ("row", "col"), 0, 0, tiled=True)
        primal, send, *cumulative = primal_step(recv, primal, cumulative, last)
        cumulative = None if last else cumulative[0]
        probe = lax.all_to_all(send, ("row", "col"), 0, 0, tiled=True)
        own, away, flat = forward(0, probe, tiles, lists)
        images = [(own, away), forward(1, flat, tiles, lists)]
        results = [dual_step(part, *images[part], duals[part], sweep == 0, last) for part in range(PARTS)]
        duals = [result[0] for result in results]
        rounded = None if last else [result[1] for result in results]
    duals_out = assemble(duals).transpose(0, 2, 1, 3).reshape(scen, row_length)
    return (primal, duals_out)


def solution(mesh):
    placed = (
        P("row", "col", None, None, None),
        P("row", "col", None),
        P("row", "col", None),
        P("row", None, "col"),
        P(None, "row"),
        P(None, "col"),
        P("col"),
        P("col"),
        P(None, "row"),
    )
    return jax.shard_map(
        per_device,
        mesh=mesh,
        in_specs=placed,
        out_specs=(P("row", None, "col"), P(None, "row")),
        check_vma=False,
    )
```

time: 178 us -> 180 us (1.011)
  waiting for transfers between devices: 26.8 us -> 14.3 us
  Pallas kernels: 20.9 us -> 29.6 us
  starting transfers between devices: 6.42 us -> 12.4 us
    ppermute x4 -> x8, waiting for transfers between devices: 19.6 us -> 11.8 us  [swap_chip(): lax.ppermute(value, 'col', [(i, i ^ 2 << (step + i % 2) % bits) for i in...]
    ppermute x4 -> x8, starting transfers between devices: 6.14 us -> 10.9 us  [swap_chip(): lax.ppermute(value, 'col', [(i, i ^ 2 << (step + i % 2) % bits) for i in...]
    ppermute x4 -> x8, waiting for transfers between devices: 7.21 us -> 2.55 us  [swap_core(): return lax.ppermute(value, 'col', [(i, i ^ 1) for i in range(n_col)])]
    pallas_call x1, Pallas kernels: 4.76 us -> 9.18 us  [first_backward(): pl.pallas_call(functools.partial(first_backward_kernel, dims, pitch), in_...]
    pallas_call x6 -> x11, Pallas kernels: 13.6 us -> 17.8 us  [the longest x4 11.5 us: forward(): pl.pallas_call(functools.partial(forward_kernel, dims, pitch, part), in_s...]
  transfers between devices with their start and end apart: 8 -> 16, of which waited for: 8 -> 8; matrix products, arithmetic and copies ran while one was open for 0% -> 0% of each run, Pallas kernels for 0% -> 3%
where the time goes in v5:
time: 180 us; the launch traced here: 179 us
  blocking collectives  122 us (68%)
  Pallas kernels  29.6 us (16%)
  waiting for transfers between devices  14.3 us (8%)
  starting transfers between devices  12.4 us (7%)
    all_to_all x2, blocking collectives, per_device(): recv = lax.all_to_all(send, ('row', 'col'), 0, 0, tiled=True)  62.9 us
    all_to_all x2, blocking collectives, per_device(): probe = lax.all_to_all(send, ('row', 'col'), 0, 0, tiled=True)  59.3 us
    ppermute x8, waiting for transfers between devices, swap_chip(): lax.ppermute(value, 'col', [(i, i ^ 2 << (step + i % 2) % bits) for i in...  11.8 us
    pallas_call x4, Pallas kernels, forward(): pl.pallas_call(functools.partial(forward_kernel, dims, pitch, part), in_s...  11.5 us
    ppermute x8, starting transfers between devices, swap_chip(): lax.ppermute(value, 'col', [(i, i ^ 2 << (step + i % 2) % bits) for i in...  10.9 us
    pallas_call x1, Pallas kernels, first_backward(): pl.pallas_call(functools.partial(first_backward_kernel, dims, pitch), in_...  9.18 us
    pallas_call x2, Pallas kernels, backward(): pl.pallas_call(functools.partial(backward_kernel, dims, pitch, part), in_...  4.86 us
  transfers between devices with their start and end apart: 16, of which 8 were waited for; matrix products, arithmetic and copies ran while one was open for 0% of the time, Pallas kernels for 3%

profile of v5, /device:TPU:0, one launch (start us, length us, event | category | flops | bytes accessed | tf_op | source)
XLA Modules:
  0.0 179.4 jit_solution(8562842139999194797)
XLA Ops:
  0.7 9.2 %first_backward_products.1 = (bf16[32,128,128]{2,1,0:T(8,128)(2,1)S(1)}, bf16[256,128,128]{2,1,0:T(8,128)(2,1)S(1)}, s32[1634]{0:T(1024)S(1)}) custom-call(s32[1]{0:T(128)} %bitcast.core_ref, s32[256]{0:T(256)} %bitcast.28, s32[256]{0:T(256)} %bitcast.29, f32[2,128,8,128]{3,2,1,0:T(8,128)} %bitcast.19, bf16[256,128,128]{2,1,0:T(8,128)(2,1)} %bitcast.26), custom_call_target="tpu_custom_call" | custom-call | flops 134217728 | bytes 4194304 | tf_op jit(solution)/shard_map/first_backward_products/pallas_call | solution.py:360
  9.9 33.3 %all_to_all.20.refs_0_ = bf16[32,128,128]{2,1,0:T(8,128)(2,1)S(1)} all-to-all(bf16[32,128,128]{2,1,0:T(8,128)(2,1)S(1)} %get-tuple-element.25), channel_id=1, replica_groups=mesh['row'=4,'col'=8] {'row','col'}, dimensions={0} | all-to-all | bytes 2097152 | tf_op jit(solution)/shard_map/all_to_all | solution.py:479
  43.2 1.0 primal_update.2
  44.2 29.7 %all_to_all.21.probe_ref = bf16[32,128,128]{2,1,0:T(8,128)(2,1)S(1)} all-to-all(bf16[32,128,128]{2,1,0:T(8,128)(2,1)S(1)} %get-tuple-element.26), channel_id=1, replica_groups=mesh['row'=4,'col'=8] {'row','col'}, dimensions={0} | all-to-all | bytes 2097152 | tf_op jit(solution)/shard_map/all_to_all | solution.py:482
  73.9 3.0 %forward_products.4 = (f32[512,128]{1,0:T(8,128)S(1)}, f32[512,128]{1,0:T(8,128)S(1)}, f32[6168,128]{1,0:T(8,128)S(1)}) custom-call(s32[1]{0:T(128)} %bitcast.core_ref, s32[1634]{0:T(1024)S(1)} %get-tuple-element.24.lists_ref, bf16[32,128,128]{2,1,0:T(8,128)(2,1)S(1)} %all_to_all.21.probe_ref, bf16[256,128,128]{2,1,0:T(8,128)(2,1)S(1)} %get-tuple-element.27.tiles_ref), custom_call_target="tpu_custom_call" | custom-call | flops 134217728 | bytes 4194304 | tf_op jit(solution)/shard_map/forward_products/pallas_call | solution.py:400
  76.9 0.1 collective-permute-start.4
  77.0 0.0 copy-start
  77.0 0.0 copy-start.1
  77.0 2.7 %forward_products.5 = (f32[512,128]{1,0:T(8,128)S(1)}, f32[512,128]{1,0:T(8,128)S(1)}) custom-call(s32[1]{0:T(128)} %bitcast.core_ref, s32[1634]{0:T(1024)S(1)} %get-tuple-element.24.lists_ref, f32[6168,128]{1,0:T(8,128)S(1)} %get-tuple-element.28.probe_ref, bf16[256,128,128]{2,1,0:T(8,128)(2,1)S(1)} %get-tuple-element.27.tiles_ref), custom_call_target="tpu_custom_call" | custom-call | flops 134217728 | bytes 4194304 | tf_op jit(solution)/shard_map/forward_products/pallas_call | solution.py:400
  79.7 0.5 collective-permute-start
  80.3 1.5 collective-permute-start.5
  81.8 1.1 collective-permute-start.1
  83.0 2.4 %collective-permute-done.5.second_ref.refs_0_ = bf16[512,128]{1,0:T(8,128)(2,1)S(1)} collective-permute-done((bf16[512,128]{1,0:T(8,128)(2,1)S(1)}, bf16[512,128]{1,0:T(8,128)(2,1)S(1)}, u32[]{:S(2)}, u32[]{:S(2)}) %collective-permute-start.5) | collective-permute-done | bytes 131104 | tf_op jit(solution)/shard_map/ppermute | solution.py:431
  85.4 1.5 collective-permute-start.6
  86.9 1.6 collective-permute-start.2
  88.5 1.9 %collective-permute-done.6.refs_1_ = bf16[512,128]{1,0:T(8,128)(2,1)S(1)} collective-permute-done((bf16[512,128]{1,0:T(8,128)(2,1)S(1)}, bf16[512,128]{1,0:T(8,128)(2,1)S(1)}, u32[]{:S(2)}, u32[]{:S(2)}) %collective-permute-start.6) | collective-permute-done | bytes 131104 | tf_op jit(solution)/shard_map/ppermute | solution.py:431
  90.4 0.1 dual_update.5
  90.5 0.1 collective-permute-start.7
  90.6 1.4 collective-permute-done.2.refs_1_
  92.0 0.1 dual_update.4
  92.1 0.1 collective-permute-start.3
  92.2 0.0 collective-permute-done.7.other_ref
  92.2 2.3 %backward_products.2.refs_0_ = f32[6168,128]{1,0:T(8,128)S(1)} custom-call(s32[1]{0:T(128)} %bitcast.core_ref, s32[1634]{0:T(1024)S(1)} %get-tuple-element.24.lists_ref, bf16[512,128]{1,0:T(8,128)(2,1)S(1)} %get-tuple-element.34.own_ref, bf16[512,128]{1,0:T(8,128)(2,1)S(1)} %collective-permute-done.7.other_ref, ...), custom_call_target="tpu_custom_call" | custom-call | flops 134217728 | bytes 4194304 | tf_op jit(solution)/shard_map/backward_products/pallas_call | solution.py:387
  94.4 0.0 collective-permute-done.3.other_ref
  94.4 2.6 %backward_products.3 = bf16[32,128,128]{2,1,0:T(8,128)(2,1)S(1)} custom-call(s32[1]{0:T(128)} %bitcast.core_ref, s32[1634]{0:T(1024)S(1)} %get-tuple-element.24.lists_ref, bf16[512,128]{1,0:T(8,128)(2,1)S(1)} %get-tuple-element.31.own_ref, bf16[512,128]{1,0:T(8,128)(2,1)S(1)} %collective-permute-done.3.other_ref, ...), custom_call_target="tpu_custom_call" | custom-call | flops 134217728 | bytes 4194304 | tf_op jit(solution)/shard_map/backward_products/pallas_call | solution.py:387
  97.1 29.6 %all_to_all.22.refs_0_ = bf16[32,128,128]{2,1,0:T(8,128)(2,1)S(1)} all-to-all(bf16[32,128,128]{2,1,0:T(8,128)(2,1)S(1)} %backward_products.3), channel_id=1, replica_groups=mesh['row'=4,'col'=8] {'row','col'}, dimensions={0} | all-to-all | bytes 2097152 | tf_op jit(solution)/shard_map/all_to_all | solution.py:479
  126.6 1.3 primal_update.3
  127.9 29.7 %all_to_all.23.probe_ref = bf16[32,128,128]{2,1,0:T(8,128)(2,1)S(1)} all-to-all(bf16[32,128,128]{2,1,0:T(8,128)(2,1)S(1)} %get-tuple-element.38), channel_id=1, replica_groups=mesh['row'=4,'col'=8] {'row','col'}, dimensions={0} | all-to-all | bytes 2097152 | tf_op jit(solution)/shard_map/all_to_all | solution.py:482
  157.6 3.0 %forward_products.6 = (f32[512,128]{1,0:T(8,128)S(1)}, f32[512,128]{1,0:T(8,128)S(1)}, f32[6168,128]{1,0:T(8,128)S(1)}) custom-call(s32[1]{0:T(128)} %bitcast.core_ref, s32[1634]{0:T(1024)S(1)} %get-tuple-element.24.lists_ref, bf16[32,128,128]{2,1,0:T(8,128)(2,1)S(1)} %all_to_all.23.probe_ref, bf16[256,128,128]{2,1,0:T(8,128)(2,1)S(1)} %get-tuple-element.27.tiles_ref), custom_call_target="tpu_custom_call" | custom-call | flops 134217728 | bytes 4194304 | tf_op jit(solution)/shard_map/forward_products/pallas_call | solution.py:400
  160.6 2.7 %forward_products.7 = (f32[512,128]{1,0:T(8,128)S(1)}, f32[512,128]{1,0:T(8,128)S(1)}) custom-call(s32[1]{0:T(128)} %bitcast.core_ref, s32[1634]{0:T(1024)S(1)} %get-tuple-element.24.lists_ref, f32[6168,128]{1,0:T(8,128)S(1)} %get-tuple-element.42.probe_ref, bf16[256,128,128]{2,1,0:T(8,128)(2,1)S(1)} %get-tuple-element.27.tiles_ref), custom_call_target="tpu_custom_call" | custom-call | flops 134217728 | bytes 4194304 | tf_op jit(solution)/shard_map/forward_products/pallas_call | solution.py:400
  163.3 0.1 collective-permute-start.11
  163.4 0.5 collective-permute-start.8
  163.9 1.0 collective-permute-done.11.second_ref.other_ref
  165.0 1.5 collective-permute-start.12
  166.6 0.6 collective-permute-start.9
  167.2 2.8 %collective-permute-done.12.second_ref.refs_0_ = bf16[512,128]{1,0:T(8,128)(2,1)S(1)} collective-permute-done((bf16[512,128]{1,0:T(8,128)(2,1)S(1)}, bf16[512,128]{1,0:T(8,128)(2,1)S(1)}, u32[]{:S(2)}, u32[]{:S(2)}) %collective-permute-start.12) | collective-permute-done | bytes 131104 | tf_op jit(solution)/shard_map/ppermute | solution.py:431
  170.1 1.5 collective-permute-start.13
  171.6 0.0 collective-permute-done.9.second_ref.refs_0_
  171.6 1.6 collective-permute-start.10
  173.2 1.9 %collective-permute-done.13.refs_1_ = bf16[512,128]{1,0:T(8,128)(2,1)S(1)} collective-permute-done((bf16[512,128]{1,0:T(8,128)(2,1)S(1)}, bf16[512,128]{1,0:T(8,128)(2,1)S(1)}, u32[]{:S(2)}, u32[]{:S(2)}) %collective-permute-start.13) | collective-permute-done | bytes 131104 | tf_op jit(solution)/shard_map/ppermute | solution.py:431
  175.1 0.1 dual_update.7.refs_1_
  175.2 0.1 collective-permute-start.15
  175.3 1.4 collective-permute-done.10.refs_1_
  176.7 0.1 dual_update.6.refs_0_
  176.8 0.1 collective-permute-start.14
  176.9 0.0 collective-permute-done.15.refs_3_
  176.9 1.5 collective-permute-done.14.refs_2_
  178.4 1.0 assemble_duals.1
  (22 shorter events, 0.3 us)
Async XLA Ops:
  0.6 42.6 %copy-start.2 = (f32[4,128,256]{2,1,0:T(8,128)S(1)}, f32[4,128,256]{2,1,0:T(8,128)}, u32[]{:S(2)}) copy-start(f32[4,128,256]{2,1,0:T(8,128)} %refs_1_.1) | copy-start | bytes 1572868
  0.7 42.6 %copy-start.3 = (f32[128,256]{1,0:T(8,128)S(1)}, f32[128,256]{1,0:T(8,128)}, u32[]{:S(2)}) copy-start(f32[128,256]{1,0:T(8,128)} %refs_3_.1) | copy-start | bytes 393220
  0.7 42.6 %copy-start.4 = (s32[256]{0:T(256)S(1)}, s32[256]{0:T(256)}, u32[]{:S(2)}) copy-start(s32[256]{0:T(256)} %param.15) | copy-start | bytes 3076
  0.7 42.6 %copy-start.5 = (s32[256]{0:T(256)S(1)}, s32[256]{0:T(256)}, u32[]{:S(2)}) copy-start(s32[256]{0:T(256)} %param.16) | copy-start | bytes 3076
  76.9 3.4 %collective-permute-start.4 = (f32[512,128]{1,0:T(8,128)S(1)}, f32[512,128]{1,0:T(8,128)S(1)}, u32[]{:S(2)}, u32[]{:S(2)}) collective-permute-start(f32[512,128]{1,0:T(8,128)S(1)} %get-tuple-element.33), channel_id=1, source_target_pairs={{0,1},{1,0},{2,3},{3,2},{4,5},{5,4},{6,7},{7,6},{8,9},{9,8},{10,11... | collective-permute-start | bytes 786440 | tf_op jit(solution)/shard_map/ppermute | solution.py:426
  77.0 13.4 %copy-start = (s32[16,16384]{1,0:T(8,128)S(1)}, s32[16,16384]{1,0:T(8,128)}, u32[]{:S(2)}) copy-start(s32[16,16384]{1,0:T(8,128)} %param.17) | copy-start | bytes 3145732
  77.0 13.4 %copy-start.1 = (f32[16,16384]{1,0:T(8,128)S(1)}, f32[16,16384]{1,0:T(8,128)}, u32[]{:S(2)}) copy-start(f32[16,16384]{1,0:T(8,128)} %param.13) | copy-start | bytes 3145732
  79.7 2.1 %collective-permute-start = (f32[512,128]{1,0:T(8,128)S(1)}, f32[512,128]{1,0:T(8,128)S(1)}, u32[]{:S(2)}, u32[]{:S(2)}) collective-permute-start(f32[512,128]{1,0:T(8,128)S(1)} %get-tuple-element.30), channel_id=1, source_target_pairs={{0,1},{1,0},{2,3},{3,2},{4,5},{5,4},{6,7},{7,6},{8,9},{9,8},{10,11... | collective-permute-start | bytes 786440 | tf_op jit(solution)/shard_map/ppermute | solution.py:426
  80.3 5.0 %collective-permute-start.5 = (bf16[512,128]{1,0:T(8,128)(2,1)S(1)}, bf16[512,128]{1,0:T(8,128)(2,1)S(1)}, u32[]{:S(2)}, u32[]{:S(2)}) collective-permute-start(bf16[512,128]{1,0:T(8,128)(2,1)S(1)} %core_pair_sum.5.first_ref), channel_id=1, source_target_pairs={{0,2},{1,5},{2,0},{3,7},{4,6},{5,1},{6,4},{7,3},{8,10},{9,13},{10,... | collective-permute-start | bytes 393224 | tf_op jit(solution)/shard_map/ppermute | solution.py:431
  81.8 5.1 %collective-permute-start.1 = (bf16[512,128]{1,0:T(8,128)(2,1)S(1)}, bf16[512,128]{1,0:T(8,128)(2,1)S(1)}, u32[]{:S(2)}, u32[]{:S(2)}) collective-permute-start(bf16[512,128]{1,0:T(8,128)(2,1)S(1)} %core_pair_sum.4.first_ref), channel_id=1, source_target_pairs={{0,2},{1,5},{2,0},{3,7},{4,6},{5,1},{6,4},{7,3},{8,10},{9,13},{10,... | collective-permute-start | bytes 393224 | tf_op jit(solution)/shard_map/ppermute | solution.py:431
  85.4 5.0 %collective-permute-start.6 = (bf16[512,128]{1,0:T(8,128)(2,1)S(1)}, bf16[512,128]{1,0:T(8,128)(2,1)S(1)}, u32[]{:S(2)}, u32[]{:S(2)}) collective-permute-start(bf16[512,128]{1,0:T(8,128)(2,1)S(1)} %chip_sum.5), channel_id=1, source_target_pairs={{0,4},{1,3},{2,6},{3,1},{4,0},{5,7},{6,2},{7,5},{8,12},{9,11},{10,... | collective-permute-start | bytes 393224 | tf_op jit(solution)/shard_map/ppermute | solution.py:431
  86.9 5.0 %collective-permute-start.2 = (bf16[512,128]{1,0:T(8,128)(2,1)S(1)}, bf16[512,128]{1,0:T(8,128)(2,1)S(1)}, u32[]{:S(2)}, u32[]{:S(2)}) collective-permute-start(bf16[512,128]{1,0:T(8,128)(2,1)S(1)} %chip_sum.4), channel_id=1, source_target_pairs={{0,4},{1,3},{2,6},{3,1},{4,0},{5,7},{6,2},{7,5},{8,12},{9,11},{10,... | collective-permute-start | bytes 393224 | tf_op jit(solution)/shard_map/ppermute | solution.py:431
  90.5 1.7 collective-permute-start.7
  92.1 2.3 %collective-permute-start.3 = (bf16[512,128]{1,0:T(8,128)(2,1)S(1)}, bf16[512,128]{1,0:T(8,128)(2,1)S(1)}, u32[]{:S(2)}, u32[]{:S(2)}) collective-permute-start(bf16[512,128]{1,0:T(8,128)(2,1)S(1)} %get-tuple-element.31.own_ref), channel_id=1, source_target_pairs={{0,1},{1,0},{2,3},{3,2},{4,5},{5,4},{6,7},{7,6},{8,9},{9,8},{10,11... | collective-permute-start | bytes 393224 | tf_op jit(solution)/shard_map/ppermute | solution.py:426
  163.3 1.6 collective-permute-start.11
  163.4 3.1 %collective-permute-start.8 = (f32[512,128]{1,0:T(8,128)S(1)}, f32[512,128]{1,0:T(8,128)S(1)}, u32[]{:S(2)}, u32[]{:S(2)}) collective-permute-start(f32[512,128]{1,0:T(8,128)S(1)} %get-tuple-element.40), channel_id=1, source_target_pairs={{0,1},{1,0},{2,3},{3,2},{4,5},{5,4},{6,7},{7,6},{8,9},{9,8},{10,11... | collective-permute-start | bytes 786440 | tf_op jit(solution)/shard_map/ppermute | solution.py:426
  165.0 5.0 %collective-permute-start.12 = (bf16[512,128]{1,0:T(8,128)(2,1)S(1)}, bf16[512,128]{1,0:T(8,128)(2,1)S(1)}, u32[]{:S(2)}, u32[]{:S(2)}) collective-permute-start(bf16[512,128]{1,0:T(8,128)(2,1)S(1)} %core_pair_sum.7.first_ref), channel_id=1, source_target_pairs={{0,2},{1,5},{2,0},{3,7},{4,6},{5,1},{6,4},{7,3},{8,10},{9,13},{10,... | collective-permute-start | bytes 393224 | tf_op jit(solution)/shard_map/ppermute | solution.py:431
  166.6 5.0 %collective-permute-start.9 = (bf16[512,128]{1,0:T(8,128)(2,1)S(1)}, bf16[512,128]{1,0:T(8,128)(2,1)S(1)}, u32[]{:S(2)}, u32[]{:S(2)}) collective-permute-start(bf16[512,128]{1,0:T(8,128)(2,1)S(1)} %core_pair_sum.6.first_ref), channel_id=1, source_target_pairs={{0,2},{1,5},{2,0},{3,7},{4,6},{5,1},{6,4},{7,3},{8,10},{9,13},{10,... | collective-permute-start | bytes 393224 | tf_op jit(solution)/shard_map/ppermute | solution.py:431
  170.1 5.0 %collective-permute-start.13 = (bf16[512,128]{1,0:T(8,128)(2,1)S(1)}, bf16[512,128]{1,0:T(8,128)(2,1)S(1)}, u32[]{:S(2)}, u32[]{:S(2)}) collective-permute-start(bf16[512,128]{1,0:T(8,128)(2,1)S(1)} %chip_sum.7), channel_id=1, source_target_pairs={{0,4},{1,3},{2,6},{3,1},{4,0},{5,7},{6,2},{7,5},{8,12},{9,11},{10,... | collective-permute-start | bytes 393224 | tf_op jit(solution)/shard_map/ppermute | solution.py:431
  171.6 5.0 %collective-permute-start.10 = (bf16[512,128]{1,0:T(8,128)(2,1)S(1)}, bf16[512,128]{1,0:T(8,128)(2,1)S(1)}, u32[]{:S(2)}, u32[]{:S(2)}) collective-permute-start(bf16[512,128]{1,0:T(8,128)(2,1)S(1)} %chip_sum.6), channel_id=1, source_target_pairs={{0,4},{1,3},{2,6},{3,1},{4,0},{5,7},{6,2},{7,5},{8,12},{9,11},{10,... | collective-permute-start | bytes 393224 | tf_op jit(solution)/shard_map/ppermute | solution.py:431
  175.2 1.7 collective-permute-start.15
  176.8 1.6 collective-permute-start.14

commit v6 on v4

--- a/solution.py
+++ b/solution.py
@@ -10,7 +10,9 @@
 
 ITERS = 2
 SIGMA_STEP = 0.2
+PARTS = 2
 UNROLL = 64
+FIRST_UNROLL = 32
 PITCH_PAD = 8
 VMEM_BYTES = 24 * 1024 * 1024
 TRANSPOSED = (((1,), (1,)), ((), ()))
@@ -40,15 +42,15 @@
     return pl.multiple_of((column % flight_tiles * time_block + column // flight_tiles) * pitch, 8)
 
 
-def backward_blocks(dims, pitch, rows_ref, cols_ref, duals_ref, tiles_ref, acc_ref, start):
+def backward_blocks(dims, pitch, width, rows_ref, cols_ref, duals_ref, tiles_ref, acc_ref, start):
     scen = dims[0] * dims[2]
     products = []
-    for u in range(0, UNROLL, 2):
+    for u in range(0, width, 2):
         pair = stacked_pair(duals_ref[rows_ref[start + u]], duals_ref[rows_ref[start + u + 1]])
         both = tiles_ref[pl.ds(start + u, 2)]
         result = jnp.dot(pair, both.reshape(-1, both.shape[2]), preferred_element_type=jnp.float32)
         products += [result[:scen], result[scen:]]
-    for u in range(UNROLL):
+    for u in range(width):
         place = column_place(dims, cols_ref[start + u], pitch)
         acc_ref[pl.ds(place, scen), :] += products[u]
 
@@ -73,16 +75,16 @@
     dims, pitch, core_ref, row_source, col_source, dual_source, source_ref, out_ref, tiles_ref,
     rows_ref, cols_ref, bands_ref, duals_ref, acc_ref, sems
 ):
-    count, parts = tiles_ref.shape[0], sems.shape[0] - 3
-    chunk = count // parts
+    count, pieces = tiles_ref.shape[0], sems.shape[0] - 3
+    chunk = count // pieces
     lists = [
-        pltpu.make_async_copy(row_source, rows_ref, sems.at[parts]),
-        pltpu.make_async_copy(col_source, cols_ref, sems.at[parts + 1]),
-        pltpu.make_async_copy(dual_source, bands_ref, sems.at[parts + 2]),
+        pltpu.make_async_copy(row_source, rows_ref, sems.at[pieces]),
+        pltpu.make_async_copy(col_source, cols_ref, sems.at[pieces + 1]),
+        pltpu.make_async_copy(dual_source, bands_ref, sems.at[pieces + 2]),
     ]
     copies = [
         pltpu.make_async_copy(source_ref.at[pl.ds(i * chunk, chunk)], tiles_ref.at[pl.ds(i * chunk, chunk)], sems.at[i])
-        for i in range(parts)
+        for i in range(pieces)
     ]
     for copy in lists + copies:
         copy.start()
@@ -93,35 +95,43 @@
     duals_ref[...] = jnp.concatenate(bands, axis=1)
 
     def body(index, _):
-        backward_blocks(dims, pitch, rows_ref, cols_ref, duals_ref, tiles_ref, acc_ref, index * UNROLL)
+        backward_blocks(
+            dims, pitch, FIRST_UNROLL, rows_ref, cols_ref, duals_ref, tiles_ref, acc_ref, index * FIRST_UNROLL
+        )
         return 0
 
     for i, copy in enumerate(copies):
         copy.wait()
-        lax.fori_loop(i * chunk // UNROLL, (i + 1) * chunk // UNROLL, body, 0)
+        lax.fori_loop(i * chunk // FIRST_UNROLL, (i + 1) * chunk // FIRST_UNROLL, body, 0)
     write_messages(dims, pitch, acc_ref, out_ref)
 
 
-def backward_kernel(dims, pitch, core_ref, rows_ref, cols_ref, own_ref, other_ref, tiles_ref, out_ref, duals_ref, acc_ref):
-    core = core_ref[0]
-    half, scen, side = duals_ref.shape[0] // 2, duals_ref.shape[1], duals_ref.shape[2]
-    duals_ref[pl.ds(core * half, half)] = own_ref[...].reshape(half, scen, side)
-    duals_ref[pl.ds((1 - core) * half, half)] = other_ref[...].reshape(half, scen, side)
+def row_part(core, part, rows):
+    return (core * PARTS + part) * rows
+
+
+def backward_kernel(dims, pitch, core_ref, rows_ref, cols_ref, tiles_ref, *refs):
+    pieces, (out_ref, duals_ref, acc_ref) = refs[: 2 * PARTS], refs[2 * PARTS :]
+    for i, piece in enumerate(pieces):
+        core = core_ref[0] if i < PARTS else 1 - core_ref[0]
+        scen, side = duals_ref.shape[1:]
+        rows = piece.shape[0] // scen
+        duals_ref[pl.ds(row_part(core, i % PARTS, rows), rows)] = piece[...].reshape(rows, scen, side)
     acc_ref[...] = jnp.zeros_like(acc_ref)
 
     def body(index, _):
-        backward_blocks(dims, pitch, rows_ref, cols_ref, duals_ref, tiles_ref, acc_ref, index * UNROLL)
+        backward_blocks(dims, pitch, UNROLL, rows_ref, cols_ref, duals_ref, tiles_ref, acc_ref, index * UNROLL)
         return 0
 
     lax.fori_loop(0, tiles_ref.shape[0] // UNROLL, body, 0)
     write_messages(dims, pitch, acc_ref, out_ref)
 
 
-def forward_kernel(dims, pitch, core_ref, rows_ref, cols_ref, probe_ref, tiles_ref, own_ref, away_ref, flat_ref, acc_ref):
+def forward_kernel(dims, pitch, core_ref, rows_ref, cols_ref, probe_ref, tiles_ref, *refs):
     n_row, n_col, scen_local, time_block, _, own_tiles = dims
     scen = n_row * scen_local
     piece = own_tiles * time_block
-    core = core_ref[0]
+    outs, (flat_ref, acc_ref) = refs[: 2 * PARTS], refs[2 * PARTS :]
     acc_ref[...] = jnp.zeros_like(acc_ref)
     for group in range(n_row):
         for column in range(n_col):
@@ -154,9 +164,10 @@
         return 0
 
     lax.fori_loop(0, tiles_ref.shape[0] // UNROLL, body, 0)
-    half = acc_ref.shape[0] // 2
-    own_ref[...] = acc_ref[pl.ds(pl.multiple_of(core * half, half), half), :]
-    away_ref[...] = acc_ref[pl.ds(pl.multiple_of((1 - core) * half, half), half), :]
+    for i, out_ref in enumerate(outs):
+        core = core_ref[0] if i < PARTS else 1 - core_ref[0]
+        size = out_ref.shape[0]
+        out_ref[...] = acc_ref[pl.ds(pl.multiple_of(row_part(core, i % PARTS, size), size), size), :]
 
 
 def running(values, trailing, terms):
@@ -223,32 +234,34 @@
     out_ref[...] = (first_ref[...].astype(jnp.float32) + second_ref[...].astype(jnp.float32)).astype(jnp.bfloat16)
 
 
-def dual_kernel(remote, first, last, core_ref, own_ref, other_ref, *refs):
+def dual_kernel(remote, part, first, last, core_ref, own_ref, other_ref, *refs):
     parts, (dual_ref, cap_ref, dual_out) = refs[:remote], refs[remote : remote + 3]
     total = own_ref[...] + other_ref[...]
-    for part in parts:
-        total = total + part[...].astype(jnp.float32)
+    for received in parts:
+        total = total + received[...].astype(jnp.float32)
     bands, row_tiles, band, side = cap_ref.shape
-    half = row_tiles // 2
-    begin = core_ref[0] * half
-
-    def own_half(ref):
-        return jnp.concatenate([ref[a, pl.ds(begin, half)] for a in range(bands)], axis=1).reshape(-1, side)
-
-    old = own_half(dual_ref) if first else dual_ref[...]
-    fresh = jnp.maximum(old + SIGMA_STEP * (total - own_half(cap_ref).astype(jnp.float32)), 0.0)
+    rows = row_tiles // (2 * PARTS)
+    begin = row_part(core_ref[0], part, rows)
+
+    def own_rows(ref):
+        return jnp.concatenate([ref[a, pl.ds(begin, rows)] for a in range(bands)], axis=1).reshape(-1, side)
+
+    old = own_rows(dual_ref) if first else dual_ref[...]
+    fresh = jnp.maximum(old + SIGMA_STEP * (total - own_rows(cap_ref).astype(jnp.float32)), 0.0)
     dual_out[...] = fresh
     if not last:
         refs[-1][...] = fresh.astype(jnp.bfloat16)
 
 
-def assemble_kernel(core_ref, own_ref, other_ref, out_ref):
+def assemble_kernel(core_ref, *refs):
+    out_ref = refs[-1]
     bands, row_tiles, band, side = out_ref.shape
-    half = row_tiles // 2
-    for ref, begin in ((own_ref, core_ref[0] * half), (other_ref, (1 - core_ref[0]) * half)):
-        value = ref[...].reshape(half, bands * band, side)
+    rows = row_tiles // (2 * PARTS)
+    for i, ref in enumerate(refs[:-1]):
+        core = core_ref[0] if i < PARTS else 1 - core_ref[0]
+        value = ref[...].reshape(rows, bands * band, side)
         for a in range(bands):
-            out_ref[a, pl.ds(begin, half)] = value[:, a * band : (a + 1) * band]
+            out_ref[a, pl.ds(row_part(core, i % PARTS, rows), rows)] = value[:, a * band : (a + 1) * band]
 
 
 def per_device(
@@ -265,7 +278,7 @@
     col_tiles = time_block * flight_tiles
     dims = (n_row, n_col, scen_local, time_block, flight_tiles, own_tiles)
     message = (n_row * n_col, scen_local * own_tiles * time_block, side)
-    half = row_tiles * scen // 2
+    part_rows = row_tiles * scen // (2 * PARTS)
     pitch = scen + PITCH_PAD
     band = 8
 
@@ -275,8 +288,8 @@
     acc_cols = pltpu.VMEM((col_tiles * pitch, side), jnp.float32)
     picked_duals = pltpu.VMEM((row_tiles, scen, side), jnp.bfloat16)
     messages = jax.ShapeDtypeStruct(message, jnp.bfloat16)
-    half_f32 = jax.ShapeDtypeStruct((half, side), jnp.float32)
-    half_bf16 = jax.ShapeDtypeStruct((half, side), jnp.bfloat16)
+    part_f32 = jax.ShapeDtypeStruct((part_rows, side), jnp.float32)
+    part_bf16 = jax.ShapeDtypeStruct((part_rows, side), jnp.bfloat16)
 
     def banded(array):
         return array.reshape(scen // band, band, row_tiles, side).transpose(0, 2, 1, 3)
@@ -296,36 +309,40 @@
                 pltpu.VMEM(duals.shape, jnp.float32),
                 picked_duals,
                 acc_cols,
-                pltpu.SemaphoreType.DMA((count // UNROLL + 3,)),
+                pltpu.SemaphoreType.DMA((count // FIRST_UNROLL + 3,)),
             ],
             compiler_params=params(),
             cost_estimate=cost,
             name="first_backward_products",
         )(core, in_hbm(rows), in_hbm(cols), in_hbm(duals), in_hbm(tile_values.reshape(count, side, side)))
 
-    def backward(own, other, tiles):
+    def in_vmem(array):
+        return pltpu.with_memory_space_constraint(array, pltpu.VMEM)
+
+    def backward(rounded, tiles):
+        pieces = [*rounded, *map(swap_core, rounded)]
         return pl.pallas_call(
             functools.partial(backward_kernel, dims, pitch),
-            in_specs=[scalars()] * 3 + [whole()] * 3,
+            in_specs=[scalars()] * 3 + [whole()] * (1 + len(pieces)),
             out_specs=whole(),
             out_shape=messages,
             scratch_shapes=[picked_duals, acc_cols],
             compiler_params=params(),
             cost_estimate=cost,
             name="backward_products",
-        )(core, rows, cols, own, other, pltpu.with_memory_space_constraint(tiles, pltpu.VMEM))
+        )(core, rows, cols, in_vmem(tiles), *pieces)
 
     def forward(probe, tiles):
         return pl.pallas_call(
             functools.partial(forward_kernel, dims, pitch),
             in_specs=[scalars()] * 3 + [whole()] * 2,
-            out_specs=[whole()] * 2,
-            out_shape=[half_f32] * 2,
+            out_specs=[whole()] * (2 * PARTS),
+            out_shape=[part_f32] * (2 * PARTS),
             scratch_shapes=[acc_cols, pltpu.VMEM((row_tiles * scen, side), jnp.float32)],
             compiler_params=params(),
             cost_estimate=cost,
             name="forward_products",
-        )(core, rows, cols, probe, pltpu.with_memory_space_constraint(tiles, pltpu.VMEM))
+        )(core, rows, cols, probe, in_vmem(tiles))
 
     def primal_step(recv, primal, cumulative, last):
         first = cumulative is None
@@ -354,12 +371,12 @@
             sum_kernel,
             in_specs=[whole()] * 2,
             out_specs=whole(),
-            out_shape=half_bf16,
+            out_shape=part_bf16,
             compiler_params=params(),
             name=name,
         )(first, second)
 
-    def dual_step(own, away, dual, first, last):
+    def dual_step(part, own, away, dual, first, last):
         other = swap_core(away)
         partial = bf16_sum(own, other, "core_pair_sum")
         parts = []
@@ -367,9 +384,9 @@
             parts.append(swap_chip(partial, step))
             if step + 1 < bits:
                 partial = bf16_sum(partial, parts[-1], "chip_sum")
-        out_shape = [half_f32] if last else [half_f32, half_bf16]
-        return pl.pallas_call(
-            functools.partial(dual_kernel, bits, first, last),
+        out_shape = [part_f32] if last else [part_f32, part_bf16]
+        return pl.pallas_call(
+            functools.partial(dual_kernel, bits, part, first, last),
             in_specs=[scalars()] + [whole()] * (bits + 4),
             out_specs=[whole()] * len(out_shape),
             out_shape=out_shape,
@@ -377,30 +394,35 @@
             name="dual_update",
         )(core, own, other, *parts, dual, banded(capacity))
 
-    def assemble(own):
+    def assemble(owned):
+        pieces = [*owned, *map(swap_core, owned)]
         return pl.pallas_call(
             assemble_kernel,
-            in_specs=[scalars()] + [whole()] * 2,
+            in_specs=[scalars()] + [whole()] * len(pieces),
             out_specs=whole(),
             out_shape=jax.ShapeDtypeStruct((scen // band, row_tiles, band, side), jnp.float32),
             compiler_params=params(),
             name="assemble_duals",
-        )(core, own, swap_core(own))
+        )(core, *pieces)
 
     send, tiles = first_backward(banded(dual_vars))
-    dual, primal, cumulative = banded(dual_vars), increments, None
+    duals, primal, cumulative = [banded(dual_vars)] * PARTS, increments, None
     for sweep in range(ITERS):
         last = sweep + 1 == ITERS
         if sweep:
-            send = backward(half_round, swap_core(half_round), tiles)
+            send = backward(rounded, tiles)
         recv = lax.all_to_all(send, ("row", "col"), 0, 0, tiled=True)
         primal, send, *cumulative = primal_step(recv, primal, cumulative, last)
         cumulative = None if last else cumulative[0]
         probe = lax.all_to_all(send, ("row", "col"), 0, 0, tiled=True)
-        own, away = forward(probe, tiles)
-        dual, *rounded = dual_step(own, away, dual, sweep == 0, last)
-        half_round = None if last else rounded[0]
-    duals_out = assemble(dual).transpose(0, 2, 1, 3).reshape(scen, row_length)
+        images = forward(probe, tiles)
+        results = [
+            dual_step(part, images[part], images[PARTS + part], duals[part], sweep == 0, last)
+            for part in range(PARTS)
+        ]
+        duals = [result[0] for result in results]
+        rounded = None if last else [result[1] for result in results]
+    duals_out = assemble(duals).transpose(0, 2, 1, 3).reshape(scen, row_length)
     return (primal, duals_out)
 
 

time: 178 us -> 173 us (0.972)
  waiting for transfers between devices: 26.8 us -> 17.1 us
  starting transfers between devices: 6.42 us -> 11.9 us
    ppermute x4 -> x8, waiting for transfers between devices: 19.6 us -> 12.2 us  [swap_chip(): lax.ppermute(value, 'col', [(i, i ^ 2 << (step + i % 2) % bits) for i in...]
    ppermute x4 -> x8, starting transfers between devices: 6.14 us -> 10.5 us  [swap_chip(): lax.ppermute(value, 'col', [(i, i ^ 2 << (step + i % 2) % bits) for i in...]
    ppermute x4 -> x8, waiting for transfers between devices: 7.21 us -> 4.9 us  [swap_core(): return lax.ppermute(value, 'col', [(i, i ^ 1) for i in range(n_col)])]
  transfers between devices with their start and end apart: 8 -> 16, of which waited for: 8 -> 10; matrix products, arithmetic and copies ran while one was open for 0% -> 0% of each run, Pallas kernels for 0% -> 0%
where the time goes in v6:
time: 173 us
  blocking collectives  122 us (71%)
  Pallas kernels  20.8 us (12%)
  waiting for transfers between devices  17.1 us (10%)
  starting transfers between devices  11.9 us (7%)
    all_to_all x2, blocking collectives, per_device(): recv = lax.all_to_all(send, ('row', 'col'), 0, 0, tiled=True)  62.8 us
    all_to_all x2, blocking collectives, per_device(): probe = lax.all_to_all(send, ('row', 'col'), 0, 0, tiled=True)  59.3 us
    ppermute x8, waiting for transfers between devices, swap_chip(): lax.ppermute(value, 'col', [(i, i ^ 2 << (step + i % 2) % bits) for i in...  12.2 us
    ppermute x8, starting transfers between devices, swap_chip(): lax.ppermute(value, 'col', [(i, i ^ 2 << (step + i % 2) % bits) for i in...  10.5 us
    pallas_call x2, Pallas kernels, forward(): pl.pallas_call(functools.partial(forward_kernel, dims, pitch), in_specs=[...  8.65 us
    ppermute x8, waiting for transfers between devices, swap_core(): return lax.ppermute(value, 'col', [(i, i ^ 1) for i in range(n_col)])  4.9 us
    pallas_call x1, Pallas kernels, first_backward(): pl.pallas_call(functools.partial(first_backward_kernel, dims, pitch), in_...  4.52 us
    pallas_call x1, Pallas kernels, backward(): pl.pallas_call(functools.partial(backward_kernel, dims, pitch), in_specs=...  3.58 us
  transfers between devices with their start and end apart: 16, of which 10 were waited for; matrix products, arithmetic and copies ran while one was open for 0% of the time, Pallas kernels for 0%

profile of v6, /device:TPU:0, one launch (start us, length us, event | category | flops | bytes accessed | tf_op | source)
XLA Modules:
  0.0 172.9 jit_solution(17495747841131604729)
XLA Ops:
  0.7 4.5 %first_backward_products.1 = (bf16[32,128,128]{2,1,0:T(8,128)(2,1)S(1)}, bf16[256,128,128]{2,1,0:T(8,128)(2,1)S(1)}) custom-call(s32[1]{0:T(128)} %bitcast.core_ref, s32[256]{0:T(256)} %bitcast.22, s32[256]{0:T(256)} %bitcast.26, f32[2,128,8,128]{3,2,1,0:T(8,128)} %bitcast.19, bf16[256,128,128]{2,1,0:T(8,128)(2,1)} %bitcast.34), custom_call_target="tpu_custom_call" | custom-call | flops 134217728 | bytes 4194304 | tf_op jit(solution)/shard_map/first_backward_products/pallas_call | solution.py:301
  5.2 0.0 copy-start
  5.2 0.0 copy-start.1
  5.3 33.3 %all_to_all.20.refs_0_ = bf16[32,128,128]{2,1,0:T(8,128)(2,1)S(1)} all-to-all(bf16[32,128,128]{2,1,0:T(8,128)(2,1)S(1)} %get-tuple-element.22), channel_id=1, replica_groups=mesh['row'=4,'col'=8] {'row','col'}, dimensions={0} | all-to-all | bytes 2097152 | tf_op jit(solution)/shard_map/all_to_all | solution.py:414
  38.6 0.9 primal_update.2
  39.6 29.7 %all_to_all.21.probe_ref = bf16[32,128,128]{2,1,0:T(8,128)(2,1)S(1)} all-to-all(bf16[32,128,128]{2,1,0:T(8,128)(2,1)S(1)} %get-tuple-element.23), channel_id=1, replica_groups=mesh['row'=4,'col'=8] {'row','col'}, dimensions={0} | all-to-all | bytes 2097152 | tf_op jit(solution)/shard_map/all_to_all | solution.py:417
  69.2 4.3 %forward_products.2 = (f32[512,128]{1,0:T(8,128)S(1)}, f32[512,128]{1,0:T(8,128)S(1)}, f32[512,128]{1,0:T(8,128)S(1)}, f32[512,128]{1,0:T(8,128)S(1)}) custom-call(s32[1]{0:T(128)} %bitcast.core_ref, s32[256]{0:T(256)S(1)} %bitcast.23, s32[256]{0:T(256)S(1)} %bitcast.27, bf16[32,128,128]{2,1,0:T(8,128)(2,1)S(1)} %all_to_all.21.probe_ref, ...), custom_call_target="tpu_custom_call" | custom-call | flops 134217728 | bytes 4194304 | tf_op jit(solution)/shard_map/forward_products/pallas_call | solution.py:336
  73.6 0.1 collective-permute-start
  73.6 0.5 collective-permute-start.3
  74.1 1.0 collective-permute-done.second_ref.other_ref
  75.2 1.5 collective-permute-start.1
  76.7 0.0 collective-permute-done.3.second_ref.other_ref
  76.8 0.6 collective-permute-start.4
  77.4 2.8 %collective-permute-done.1.second_ref.refs_0_ = bf16[512,128]{1,0:T(8,128)(2,1)S(1)} collective-permute-done((bf16[512,128]{1,0:T(8,128)(2,1)S(1)}, bf16[512,128]{1,0:T(8,128)(2,1)S(1)}, u32[]{:S(2)}, u32[]{:S(2)}) %collective-permute-start.1) | collective-permute-done | bytes 131104 | tf_op jit(solution)/shard_map/ppermute | solution.py:367
  80.3 1.5 collective-permute-start.2
  81.8 0.0 collective-permute-done.4.second_ref.refs_0_
  81.8 1.6 collective-permute-start.5
  83.4 1.9 %collective-permute-done.2.refs_1_ = bf16[512,128]{1,0:T(8,128)(2,1)S(1)} collective-permute-done((bf16[512,128]{1,0:T(8,128)(2,1)S(1)}, bf16[512,128]{1,0:T(8,128)(2,1)S(1)}, u32[]{:S(2)}, u32[]{:S(2)}) %collective-permute-start.2) | collective-permute-done | bytes 131104 | tf_op jit(solution)/shard_map/ppermute | solution.py:367
  85.3 0.1 dual_update.4
  85.4 0.1 collective-permute-start.6
  85.5 1.4 collective-permute-done.5.refs_1_
  86.9 0.1 dual_update.5
  87.0 0.1 collective-permute-start.7
  87.1 0.0 collective-permute-done.6.refs_2_
  87.1 1.3 collective-permute-done.7.refs_3_
  88.4 3.6 %backward_products.1 = bf16[32,128,128]{2,1,0:T(8,128)(2,1)S(1)} custom-call(s32[1]{0:T(128)} %bitcast.core_ref, s32[256]{0:T(256)S(1)} %bitcast.24, s32[256]{0:T(256)S(1)} %bitcast.28, bf16[256,128,128]{2,1,0:T(8,128)(2,1)S(1)} %get-tuple-element.21.tiles_ref, bf16[512,128]{1,0:T(8,128)(2,1)S(1)} %get-tuple-element.26.refs_0_, ...), custom_call_target="tpu_custom_call" | custom-call | flops 134217728 | bytes 4194304 | tf_op jit(solution)/shard_map/backward_products/pallas_call | solution.py:324
  92.0 29.5 %all_to_all.22.refs_0_ = bf16[32,128,128]{2,1,0:T(8,128)(2,1)S(1)} all-to-all(bf16[32,128,128]{2,1,0:T(8,128)(2,1)S(1)} %backward_products.1), channel_id=1, replica_groups=mesh['row'=4,'col'=8] {'row','col'}, dimensions={0} | all-to-all | bytes 2097152 | tf_op jit(solution)/shard_map/all_to_all | solution.py:414
  121.5 1.3 primal_update.3
  122.8 29.7 %all_to_all.23.probe_ref = bf16[32,128,128]{2,1,0:T(8,128)(2,1)S(1)} all-to-all(bf16[32,128,128]{2,1,0:T(8,128)(2,1)S(1)} %get-tuple-element.33), channel_id=1, replica_groups=mesh['row'=4,'col'=8] {'row','col'}, dimensions={0} | all-to-all | bytes 2097152 | tf_op jit(solution)/shard_map/all_to_all | solution.py:417
  152.5 4.3 %forward_products.3 = (f32[512,128]{1,0:T(8,128)S(1)}, f32[512,128]{1,0:T(8,128)S(1)}, f32[512,128]{1,0:T(8,128)S(1)}, f32[512,128]{1,0:T(8,128)S(1)}) custom-call(s32[1]{0:T(128)} %bitcast.core_ref, s32[256]{0:T(256)S(1)} %bitcast.25, s32[256]{0:T(256)S(1)} %bitcast.29, bf16[32,128,128]{2,1,0:T(8,128)(2,1)S(1)} %all_to_all.23.probe_ref, ...), custom_call_target="tpu_custom_call" | custom-call | flops 134217728 | bytes 4194304 | tf_op jit(solution)/shard_map/forward_products/pallas_call | solution.py:336
  156.8 0.1 collective-permute-start.8
  156.9 0.5 collective-permute-start.11
  157.4 1.0 collective-permute-done.8.second_ref.other_ref
  158.4 1.5 collective-permute-start.9
  159.9 0.0 collective-permute-done.11.second_ref.other_ref
  160.0 0.6 collective-permute-start.12
  160.6 2.8 %collective-permute-done.9.second_ref.refs_0_ = bf16[512,128]{1,0:T(8,128)(2,1)S(1)} collective-permute-done((bf16[512,128]{1,0:T(8,128)(2,1)S(1)}, bf16[512,128]{1,0:T(8,128)(2,1)S(1)}, u32[]{:S(2)}, u32[]{:S(2)}) %collective-permute-start.9) | collective-permute-done | bytes 131104 | tf_op jit(solution)/shard_map/ppermute | solution.py:367
  163.5 1.5 collective-permute-start.10
  165.1 1.5 collective-permute-start.13
  166.6 1.9 %collective-permute-done.10.refs_1_ = bf16[512,128]{1,0:T(8,128)(2,1)S(1)} collective-permute-done((bf16[512,128]{1,0:T(8,128)(2,1)S(1)}, bf16[512,128]{1,0:T(8,128)(2,1)S(1)}, u32[]{:S(2)}, u32[]{:S(2)}) %collective-permute-start.10) | collective-permute-done | bytes 131104 | tf_op jit(solution)/shard_map/ppermute | solution.py:367
  168.5 0.1 dual_update.6.refs_0_
  168.6 0.1 collective-permute-start.14
  168.7 1.4 collective-permute-done.13.refs_1_
  170.1 0.1 dual_update.7.refs_1_
  170.2 0.1 collective-permute-start.15
  170.3 0.0 collective-permute-done.14.refs_2_
  170.3 1.5 collective-permute-done.15.refs_3_
  171.8 1.0 assemble_duals.1
  (23 shorter events, 0.3 us)
Async XLA Ops:
  0.6 68.6 %copy-start.5 = (s32[1,1,256]{2,1,0:T(1,128)S(1)}, s32[1,1,256]{2,1,0:T(1,128)}, u32[]{:S(2)}) copy-start(s32[1,1,256]{2,1,0:T(1,128)} %param.11) | copy-start | bytes 3076
  0.6 68.6 %copy-start.4 = (s32[1,1,256]{2,1,0:T(1,128)S(1)}, s32[1,1,256]{2,1,0:T(1,128)}, u32[]{:S(2)}) copy-start(s32[1,1,256]{2,1,0:T(1,128)} %param.10) | copy-start | bytes 3076
  0.7 37.9 %copy-start.3 = (f32[128,256]{1,0:T(8,128)S(1)}, f32[128,256]{1,0:T(8,128)}, u32[]{:S(2)}) copy-start(f32[128,256]{1,0:T(8,128)} %refs_3_.1) | copy-start | bytes 393220
  0.7 37.9 %copy-start.7 = (s32[256]{0:T(256)S(1)}, s32[256]{0:T(256)}, u32[]{:S(2)}) copy-start(s32[256]{0:T(256)} %param.16) | copy-start | bytes 3076
  0.7 37.9 %copy-start.6 = (s32[256]{0:T(256)S(1)}, s32[256]{0:T(256)}, u32[]{:S(2)}) copy-start(s32[256]{0:T(256)} %param.15) | copy-start | bytes 3076
  0.7 37.9 %copy-start.2 = (f32[4,128,256]{2,1,0:T(8,128)S(1)}, f32[4,128,256]{2,1,0:T(8,128)}, u32[]{:S(2)}) copy-start(f32[4,128,256]{2,1,0:T(8,128)} %refs_1_.1) | copy-start | bytes 1572868
  5.2 80.1 %copy-start = (s32[16,16384]{1,0:T(8,128)S(1)}, s32[16,16384]{1,0:T(8,128)}, u32[]{:S(2)}) copy-start(s32[16,16384]{1,0:T(8,128)} %param.17) | copy-start | bytes 3145732
  5.2 80.1 %copy-start.1 = (f32[16,16384]{1,0:T(8,128)S(1)}, f32[16,16384]{1,0:T(8,128)}, u32[]{:S(2)}) copy-start(f32[16,16384]{1,0:T(8,128)} %param.13) | copy-start | bytes 3145732
  73.6 1.6 collective-permute-start
  73.6 3.1 %collective-permute-start.3 = (f32[512,128]{1,0:T(8,128)S(1)}, f32[512,128]{1,0:T(8,128)S(1)}, u32[]{:S(2)}, u32[]{:S(2)}) collective-permute-start(f32[512,128]{1,0:T(8,128)S(1)} %get-tuple-element.28), channel_id=1, source_target_pairs={{0,1},{1,0},{2,3},{3,2},{4,5},{5,4},{6,7},{7,6},{8,9},{9,8},{10,11... | collective-permute-start | bytes 786440 | tf_op jit(solution)/shard_map/ppermute | solution.py:362
  75.2 5.0 %collective-permute-start.1 = (bf16[512,128]{1,0:T(8,128)(2,1)S(1)}, bf16[512,128]{1,0:T(8,128)(2,1)S(1)}, u32[]{:S(2)}, u32[]{:S(2)}) collective-permute-start(bf16[512,128]{1,0:T(8,128)(2,1)S(1)} %core_pair_sum.4.first_ref), channel_id=1, source_target_pairs={{0,2},{1,5},{2,0},{3,7},{4,6},{5,1},{6,4},{7,3},{8,10},{9,13},{10,... | collective-permute-start | bytes 393224 | tf_op jit(solution)/shard_map/ppermute | solution.py:367
  76.8 5.0 %collective-permute-start.4 = (bf16[512,128]{1,0:T(8,128)(2,1)S(1)}, bf16[512,128]{1,0:T(8,128)(2,1)S(1)}, u32[]{:S(2)}, u32[]{:S(2)}) collective-permute-start(bf16[512,128]{1,0:T(8,128)(2,1)S(1)} %core_pair_sum.5.first_ref), channel_id=1, source_target_pairs={{0,2},{1,5},{2,0},{3,7},{4,6},{5,1},{6,4},{7,3},{8,10},{9,13},{10,... | collective-permute-start | bytes 393224 | tf_op jit(solution)/shard_map/ppermute | solution.py:367
  80.3 5.0 %collective-permute-start.2 = (bf16[512,128]{1,0:T(8,128)(2,1)S(1)}, bf16[512,128]{1,0:T(8,128)(2,1)S(1)}, u32[]{:S(2)}, u32[]{:S(2)}) collective-permute-start(bf16[512,128]{1,0:T(8,128)(2,1)S(1)} %chip_sum.4), channel_id=1, source_target_pairs={{0,4},{1,3},{2,6},{3,1},{4,0},{5,7},{6,2},{7,5},{8,12},{9,11},{10,... | collective-permute-start | bytes 393224 | tf_op jit(solution)/shard_map/ppermute | solution.py:367
  81.8 5.0 %collective-permute-start.5 = (bf16[512,128]{1,0:T(8,128)(2,1)S(1)}, bf16[512,128]{1,0:T(8,128)(2,1)S(1)}, u32[]{:S(2)}, u32[]{:S(2)}) collective-permute-start(bf16[512,128]{1,0:T(8,128)(2,1)S(1)} %chip_sum.5), channel_id=1, source_target_pairs={{0,4},{1,3},{2,6},{3,1},{4,0},{5,7},{6,2},{7,5},{8,12},{9,11},{10,... | collective-permute-start | bytes 393224 | tf_op jit(solution)/shard_map/ppermute | solution.py:367
  85.4 1.7 collective-permute-start.6
  87.0 1.4 collective-permute-start.7
  156.8 1.6 collective-permute-start.8
  156.9 3.1 %collective-permute-start.11 = (f32[512,128]{1,0:T(8,128)S(1)}, f32[512,128]{1,0:T(8,128)S(1)}, u32[]{:S(2)}, u32[]{:S(2)}) collective-permute-start(f32[512,128]{1,0:T(8,128)S(1)} %get-tuple-element.38), channel_id=1, source_target_pairs={{0,1},{1,0},{2,3},{3,2},{4,5},{5,4},{6,7},{7,6},{8,9},{9,8},{10,11... | collective-permute-start | bytes 786440 | tf_op jit(solution)/shard_map/ppermute | solution.py:362
  158.4 5.0 %collective-permute-start.9 = (bf16[512,128]{1,0:T(8,128)(2,1)S(1)}, bf16[512,128]{1,0:T(8,128)(2,1)S(1)}, u32[]{:S(2)}, u32[]{:S(2)}) collective-permute-start(bf16[512,128]{1,0:T(8,128)(2,1)S(1)} %core_pair_sum.6.first_ref), channel_id=1, source_target_pairs={{0,2},{1,5},{2,0},{3,7},{4,6},{5,1},{6,4},{7,3},{8,10},{9,13},{10,... | collective-permute-start | bytes 393224 | tf_op jit(solution)/shard_map/ppermute | solution.py:367
  160.0 5.0 %collective-permute-start.12 = (bf16[512,128]{1,0:T(8,128)(2,1)S(1)}, bf16[512,128]{1,0:T(8,128)(2,1)S(1)}, u32[]{:S(2)}, u32[]{:S(2)}) collective-permute-start(bf16[512,128]{1,0:T(8,128)(2,1)S(1)} %core_pair_sum.7.first_ref), channel_id=1, source_target_pairs={{0,2},{1,5},{2,0},{3,7},{4,6},{5,1},{6,4},{7,3},{8,10},{9,13},{10,... | collective-permute-start | bytes 393224 | tf_op jit(solution)/shard_map/ppermute | solution.py:367
  163.5 5.0 %collective-permute-start.10 = (bf16[512,128]{1,0:T(8,128)(2,1)S(1)}, bf16[512,128]{1,0:T(8,128)(2,1)S(1)}, u32[]{:S(2)}, u32[]{:S(2)}) collective-permute-start(bf16[512,128]{1,0:T(8,128)(2,1)S(1)} %chip_sum.6), channel_id=1, source_target_pairs={{0,4},{1,3},{2,6},{3,1},{4,0},{5,7},{6,2},{7,5},{8,12},{9,11},{10,... | collective-permute-start | bytes 393224 | tf_op jit(solution)/shard_map/ppermute | solution.py:367
  165.1 5.0 %collective-permute-start.13 = (bf16[512,128]{1,0:T(8,128)(2,1)S(1)}, bf16[512,128]{1,0:T(8,128)(2,1)S(1)}, u32[]{:S(2)}, u32[]{:S(2)}) collective-permute-start(bf16[512,128]{1,0:T(8,128)(2,1)S(1)} %chip_sum.7), channel_id=1, source_target_pairs={{0,4},{1,3},{2,6},{3,1},{4,0},{5,7},{6,2},{7,5},{8,12},{9,11},{10,... | collective-permute-start | bytes 393224 | tf_op jit(solution)/shard_map/ppermute | solution.py:367
  168.6 1.7 collective-permute-start.14
  170.2 1.6 collective-permute-start.15

commit v7 on v6

--- a/solution.py
+++ b/solution.py
@@ -11,8 +11,9 @@
 ITERS = 2
 SIGMA_STEP = 0.2
 PARTS = 2
-UNROLL = 64
+UNROLL = 256
 FIRST_UNROLL = 32
+TRAIL = 16
 PITCH_PAD = 8
 VMEM_BYTES = 24 * 1024 * 1024
 TRANSPOSED = (((1,), (1,)), ((), ()))
@@ -42,17 +43,30 @@
     return pl.multiple_of((column % flight_tiles * time_block + column // flight_tiles) * pitch, 8)
 
 
+def trailing_adds(width, products, add):
+    waiting = []
+    for u in range(0, width, 2):
+        waiting += zip((u, u + 1), products(u))
+        while len(waiting) > TRAIL:
+            add(*waiting.pop(0))
+    for item in waiting:
+        add(*item)
+
+
 def backward_blocks(dims, pitch, width, rows_ref, cols_ref, duals_ref, tiles_ref, acc_ref, start):
     scen = dims[0] * dims[2]
-    products = []
-    for u in range(0, width, 2):
+
+    def products(u):
         pair = stacked_pair(duals_ref[rows_ref[start + u]], duals_ref[rows_ref[start + u + 1]])
         both = tiles_ref[pl.ds(start + u, 2)]
         result = jnp.dot(pair, both.reshape(-1, both.shape[2]), preferred_element_type=jnp.float32)
-        products += [result[:scen], result[scen:]]
-    for u in range(width):
+        return result[:scen], result[scen:]
+
+    def add(u, product):
         place = column_place(dims, cols_ref[start + u], pitch)
-        acc_ref[pl.ds(place, scen), :] += products[u]
+        acc_ref[pl.ds(place, scen), :] += product
+
+    trailing_adds(width, products, add)
 
 
 def write_messages(dims, pitch, acc_ref, out_ref):
@@ -119,11 +133,13 @@
         duals_ref[pl.ds(row_part(core, i % PARTS, rows), rows)] = piece[...].reshape(rows, scen, side)
     acc_ref[...] = jnp.zeros_like(acc_ref)
 
+    width = min(UNROLL, tiles_ref.shape[0])
+
     def body(index, _):
-        backward_blocks(dims, pitch, UNROLL, rows_ref, cols_ref, duals_ref, tiles_ref, acc_ref, index * UNROLL)
+        backward_blocks(dims, pitch, width, rows_ref, cols_ref, duals_ref, tiles_ref, acc_ref, index * width)
         return 0
 
-    lax.fori_loop(0, tiles_ref.shape[0] // UNROLL, body, 0)
+    lax.fori_loop(0, tiles_ref.shape[0] // width, body, 0)
     write_messages(dims, pitch, acc_ref, out_ref)
 
 
@@ -146,10 +162,12 @@
     def picked(index):
         return flat_ref[pl.ds(column_place(dims, cols_ref[index], pitch), scen), :].astype(jnp.bfloat16)
 
+    width = min(UNROLL, tiles_ref.shape[0])
+
     def body(index, _):
-        start = index * UNROLL
-        products = []
-        for u in range(0, UNROLL, 2):
+        start = index * width
+
+        def products(u):
             both = jnp.concatenate([tiles_ref[start + u], tiles_ref[start + u + 1]], axis=1)
             result = lax.dot_general(
                 stacked_pair(picked(start + u), picked(start + u + 1)),
@@ -157,13 +175,16 @@
                 TRANSPOSED,
                 preferred_element_type=jnp.float32,
             )
-            products += [result[:scen], result[scen:]]
-        for u in range(UNROLL):
+            return result[:scen], result[scen:]
+
+        def add(u, product):
             place = pl.multiple_of(rows_ref[start + u] * scen, scen)
-            acc_ref[pl.ds(place, scen), :] += products[u]
+            acc_ref[pl.ds(place, scen), :] += product
+
+        trailing_adds(width, products, add)
         return 0
 
-    lax.fori_loop(0, tiles_ref.shape[0] // UNROLL, body, 0)
+    lax.fori_loop(0, tiles_ref.shape[0] // width, body, 0)
     for i, out_ref in enumerate(outs):
         core = core_ref[0] if i < PARTS else 1 - core_ref[0]
         size = out_ref.shape[0]
@@ -248,20 +269,42 @@
 
     old = own_rows(dual_ref) if first else dual_ref[...]
     fresh = jnp.maximum(old + SIGMA_STEP * (total - own_rows(cap_ref).astype(jnp.float32)), 0.0)
-    dual_out[...] = fresh
-    if not last:
+    if last:
+        value = fresh.reshape(rows, bands * band, side)
+        for a in range(bands):
+            dual_out[a] = value[:, a * band : (a + 1) * band]
+    else:
+        dual_out[...] = fresh
         refs[-1][...] = fresh.astype(jnp.bfloat16)
 
 
-def assemble_kernel(core_ref, *refs):
-    out_ref = refs[-1]
-    bands, row_tiles, band, side = out_ref.shape
-    rows = row_tiles // (2 * PARTS)
-    for i, ref in enumerate(refs[:-1]):
-        core = core_ref[0] if i < PARTS else 1 - core_ref[0]
-        value = ref[...].reshape(rows, bands * band, side)
+def part_copies(core, parts, out_ref, sems):
+    copies = []
+    for i, ref in enumerate(parts):
+        bands, rows = ref.shape[:2]
         for a in range(bands):
-            out_ref[a, pl.ds(row_part(core, i % PARTS, rows), rows)] = value[:, a * band : (a + 1) * band]
+            place = out_ref.at[a, pl.ds(row_part(core, i, rows), rows)]
+            copies.append(pltpu.make_async_copy(ref.at[a], place, sems.at[len(copies)]))
+    return copies
+
+
+def own_results_kernel(core_ref, primal_ref, *refs):
+    parts, (primal_out, duals_out, sems) = refs[:PARTS], refs[PARTS:]
+    copies = part_copies(core_ref[0], parts, duals_out, sems)
+    copies.append(pltpu.make_async_copy(primal_ref, primal_out, sems.at[len(copies)]))
+    for copy in copies:
+        copy.start()
+    for copy in copies:
+        copy.wait()
+
+
+def other_results_kernel(core_ref, _, *refs):
+    parts, (duals_out, sems) = refs[:PARTS], refs[PARTS:]
+    copies = part_copies(1 - core_ref[0], parts, duals_out, sems)
+    for copy in copies:
+        copy.start()
+    for copy in copies:
+        copy.wait()
 
 
 def per_device(
@@ -289,6 +332,7 @@
     picked_duals = pltpu.VMEM((row_tiles, scen, side), jnp.bfloat16)
     messages = jax.ShapeDtypeStruct(message, jnp.bfloat16)
     part_f32 = jax.ShapeDtypeStruct((part_rows, side), jnp.float32)
+    part_out = jax.ShapeDtypeStruct((scen // band, row_tiles // (2 * PARTS), band, side), jnp.float32)
     part_bf16 = jax.ShapeDtypeStruct((part_rows, side), jnp.bfloat16)
 
     def banded(array):
@@ -348,7 +392,7 @@
         first = cumulative is None
         state = (primal,) if first else (primal, cumulative)
         shape = jax.ShapeDtypeStruct(primal.shape, jnp.float32)
-        out_shape = [shape, messages] if last else [shape, messages, shape]
+        out_shape = [pltpu.VMEM(primal.shape, jnp.float32), messages] if last else [shape, messages, shape]
         return pl.pallas_call(
             functools.partial(primal_kernel, dims, first, last),
             in_specs=[whole()] * (4 + len(state)),
@@ -384,7 +428,7 @@
             parts.append(swap_chip(partial, step))
             if step + 1 < bits:
                 partial = bf16_sum(partial, parts[-1], "chip_sum")
-        out_shape = [part_f32] if last else [part_f32, part_bf16]
+        out_shape = [part_out] if last else [part_f32, part_bf16]
         return pl.pallas_call(
             functools.partial(dual_kernel, bits, part, first, last),
             in_specs=[scalars()] + [whole()] * (bits + 4),
@@ -394,16 +438,30 @@
             name="dual_update",
         )(core, own, other, *parts, dual, banded(capacity))
 
-    def assemble(owned):
-        pieces = [*owned, *map(swap_core, owned)]
-        return pl.pallas_call(
-            assemble_kernel,
-            in_specs=[scalars()] + [whole()] * len(pieces),
-            out_specs=whole(),
-            out_shape=jax.ShapeDtypeStruct((scen // band, row_tiles, band, side), jnp.float32),
-            compiler_params=params(),
-            name="assemble_duals",
-        )(core, *pieces)
+    def results(primal, owned):
+        duals_shape = jax.ShapeDtypeStruct((scen // band, row_tiles, band, side), jnp.float32)
+        hbm = pl.BlockSpec(memory_space=pltpu.HBM)
+        copies = PARTS * (scen // band)
+        primal_out, duals_out = pl.pallas_call(
+            own_results_kernel,
+            in_specs=[scalars()] + [whole()] * (1 + PARTS),
+            out_specs=[hbm, hbm],
+            out_shape=[jax.ShapeDtypeStruct(primal.shape, jnp.float32), duals_shape],
+            scratch_shapes=[pltpu.SemaphoreType.DMA((copies + 1,))],
+            compiler_params=params(),
+            name="own_results",
+        )(core, in_vmem(primal), *owned)
+        duals_out = pl.pallas_call(
+            other_results_kernel,
+            in_specs=[scalars(), hbm] + [whole()] * PARTS,
+            out_specs=hbm,
+            out_shape=duals_shape,
+            input_output_aliases={1: 0},
+            scratch_shapes=[pltpu.SemaphoreType.DMA((copies,))],
+            compiler_params=params(),
+            name="other_results",
+        )(core, duals_out, *map(swap_core, owned))
+        return primal_out, duals_out.transpose(0, 2, 1, 3).reshape(scen, row_length)
 
     send, tiles = first_backward(banded(dual_vars))
     duals, primal, cumulative = [banded(dual_vars)] * PARTS, increments, None
@@ -416,14 +474,13 @@
         cumulative = None if last else cumulative[0]
         probe = lax.all_to_all(send, ("row", "col"), 0, 0, tiled=True)
         images = forward(probe, tiles)
-        results = [
+        updates = [
             dual_step(part, images[part], images[PARTS + part], duals[part], sweep == 0, last)
             for part in range(PARTS)
         ]
-        duals = [result[0] for result in results]
-        rounded = None if last else [result[1] for result in results]
-    duals_out = assemble(duals).transpose(0, 2, 1, 3).reshape(scen, row_length)
-    return (primal, duals_out)
+        duals = [update[0] for update in updates]
+        rounded = None if last else [update[1] for update in updates]
+    return results(primal, duals)
 
 
 def solution(mesh):

time: 173 us -> 171 us (0.988)
  transfers between devices with their start and end apart: 16 -> 16, of which waited for: 10 -> 10; matrix products, arithmetic and copies ran while one was open for 0% -> 0% of each run, Pallas kernels for 0% -> 1%
where the time goes in v7:
time: 171 us
  blocking collectives  122 us (71%)
  Pallas kernels  19.7 us (12%)
  waiting for transfers between devices  16.1 us (9%)
  starting transfers between devices  11.9 us (7%)
    all_to_all x2, blocking collectives, per_device(): recv = lax.all_to_all(send, ('row', 'col'), 0, 0, tiled=True)  62.8 us
    all_to_all x2, blocking collectives, per_device(): probe = lax.all_to_all(send, ('row', 'col'), 0, 0, tiled=True)  59.3 us
    ppermute x8, waiting for transfers between devices, swap_chip(): lax.ppermute(value, 'col', [(i, i ^ 2 << (step + i % 2) % bits) for i in...  12.2 us
    ppermute x8, starting transfers between devices, swap_chip(): lax.ppermute(value, 'col', [(i, i ^ 2 << (step + i % 2) % bits) for i in...  10.5 us
    pallas_call x2, Pallas kernels, forward(): pl.pallas_call(functools.partial(forward_kernel, dims, pitch), in_specs=[...  7.82 us
    pallas_call x1, Pallas kernels, first_backward(): pl.pallas_call(functools.partial(first_backward_kernel, dims, pitch), in_...  4.51 us
    ppermute x8, waiting for transfers between devices, swap_core(): return lax.ppermute(value, 'col', [(i, i ^ 1) for i in range(n_col)])  3.88 us
  transfers between devices with their start and end apart: 16, of which 10 were waited for; matrix products, arithmetic and copies ran while one was open for 0% of the time, Pallas kernels for 1%

profile of v7, /device:TPU:0, one launch (start us, length us, event | category | flops | bytes accessed | tf_op | source)
XLA Modules:
  0.0 171.0 jit_solution(7983618092624070504)
XLA Ops:
  0.7 4.5 %first_backward_products.1 = (bf16[32,128,128]{2,1,0:T(8,128)(2,1)S(1)}, bf16[256,128,128]{2,1,0:T(8,128)(2,1)S(1)}) custom-call(s32[1]{0:T(128)} %bitcast.core_ref, s32[256]{0:T(256)} %bitcast.22, s32[256]{0:T(256)} %bitcast.26, f32[2,128,8,128]{3,2,1,0:T(8,128)} %bitcast.19, bf16[256,128,128]{2,1,0:T(8,128)(2,1)} %bitcast.34), custom_call_target="tpu_custom_call" | custom-call | flops 134217728 | bytes 4194304 | tf_op jit(solution)/shard_map/first_backward_products/pallas_call | solution.py:345
  5.2 0.0 copy-start
  5.2 0.0 copy-start.1
  5.2 33.3 %all_to_all.20.refs_0_ = bf16[32,128,128]{2,1,0:T(8,128)(2,1)S(1)} all-to-all(bf16[32,128,128]{2,1,0:T(8,128)(2,1)S(1)} %get-tuple-element.24), channel_id=1, replica_groups=mesh['row'=4,'col'=8] {'row','col'}, dimensions={0} | all-to-all | bytes 2097152 | tf_op jit(solution)/shard_map/all_to_all | solution.py:472
  38.6 0.9 primal_update.2
  39.6 29.7 %all_to_all.21.probe_ref = bf16[32,128,128]{2,1,0:T(8,128)(2,1)S(1)} all-to-all(bf16[32,128,128]{2,1,0:T(8,128)(2,1)S(1)} %get-tuple-element.25), channel_id=1, replica_groups=mesh['row'=4,'col'=8] {'row','col'}, dimensions={0} | all-to-all | bytes 2097152 | tf_op jit(solution)/shard_map/all_to_all | solution.py:475
  69.2 3.9 %forward_products.2 = (f32[512,128]{1,0:T(8,128)S(1)}, f32[512,128]{1,0:T(8,128)S(1)}, f32[512,128]{1,0:T(8,128)S(1)}, f32[512,128]{1,0:T(8,128)S(1)}) custom-call(s32[1]{0:T(128)} %bitcast.core_ref, s32[256]{0:T(256)S(1)} %bitcast.23, s32[256]{0:T(256)S(1)} %bitcast.27, bf16[32,128,128]{2,1,0:T(8,128)(2,1)S(1)} %all_to_all.21.probe_ref, ...), custom_call_target="tpu_custom_call" | custom-call | flops 134217728 | bytes 4194304 | tf_op jit(solution)/shard_map/forward_products/pallas_call | solution.py:380
  73.2 0.1 collective-permute-start
  73.2 0.5 collective-permute-start.3
  73.7 1.0 collective-permute-done.second_ref.other_ref
  74.8 1.5 collective-permute-start.1
  76.3 0.0 collective-permute-done.3.second_ref.other_ref
  76.4 0.6 collective-permute-start.4
  77.0 2.8 %collective-permute-done.1.second_ref.refs_0_ = bf16[512,128]{1,0:T(8,128)(2,1)S(1)} collective-permute-done((bf16[512,128]{1,0:T(8,128)(2,1)S(1)}, bf16[512,128]{1,0:T(8,128)(2,1)S(1)}, u32[]{:S(2)}, u32[]{:S(2)}) %collective-permute-start.1) | collective-permute-done | bytes 131104 | tf_op jit(solution)/shard_map/ppermute | solution.py:411
  79.9 1.6 collective-permute-start.2
  81.4 0.0 collective-permute-done.4.second_ref.refs_0_
  81.5 1.6 collective-permute-start.5
  83.0 1.9 %collective-permute-done.2.refs_1_ = bf16[512,128]{1,0:T(8,128)(2,1)S(1)} collective-permute-done((bf16[512,128]{1,0:T(8,128)(2,1)S(1)}, bf16[512,128]{1,0:T(8,128)(2,1)S(1)}, u32[]{:S(2)}, u32[]{:S(2)}) %collective-permute-start.2) | collective-permute-done | bytes 131104 | tf_op jit(solution)/shard_map/ppermute | solution.py:411
  84.9 0.1 dual_update.4
  85.0 0.1 collective-permute-start.6
  85.1 1.4 collective-permute-done.5.refs_1_
  86.5 0.1 dual_update.5
  86.6 0.1 collective-permute-start.7
  86.7 0.0 collective-permute-done.6.refs_2_
  86.7 1.3 collective-permute-done.7.refs_3_
  88.0 3.0 %backward_products.1 = bf16[32,128,128]{2,1,0:T(8,128)(2,1)S(1)} custom-call(s32[1]{0:T(128)} %bitcast.core_ref, s32[256]{0:T(256)S(1)} %bitcast.24, s32[256]{0:T(256)S(1)} %bitcast.28, bf16[256,128,128]{2,1,0:T(8,128)(2,1)S(1)} %get-tuple-element.23.tiles_ref, bf16[512,128]{1,0:T(8,128)(2,1)S(1)} %get-tuple-element.28.refs_0_, ...), custom_call_target="tpu_custom_call" | custom-call | flops 134217728 | bytes 4194304 | tf_op jit(solution)/shard_map/backward_products/pallas_call | solution.py:368
  91.1 29.5 %all_to_all.22.refs_0_ = bf16[32,128,128]{2,1,0:T(8,128)(2,1)S(1)} all-to-all(bf16[32,128,128]{2,1,0:T(8,128)(2,1)S(1)} %backward_products.1), channel_id=1, replica_groups=mesh['row'=4,'col'=8] {'row','col'}, dimensions={0} | all-to-all | bytes 2097152 | tf_op jit(solution)/shard_map/all_to_all | solution.py:472
  120.5 0.8 primal_update.3
  121.4 29.7 %all_to_all.23.probe_ref = bf16[32,128,128]{2,1,0:T(8,128)(2,1)S(1)} all-to-all(bf16[32,128,128]{2,1,0:T(8,128)(2,1)S(1)} %get-tuple-element.35), channel_id=1, replica_groups=mesh['row'=4,'col'=8] {'row','col'}, dimensions={0} | all-to-all | bytes 2097152 | tf_op jit(solution)/shard_map/all_to_all | solution.py:475
  151.0 3.9 %forward_products.3 = (f32[512,128]{1,0:T(8,128)S(1)}, f32[512,128]{1,0:T(8,128)S(1)}, f32[512,128]{1,0:T(8,128)S(1)}, f32[512,128]{1,0:T(8,128)S(1)}) custom-call(s32[1]{0:T(128)} %bitcast.core_ref, s32[256]{0:T(256)S(1)} %bitcast.25, s32[256]{0:T(256)S(1)} %bitcast.29, bf16[32,128,128]{2,1,0:T(8,128)(2,1)S(1)} %all_to_all.23.probe_ref, ...), custom_call_target="tpu_custom_call" | custom-call | flops 134217728 | bytes 4194304 | tf_op jit(solution)/shard_map/forward_products/pallas_call | solution.py:380
  154.9 0.1 collective-permute-start.8
  155.0 0.5 collective-permute-start.11
  155.5 1.0 collective-permute-done.8.second_ref.other_ref
  156.6 1.5 collective-permute-start.9
  158.1 0.0 collective-permute-done.11.second_ref.other_ref
  158.2 0.6 collective-permute-start.12
  158.8 2.8 %collective-permute-done.9.second_ref.refs_0_ = bf16[512,128]{1,0:T(8,128)(2,1)S(1)} collective-permute-done((bf16[512,128]{1,0:T(8,128)(2,1)S(1)}, bf16[512,128]{1,0:T(8,128)(2,1)S(1)}, u32[]{:S(2)}, u32[]{:S(2)}) %collective-permute-start.9) | collective-permute-done | bytes 131104 | tf_op jit(solution)/shard_map/ppermute | solution.py:411
  161.6 1.6 collective-permute-start.10
  163.2 1.6 collective-permute-start.13
  164.8 1.9 %collective-permute-done.10.refs_1_ = bf16[512,128]{1,0:T(8,128)(2,1)S(1)} collective-permute-done((bf16[512,128]{1,0:T(8,128)(2,1)S(1)}, bf16[512,128]{1,0:T(8,128)(2,1)S(1)}, u32[]{:S(2)}, u32[]{:S(2)}) %collective-permute-start.10) | collective-permute-done | bytes 131104 | tf_op jit(solution)/shard_map/ppermute | solution.py:411
  166.7 0.1 dual_update.6.refs_0_
  166.8 0.1 collective-permute-start.14
  166.9 1.4 collective-permute-done.13.refs_1_
  168.3 0.1 dual_update.7.refs_1_
  168.4 0.1 collective-permute-start.15
  168.5 1.0 own_results.1
  169.5 0.5 collective-permute-done.15.refs_1_
  170.0 0.8 other_results.1
  (24 shorter events, 0.3 us)
Async XLA Ops:
  0.6 68.6 %copy-start.5 = (s32[1,1,256]{2,1,0:T(1,128)S(1)}, s32[1,1,256]{2,1,0:T(1,128)}, u32[]{:S(2)}) copy-start(s32[1,1,256]{2,1,0:T(1,128)} %param.11) | copy-start | bytes 3076
  0.6 68.6 %copy-start.4 = (s32[1,1,256]{2,1,0:T(1,128)S(1)}, s32[1,1,256]{2,1,0:T(1,128)}, u32[]{:S(2)}) copy-start(s32[1,1,256]{2,1,0:T(1,128)} %param.10) | copy-start | bytes 3076
  0.7 37.9 %copy-start.3 = (f32[128,256]{1,0:T(8,128)S(1)}, f32[128,256]{1,0:T(8,128)}, u32[]{:S(2)}) copy-start(f32[128,256]{1,0:T(8,128)} %refs_3_.1) | copy-start | bytes 393220
  0.7 37.9 %copy-start.7 = (s32[256]{0:T(256)S(1)}, s32[256]{0:T(256)}, u32[]{:S(2)}) copy-start(s32[256]{0:T(256)} %param.16) | copy-start | bytes 3076
  0.7 37.9 %copy-start.6 = (s32[256]{0:T(256)S(1)}, s32[256]{0:T(256)}, u32[]{:S(2)}) copy-start(s32[256]{0:T(256)} %param.15) | copy-start | bytes 3076
  0.7 37.9 %copy-start.2 = (f32[4,128,256]{2,1,0:T(8,128)S(1)}, f32[4,128,256]{2,1,0:T(8,128)}, u32[]{:S(2)}) copy-start(f32[4,128,256]{2,1,0:T(8,128)} %refs_1_.1) | copy-start | bytes 1572868
  5.2 79.7 %copy-start = (s32[16,16384]{1,0:T(8,128)S(1)}, s32[16,16384]{1,0:T(8,128)}, u32[]{:S(2)}) copy-start(s32[16,16384]{1,0:T(8,128)} %param.17) | copy-start | bytes 3145732
  5.2 79.7 %copy-start.1 = (f32[16,16384]{1,0:T(8,128)S(1)}, f32[16,16384]{1,0:T(8,128)}, u32[]{:S(2)}) copy-start(f32[16,16384]{1,0:T(8,128)} %param.13) | copy-start | bytes 3145732
  73.2 1.6 collective-permute-start
  73.2 3.1 %collective-permute-start.3 = (f32[512,128]{1,0:T(8,128)S(1)}, f32[512,128]{1,0:T(8,128)S(1)}, u32[]{:S(2)}, u32[]{:S(2)}) collective-permute-start(f32[512,128]{1,0:T(8,128)S(1)} %get-tuple-element.30), channel_id=1, source_target_pairs={{0,1},{1,0},{2,3},{3,2},{4,5},{5,4},{6,7},{7,6},{8,9},{9,8},{10,11... | collective-permute-start | bytes 786440 | tf_op jit(solution)/shard_map/ppermute | solution.py:406
  74.8 5.0 %collective-permute-start.1 = (bf16[512,128]{1,0:T(8,128)(2,1)S(1)}, bf16[512,128]{1,0:T(8,128)(2,1)S(1)}, u32[]{:S(2)}, u32[]{:S(2)}) collective-permute-start(bf16[512,128]{1,0:T(8,128)(2,1)S(1)} %core_pair_sum.4.first_ref), channel_id=1, source_target_pairs={{0,2},{1,5},{2,0},{3,7},{4,6},{5,1},{6,4},{7,3},{8,10},{9,13},{10,... | collective-permute-start | bytes 393224 | tf_op jit(solution)/shard_map/ppermute | solution.py:411
  76.4 5.0 %collective-permute-start.4 = (bf16[512,128]{1,0:T(8,128)(2,1)S(1)}, bf16[512,128]{1,0:T(8,128)(2,1)S(1)}, u32[]{:S(2)}, u32[]{:S(2)}) collective-permute-start(bf16[512,128]{1,0:T(8,128)(2,1)S(1)} %core_pair_sum.5.first_ref), channel_id=1, source_target_pairs={{0,2},{1,5},{2,0},{3,7},{4,6},{5,1},{6,4},{7,3},{8,10},{9,13},{10,... | collective-permute-start | bytes 393224 | tf_op jit(solution)/shard_map/ppermute | solution.py:411
  79.9 5.0 %collective-permute-start.2 = (bf16[512,128]{1,0:T(8,128)(2,1)S(1)}, bf16[512,128]{1,0:T(8,128)(2,1)S(1)}, u32[]{:S(2)}, u32[]{:S(2)}) collective-permute-start(bf16[512,128]{1,0:T(8,128)(2,1)S(1)} %chip_sum.4), channel_id=1, source_target_pairs={{0,4},{1,3},{2,6},{3,1},{4,0},{5,7},{6,2},{7,5},{8,12},{9,11},{10,... | collective-permute-start | bytes 393224 | tf_op jit(solution)/shard_map/ppermute | solution.py:411
  81.5 5.0 %collective-permute-start.5 = (bf16[512,128]{1,0:T(8,128)(2,1)S(1)}, bf16[512,128]{1,0:T(8,128)(2,1)S(1)}, u32[]{:S(2)}, u32[]{:S(2)}) collective-permute-start(bf16[512,128]{1,0:T(8,128)(2,1)S(1)} %chip_sum.5), channel_id=1, source_target_pairs={{0,4},{1,3},{2,6},{3,1},{4,0},{5,7},{6,2},{7,5},{8,12},{9,11},{10,... | collective-permute-start | bytes 393224 | tf_op jit(solution)/shard_map/ppermute | solution.py:411
  85.0 1.7 collective-permute-start.6
  86.6 1.4 collective-permute-start.7
  154.9 1.6 collective-permute-start.8
  155.0 3.1 %collective-permute-start.11 = (f32[512,128]{1,0:T(8,128)S(1)}, f32[512,128]{1,0:T(8,128)S(1)}, u32[]{:S(2)}, u32[]{:S(2)}) collective-permute-start(f32[512,128]{1,0:T(8,128)S(1)} %get-tuple-element.40), channel_id=1, source_target_pairs={{0,1},{1,0},{2,3},{3,2},{4,5},{5,4},{6,7},{7,6},{8,9},{9,8},{10,11... | collective-permute-start | bytes 786440 | tf_op jit(solution)/shard_map/ppermute | solution.py:406
  156.6 5.0 %collective-permute-start.9 = (bf16[512,128]{1,0:T(8,128)(2,1)S(1)}, bf16[512,128]{1,0:T(8,128)(2,1)S(1)}, u32[]{:S(2)}, u32[]{:S(2)}) collective-permute-start(bf16[512,128]{1,0:T(8,128)(2,1)S(1)} %core_pair_sum.6.first_ref), channel_id=1, source_target_pairs={{0,2},{1,5},{2,0},{3,7},{4,6},{5,1},{6,4},{7,3},{8,10},{9,13},{10,... | collective-permute-start | bytes 393224 | tf_op jit(solution)/shard_map/ppermute | solution.py:411
  158.2 5.0 %collective-permute-start.12 = (bf16[512,128]{1,0:T(8,128)(2,1)S(1)}, bf16[512,128]{1,0:T(8,128)(2,1)S(1)}, u32[]{:S(2)}, u32[]{:S(2)}) collective-permute-start(bf16[512,128]{1,0:T(8,128)(2,1)S(1)} %core_pair_sum.7.first_ref), channel_id=1, source_target_pairs={{0,2},{1,5},{2,0},{3,7},{4,6},{5,1},{6,4},{7,3},{8,10},{9,13},{10,... | collective-permute-start | bytes 393224 | tf_op jit(solution)/shard_map/ppermute | solution.py:411
  161.6 5.0 %collective-permute-start.10 = (bf16[512,128]{1,0:T(8,128)(2,1)S(1)}, bf16[512,128]{1,0:T(8,128)(2,1)S(1)}, u32[]{:S(2)}, u32[]{:S(2)}) collective-permute-start(bf16[512,128]{1,0:T(8,128)(2,1)S(1)} %chip_sum.6), channel_id=1, source_target_pairs={{0,4},{1,3},{2,6},{3,1},{4,0},{5,7},{6,2},{7,5},{8,12},{9,11},{10,... | collective-permute-start | bytes 393224 | tf_op jit(solution)/shard_map/ppermute | solution.py:411
  163.2 5.0 %collective-permute-start.13 = (bf16[512,128]{1,0:T(8,128)(2,1)S(1)}, bf16[512,128]{1,0:T(8,128)(2,1)S(1)}, u32[]{:S(2)}, u32[]{:S(2)}) collective-permute-start(bf16[512,128]{1,0:T(8,128)(2,1)S(1)} %chip_sum.7), channel_id=1, source_target_pairs={{0,4},{1,3},{2,6},{3,1},{4,0},{5,7},{6,2},{7,5},{8,12},{9,11},{10,... | collective-permute-start | bytes 393224 | tf_op jit(solution)/shard_map/ppermute | solution.py:411
  166.8 2.7 %collective-permute-start.14 = (f32[2,32,8,128]{3,2,1,0:T(8,128)S(1)}, f32[2,32,8,128]{3,2,1,0:T(8,128)S(1)}, u32[]{:S(2)}, u32[]{:S(2)}) collective-permute-start(f32[2,32,8,128]{3,2,1,0:T(8,128)S(1)} %dual_update.6.refs_0_), channel_id=1, source_target_pairs={{0,1},{1,0},{2,3},{3,2},{4,5},{5,4},{6,7},{7,6},{8,9},{9,8},{10,11... | collective-permute-start | bytes 786440 | tf_op jit(solution)/shard_map/ppermute | solution.py:406
  168.4 1.6 collective-permute-start.15

commit v8 on v7

--- a/solution.py
+++ b/solution.py
@@ -11,6 +11,7 @@
 ITERS = 2
 SIGMA_STEP = 0.2
 PARTS = 2
+CHUNKS = 4
 UNROLL = 256
 FIRST_UNROLL = 32
 TRAIL = 16
@@ -41,6 +42,52 @@
 def column_place(dims, column, pitch):
     time_block, flight_tiles = dims[3], dims[4]
     return pl.multiple_of((column % flight_tiles * time_block + column // flight_tiles) * pitch, 8)
+
+
+def chunk_sizes(dims):
+    n_row, _, scen_local, time_block, flight_tiles, _ = dims
+    return n_row * scen_local // 2, flight_tiles // CHUNKS, time_block
+
+
+def scenario_offset(dims, index):
+    scen_local = dims[2]
+    return index // scen_local * 2 * scen_local + index % scen_local
+
+
+def split_dot(matrix, values, terms):
+    total = None
+    for _ in range(terms):
+        term = values.astype(jnp.bfloat16)
+        values = values - term.astype(jnp.float32)
+        part = jnp.dot(matrix, term, preferred_element_type=jnp.float32)
+        total = part if total is None else total + part
+    return total
+
+
+def zero_one(condition):
+    return condition.astype(jnp.float32).astype(jnp.bfloat16)
+
+
+def block_ones(rows, block):
+    row_iota = lax.broadcasted_iota(jnp.int32, (rows, rows * block), 0)
+    col_iota = lax.broadcasted_iota(jnp.int32, (rows, rows * block), 1)
+    return zero_one((col_iota >= row_iota * block) & (col_iota < (row_iota + 1) * block))
+
+
+def running(values, block, trailing, terms):
+    rows, side = values.shape
+    shape = (side, side)
+    row_iota, col_iota = lax.broadcasted_iota(jnp.int32, shape, 0), lax.broadcasted_iota(jnp.int32, shape, 1)
+    ordered = (col_iota >= row_iota) if trailing else (row_iota >= col_iota)
+    keep = zero_one(ordered & (row_iota // block == col_iota // block))
+    wide = jnp.concatenate([values[i : i + side] for i in range(0, rows, side)], axis=1)
+    sums = split_dot(keep, wide, terms)
+    return jnp.concatenate([sums[:, i : i + side] for i in range(0, rows, side)], axis=0)
+
+
+def spread(values, block):
+    rows, side = values.shape
+    return jnp.broadcast_to(values[:, None, :], (rows, block, side)).reshape(rows * block, side)
 
 
 def trailing_adds(width, products, add):
@@ -69,26 +116,28 @@
     trailing_adds(width, products, add)
 
 
-def write_messages(dims, pitch, acc_ref, out_ref):
-    n_row, n_col, scen_local, time_block, _, own_tiles = dims
-    piece = own_tiles * time_block
-    for group in range(n_row):
-        for column in range(n_col):
-            for j in range(scen_local):
-                base = column * own_tiles * time_block * pitch + group * scen_local + j
+def write_sums(dims, pitch, row, acc_ref, outs):
+    half, tiles, block = chunk_sizes(dims)
+    keeps, sends, (keep_totals, send_totals) = outs[:CHUNKS], outs[CHUNKS : 2 * CHUNKS], outs[2 * CHUNKS :]
+    ones = block_ones(half * tiles, block)
+    for refs, totals, parity, terms in ((sends, send_totals, 1 - row % 2, 1), (keeps, keep_totals, row % 2, 2)):
+        for c, ref in enumerate(refs):
+            for i in range(half):
+                start = scenario_offset(dims, i) + parity * dims[2]
                 parts = [
-                    acc_ref[pl.ds(base + f * time_block * pitch, time_block, stride=pitch), :]
-                    for f in range(own_tiles)
+                    acc_ref[pl.ds((c * tiles + t) * block * pitch + start, block, stride=pitch), :]
+                    for t in range(tiles)
                 ]
-                out_ref[group * n_col + column, pl.ds(j * piece, piece), :] = jnp.concatenate(
-                    parts, axis=0
-                ).astype(jnp.bfloat16)
+                ref[pl.ds(i * tiles * block, tiles * block), :] = jnp.concatenate(parts, axis=0).astype(ref.dtype)
+            totals[pl.ds(c * half * tiles, half * tiles), :] = split_dot(
+                ones, ref[...].astype(jnp.float32), terms
+            )
 
 
 def first_backward_kernel(
-    dims, pitch, core_ref, row_source, col_source, dual_source, source_ref, out_ref, tiles_ref,
-    rows_ref, cols_ref, bands_ref, duals_ref, acc_ref, sems
+    dims, pitch, where_ref, row_source, col_source, dual_source, source_ref, tiles_ref, *refs
 ):
+    outs, (rows_ref, cols_ref, bands_ref, duals_ref, acc_ref, sems) = refs[: 2 * CHUNKS + 2], refs[2 * CHUNKS + 2 :]
     count, pieces = tiles_ref.shape[0], sems.shape[0] - 3
     chunk = count // pieces
     lists = [
@@ -117,17 +166,17 @@
     for i, copy in enumerate(copies):
         copy.wait()
         lax.fori_loop(i * chunk // FIRST_UNROLL, (i + 1) * chunk // FIRST_UNROLL, body, 0)
-    write_messages(dims, pitch, acc_ref, out_ref)
+    write_sums(dims, pitch, where_ref[1], acc_ref, outs)
 
 
 def row_part(core, part, rows):
     return (core * PARTS + part) * rows
 
 
-def backward_kernel(dims, pitch, core_ref, rows_ref, cols_ref, tiles_ref, *refs):
-    pieces, (out_ref, duals_ref, acc_ref) = refs[: 2 * PARTS], refs[2 * PARTS :]
+def backward_kernel(dims, pitch, where_ref, rows_ref, cols_ref, tiles_ref, *refs):
+    pieces, outs, (duals_ref, acc_ref) = refs[: 2 * PARTS], refs[2 * PARTS : -2], refs[-2:]
     for i, piece in enumerate(pieces):
-        core = core_ref[0] if i < PARTS else 1 - core_ref[0]
+        core = where_ref[0] if i < PARTS else 1 - where_ref[0]
         scen, side = duals_ref.shape[1:]
         rows = piece.shape[0] // scen
         duals_ref[pl.ds(row_part(core, i % PARTS, rows), rows)] = piece[...].reshape(rows, scen, side)
@@ -140,23 +189,28 @@
         return 0
 
     lax.fori_loop(0, tiles_ref.shape[0] // width, body, 0)
-    write_messages(dims, pitch, acc_ref, out_ref)
-
-
-def forward_kernel(dims, pitch, core_ref, rows_ref, cols_ref, probe_ref, tiles_ref, *refs):
-    n_row, n_col, scen_local, time_block, _, own_tiles = dims
-    scen = n_row * scen_local
-    piece = own_tiles * time_block
+    write_sums(dims, pitch, where_ref[1], acc_ref, outs)
+
+
+def forward_kernel(dims, pitch, where_ref, rows_ref, cols_ref, tiles_ref, *refs):
+    scen = dims[0] * dims[2]
+    half, tiles, block = chunk_sizes(dims)
+    local, offsets, refs = refs[: 2 * CHUNKS], refs[2 * CHUNKS : 2 * CHUNKS + 2], refs[2 * CHUNKS + 2 :]
     outs, (flat_ref, acc_ref) = refs[: 2 * PARTS], refs[2 * PARTS :]
     acc_ref[...] = jnp.zeros_like(acc_ref)
-    for group in range(n_row):
-        for column in range(n_col):
-            for j in range(scen_local):
-                base = column * own_tiles * time_block * pitch + group * scen_local + j
-                block = probe_ref[group * n_col + column, pl.ds(j * piece, piece), :].astype(jnp.float32)
-                for f in range(own_tiles):
-                    flat_ref[pl.ds(base + f * time_block * pitch, time_block, stride=pitch), :] = block[
-                        f * time_block : (f + 1) * time_block
+    for parts, offset_ref, parity in (
+        (local[:CHUNKS], offsets[0], where_ref[1] % 2),
+        (local[CHUNKS:], offsets[1], 1 - where_ref[1] % 2),
+    ):
+        for c, ref in enumerate(parts):
+            offset = offset_ref[pl.ds(c * half * tiles, half * tiles), :]
+            value = ref[...].astype(jnp.float32) + spread(offset, block)
+            for i in range(half):
+                start = scenario_offset(dims, i) + parity * dims[2]
+                for t in range(tiles):
+                    row = (i * tiles + t) * block
+                    flat_ref[pl.ds((c * tiles + t) * block * pitch + start, block, stride=pitch), :] = value[
+                        row : row + block
                     ]
 
     def picked(index):
@@ -186,73 +240,144 @@
 
     lax.fori_loop(0, tiles_ref.shape[0] // width, body, 0)
     for i, out_ref in enumerate(outs):
-        core = core_ref[0] if i < PARTS else 1 - core_ref[0]
+        core = where_ref[0] if i < PARTS else 1 - where_ref[0]
         size = out_ref.shape[0]
         out_ref[...] = acc_ref[pl.ds(pl.multiple_of(row_part(core, i % PARTS, size), size), size), :]
 
 
-def running(values, trailing, terms):
-    length = values.shape[0]
-    row_iota = lax.broadcasted_iota(jnp.int32, (length, length), 0)
-    col_iota = lax.broadcasted_iota(jnp.int32, (length, length), 1)
-    keep = ((col_iota >= row_iota) if trailing else (row_iota >= col_iota)).astype(jnp.float32).astype(jnp.bfloat16)
-    total = None
-    for _ in range(terms):
-        term = values.astype(jnp.bfloat16)
-        values = values - term.astype(jnp.float32)
-        part = jnp.dot(keep, term, preferred_element_type=jnp.float32)
-        total = part if total is None else total + part
-    return total
-
-
-def primal_kernel(dims, first, last, *refs):
-    n_row, n_col, scen_local, time_block, _, own_tiles = dims
-    refs = list(refs)
-    recv_ref, inc_ref = refs[:2]
-    cum_ref = None if first else refs[2]
-    cost_ref, start_ref, len_ref, inc_out, send_ref = refs[2 + (not first) :][:5]
-    cum_out = None if last else refs[-1]
-    window, flight_local = cost_ref.shape
-    side = flight_local // own_tiles
-    piece = own_tiles * time_block
-    tau_step = 0.6 / math.sqrt(window)
-    minutes = lax.broadcasted_iota(jnp.int32, (window, flight_local), 0)
-    begin = start_ref[...]
-    upper = ((minutes >= begin) & (minutes < begin + len_ref[...])).astype(jnp.float32)
-    slopes = []
-    for j in range(scen_local):
+def add_kernel(*refs):
+    total = refs[0][...].astype(jnp.float32)
+    for ref in refs[1:-1]:
+        total = total + ref[...].astype(jnp.float32)
+    refs[-1][...] = total.astype(refs[-1].dtype)
+
+
+def pair_kernel(first_ref, second_ref, sum_ref, rounded_ref):
+    total = first_ref[...] + second_ref[...].astype(jnp.float32)
+    sum_ref[...] = total
+    rounded_ref[...] = total.astype(jnp.bfloat16)
+
+
+def scan_kernel(bit, trailing, begin, where_ref, total_ref, other_ref, *refs):
+    later = (where_ref[2] >> bit) & 1
+    part = other_ref[...] * ((1 - later) if trailing else later).astype(jnp.float32)
+    scan_out, total_out = refs[-2:]
+    scan_out[...] = part if begin else refs[0][...] + part
+    total_out[...] = total_ref[...] + other_ref[...]
+
+
+def primal_kernel(dims, chunk, first, where_ref, pair_ref, far_ref, tail_ref, inc_ref, *refs):
+    half, tiles, block = chunk_sizes(dims)
+    if not first:
+        cum_ref, refs = refs[0], refs[1:]
+    cost_ref, start_ref, len_ref, inc_out, cum_out, local_out, send_out, total_out = refs
+    tau_step = 0.6 / math.sqrt(block * dims[1])
+    slope = pair_ref[...] + far_ref[...].astype(jnp.float32) + jnp.concatenate([cost_ref[...]] * half, axis=0)
+    tail = tail_ref[pl.ds(chunk * half * tiles, half * tiles), :]
+    gradient = running(slope, block, True, 2) + spread(tail, block)
+    begin = spread(start_ref[...][chunk * tiles : (chunk + 1) * tiles], block)
+    end = begin + spread(len_ref[...][chunk * tiles : (chunk + 1) * tiles], block)
+    side = begin.shape[1]
+    minute = lax.broadcasted_iota(jnp.int32, (tiles, block, side), 1).reshape(tiles * block, side)
+    minute = (minute + where_ref[2] * block).astype(jnp.float32)
+    upper = ((minute >= begin) & (minute < end)).astype(jnp.float32)
+    old = inc_ref[...]
+    old_sum = running(old, block, False, 3) if first else cum_ref[...]
+    fresh = jnp.clip(old - tau_step * gradient, 0.0, jnp.concatenate([upper] * half, axis=0))
+    inc_out[...] = fresh
+    fresh_sum = running(fresh, block, False, 3)
+    cum_out[...] = fresh_sum
+    local = 2.0 * fresh_sum - old_sum
+    local_out[...] = local
+    send_out[...] = local.astype(jnp.bfloat16)
+    total_out[...] = local_out[pl.ds(block - 1, half * tiles, stride=block), :]
+
+
+def join_kernel(*refs):
+    refs[-1][...] = jnp.concatenate([ref[...] for ref in refs[:-1]], axis=0)
+
+
+def outward_kernel(dims, inc_ref, cost_ref, start_ref, len_ref, out_ref):
+    _, n_col, scen_local, block, _, own_tiles = dims
+    side = inc_ref.shape[2] // own_tiles
+    piece = own_tiles * block
+
+    def lanes(value):
+        return jnp.concatenate([value[:, f * side : (f + 1) * side] for f in range(own_tiles)], axis=0)
+
+    window = jnp.concatenate([lanes(start_ref[...]), lanes(len_ref[...])], axis=0).astype(jnp.float32)
+    window = jnp.concatenate([window, jnp.zeros((16 - window.shape[0], side), jnp.float32)], axis=0)
+    for h in range(n_col):
+        minutes = pl.ds(h * block, block)
+        cost = lanes(cost_ref[minutes, :])
+        high = cost.astype(jnp.bfloat16)
+        bands = [lanes(inc_ref[j, minutes, :]).astype(jnp.bfloat16) for j in range(scen_local)]
+        bands += [high, (cost - high.astype(jnp.float32)).astype(jnp.bfloat16)]
+        for i, band in enumerate(bands):
+            out_ref[h, pl.ds(i * piece, piece), :] = band
+        out_ref[h, pl.ds(len(bands) * piece, 16), :] = window.astype(jnp.bfloat16)
+
+
+def arrive_kernel(dims, groups, where_ref, *refs):
+    _, n_col, scen_local, block, _, own_tiles = dims
+    half, tiles, _ = chunk_sizes(dims)
+    piece = own_tiles * block
+    sources, refs = refs[:groups], refs[groups:]
+    incs, costs, (start_out, len_out, total_out) = refs[:CHUNKS], refs[CHUNKS : 2 * CHUNKS], refs[2 * CHUNKS :]
+    for h in range(n_col):
         bands = []
-        for h in range(n_col):
-            total = recv_ref[h, pl.ds(j * piece, piece), :].astype(jnp.float32)
-            for g in range(1, n_row):
-                total = total + recv_ref[g * n_col + h, pl.ds(j * piece, piece), :].astype(jnp.float32)
-            bands.append(
-                jnp.concatenate([total[f * time_block : (f + 1) * time_block] for f in range(own_tiles)], axis=1)
-            )
-        slopes.append(jnp.concatenate(bands, axis=0) + cost_ref[...])
-    gradient = running(jnp.concatenate(slopes, axis=1), True, 2)
-    old = jnp.concatenate([inc_ref[j] for j in range(scen_local)], axis=1)
-    if first:
-        old_sum = running(old, False, 3)
-    else:
-        old_sum = jnp.concatenate([cum_ref[j] for j in range(scen_local)], axis=1)
-    fresh = jnp.clip(old - tau_step * gradient, 0.0, jnp.concatenate([upper] * scen_local, axis=1))
-    fresh_sum = running(fresh, False, 3)
-    probe = (2.0 * fresh_sum - old_sum).astype(jnp.bfloat16)
-    for j in range(scen_local):
-        lanes = slice(j * flight_local, (j + 1) * flight_local)
-        inc_out[j] = fresh[:, lanes]
-        if not last:
-            cum_out[j] = fresh_sum[:, lanes]
-        for h in range(n_col):
-            band = probe[h * time_block : (h + 1) * time_block, lanes]
-            block = jnp.concatenate([band[:, f * side : (f + 1) * side] for f in range(own_tiles)], axis=0)
-            for g in range(n_row):
-                send_ref[g * n_col + h, pl.ds(j * piece, piece), :] = block
-
-
-def sum_kernel(first_ref, second_ref, out_ref):
-    out_ref[...] = (first_ref[...].astype(jnp.float32) + second_ref[...].astype(jnp.float32)).astype(jnp.bfloat16)
+        for x, ref in enumerate(sources):
+            group = (where_ref[1] >> 1) ^ x
+            for j in range(scen_local):
+                band = ref[h, pl.ds(j * piece, piece), :].astype(jnp.float32)
+                for f in range(own_tiles):
+                    c, t = divmod(h * own_tiles + f, tiles)
+                    row = ((group * scen_local + j) * tiles + t) * block
+                    incs[c][pl.ds(pl.multiple_of(row, 8), block), :] = band[f * block : (f + 1) * block]
+        own = sources[0]
+        cost = own[h, pl.ds(scen_local * piece, piece), :].astype(jnp.float32)
+        cost = cost + own[h, pl.ds((scen_local + 1) * piece, piece), :].astype(jnp.float32)
+        window = own[h, pl.ds((scen_local + 2) * piece, 16), :].astype(jnp.float32)
+        for f in range(own_tiles):
+            tile = h * own_tiles + f
+            c, t = divmod(tile, tiles)
+            costs[c][pl.ds(t * block, block), :] = cost[f * block : (f + 1) * block]
+            start_out[pl.ds(tile, 1), :] = window[f : f + 1]
+            len_out[pl.ds(tile, 1), :] = window[own_tiles + f : own_tiles + f + 1]
+    ones = block_ones(tiles, block)
+    for c in range(CHUNKS):
+        total = split_dot(ones, costs[c][...], 3)
+        total_out[pl.ds(c * half * tiles, half * tiles), :] = jnp.concatenate([total] * half, axis=0)
+
+
+def homeward_kernel(dims, where_ref, *refs):
+    _, n_col, scen_local, block, _, own_tiles = dims
+    half, tiles, _ = chunk_sizes(dims)
+    chunks, outs, flat_ref = refs[:CHUNKS], refs[CHUNKS:-1], refs[-1]
+    rows = half * tiles * block
+    for c, ref in enumerate(chunks):
+        flat_ref[pl.ds(c * rows, rows), :] = ref[...]
+    first = (where_ref[1] >> 1) * scen_local
+    for d, out_ref in enumerate(outs):
+        bands = []
+        for j in range(scen_local):
+            for f in range(own_tiles):
+                tile = (where_ref[2] ^ d) * own_tiles + f
+                row = tile // tiles * rows + ((first + j) * tiles + tile % tiles) * block
+                bands.append(flat_ref[pl.ds(pl.multiple_of(row, 8), block), :])
+        out_ref[...] = jnp.concatenate(bands, axis=0).astype(jnp.bfloat16)
+
+
+def home_kernel(dims, where_ref, *refs):
+    _, _, scen_local, block, _, own_tiles = dims
+    out_ref = refs[-1]
+    side = out_ref.shape[2] // own_tiles
+    for d, ref in enumerate(refs[:-1]):
+        minutes = pl.ds(pl.multiple_of((where_ref[2] ^ d) * block, 8), block)
+        for j in range(scen_local):
+            band = ref[pl.ds(j * own_tiles * block, own_tiles * block), :].astype(jnp.float32)
+            for f in range(own_tiles):
+                out_ref[j, minutes, f * side : (f + 1) * side] = band[f * block : (f + 1) * block]
 
 
 def dual_kernel(remote, part, first, last, core_ref, own_ref, other_ref, *refs):
@@ -320,17 +445,41 @@
     own_tiles = flight_local // side
     col_tiles = time_block * flight_tiles
     dims = (n_row, n_col, scen_local, time_block, flight_tiles, own_tiles)
-    message = (n_row * n_col, scen_local * own_tiles * time_block, side)
     part_rows = row_tiles * scen // (2 * PARTS)
     pitch = scen + PITCH_PAD
     band = 8
 
     rows, cols = tile_rows.reshape(count), tile_cols.reshape(count)
-    core = (lax.axis_index("col") % 2).reshape(1)
+    column = lax.axis_index("col")
+    where = jnp.stack([column % 2, lax.axis_index("row"), column]).astype(jnp.int32)
     cost = pl.CostEstimate(flops=2 * count * scen * side * side, bytes_accessed=count * side * side, transcendentals=0)
     acc_cols = pltpu.VMEM((col_tiles * pitch, side), jnp.float32)
     picked_duals = pltpu.VMEM((row_tiles, scen, side), jnp.bfloat16)
-    messages = jax.ShapeDtypeStruct(message, jnp.bfloat16)
+    half, tiles_each, _ = chunk_sizes(dims)
+
+    def f32(*shape):
+        return jax.ShapeDtypeStruct(shape, jnp.float32)
+
+    def bf16(*shape):
+        return jax.ShapeDtypeStruct(shape, jnp.bfloat16)
+
+    chunk_shape = (half * tiles_each * time_block, side)
+    totals_shape = (half * flight_tiles, side)
+    home_rows = scen_local * own_tiles * time_block
+    out_rows = (scen_local + 2) * own_tiles * time_block + 16
+    sums_shape = [f32(*chunk_shape)] * CHUNKS + [bf16(*chunk_shape)] * CHUNKS + [f32(*totals_shape)] * 2
+
+    def call(kernel, name, out_shape, *args, scalar=0, scratch=()):
+        return pl.pallas_call(
+            kernel,
+            in_specs=[scalars()] * scalar + [whole()] * (len(args) - scalar),
+            out_specs=jax.tree.map(lambda _: whole(), out_shape),
+            out_shape=out_shape,
+            scratch_shapes=list(scratch),
+            compiler_params=params(),
+            name=name,
+        )(*args)
+
     part_f32 = jax.ShapeDtypeStruct((part_rows, side), jnp.float32)
     part_out = jax.ShapeDtypeStruct((scen // band, row_tiles // (2 * PARTS), band, side), jnp.float32)
     part_bf16 = jax.ShapeDtypeStruct((part_rows, side), jnp.bfloat16)
@@ -345,8 +494,8 @@
         return pl.pallas_call(
             functools.partial(first_backward_kernel, dims, pitch),
             in_specs=[scalars()] + [pl.BlockSpec(memory_space=pltpu.HBM)] * 4,
-            out_specs=[whole(), whole()],
-            out_shape=[messages, pltpu.VMEM((count, side, side), jnp.bfloat16)],
+            out_specs=[whole()] * (1 + len(sums_shape)),
+            out_shape=[pltpu.VMEM((count, side, side), jnp.bfloat16), *sums_shape],
             scratch_shapes=[
                 pltpu.SMEM((count,), jnp.int32),
                 pltpu.SMEM((count,), jnp.int32),
@@ -358,7 +507,7 @@
             compiler_params=params(),
             cost_estimate=cost,
             name="first_backward_products",
-        )(core, in_hbm(rows), in_hbm(cols), in_hbm(duals), in_hbm(tile_values.reshape(count, side, side)))
+        )(where, in_hbm(rows), in_hbm(cols), in_hbm(duals), in_hbm(tile_values.reshape(count, side, side)))
 
     def in_vmem(array):
         return pltpu.with_memory_space_constraint(array, pltpu.VMEM)
@@ -368,39 +517,91 @@
         return pl.pallas_call(
             functools.partial(backward_kernel, dims, pitch),
             in_specs=[scalars()] * 3 + [whole()] * (1 + len(pieces)),
-            out_specs=whole(),
-            out_shape=messages,
+            out_specs=[whole()] * len(sums_shape),
+            out_shape=sums_shape,
             scratch_shapes=[picked_duals, acc_cols],
             compiler_params=params(),
             cost_estimate=cost,
             name="backward_products",
-        )(core, rows, cols, in_vmem(tiles), *pieces)
-
-    def forward(probe, tiles):
+        )(where, rows, cols, in_vmem(tiles), *pieces)
+
+    def forward(tiles, *probes):
         return pl.pallas_call(
             functools.partial(forward_kernel, dims, pitch),
-            in_specs=[scalars()] * 3 + [whole()] * 2,
+            in_specs=[scalars()] * 3 + [whole()] * (1 + len(probes)),
             out_specs=[whole()] * (2 * PARTS),
             out_shape=[part_f32] * (2 * PARTS),
             scratch_shapes=[acc_cols, pltpu.VMEM((row_tiles * scen, side), jnp.float32)],
             compiler_params=params(),
             cost_estimate=cost,
             name="forward_products",
-        )(core, rows, cols, probe, in_vmem(tiles))
-
-    def primal_step(recv, primal, cumulative, last):
-        first = cumulative is None
-        state = (primal,) if first else (primal, cumulative)
-        shape = jax.ShapeDtypeStruct(primal.shape, jnp.float32)
-        out_shape = [pltpu.VMEM(primal.shape, jnp.float32), messages] if last else [shape, messages, shape]
-        return pl.pallas_call(
-            functools.partial(primal_kernel, dims, first, last),
-            in_specs=[whole()] * (4 + len(state)),
-            out_specs=[whole()] * len(out_shape),
-            out_shape=out_shape,
-            compiler_params=params(),
-            name="primal_update",
-        )(recv, *state, flight_cost, win_start.reshape(1, -1), win_len.reshape(1, -1))
+        )(where, rows, cols, in_vmem(tiles), *probes)
+
+    def swap_row(value, bit):
+        return lax.ppermute(value, "row", [(i, i ^ (1 << bit)) for i in range(n_row)])
+
+    row_bits, col_bits = n_row.bit_length() - 1, n_col.bit_length() - 1
+
+    def scan_blocks(total, trailing, name):
+        scanned = []
+        for bit in range(col_bits):
+            other = lax.ppermute(total, "col", [(i, i ^ (1 << bit)) for i in range(n_col)])
+            kernel = functools.partial(scan_kernel, bit, trailing, bit == 0)
+            *scanned, total = call(
+                kernel, name, [f32(*totals_shape)] * 2, where, total, other, *scanned, scalar=1
+            )
+        return scanned[0]
+
+    def arrive():
+        message = call(
+            functools.partial(outward_kernel, dims),
+            "primal_outward",
+            bf16(n_col, out_rows, side),
+            increments,
+            flight_cost,
+            win_start.reshape(1, -1),
+            win_len.reshape(1, -1),
+        )
+        own = lax.all_to_all(message, "col", 0, 0, tiled=True)
+        groups = [own[:, :home_rows]]
+        for bit in range(1, row_bits):
+            groups += [swap_row(group, bit) for group in groups]
+        groups[0] = own
+        got = call(
+            functools.partial(arrive_kernel, dims, len(groups)),
+            "primal_arrive",
+            [f32(*chunk_shape)] * CHUNKS
+            + [f32(tiles_each * time_block, side)] * CHUNKS
+            + [f32(flight_tiles, side)] * 2
+            + [f32(*totals_shape)],
+            where,
+            *groups,
+            scalar=1,
+        )
+        return got[:CHUNKS], got[CHUNKS : 2 * CHUNKS], *got[2 * CHUNKS :]
+
+    def go_home(chunks):
+        pieces = call(
+            functools.partial(homeward_kernel, dims),
+            "primal_homeward",
+            [bf16(home_rows, side)] * n_col,
+            where,
+            *chunks,
+            scalar=1,
+            scratch=[pltpu.VMEM((CHUNKS * chunk_shape[0], side), jnp.float32)],
+        )
+        got = [
+            lax.ppermute(piece, "col", [(i, i ^ d) for i in range(n_col)]) if d else piece
+            for d, piece in enumerate(pieces)
+        ]
+        return call(
+            functools.partial(home_kernel, dims),
+            "primal_home",
+            pltpu.VMEM(increments.shape, jnp.float32),
+            where,
+            *got,
+            scalar=1,
+        )
 
     def swap_core(value):
         return lax.ppermute(value, "col", [(i, i ^ 1) for i in range(n_col)])
@@ -412,7 +613,7 @@
 
     def bf16_sum(first, second, name):
         return pl.pallas_call(
-            sum_kernel,
+            add_kernel,
             in_specs=[whole()] * 2,
             out_specs=whole(),
             out_shape=part_bf16,
@@ -436,7 +637,7 @@
             out_shape=out_shape,
             compiler_params=params(),
             name="dual_update",
-        )(core, own, other, *parts, dual, banded(capacity))
+        )(where, own, other, *parts, dual, banded(capacity))
 
     def results(primal, owned):
         duals_shape = jax.ShapeDtypeStruct((scen // band, row_tiles, band, side), jnp.float32)
@@ -450,7 +651,7 @@
             scratch_shapes=[pltpu.SemaphoreType.DMA((copies + 1,))],
             compiler_params=params(),
             name="own_results",
-        )(core, in_vmem(primal), *owned)
+        )(where, in_vmem(primal), *owned)
         duals_out = pl.pallas_call(
             other_results_kernel,
             in_specs=[scalars(), hbm] + [whole()] * PARTS,
@@ -460,27 +661,61 @@
             scratch_shapes=[pltpu.SemaphoreType.DMA((copies,))],
             compiler_params=params(),
             name="other_results",
-        )(core, duals_out, *map(swap_core, owned))
+        )(where, duals_out, *map(swap_core, owned))
         return primal_out, duals_out.transpose(0, 2, 1, 3).reshape(scen, row_length)
 
-    send, tiles = first_backward(banded(dual_vars))
-    duals, primal, cumulative = [banded(dual_vars)] * PARTS, increments, None
+    incs, costs, starts, lengths, cost_totals = arrive()
+    tiles, *sums = first_backward(banded(dual_vars))
+    duals, cums = [banded(dual_vars)] * PARTS, [()] * CHUNKS
     for sweep in range(ITERS):
         last = sweep + 1 == ITERS
         if sweep:
-            send = backward(rounded, tiles)
-        recv = lax.all_to_all(send, ("row", "col"), 0, 0, tiled=True)
-        primal, send, *cumulative = primal_step(recv, primal, cumulative, last)
-        cumulative = None if last else cumulative[0]
-        probe = lax.all_to_all(send, ("row", "col"), 0, 0, tiled=True)
-        images = forward(probe, tiles)
+            sums = backward(rounded, tiles)
+        keeps, sends, (keep_total, send_total) = sums[:CHUNKS], sums[CHUNKS : 2 * CHUNKS], sums[2 * CHUNKS :]
+        near = [swap_row(send, 0) for send in sends]
+        total = call(add_kernel, "totals", f32(*totals_shape), keep_total, swap_row(send_total, 0))
+        pairs = [call(pair_kernel, "row_pair_sum", [f32(*chunk_shape), bf16(*chunk_shape)], *x) for x in zip(keeps, near)]
+        for bit in range(1, row_bits):
+            ends = bit + 1 == row_bits
+            far = [swap_row(pair[1], bit) for pair in pairs]
+            more = [cost_totals] if ends else []
+            total = call(add_kernel, "totals", f32(*totals_shape), total, swap_row(total, bit), *more)
+            if not ends:
+                pairs = [
+                    call(pair_kernel, "row_pair_sum", [f32(*chunk_shape), bf16(*chunk_shape)], pair[0], x)
+                    for pair, x in zip(pairs, far)
+                ]
+        tail = scan_blocks(total, True, "later_blocks")
+        steps = [
+            call(
+                functools.partial(primal_kernel, dims, c, sweep == 0),
+                "primal_update",
+                [f32(*chunk_shape)] * 3 + [bf16(*chunk_shape), f32(half * tiles_each, side)],
+                where,
+                pairs[c][0],
+                far[c],
+                tail,
+                incs[c],
+                *cums[c],
+                costs[c],
+                starts,
+                lengths,
+                scalar=1,
+            )
+            for c in range(CHUNKS)
+        ]
+        incs, cums = [step[0] for step in steps], [(step[1],) for step in steps]
+        returned = [swap_row(step[3], 0) for step in steps]
+        block_total = call(join_kernel, "block_totals", f32(*totals_shape), *(step[4] for step in steps))
+        offset = scan_blocks(block_total, False, "earlier_blocks")
+        images = forward(tiles, *(step[2] for step in steps), *returned, offset, swap_row(offset, 0))
         updates = [
             dual_step(part, images[part], images[PARTS + part], duals[part], sweep == 0, last)
             for part in range(PARTS)
         ]
         duals = [update[0] for update in updates]
         rounded = None if last else [update[1] for update in updates]
-    return results(primal, duals)
+    return results(go_home(incs), duals)
 
 
 def solution(mesh):

time: 171 us -> 203 us (1.19)
  blocking collectives: 122 us -> 13.7 us
  waiting for transfers between devices: 16.1 us -> 85.3 us
  starting transfers between devices: 11.9 us -> 53 us
  Pallas kernels: 19.7 us -> 46.5 us
  local copies, waits for them, and re-layouts: 0.04 us -> 3.33 us
    all_to_all x4 -> x1, blocking collectives: 122 us -> 13.7 us  [arrive(): own = lax.all_to_all(message, 'col', 0, 0, tiled=True)]
    ppermute x0 -> x50, waiting for transfers between devices: none -> 67.9 us  [the longest x31 45 us: swap_row(): return lax.ppermute(value, 'row', [(i, i ^ 1 << bit) for i in range(n_row)])]
    ppermute x0 -> x50, starting transfers between devices: none -> 44.3 us  [the longest x31 31.7 us: swap_row(): return lax.ppermute(value, 'row', [(i, i ^ 1 << bit) for i in range(n_row)])]
    pallas_call x10 -> x46, Pallas kernels: 2.03 us -> 23.7 us  [the longest x38 23.4 us: call(): pl.pallas_call(kernel, in_specs=[scalars()] * scalar + [whole()] * (len(a...]
    unnamed x16, local copies, waits for them, and re-layouts: 0.04 us -> 3.32 us
    ppermute x8, starting transfers between devices: 10.5 us -> 7.32 us  [swap_chip(): lax.ppermute(value, 'col', [(i, i ^ 2 << (step + i % 2) % bits) for i in...]
    pallas_call x4, Pallas kernels: 0.47 us -> 2.63 us  [dual_step(): pl.pallas_call(functools.partial(dual_kernel, bits, part, first, last), i...]
  transfers between devices with their start and end apart: 16 -> 66, of which waited for: 10 -> 48; matrix products, arithmetic and copies ran while one was open for 0% -> 0% of each run, Pallas kernels for 1% -> 14%
where the time goes in v8:
time: 203 us
  waiting for transfers between devices  85.3 us (42%)
  starting transfers between devices  53 us (26%)
  Pallas kernels  46.5 us (23%)
  blocking collectives  13.7 us (7%)
  local copies, waits for them, and re-layouts  3.33 us (2%)
    ppermute x31, waiting for transfers between devices, swap_row(): return lax.ppermute(value, 'row', [(i, i ^ 1 << bit) for i in range(n_row)])  45 us
    ppermute x31, starting transfers between devices, swap_row(): return lax.ppermute(value, 'row', [(i, i ^ 1 << bit) for i in range(n_row)])  31.7 us
    pallas_call x38, Pallas kernels, call(): pl.pallas_call(kernel, in_specs=[scalars()] * scalar + [whole()] * (len(a...  23.4 us
    ppermute x12, waiting for transfers between devices, scan_blocks(): lax.ppermute(total, 'col', [(i, i ^ 1 << bit) for i in range(n_col)])  17.5 us
    ppermute x8, waiting for transfers between devices, swap_chip(): lax.ppermute(value, 'col', [(i, i ^ 2 << (step + i % 2) % bits) for i in...  14 us
    all_to_all x1, blocking collectives, arrive(): own = lax.all_to_all(message, 'col', 0, 0, tiled=True)  13.7 us
    pallas_call x2, Pallas kernels, forward(): pl.pallas_call(functools.partial(forward_kernel, dims, pitch), in_specs=[...  8.29 us
    ppermute x12, starting transfers between devices, scan_blocks(): lax.ppermute(total, 'col', [(i, i ^ 1 << bit) for i in range(n_col)])  7.36 us
  transfers between devices with their start and end apart: 66, of which 48 were waited for; matrix products, arithmetic and copies ran while one was open for 0% of the time, Pallas kernels for 14%

profile of v8, /device:TPU:0, one launch (start us, length us, event | category | flops | bytes accessed | tf_op | source)
XLA Modules:
  0.0 203.1 jit_solution(11242016100590666727)
XLA Ops:
  4.0 13.7 %all_to_all.5.refs_0_ = bf16[8,208,128]{2,1,0:T(8,128)(2,1)S(1)} all-to-all(bf16[8,208,128]{2,1,0:T(8,128)(2,1)S(1)} %primal_outward.1), channel_id=1, replica_groups=mesh['row'=4,'col'=8] {'col'}, dimensions={0} | all-to-all | bytes 851968 | tf_op jit(solution)/shard_map/all_to_all | solution.py:565
  17.7 2.7 %collective-permute-start.4 = (bf16[8,128,128]{2,1,0:T(8,128)(2,1)S(1)}, bf16[8,128,128]{2,1,0:T(8,128)(2,1)S(1)}, u32[]{:S(2)}, u32[]{:S(2)}) collective-permute-start(bf16[8,128,128]{2,1,0:T(8,128)(2,1)S(1)} %slice.4), channel_id=1, source_target_pairs={{0,16},{8,24},{16,0},{24,8},{1,17},{9,25},{17,1},{25,9},{2,18},{10... | collective-permute-start | bytes 786440 | tf_op jit(solution)/shard_map/ppermute | solution.py:541
  20.4 5.4 %first_backward_products.1 = (bf16[256,128,128]{2,1,0:T(8,128)(2,1)S(1)}, f32[512,128]{1,0:T(8,128)S(1)}, f32[512,128]{1,0:T(8,128)S(1)}, f32[512,128]{1,0:T(8,1...) custom-call(s32[3]{0:T(128)S(1)} %pad_add_fusion.where_ref.core_ref,, ...), custom_call_target="tpu_custom_call" | custom-call | flops 134217728 | bytes 4194304 | tf_op jit(solution)/shard_map/first_backward_products/pallas_call | solution.py:494
  25.8 1.6 collective-permute-start.2
  27.5 6.0 %collective-permute-done.2.refs_1_ = f32[128,128]{1,0:T(8,128)S(1)} collective-permute-done((f32[128,128]{1,0:T(8,128)S(1)}, f32[128,128]{1,0:T(8,128)S(1)}, u32[]{:S(2)}, u32[]{:S(2)}) %collective-permute-start.2) | collective-permute-done | bytes 65568 | tf_op jit(solution)/shard_map/ppermute | solution.py:541
  34.5 2.4 %collective-permute-start.12 = (bf16[512,128]{1,0:T(8,128)(2,1)S(1)}, bf16[512,128]{1,0:T(8,128)(2,1)S(1)}, u32[]{:S(2)}, u32[]{:S(2)}) collective-permute-start(bf16[512,128]{1,0:T(8,128)(2,1)S(1)} %get-tuple-element.161), channel_id=1, source_target_pairs={{0,8},{8,0},{16,24},{24,16},{1,9},{9,1},{17,25},{25,17},{2,10},{10... | collective-permute-start | bytes 393224 | tf_op jit(solution)/shard_map/ppermute | solution.py:541
  37.0 2.0 collective-permute-start.8
  42.7 1.6 collective-permute-start.13
  45.8 5.5 %collective-permute-done.8.second_ref = bf16[512,128]{1,0:T(8,128)(2,1)S(1)} collective-permute-done((bf16[512,128]{1,0:T(8,128)(2,1)S(1)}, bf16[512,128]{1,0:T(8,128)(2,1)S(1)}, u32[]{:S(2)}, u32[]{:S(2)}) %collective-permute-start.8) | collective-permute-done | bytes 131104 | tf_op jit(solution)/shard_map/ppermute | solution.py:541
  52.8 1.7 collective-permute-start.1
  55.8 3.6 %collective-permute-done.7.other_ref = f32[128,128]{1,0:T(8,128)S(1)} collective-permute-done((f32[128,128]{1,0:T(8,128)S(1)}, f32[128,128]{1,0:T(8,128)S(1)}, u32[]{:S(2)}, u32[]{:S(2)}) %collective-permute-start.7) | collective-permute-done | bytes 65568 | tf_op jit(solution)/shard_map/ppermute | solution.py:548
  62.4 1.7 collective-permute-done.11.far_ref
  65.2 1.7 collective-permute-done.9.far_ref
  72.9 2.0 collective-permute-start.16
  77.1 2.0 collective-permute-start.14
  79.1 1.8 collective-permute-done.20.other_ref
  82.1 2.8 %collective-permute-done.15.refs_5_ = bf16[512,128]{1,0:T(8,128)(2,1)S(1)} collective-permute-done((bf16[512,128]{1,0:T(8,128)(2,1)S(1)}, bf16[512,128]{1,0:T(8,128)(2,1)S(1)}, u32[]{:S(2)}, u32[]{:S(2)}) %collective-permute-start.15) | collective-permute-done | bytes 131104 | tf_op jit(solution)/shard_map/ppermute | solution.py:541
  84.9 2.4 %collective-permute-done.14.refs_4_ = bf16[512,128]{1,0:T(8,128)(2,1)S(1)} collective-permute-done((bf16[512,128]{1,0:T(8,128)(2,1)S(1)}, bf16[512,128]{1,0:T(8,128)(2,1)S(1)}, u32[]{:S(2)}, u32[]{:S(2)}) %collective-permute-start.14) | collective-permute-done | bytes 131104 | tf_op jit(solution)/shard_map/ppermute | solution.py:541
  88.0 4.1 %forward_products.2 = (f32[512,128]{1,0:T(8,128)S(1)}, f32[512,128]{1,0:T(8,128)S(1)}, f32[512,128]{1,0:T(8,128)S(1)}, f32[512,128]{1,0:T(8,128)S(1)}) custom-call(s32[3]{0:T(128)S(1)} %pad_add_fusion.where_ref.core_ref, s32[256]{0:T(256)S(1)} %bitcast.25, s32[256]{0:T(256)S(1)} %bitcast.29, bf16[256,128,128]{2,1,0:T(8,128)(2,1)S(1)} %get-tuple-element.128.tiles_ref, ...), custom_call_target="tpu_custom_call" | custom-call | flops 134217728 | bytes 4194304 | tf_op jit(solution)/shard_map/forward_products/pallas_call | solution.py:529
  96.0 2.8 %collective-permute-done.23.refs_1_.refs_0_ = bf16[512,128]{1,0:T(8,128)(2,1)S(1)} collective-permute-done((bf16[512,128]{1,0:T(8,128)(2,1)S(1)}, bf16[512,128]{1,0:T(8,128)(2,1)S(1)}, u32[]{:S(2)}, u32[]{:S(2)}) %collective-permute-start.23) | collective-permute-done | bytes 131104 | tf_op jit(solution)/shard_map/ppermute | solution.py:612
  101.1 2.8 %collective-permute-done.24.refs_1_ = bf16[512,128]{1,0:T(8,128)(2,1)S(1)} collective-permute-done((bf16[512,128]{1,0:T(8,128)(2,1)S(1)}, bf16[512,128]{1,0:T(8,128)(2,1)S(1)}, u32[]{:S(2)}, u32[]{:S(2)}) %collective-permute-start.24) | collective-permute-done | bytes 131104 | tf_op jit(solution)/shard_map/ppermute | solution.py:612
  106.1 1.3 collective-permute-done.29.refs_3_
  107.4 3.6 %backward_products.1 = (f32[512,128]{1,0:T(8,128)S(1)}, f32[512,128]{1,0:T(8,128)S(1)}, f32[512,128]{1,0:T(8,128)S(1)}, f32[512,128]{1,0:T(8,128)S(1)}, bf16[512...) custom-call(s32[3]{0:T(128)S(1)} %pad_add_fusion.where_ref.core_ref,, ...), custom_call_target="tpu_custom_call" | custom-call | flops 134217728 | bytes 4194304 | tf_op jit(solution)/shard_map/backward_products/pallas_call | solution.py:517
  111.3 4.0 %collective-permute-done.32.refs_1_ = f32[128,128]{1,0:T(8,128)S(1)} collective-permute-done((f32[128,128]{1,0:T(8,128)S(1)}, f32[128,128]{1,0:T(8,128)S(1)}, u32[]{:S(2)}, u32[]{:S(2)}) %collective-permute-start.32) | collective-permute-done | bytes 65568 | tf_op jit(solution)/shard_map/ppermute | solution.py:541
  116.2 1.7 collective-permute-start.30
  118.2 1.7 collective-permute-start.39
  126.2 1.4 collective-permute-start.38
  127.7 4.3 %collective-permute-done.39.second_ref = bf16[512,128]{1,0:T(8,128)(2,1)S(1)} collective-permute-done((bf16[512,128]{1,0:T(8,128)(2,1)S(1)}, bf16[512,128]{1,0:T(8,128)(2,1)S(1)}, u32[]{:S(2)}, u32[]{:S(2)}) %collective-permute-start.39) | collective-permute-done | bytes 131104 | tf_op jit(solution)/shard_map/ppermute | solution.py:541
  132.0 1.7 collective-permute-done.41.second_ref
  136.4 3.5 %collective-permute-done.36.other_ref = f32[128,128]{1,0:T(8,128)S(1)} collective-permute-done((f32[128,128]{1,0:T(8,128)S(1)}, f32[128,128]{1,0:T(8,128)S(1)}, u32[]{:S(2)}, u32[]{:S(2)}) %collective-permute-start.36) | collective-permute-done | bytes 65568 | tf_op jit(solution)/shard_map/ppermute | solution.py:548
  141.1 1.5 collective-permute-done.31.far_ref
  142.6 1.8 primal_update.12
  145.4 1.8 primal_update.13
  148.2 1.8 primal_update.14
  150.0 1.8 primal_update.15
  154.9 2.0 collective-permute-start.51
  159.4 2.0 collective-permute-start.53
  161.4 1.5 collective-permute-done.56.other_ref
  164.1 2.8 %collective-permute-done.52.refs_6_ = bf16[512,128]{1,0:T(8,128)(2,1)S(1)} collective-permute-done((bf16[512,128]{1,0:T(8,128)(2,1)S(1)}, bf16[512,128]{1,0:T(8,128)(2,1)S(1)}, u32[]{:S(2)}, u32[]{:S(2)}) %collective-permute-start.52) | collective-permute-done | bytes 131104 | tf_op jit(solution)/shard_map/ppermute | solution.py:541
  166.9 2.4 %collective-permute-done.53.refs_7_ = bf16[512,128]{1,0:T(8,128)(2,1)S(1)} collective-permute-done((bf16[512,128]{1,0:T(8,128)(2,1)S(1)}, bf16[512,128]{1,0:T(8,128)(2,1)S(1)}, u32[]{:S(2)}, u32[]{:S(2)}) %collective-permute-start.53) | collective-permute-done | bytes 131104 | tf_op jit(solution)/shard_map/ppermute | solution.py:541
  170.0 4.1 %forward_products.3 = (f32[512,128]{1,0:T(8,128)S(1)}, f32[512,128]{1,0:T(8,128)S(1)}, f32[512,128]{1,0:T(8,128)S(1)}, f32[512,128]{1,0:T(8,128)S(1)}) custom-call(s32[3]{0:T(128)S(1)} %pad_add_fusion.where_ref.core_ref, s32[256]{0:T(256)S(1)} %bitcast.27, s32[256]{0:T(256)S(1)} %bitcast.31, bf16[256,128,128]{2,1,0:T(8,128)(2,1)S(1)} %get-tuple-element.128.tiles_ref, ...), custom_call_target="tpu_custom_call" | custom-call | flops 134217728 | bytes 4194304 | tf_op jit(solution)/shard_map/forward_products/pallas_call | solution.py:529
  178.0 2.8 %collective-permute-done.59.refs_1_.refs_0_ = bf16[512,128]{1,0:T(8,128)(2,1)S(1)} collective-permute-done((bf16[512,128]{1,0:T(8,128)(2,1)S(1)}, bf16[512,128]{1,0:T(8,128)(2,1)S(1)}, u32[]{:S(2)}, u32[]{:S(2)}) %collective-permute-start.59) | collective-permute-done | bytes 131104 | tf_op jit(solution)/shard_map/ppermute | solution.py:612
  183.1 2.8 %collective-permute-done.60.refs_1_ = bf16[512,128]{1,0:T(8,128)(2,1)S(1)} collective-permute-done((bf16[512,128]{1,0:T(8,128)(2,1)S(1)}, bf16[512,128]{1,0:T(8,128)(2,1)S(1)}, u32[]{:S(2)}, u32[]{:S(2)}) %collective-permute-start.60) | collective-permute-done | bytes 131104 | tf_op jit(solution)/shard_map/ppermute | solution.py:612
  191.5 1.8 collective-permute-done.44.refs_2_
  193.9 1.3 collective-permute-start.48
  196.7 2.0 collective-permute-done.48.refs_6_
  200.0 1.6 own_results.1
  201.6 1.4 other_results.1
  (159 shorter events, 70.7 us)
Async XLA Ops:
  17.7 21.3 %collective-permute-start.4 = (bf16[8,128,128]{2,1,0:T(8,128)(2,1)S(1)}, bf16[8,128,128]{2,1,0:T(8,128)(2,1)S(1)}, u32[]{:S(2)}, u32[]{:S(2)}) collective-permute-start(bf16[8,128,128]{2,1,0:T(8,128)(2,1)S(1)} %slice.4), channel_id=1, source_target_pairs={{0,16},{8,24},{16,0},{24,8},{1,17},{9,25},{17,1},{25,9},{2,18},{10... | collective-permute-start | bytes 786440 | tf_op jit(solution)/shard_map/ppermute | solution.py:541
  25.8 7.7 %collective-permute-start.2 = (f32[128,128]{1,0:T(8,128)S(1)}, f32[128,128]{1,0:T(8,128)S(1)}, u32[]{:S(2)}, u32[]{:S(2)}) collective-permute-start(f32[128,128]{1,0:T(8,128)S(1)} %get-tuple-element.134), channel_id=1, source_target_pairs={{0,8},{8,0},{16,24},{24,16},{1,9},{9,1},{17,25},{25,17},{2,10},{10... | collective-permute-start | bytes 196616 | tf_op jit(solution)/shard_map/ppermute | solution.py:541
  33.5 6.3 %collective-permute-start.3 = (f32[128,128]{1,0:T(8,128)S(1)}, f32[128,128]{1,0:T(8,128)S(1)}, u32[]{:S(2)}, u32[]{:S(2)}) collective-permute-start(f32[128,128]{1,0:T(8,128)S(1)} %totals.4.refs_0_), channel_id=1, source_target_pairs={{0,16},{8,24},{16,0},{24,8},{1,17},{9,25},{17,1},{25,9},{2,18},{10... | collective-permute-start | bytes 196616 | tf_op jit(solution)/shard_map/ppermute | solution.py:541
  34.5 8.1 %collective-permute-start.12 = (bf16[512,128]{1,0:T(8,128)(2,1)S(1)}, bf16[512,128]{1,0:T(8,128)(2,1)S(1)}, u32[]{:S(2)}, u32[]{:S(2)}) collective-permute-start(bf16[512,128]{1,0:T(8,128)(2,1)S(1)} %get-tuple-element.161), channel_id=1, source_target_pairs={{0,8},{8,0},{16,24},{24,16},{1,9},{9,1},{17,25},{25,17},{2,10},{10... | collective-permute-start | bytes 393224 | tf_op jit(solution)/shard_map/ppermute | solution.py:541
  37.0 7.8 %collective-permute-start.10 = (bf16[512,128]{1,0:T(8,128)(2,1)S(1)}, bf16[512,128]{1,0:T(8,128)(2,1)S(1)}, u32[]{:S(2)}, u32[]{:S(2)}) collective-permute-start(bf16[512,128]{1,0:T(8,128)(2,1)S(1)} %get-tuple-element.154), channel_id=1, source_target_pairs={{0,8},{8,0},{16,24},{24,16},{1,9},{9,1},{17,25},{25,17},{2,10},{10... | collective-permute-start | bytes 393224 | tf_op jit(solution)/shard_map/ppermute | solution.py:541
  37.0 14.3 %collective-permute-start.8 = (bf16[512,128]{1,0:T(8,128)(2,1)S(1)}, bf16[512,128]{1,0:T(8,128)(2,1)S(1)}, u32[]{:S(2)}, u32[]{:S(2)}) collective-permute-start(bf16[512,128]{1,0:T(8,128)(2,1)S(1)} %get-tuple-element.147), channel_id=1, source_target_pairs={{0,8},{8,0},{16,24},{24,16},{1,9},{9,1},{17,25},{25,17},{2,10},{10... | collective-permute-start | bytes 393224 | tf_op jit(solution)/shard_map/ppermute | solution.py:541
  39.0 13.8 %collective-permute-start = (bf16[512,128]{1,0:T(8,128)(2,1)S(1)}, bf16[512,128]{1,0:T(8,128)(2,1)S(1)}, u32[]{:S(2)}, u32[]{:S(2)}) collective-permute-start(bf16[512,128]{1,0:T(8,128)(2,1)S(1)} %get-tuple-element.130), channel_id=1, source_target_pairs={{0,8},{8,0},{16,24},{24,16},{1,9},{9,1},{17,25},{25,17},{2,10},{10... | collective-permute-start | bytes 393224 | tf_op jit(solution)/shard_map/ppermute | solution.py:541
  41.7 12.8 %collective-permute-start.6 = (f32[128,128]{1,0:T(8,128)S(1)}, f32[128,128]{1,0:T(8,128)S(1)}, u32[]{:S(2)}, u32[]{:S(2)}) collective-permute-start(f32[128,128]{1,0:T(8,128)S(1)} %get-tuple-element.136.total_ref), channel_id=1, source_target_pairs={{0,2},{1,3},{2,0},{3,1},{4,6},{5,7},{6,4},{7,5},{8,10},{9,11},{10,... | collective-permute-start | bytes 196616 | tf_op jit(solution)/shard_map/ppermute | solution.py:548
  42.7 18.6 %collective-permute-start.13 = (bf16[512,128]{1,0:T(8,128)(2,1)S(1)}, bf16[512,128]{1,0:T(8,128)(2,1)S(1)}, u32[]{:S(2)}, u32[]{:S(2)}) collective-permute-start(bf16[512,128]{1,0:T(8,128)(2,1)S(1)} %get-tuple-element.163), channel_id=1, source_target_pairs={{0,16},{8,24},{16,0},{24,8},{1,17},{9,25},{17,1},{25,9},{2,18},{10... | collective-permute-start | bytes 393224 | tf_op jit(solution)/shard_map/ppermute | solution.py:541
  44.8 19.3 %collective-permute-start.11 = (bf16[512,128]{1,0:T(8,128)(2,1)S(1)}, bf16[512,128]{1,0:T(8,128)(2,1)S(1)}, u32[]{:S(2)}, u32[]{:S(2)}) collective-permute-start(bf16[512,128]{1,0:T(8,128)(2,1)S(1)} %get-tuple-element.156), channel_id=1, source_target_pairs={{0,16},{8,24},{16,0},{24,8},{1,17},{9,25},{17,1},{25,9},{2,18},{10... | collective-permute-start | bytes 393224 | tf_op jit(solution)/shard_map/ppermute | solution.py:541
  51.4 15.5 %collective-permute-start.9 = (bf16[512,128]{1,0:T(8,128)(2,1)S(1)}, bf16[512,128]{1,0:T(8,128)(2,1)S(1)}, u32[]{:S(2)}, u32[]{:S(2)}) collective-permute-start(bf16[512,128]{1,0:T(8,128)(2,1)S(1)} %get-tuple-element.149), channel_id=1, source_target_pairs={{0,16},{8,24},{16,0},{24,8},{1,17},{9,25},{17,1},{25,9},{2,18},{10... | collective-permute-start | bytes 393224 | tf_op jit(solution)/shard_map/ppermute | solution.py:541
  52.8 15.9 %collective-permute-start.1 = (bf16[512,128]{1,0:T(8,128)(2,1)S(1)}, bf16[512,128]{1,0:T(8,128)(2,1)S(1)}, u32[]{:S(2)}, u32[]{:S(2)}) collective-permute-start(bf16[512,128]{1,0:T(8,128)(2,1)S(1)} %get-tuple-element.132), channel_id=1, source_target_pairs={{0,16},{8,24},{16,0},{24,8},{1,17},{9,25},{17,1},{25,9},{2,18},{10... | collective-permute-start | bytes 393224 | tf_op jit(solution)/shard_map/ppermute | solution.py:541
  71.7 4.3 %collective-permute-start.19 = (f32[128,128]{1,0:T(8,128)S(1)}, f32[128,128]{1,0:T(8,128)S(1)}, u32[]{:S(2)}, u32[]{:S(2)}) collective-permute-start(f32[128,128]{1,0:T(8,128)S(1)} %get-tuple-element.175.total_ref), channel_id=1, source_target_pairs={{0,2},{1,3},{2,0},{3,1},{4,6},{5,7},{6,4},{7,5},{8,10},{9,11},{10,... | collective-permute-start | bytes 196616 | tf_op jit(solution)/shard_map/ppermute | solution.py:548
  72.9 9.2 %collective-permute-start.17 = (bf16[512,128]{1,0:T(8,128)(2,1)S(1)}, bf16[512,128]{1,0:T(8,128)(2,1)S(1)}, u32[]{:S(2)}, u32[]{:S(2)}) collective-permute-start(bf16[512,128]{1,0:T(8,128)(2,1)S(1)} %get-tuple-element.170), channel_id=1, source_target_pairs={{0,8},{8,0},{16,24},{24,16},{1,9},{9,1},{17,25},{25,17},{2,10},{10... | collective-permute-start | bytes 393224 | tf_op jit(solution)/shard_map/ppermute | solution.py:541
  72.9 9.2 %collective-permute-start.16 = (bf16[512,128]{1,0:T(8,128)(2,1)S(1)}, bf16[512,128]{1,0:T(8,128)(2,1)S(1)}, u32[]{:S(2)}, u32[]{:S(2)}) collective-permute-start(bf16[512,128]{1,0:T(8,128)(2,1)S(1)} %get-tuple-element.169), channel_id=1, source_target_pairs={{0,8},{8,0},{16,24},{24,16},{1,9},{9,1},{17,25},{25,17},{2,10},{10... | collective-permute-start | bytes 393224 | tf_op jit(solution)/shard_map/ppermute | solution.py:541
  76.6 4.3 %collective-permute-start.20 = (f32[128,128]{1,0:T(8,128)S(1)}, f32[128,128]{1,0:T(8,128)S(1)}, u32[]{:S(2)}, u32[]{:S(2)}) collective-permute-start(f32[128,128]{1,0:T(8,128)S(1)} %get-tuple-element.177.total_ref), channel_id=1, source_target_pairs={{0,4},{1,5},{2,6},{3,7},{4,0},{5,1},{6,2},{7,3},{8,12},{9,13},{10,... | collective-permute-start | bytes 196616 | tf_op jit(solution)/shard_map/ppermute | solution.py:548
  77.1 7.8 %collective-permute-start.15 = (bf16[512,128]{1,0:T(8,128)(2,1)S(1)}, bf16[512,128]{1,0:T(8,128)(2,1)S(1)}, u32[]{:S(2)}, u32[]{:S(2)}) collective-permute-start(bf16[512,128]{1,0:T(8,128)(2,1)S(1)} %get-tuple-element.168), channel_id=1, source_target_pairs={{0,8},{8,0},{16,24},{24,16},{1,9},{9,1},{17,25},{25,17},{2,10},{10... | collective-permute-start | bytes 393224 | tf_op jit(solution)/shard_map/ppermute | solution.py:541
  77.1 10.2 %collective-permute-start.14 = (bf16[512,128]{1,0:T(8,128)(2,1)S(1)}, bf16[512,128]{1,0:T(8,128)(2,1)S(1)}, u32[]{:S(2)}, u32[]{:S(2)}) collective-permute-start(bf16[512,128]{1,0:T(8,128)(2,1)S(1)} %get-tuple-element.167), channel_id=1, source_target_pairs={{0,8},{8,0},{16,24},{24,16},{1,9},{9,1},{17,25},{25,17},{2,10},{10... | collective-permute-start | bytes 393224 | tf_op jit(solution)/shard_map/ppermute | solution.py:541
  82.1 5.9 %collective-permute-start.21 = (f32[128,128]{1,0:T(8,128)S(1)}, f32[128,128]{1,0:T(8,128)S(1)}, u32[]{:S(2)}, u32[]{:S(2)}) collective-permute-start(f32[128,128]{1,0:T(8,128)S(1)} %get-tuple-element.179.refs_8_), channel_id=1, source_target_pairs={{0,8},{8,0},{16,24},{24,16},{1,9},{9,1},{17,25},{25,17},{2,10},{10... | collective-permute-start | bytes 196616 | tf_op jit(solution)/shard_map/ppermute | solution.py:541
  93.8 5.0 %collective-permute-start.23 = (bf16[512,128]{1,0:T(8,128)(2,1)S(1)}, bf16[512,128]{1,0:T(8,128)(2,1)S(1)}, u32[]{:S(2)}, u32[]{:S(2)}) collective-permute-start(bf16[512,128]{1,0:T(8,128)(2,1)S(1)} %core_pair_sum.4.refs_0_), channel_id=1, source_target_pairs={{0,2},{1,5},{2,0},{3,7},{4,6},{5,1},{6,4},{7,3},{8,10},{9,13},{10,... | collective-permute-start | bytes 393224 | tf_op jit(solution)/shard_map/ppermute | solution.py:612
  94.8 5.5 %collective-permute-start.26 = (bf16[512,128]{1,0:T(8,128)(2,1)S(1)}, bf16[512,128]{1,0:T(8,128)(2,1)S(1)}, u32[]{:S(2)}, u32[]{:S(2)}) collective-permute-start(bf16[512,128]{1,0:T(8,128)(2,1)S(1)} %core_pair_sum.5.refs_0_), channel_id=1, source_target_pairs={{0,2},{1,5},{2,0},{3,7},{4,6},{5,1},{6,4},{7,3},{8,10},{9,13},{10,... | collective-permute-start | bytes 393224 | tf_op jit(solution)/shard_map/ppermute | solution.py:612
  98.9 5.0 %collective-permute-start.24 = (bf16[512,128]{1,0:T(8,128)(2,1)S(1)}, bf16[512,128]{1,0:T(8,128)(2,1)S(1)}, u32[]{:S(2)}, u32[]{:S(2)}) collective-permute-start(bf16[512,128]{1,0:T(8,128)(2,1)S(1)} %chip_sum.4), channel_id=1, source_target_pairs={{0,4},{1,3},{2,6},{3,1},{4,0},{5,7},{6,2},{7,5},{8,12},{9,11},{10,... | collective-permute-start | bytes 393224 | tf_op jit(solution)/shard_map/ppermute | solution.py:612
  100.3 5.0 %collective-permute-start.27 = (bf16[512,128]{1,0:T(8,128)(2,1)S(1)}, bf16[512,128]{1,0:T(8,128)(2,1)S(1)}, u32[]{:S(2)}, u32[]{:S(2)}) collective-permute-start(bf16[512,128]{1,0:T(8,128)(2,1)S(1)} %chip_sum.5), channel_id=1, source_target_pairs={{0,4},{1,3},{2,6},{3,1},{4,0},{5,7},{6,2},{7,5},{8,12},{9,11},{10,... | collective-permute-start | bytes 393224 | tf_op jit(solution)/shard_map/ppermute | solution.py:612
  115.3 5.9 %collective-permute-start.33 = (f32[128,128]{1,0:T(8,128)S(1)}, f32[128,128]{1,0:T(8,128)S(1)}, u32[]{:S(2)}, u32[]{:S(2)}) collective-permute-start(f32[128,128]{1,0:T(8,128)S(1)} %totals.6.refs_0_), channel_id=1, source_target_pairs={{0,16},{8,24},{16,0},{24,8},{1,17},{9,25},{17,1},{25,9},{2,18},{10... | collective-permute-start | bytes 196616 | tf_op jit(solution)/shard_map/ppermute | solution.py:541
  116.2 7.8 %collective-permute-start.30 = (bf16[512,128]{1,0:T(8,128)(2,1)S(1)}, bf16[512,128]{1,0:T(8,128)(2,1)S(1)}, u32[]{:S(2)}, u32[]{:S(2)}) collective-permute-start(bf16[512,128]{1,0:T(8,128)(2,1)S(1)} %get-tuple-element.187), channel_id=1, source_target_pairs={{0,8},{8,0},{16,24},{24,16},{1,9},{9,1},{17,25},{25,17},{2,10},{10... | collective-permute-start | bytes 393224 | tf_op jit(solution)/shard_map/ppermute | solution.py:541
  118.0 8.2 %collective-permute-start.37 = (bf16[512,128]{1,0:T(8,128)(2,1)S(1)}, bf16[512,128]{1,0:T(8,128)(2,1)S(1)}, u32[]{:S(2)}, u32[]{:S(2)}) collective-permute-start(bf16[512,128]{1,0:T(8,128)(2,1)S(1)} %get-tuple-element.201), channel_id=1, source_target_pairs={{0,8},{8,0},{16,24},{24,16},{1,9},{9,1},{17,25},{25,17},{2,10},{10... | collective-permute-start | bytes 393224 | tf_op jit(solution)/shard_map/ppermute | solution.py:541
  118.2 13.7 %collective-permute-start.39 = (bf16[512,128]{1,0:T(8,128)(2,1)S(1)}, bf16[512,128]{1,0:T(8,128)(2,1)S(1)}, u32[]{:S(2)}, u32[]{:S(2)}) collective-permute-start(bf16[512,128]{1,0:T(8,128)(2,1)S(1)} %get-tuple-element.208), channel_id=1, source_target_pairs={{0,8},{8,0},{16,24},{24,16},{1,9},{9,1},{17,25},{25,17},{2,10},{10... | collective-permute-start | bytes 393224 | tf_op jit(solution)/shard_map/ppermute | solution.py:541
  120.0 13.8 %collective-permute-start.41 = (bf16[512,128]{1,0:T(8,128)(2,1)S(1)}, bf16[512,128]{1,0:T(8,128)(2,1)S(1)}, u32[]{:S(2)}, u32[]{:S(2)}) collective-permute-start(bf16[512,128]{1,0:T(8,128)(2,1)S(1)} %get-tuple-element.215), channel_id=1, source_target_pairs={{0,8},{8,0},{16,24},{24,16},{1,9},{9,1},{17,25},{25,17},{2,10},{10... | collective-permute-start | bytes 393224 | tf_op jit(solution)/shard_map/ppermute | solution.py:541
  123.1 12.0 %collective-permute-start.35 = (f32[128,128]{1,0:T(8,128)S(1)}, f32[128,128]{1,0:T(8,128)S(1)}, u32[]{:S(2)}, u32[]{:S(2)}) collective-permute-start(f32[128,128]{1,0:T(8,128)S(1)} %get-tuple-element.192.total_ref), channel_id=1, source_target_pairs={{0,2},{1,3},{2,0},{3,1},{4,6},{5,7},{6,4},{7,5},{8,10},{9,11},{10,... | collective-permute-start | bytes 196616 | tf_op jit(solution)/shard_map/ppermute | solution.py:548
  124.0 18.6 %collective-permute-start.31 = (bf16[512,128]{1,0:T(8,128)(2,1)S(1)}, bf16[512,128]{1,0:T(8,128)(2,1)S(1)}, u32[]{:S(2)}, u32[]{:S(2)}) collective-permute-start(bf16[512,128]{1,0:T(8,128)(2,1)S(1)} %get-tuple-element.189), channel_id=1, source_target_pairs={{0,16},{8,24},{16,0},{24,8},{1,17},{9,25},{17,1},{25,9},{2,18},{10... | collective-permute-start | bytes 393224 | tf_op jit(solution)/shard_map/ppermute | solution.py:541
  126.2 19.2 %collective-permute-start.38 = (bf16[512,128]{1,0:T(8,128)(2,1)S(1)}, bf16[512,128]{1,0:T(8,128)(2,1)S(1)}, u32[]{:S(2)}, u32[]{:S(2)}) collective-permute-start(bf16[512,128]{1,0:T(8,128)(2,1)S(1)} %get-tuple-element.203), channel_id=1, source_target_pairs={{0,16},{8,24},{16,0},{24,8},{1,17},{9,25},{17,1},{25,9},{2,18},{10... | collective-permute-start | bytes 393224 | tf_op jit(solution)/shard_map/ppermute | solution.py:541
  132.0 16.3 %collective-permute-start.40 = (bf16[512,128]{1,0:T(8,128)(2,1)S(1)}, bf16[512,128]{1,0:T(8,128)(2,1)S(1)}, u32[]{:S(2)}, u32[]{:S(2)}) collective-permute-start(bf16[512,128]{1,0:T(8,128)(2,1)S(1)} %get-tuple-element.210), channel_id=1, source_target_pairs={{0,16},{8,24},{16,0},{24,8},{1,17},{9,25},{17,1},{25,9},{2,18},{10... | collective-permute-start | bytes 393224 | tf_op jit(solution)/shard_map/ppermute | solution.py:541
  133.8 16.2 %collective-permute-start.42 = (bf16[512,128]{1,0:T(8,128)(2,1)S(1)}, bf16[512,128]{1,0:T(8,128)(2,1)S(1)}, u32[]{:S(2)}, u32[]{:S(2)}) collective-permute-start(bf16[512,128]{1,0:T(8,128)(2,1)S(1)} %get-tuple-element.217), channel_id=1, source_target_pairs={{0,16},{8,24},{16,0},{24,8},{1,17},{9,25},{17,1},{25,9},{2,18},{10... | collective-permute-start | bytes 393224 | tf_op jit(solution)/shard_map/ppermute | solution.py:541
  135.6 4.3 %collective-permute-start.36 = (f32[128,128]{1,0:T(8,128)S(1)}, f32[128,128]{1,0:T(8,128)S(1)}, u32[]{:S(2)}, u32[]{:S(2)}) collective-permute-start(f32[128,128]{1,0:T(8,128)S(1)} %get-tuple-element.194.total_ref), channel_id=1, source_target_pairs={{0,4},{1,5},{2,6},{3,7},{4,0},{5,1},{6,2},{7,3},{8,12},{9,13},{10,... | collective-permute-start | bytes 196616 | tf_op jit(solution)/shard_map/ppermute | solution.py:548
  153.7 4.3 %collective-permute-start.55 = (f32[128,128]{1,0:T(8,128)S(1)}, f32[128,128]{1,0:T(8,128)S(1)}, u32[]{:S(2)}, u32[]{:S(2)}) collective-permute-start(f32[128,128]{1,0:T(8,128)S(1)} %get-tuple-element.241.total_ref), channel_id=1, source_target_pairs={{0,2},{1,3},{2,0},{3,1},{4,6},{5,7},{6,4},{7,5},{8,10},{9,11},{10,... | collective-permute-start | bytes 196616 | tf_op jit(solution)/shard_map/ppermute | solution.py:548
  154.9 9.2 %collective-permute-start.50 = (bf16[512,128]{1,0:T(8,128)(2,1)S(1)}, bf16[512,128]{1,0:T(8,128)(2,1)S(1)}, u32[]{:S(2)}, u32[]{:S(2)}) collective-permute-start(bf16[512,128]{1,0:T(8,128)(2,1)S(1)} %get-tuple-element.233), channel_id=1, source_target_pairs={{0,8},{8,0},{16,24},{24,16},{1,9},{9,1},{17,25},{25,17},{2,10},{10... | collective-permute-start | bytes 393224 | tf_op jit(solution)/shard_map/ppermute | solution.py:541
  154.9 9.2 %collective-permute-start.51 = (bf16[512,128]{1,0:T(8,128)(2,1)S(1)}, bf16[512,128]{1,0:T(8,128)(2,1)S(1)}, u32[]{:S(2)}, u32[]{:S(2)}) collective-permute-start(bf16[512,128]{1,0:T(8,128)(2,1)S(1)} %get-tuple-element.234), channel_id=1, source_target_pairs={{0,8},{8,0},{16,24},{24,16},{1,9},{9,1},{17,25},{25,17},{2,10},{10... | collective-permute-start | bytes 393224 | tf_op jit(solution)/shard_map/ppermute | solution.py:541
  159.4 7.6 %collective-permute-start.52 = (bf16[512,128]{1,0:T(8,128)(2,1)S(1)}, bf16[512,128]{1,0:T(8,128)(2,1)S(1)}, u32[]{:S(2)}, u32[]{:S(2)}) collective-permute-start(bf16[512,128]{1,0:T(8,128)(2,1)S(1)} %get-tuple-element.235), channel_id=1, source_target_pairs={{0,8},{8,0},{16,24},{24,16},{1,9},{9,1},{17,25},{25,17},{2,10},{10... | collective-permute-start | bytes 393224 | tf_op jit(solution)/shard_map/ppermute | solution.py:541
  159.4 10.0 %collective-permute-start.53 = (bf16[512,128]{1,0:T(8,128)(2,1)S(1)}, bf16[512,128]{1,0:T(8,128)(2,1)S(1)}, u32[]{:S(2)}, u32[]{:S(2)}) collective-permute-start(bf16[512,128]{1,0:T(8,128)(2,1)S(1)} %get-tuple-element.236), channel_id=1, source_target_pairs={{0,8},{8,0},{16,24},{24,16},{1,9},{9,1},{17,25},{25,17},{2,10},{10... | collective-permute-start | bytes 393224 | tf_op jit(solution)/shard_map/ppermute | solution.py:541
  164.1 5.9 %collective-permute-start.57 = (f32[128,128]{1,0:T(8,128)S(1)}, f32[128,128]{1,0:T(8,128)S(1)}, u32[]{:S(2)}, u32[]{:S(2)}) collective-permute-start(f32[128,128]{1,0:T(8,128)S(1)} %get-tuple-element.245.refs_8_), channel_id=1, source_target_pairs={{0,8},{8,0},{16,24},{24,16},{1,9},{9,1},{17,25},{25,17},{2,10},{10... | collective-permute-start | bytes 196616 | tf_op jit(solution)/shard_map/ppermute | solution.py:541
  175.8 5.0 %collective-permute-start.59 = (bf16[512,128]{1,0:T(8,128)(2,1)S(1)}, bf16[512,128]{1,0:T(8,128)(2,1)S(1)}, u32[]{:S(2)}, u32[]{:S(2)}) collective-permute-start(bf16[512,128]{1,0:T(8,128)(2,1)S(1)} %core_pair_sum.6.refs_0_), channel_id=1, source_target_pairs={{0,2},{1,5},{2,0},{3,7},{4,6},{5,1},{6,4},{7,3},{8,10},{9,13},{10,... | collective-permute-start | bytes 393224 | tf_op jit(solution)/shard_map/ppermute | solution.py:612
  176.8 5.5 %collective-permute-start.62 = (bf16[512,128]{1,0:T(8,128)(2,1)S(1)}, bf16[512,128]{1,0:T(8,128)(2,1)S(1)}, u32[]{:S(2)}, u32[]{:S(2)}) collective-permute-start(bf16[512,128]{1,0:T(8,128)(2,1)S(1)} %core_pair_sum.7.refs_0_), channel_id=1, source_target_pairs={{0,2},{1,5},{2,0},{3,7},{4,6},{5,1},{6,4},{7,3},{8,10},{9,13},{10,... | collective-permute-start | bytes 393224 | tf_op jit(solution)/shard_map/ppermute | solution.py:612
  180.9 5.0 %collective-permute-start.60 = (bf16[512,128]{1,0:T(8,128)(2,1)S(1)}, bf16[512,128]{1,0:T(8,128)(2,1)S(1)}, u32[]{:S(2)}, u32[]{:S(2)}) collective-permute-start(bf16[512,128]{1,0:T(8,128)(2,1)S(1)} %chip_sum.6), channel_id=1, source_target_pairs={{0,4},{1,3},{2,6},{3,1},{4,0},{5,7},{6,2},{7,5},{8,12},{9,11},{10,... | collective-permute-start | bytes 393224 | tf_op jit(solution)/shard_map/ppermute | solution.py:612
  182.3 5.0 %collective-permute-start.63 = (bf16[512,128]{1,0:T(8,128)(2,1)S(1)}, bf16[512,128]{1,0:T(8,128)(2,1)S(1)}, u32[]{:S(2)}, u32[]{:S(2)}) collective-permute-start(bf16[512,128]{1,0:T(8,128)(2,1)S(1)} %chip_sum.7), channel_id=1, source_target_pairs={{0,4},{1,3},{2,6},{3,1},{4,0},{5,7},{6,2},{7,5},{8,12},{9,11},{10,... | collective-permute-start | bytes 393224 | tf_op jit(solution)/shard_map/ppermute | solution.py:612
  186.6 15.0 %collective-permute-start.64 = (f32[2,32,8,128]{3,2,1,0:T(8,128)S(1)}, f32[2,32,8,128]{3,2,1,0:T(8,128)S(1)}, u32[]{:S(2)}, u32[]{:S(2)}) collective-permute-start(f32[2,32,8,128]{3,2,1,0:T(8,128)S(1)} %dual_update.6.refs_0_), channel_id=1, source_target_pairs={{0,1},{1,0},{2,3},{3,2},{4,5},{5,4},{6,7},{7,6},{8,9},{9,8},{10,11... | collective-permute-start | bytes 786440 | tf_op jit(solution)/shard_map/ppermute | solution.py:607
  188.0 13.6 %collective-permute-start.65 = (f32[2,32,8,128]{3,2,1,0:T(8,128)S(1)}, f32[2,32,8,128]{3,2,1,0:T(8,128)S(1)}, u32[]{:S(2)}, u32[]{:S(2)}) collective-permute-start(f32[2,32,8,128]{3,2,1,0:T(8,128)S(1)} %dual_update.7.refs_1_), channel_id=1, source_target_pairs={{0,1},{1,0},{2,3},{3,2},{4,5},{5,4},{6,7},{7,6},{8,9},{9,8},{10,11... | collective-permute-start | bytes 786440 | tf_op jit(solution)/shard_map/ppermute | solution.py:607
  190.8 4.4 %collective-permute-start.46 = (bf16[128,128]{1,0:T(8,128)(2,1)S(1)}, bf16[128,128]{1,0:T(8,128)(2,1)S(1)}, u32[]{:S(2)}, u32[]{:S(2)}) collective-permute-start(bf16[128,128]{1,0:T(8,128)(2,1)S(1)} %get-tuple-element.225), channel_id=1, source_target_pairs={{0,4},{1,5},{2,6},{3,7},{4,0},{5,1},{6,2},{7,3},{8,12},{9,13},{10,... | collective-permute-start | bytes 98312 | tf_op jit(solution)/shard_map/ppermute | solution.py:594
  193.9 4.8 %collective-permute-start.48 = (bf16[128,128]{1,0:T(8,128)(2,1)S(1)}, bf16[128,128]{1,0:T(8,128)(2,1)S(1)}, u32[]{:S(2)}, u32[]{:S(2)}) collective-permute-start(bf16[128,128]{1,0:T(8,128)(2,1)S(1)} %get-tuple-element.227), channel_id=1, source_target_pairs={{0,6},{1,7},{2,4},{3,5},{4,2},{5,3},{6,0},{7,1},{8,14},{9,15},{10,... | collective-permute-start | bytes 98312 | tf_op jit(solution)/shard_map/ppermute | solution.py:594
  (26 other events, 292.9 us)

commit v9 on v7

--- a/solution.py
+++ b/solution.py
@@ -124,6 +124,10 @@
     return (core * PARTS + part) * rows
 
 
+def part_rows_of(ref, core, part, size):
+    return ref[pl.ds(pl.multiple_of(row_part(core, part, size), size), size), :]
+
+
 def backward_kernel(dims, pitch, core_ref, rows_ref, cols_ref, tiles_ref, *refs):
     pieces, (out_ref, duals_ref, acc_ref) = refs[: 2 * PARTS], refs[2 * PARTS :]
     for i, piece in enumerate(pieces):
@@ -131,7 +135,9 @@
         scen, side = duals_ref.shape[1:]
         rows = piece.shape[0] // scen
         duals_ref[pl.ds(row_part(core, i % PARTS, rows), rows)] = piece[...].reshape(rows, scen, side)
-    acc_ref[...] = jnp.zeros_like(acc_ref)
+    scen = duals_ref.shape[1]
+    for row in range(0, acc_ref.shape[0], pitch):
+        acc_ref[pl.ds(row, scen), :] = jnp.zeros((scen, acc_ref.shape[1]), jnp.float32)
 
     width = min(UNROLL, tiles_ref.shape[0])
 
@@ -147,7 +153,7 @@
     n_row, n_col, scen_local, time_block, _, own_tiles = dims
     scen = n_row * scen_local
     piece = own_tiles * time_block
-    outs, (flat_ref, acc_ref) = refs[: 2 * PARTS], refs[2 * PARTS :]
+    (acc_ref, *outs), flat_ref = refs[:-1], refs[-1]
     acc_ref[...] = jnp.zeros_like(acc_ref)
     for group in range(n_row):
         for column in range(n_col):
@@ -185,10 +191,8 @@
         return 0
 
     lax.fori_loop(0, tiles_ref.shape[0] // width, body, 0)
-    for i, out_ref in enumerate(outs):
-        core = core_ref[0] if i < PARTS else 1 - core_ref[0]
-        size = out_ref.shape[0]
-        out_ref[...] = acc_ref[pl.ds(pl.multiple_of(row_part(core, i % PARTS, size), size), size), :]
+    for part, out_ref in enumerate(outs):
+        out_ref[...] = part_rows_of(acc_ref, 1 - core_ref[0], part, out_ref.shape[0]).astype(jnp.bfloat16)
 
 
 def running(values, trailing, terms):
@@ -251,13 +255,22 @@
                 send_ref[g * n_col + h, pl.ds(j * piece, piece), :] = block
 
 
+def own_sum(part, core_ref, image_ref, other_ref):
+    own = part_rows_of(image_ref, core_ref[0], part, other_ref.shape[0])
+    return own + other_ref[...].astype(jnp.float32)
+
+
+def pair_kernel(part, core_ref, image_ref, other_ref, out_ref):
+    out_ref[...] = own_sum(part, core_ref, image_ref, other_ref).astype(jnp.bfloat16)
+
+
 def sum_kernel(first_ref, second_ref, out_ref):
     out_ref[...] = (first_ref[...].astype(jnp.float32) + second_ref[...].astype(jnp.float32)).astype(jnp.bfloat16)
 
 
-def dual_kernel(remote, part, first, last, core_ref, own_ref, other_ref, *refs):
+def dual_kernel(remote, part, first, last, core_ref, image_ref, other_ref, *refs):
     parts, (dual_ref, cap_ref, dual_out) = refs[:remote], refs[remote : remote + 3]
-    total = own_ref[...] + other_ref[...]
+    total = own_sum(part, core_ref, image_ref, other_ref)
     for received in parts:
         total = total + received[...].astype(jnp.float32)
     bands, row_tiles, band, side = cap_ref.shape
@@ -380,9 +393,9 @@
         return pl.pallas_call(
             functools.partial(forward_kernel, dims, pitch),
             in_specs=[scalars()] * 3 + [whole()] * 2,
-            out_specs=[whole()] * (2 * PARTS),
-            out_shape=[part_f32] * (2 * PARTS),
-            scratch_shapes=[acc_cols, pltpu.VMEM((row_tiles * scen, side), jnp.float32)],
+            out_specs=[whole()] * (1 + PARTS),
+            out_shape=[jax.ShapeDtypeStruct((row_tiles * scen, side), jnp.float32)] + [part_bf16] * PARTS,
+            scratch_shapes=[acc_cols],
             compiler_params=params(),
             cost_estimate=cost,
             name="forward_products",
@@ -420,9 +433,16 @@
             name=name,
         )(first, second)
 
-    def dual_step(part, own, away, dual, first, last):
+    def dual_step(part, image, away, dual, first, last):
         other = swap_core(away)
-        partial = bf16_sum(own, other, "core_pair_sum")
+        partial = pl.pallas_call(
+            functools.partial(pair_kernel, part),
+            in_specs=[scalars()] + [whole()] * 2,
+            out_specs=whole(),
+            out_shape=part_bf16,
+            compiler_params=params(),
+            name="core_pair_sum",
+        )(core, image, other)
         parts = []
         for step in range(bits):
             parts.append(swap_chip(partial, step))
@@ -436,7 +456,7 @@
             out_shape=out_shape,
             compiler_params=params(),
             name="dual_update",
-        )(core, own, other, *parts, dual, banded(capacity))
+        )(core, image, other, *parts, dual, banded(capacity))
 
     def results(primal, owned):
         duals_shape = jax.ShapeDtypeStruct((scen // band, row_tiles, band, side), jnp.float32)
@@ -473,9 +493,9 @@
         primal, send, *cumulative = primal_step(recv, primal, cumulative, last)
         cumulative = None if last else cumulative[0]
         probe = lax.all_to_all(send, ("row", "col"), 0, 0, tiled=True)
-        images = forward(probe, tiles)
+        image, *aways = forward(probe, tiles)
         updates = [
-            dual_step(part, images[part], images[PARTS + part], duals[part], sweep == 0, last)
+            dual_step(part, image, aways[part], duals[part], sweep == 0, last)
             for part in range(PARTS)
         ]
         duals = [update[0] for update in updates]

time: 171 us -> 171 us (level)
  no operation moved by 1% of the time
where the time goes in v9:
time: 171 us; the launch traced here: 170 us
  blocking collectives  122 us (71%)
  Pallas kernels  19.6 us (11%)
  waiting for transfers between devices  15.7 us (9%)
  starting transfers between devices  11.9 us (7%)
    all_to_all x2, blocking collectives, per_device(): recv = lax.all_to_all(send, ('row', 'col'), 0, 0, tiled=True)  62.8 us
    all_to_all x2, blocking collectives, per_device(): probe = lax.all_to_all(send, ('row', 'col'), 0, 0, tiled=True)  59.3 us
    ppermute x8, waiting for transfers between devices, swap_chip(): lax.ppermute(value, 'col', [(i, i ^ 2 << (step + i % 2) % bits) for i in...  12.2 us
    ppermute x8, starting transfers between devices, swap_chip(): lax.ppermute(value, 'col', [(i, i ^ 2 << (step + i % 2) % bits) for i in...  10.5 us
    pallas_call x2, Pallas kernels, forward(): pl.pallas_call(functools.partial(forward_kernel, dims, pitch), in_specs=[...  7.75 us
    pallas_call x1, Pallas kernels, first_backward(): pl.pallas_call(functools.partial(first_backward_kernel, dims, pitch), in_...  4.52 us
    ppermute x8, waiting for transfers between devices, swap_core(): return lax.ppermute(value, 'col', [(i, i ^ 1) for i in range(n_col)])  3.5 us
  transfers between devices with their start and end apart: 16, of which 10 were waited for; matrix products, arithmetic and copies ran while one was open for 0% of the time, Pallas kernels for 1%

profile of v9, /device:TPU:0, one launch (start us, length us, event | category | flops | bytes accessed | tf_op | source)
XLA Modules:
  0.0 170.4 jit_solution(5515499094928290286)
XLA Ops:
  0.7 4.5 %first_backward_products.1 = (bf16[32,128,128]{2,1,0:T(8,128)(2,1)S(1)}, bf16[256,128,128]{2,1,0:T(8,128)(2,1)S(1)}) custom-call(s32[1]{0:T(128)} %bitcast.core_ref, s32[256]{0:T(256)} %bitcast.22, s32[256]{0:T(256)} %bitcast.26, f32[2,128,8,128]{3,2,1,0:T(8,128)} %bitcast.19, bf16[256,128,128]{2,1,0:T(8,128)(2,1)} %bitcast.34), custom_call_target="tpu_custom_call" | custom-call | flops 134217728 | bytes 4194304 | tf_op jit(solution)/shard_map/first_backward_products/pallas_call | solution.py:358
  5.2 33.3 %all_to_all.20.refs_0_ = bf16[32,128,128]{2,1,0:T(8,128)(2,1)S(1)} all-to-all(bf16[32,128,128]{2,1,0:T(8,128)(2,1)S(1)} %get-tuple-element.22), channel_id=1, replica_groups=mesh['row'=4,'col'=8] {'row','col'}, dimensions={0} | all-to-all | bytes 2097152 | tf_op jit(solution)/shard_map/all_to_all | solution.py:492
  38.6 0.9 primal_update.2
  39.6 29.7 %all_to_all.21.probe_ref = bf16[32,128,128]{2,1,0:T(8,128)(2,1)S(1)} all-to-all(bf16[32,128,128]{2,1,0:T(8,128)(2,1)S(1)} %get-tuple-element.23), channel_id=1, replica_groups=mesh['row'=4,'col'=8] {'row','col'}, dimensions={0} | all-to-all | bytes 2097152 | tf_op jit(solution)/shard_map/all_to_all | solution.py:495
  69.2 3.9 %forward_products.2 = (f32[2048,128]{1,0:T(8,128)S(1)}, bf16[512,128]{1,0:T(8,128)(2,1)S(1)}, bf16[512,128]{1,0:T(8,128)(2,1)S(1)}) custom-call(s32[1]{0:T(128)} %bitcast.core_ref, s32[256]{0:T(256)S(1)} %bitcast.23, s32[256]{0:T(256)S(1)} %bitcast.27, bf16[32,128,128]{2,1,0:T(8,128)(2,1)S(1)} %all_to_all.21.probe_ref, ...), custom_call_target="tpu_custom_call" | custom-call | flops 134217728 | bytes 4194304 | tf_op jit(solution)/shard_map/forward_products/pallas_call | solution.py:393
  73.1 0.1 collective-permute-start
  73.2 0.5 collective-permute-start.3
  73.7 0.8 collective-permute-done.other_ref
  74.6 1.5 collective-permute-start.1
  76.1 0.0 collective-permute-done.3.other_ref
  76.1 0.6 collective-permute-start.4
  76.8 2.8 %collective-permute-done.1.second_ref.refs_0_ = bf16[512,128]{1,0:T(8,128)(2,1)S(1)} collective-permute-done((bf16[512,128]{1,0:T(8,128)(2,1)S(1)}, bf16[512,128]{1,0:T(8,128)(2,1)S(1)}, u32[]{:S(2)}, u32[]{:S(2)}) %collective-permute-start.1) | collective-permute-done | bytes 131104 | tf_op jit(solution)/shard_map/ppermute | solution.py:424
  79.6 1.6 collective-permute-start.2
  81.2 0.0 collective-permute-done.4.second_ref.refs_0_
  81.2 1.5 collective-permute-start.5
  82.8 1.9 %collective-permute-done.2.refs_1_ = bf16[512,128]{1,0:T(8,128)(2,1)S(1)} collective-permute-done((bf16[512,128]{1,0:T(8,128)(2,1)S(1)}, bf16[512,128]{1,0:T(8,128)(2,1)S(1)}, u32[]{:S(2)}, u32[]{:S(2)}) %collective-permute-start.2) | collective-permute-done | bytes 131104 | tf_op jit(solution)/shard_map/ppermute | solution.py:424
  84.7 0.1 dual_update.4
  84.8 0.1 collective-permute-start.6
  84.9 1.4 collective-permute-done.5.refs_1_
  86.3 0.1 dual_update.5
  86.4 0.1 collective-permute-start.7
  86.5 0.0 collective-permute-done.6.refs_2_
  86.5 1.3 collective-permute-done.7.refs_3_
  87.8 3.0 %backward_products.1 = bf16[32,128,128]{2,1,0:T(8,128)(2,1)S(1)} custom-call(s32[1]{0:T(128)} %bitcast.core_ref, s32[256]{0:T(256)S(1)} %bitcast.24, s32[256]{0:T(256)S(1)} %bitcast.28, bf16[256,128,128]{2,1,0:T(8,128)(2,1)S(1)} %get-tuple-element.21.tiles_ref, bf16[512,128]{1,0:T(8,128)(2,1)S(1)} %get-tuple-element.26.refs_0_, ...), custom_call_target="tpu_custom_call" | custom-call | flops 134217728 | bytes 4194304 | tf_op jit(solution)/shard_map/backward_products/pallas_call | solution.py:381
  90.8 29.5 %all_to_all.22.refs_0_ = bf16[32,128,128]{2,1,0:T(8,128)(2,1)S(1)} all-to-all(bf16[32,128,128]{2,1,0:T(8,128)(2,1)S(1)} %backward_products.1), channel_id=1, replica_groups=mesh['row'=4,'col'=8] {'row','col'}, dimensions={0} | all-to-all | bytes 2097152 | tf_op jit(solution)/shard_map/all_to_all | solution.py:492
  120.2 0.8 primal_update.3
  121.0 29.7 %all_to_all.23.probe_ref = bf16[32,128,128]{2,1,0:T(8,128)(2,1)S(1)} all-to-all(bf16[32,128,128]{2,1,0:T(8,128)(2,1)S(1)} %get-tuple-element.32), channel_id=1, replica_groups=mesh['row'=4,'col'=8] {'row','col'}, dimensions={0} | all-to-all | bytes 2097152 | tf_op jit(solution)/shard_map/all_to_all | solution.py:495
  150.7 3.9 %forward_products.3 = (f32[2048,128]{1,0:T(8,128)S(1)}, bf16[512,128]{1,0:T(8,128)(2,1)S(1)}, bf16[512,128]{1,0:T(8,128)(2,1)S(1)}) custom-call(s32[1]{0:T(128)} %bitcast.core_ref, s32[256]{0:T(256)S(1)} %bitcast.25, s32[256]{0:T(256)S(1)} %bitcast.29, bf16[32,128,128]{2,1,0:T(8,128)(2,1)S(1)} %all_to_all.23.probe_ref, ...), custom_call_target="tpu_custom_call" | custom-call | flops 134217728 | bytes 4194304 | tf_op jit(solution)/shard_map/forward_products/pallas_call | solution.py:393
  154.6 0.1 collective-permute-start.11
  154.7 0.5 collective-permute-start.8
  155.2 0.8 collective-permute-done.11.other_ref
  156.0 1.5 collective-permute-start.12
  157.6 0.0 collective-permute-done.8.other_ref
  157.6 0.6 collective-permute-start.9
  158.2 2.8 %collective-permute-done.12.second_ref.refs_0_ = bf16[512,128]{1,0:T(8,128)(2,1)S(1)} collective-permute-done((bf16[512,128]{1,0:T(8,128)(2,1)S(1)}, bf16[512,128]{1,0:T(8,128)(2,1)S(1)}, u32[]{:S(2)}, u32[]{:S(2)}) %collective-permute-start.12) | collective-permute-done | bytes 131104 | tf_op jit(solution)/shard_map/ppermute | solution.py:424
  161.1 1.6 collective-permute-start.13
  162.7 0.0 collective-permute-done.9.second_ref.refs_0_
  162.7 1.5 collective-permute-start.10
  164.2 1.9 %collective-permute-done.13.refs_1_ = bf16[512,128]{1,0:T(8,128)(2,1)S(1)} collective-permute-done((bf16[512,128]{1,0:T(8,128)(2,1)S(1)}, bf16[512,128]{1,0:T(8,128)(2,1)S(1)}, u32[]{:S(2)}, u32[]{:S(2)}) %collective-permute-start.13) | collective-permute-done | bytes 131104 | tf_op jit(solution)/shard_map/ppermute | solution.py:424
  166.1 0.1 dual_update.7.refs_1_
  166.3 0.1 collective-permute-start.15
  166.4 1.4 collective-permute-done.10.refs_1_
  167.7 0.1 dual_update.6.refs_0_
  167.9 0.1 collective-permute-start.14
  167.9 1.0 own_results.1
  169.0 0.0 collective-permute-done.15.refs_1_
  169.0 0.5 collective-permute-done.14.refs_0_
  169.5 0.8 other_results.1
  (24 shorter events, 0.3 us)
Async XLA Ops:
  0.6 68.6 %copy-start.5 = (s32[1,1,256]{2,1,0:T(1,128)S(1)}, s32[1,1,256]{2,1,0:T(1,128)}, u32[]{:S(2)}) copy-start(s32[1,1,256]{2,1,0:T(1,128)} %param.11) | copy-start | bytes 3076
  0.6 68.6 %copy-start.4 = (s32[1,1,256]{2,1,0:T(1,128)S(1)}, s32[1,1,256]{2,1,0:T(1,128)}, u32[]{:S(2)}) copy-start(s32[1,1,256]{2,1,0:T(1,128)} %param.10) | copy-start | bytes 3076
  0.7 37.9 %copy-start.3 = (f32[128,256]{1,0:T(8,128)S(1)}, f32[128,256]{1,0:T(8,128)}, u32[]{:S(2)}) copy-start(f32[128,256]{1,0:T(8,128)} %refs_3_.1) | copy-start | bytes 393220
  0.7 37.9 %copy-start.7 = (s32[256]{0:T(256)S(1)}, s32[256]{0:T(256)}, u32[]{:S(2)}) copy-start(s32[256]{0:T(256)} %param.16) | copy-start | bytes 3076
  0.7 37.9 %copy-start.6 = (s32[256]{0:T(256)S(1)}, s32[256]{0:T(256)}, u32[]{:S(2)}) copy-start(s32[256]{0:T(256)} %param.15) | copy-start | bytes 3076
  0.7 37.9 %copy-start.2 = (f32[4,128,256]{2,1,0:T(8,128)S(1)}, f32[4,128,256]{2,1,0:T(8,128)}, u32[]{:S(2)}) copy-start(f32[4,128,256]{2,1,0:T(8,128)} %refs_1_.1) | copy-start | bytes 1572868
  38.6 46.1 %copy-start = (s32[16,16384]{1,0:T(8,128)S(1)}, s32[16,16384]{1,0:T(8,128)}, u32[]{:S(2)}) copy-start(s32[16,16384]{1,0:T(8,128)} %param.17) | copy-start | bytes 3145732
  38.6 46.1 %copy-start.1 = (f32[16,16384]{1,0:T(8,128)S(1)}, f32[16,16384]{1,0:T(8,128)}, u32[]{:S(2)}) copy-start(f32[16,16384]{1,0:T(8,128)} %param.13) | copy-start | bytes 3145732
  73.1 1.4 collective-permute-start
  73.2 2.9 %collective-permute-start.3 = (bf16[512,128]{1,0:T(8,128)(2,1)S(1)}, bf16[512,128]{1,0:T(8,128)(2,1)S(1)}, u32[]{:S(2)}, u32[]{:S(2)}) collective-permute-start(bf16[512,128]{1,0:T(8,128)(2,1)S(1)} %get-tuple-element.27), channel_id=1, source_target_pairs={{0,1},{1,0},{2,3},{3,2},{4,5},{5,4},{6,7},{7,6},{8,9},{9,8},{10,11... | collective-permute-start | bytes 393224 | tf_op jit(solution)/shard_map/ppermute | solution.py:419
  74.6 5.0 %collective-permute-start.1 = (bf16[512,128]{1,0:T(8,128)(2,1)S(1)}, bf16[512,128]{1,0:T(8,128)(2,1)S(1)}, u32[]{:S(2)}, u32[]{:S(2)}) collective-permute-start(bf16[512,128]{1,0:T(8,128)(2,1)S(1)} %core_pair_sum.4.first_ref), channel_id=1, source_target_pairs={{0,2},{1,5},{2,0},{3,7},{4,6},{5,1},{6,4},{7,3},{8,10},{9,13},{10,... | collective-permute-start | bytes 393224 | tf_op jit(solution)/shard_map/ppermute | solution.py:424
  76.1 5.1 %collective-permute-start.4 = (bf16[512,128]{1,0:T(8,128)(2,1)S(1)}, bf16[512,128]{1,0:T(8,128)(2,1)S(1)}, u32[]{:S(2)}, u32[]{:S(2)}) collective-permute-start(bf16[512,128]{1,0:T(8,128)(2,1)S(1)} %core_pair_sum.5.first_ref), channel_id=1, source_target_pairs={{0,2},{1,5},{2,0},{3,7},{4,6},{5,1},{6,4},{7,3},{8,10},{9,13},{10,... | collective-permute-start | bytes 393224 | tf_op jit(solution)/shard_map/ppermute | solution.py:424
  79.6 5.0 %collective-permute-start.2 = (bf16[512,128]{1,0:T(8,128)(2,1)S(1)}, bf16[512,128]{1,0:T(8,128)(2,1)S(1)}, u32[]{:S(2)}, u32[]{:S(2)}) collective-permute-start(bf16[512,128]{1,0:T(8,128)(2,1)S(1)} %chip_sum.4), channel_id=1, source_target_pairs={{0,4},{1,3},{2,6},{3,1},{4,0},{5,7},{6,2},{7,5},{8,12},{9,11},{10,... | collective-permute-start | bytes 393224 | tf_op jit(solution)/shard_map/ppermute | solution.py:424
  81.2 5.0 %collective-permute-start.5 = (bf16[512,128]{1,0:T(8,128)(2,1)S(1)}, bf16[512,128]{1,0:T(8,128)(2,1)S(1)}, u32[]{:S(2)}, u32[]{:S(2)}) collective-permute-start(bf16[512,128]{1,0:T(8,128)(2,1)S(1)} %chip_sum.5), channel_id=1, source_target_pairs={{0,4},{1,3},{2,6},{3,1},{4,0},{5,7},{6,2},{7,5},{8,12},{9,11},{10,... | collective-permute-start | bytes 393224 | tf_op jit(solution)/shard_map/ppermute | solution.py:424
  84.8 1.7 collective-permute-start.6
  86.4 1.4 collective-permute-start.7
  154.6 1.4 collective-permute-start.11
  154.7 2.9 %collective-permute-start.8 = (bf16[512,128]{1,0:T(8,128)(2,1)S(1)}, bf16[512,128]{1,0:T(8,128)(2,1)S(1)}, u32[]{:S(2)}, u32[]{:S(2)}) collective-permute-start(bf16[512,128]{1,0:T(8,128)(2,1)S(1)} %get-tuple-element.34), channel_id=1, source_target_pairs={{0,1},{1,0},{2,3},{3,2},{4,5},{5,4},{6,7},{7,6},{8,9},{9,8},{10,11... | collective-permute-start | bytes 393224 | tf_op jit(solution)/shard_map/ppermute | solution.py:419
  156.0 5.0 %collective-permute-start.12 = (bf16[512,128]{1,0:T(8,128)(2,1)S(1)}, bf16[512,128]{1,0:T(8,128)(2,1)S(1)}, u32[]{:S(2)}, u32[]{:S(2)}) collective-permute-start(bf16[512,128]{1,0:T(8,128)(2,1)S(1)} %core_pair_sum.7.first_ref), channel_id=1, source_target_pairs={{0,2},{1,5},{2,0},{3,7},{4,6},{5,1},{6,4},{7,3},{8,10},{9,13},{10,... | collective-permute-start | bytes 393224 | tf_op jit(solution)/shard_map/ppermute | solution.py:424
  157.6 5.1 %collective-permute-start.9 = (bf16[512,128]{1,0:T(8,128)(2,1)S(1)}, bf16[512,128]{1,0:T(8,128)(2,1)S(1)}, u32[]{:S(2)}, u32[]{:S(2)}) collective-permute-start(bf16[512,128]{1,0:T(8,128)(2,1)S(1)} %core_pair_sum.6.first_ref), channel_id=1, source_target_pairs={{0,2},{1,5},{2,0},{3,7},{4,6},{5,1},{6,4},{7,3},{8,10},{9,13},{10,... | collective-permute-start | bytes 393224 | tf_op jit(solution)/shard_map/ppermute | solution.py:424
  161.1 5.0 %collective-permute-start.13 = (bf16[512,128]{1,0:T(8,128)(2,1)S(1)}, bf16[512,128]{1,0:T(8,128)(2,1)S(1)}, u32[]{:S(2)}, u32[]{:S(2)}) collective-permute-start(bf16[512,128]{1,0:T(8,128)(2,1)S(1)} %chip_sum.7), channel_id=1, source_target_pairs={{0,4},{1,3},{2,6},{3,1},{4,0},{5,7},{6,2},{7,5},{8,12},{9,11},{10,... | collective-permute-start | bytes 393224 | tf_op jit(solution)/shard_map/ppermute | solution.py:424
  162.7 5.0 %collective-permute-start.10 = (bf16[512,128]{1,0:T(8,128)(2,1)S(1)}, bf16[512,128]{1,0:T(8,128)(2,1)S(1)}, u32[]{:S(2)}, u32[]{:S(2)}) collective-permute-start(bf16[512,128]{1,0:T(8,128)(2,1)S(1)} %chip_sum.6), channel_id=1, source_target_pairs={{0,4},{1,3},{2,6},{3,1},{4,0},{5,7},{6,2},{7,5},{8,12},{9,11},{10,... | collective-permute-start | bytes 393224 | tf_op jit(solution)/shard_map/ppermute | solution.py:424
  166.3 2.7 %collective-permute-start.15 = (f32[2,32,8,128]{3,2,1,0:T(8,128)S(1)}, f32[2,32,8,128]{3,2,1,0:T(8,128)S(1)}, u32[]{:S(2)}, u32[]{:S(2)}) collective-permute-start(f32[2,32,8,128]{3,2,1,0:T(8,128)S(1)} %dual_update.7.refs_1_), channel_id=1, source_target_pairs={{0,1},{1,0},{2,3},{3,2},{4,5},{5,4},{6,7},{7,6},{8,9},{9,8},{10,11... | collective-permute-start | bytes 786440 | tf_op jit(solution)/shard_map/ppermute | solution.py:419
  167.9 1.6 collective-permute-start.14

commit v10 on v9

--- a/solution.py
+++ b/solution.py
@@ -69,9 +69,22 @@
     trailing_adds(width, products, add)
 
 
+def round_sums(dims, pitch, acc_ref):
+    scen, time_block, flight_tiles = dims[0] * dims[2], dims[3], dims[4]
+    lost = [jnp.zeros((scen, acc_ref.shape[1]), jnp.float32)] * flight_tiles
+    for minute in reversed(range(time_block)):
+        for f in range(flight_tiles):
+            place = pl.ds((f * time_block + minute) * pitch, scen)
+            value = acc_ref[place, :] + lost[f]
+            rounded = value.astype(jnp.bfloat16).astype(jnp.float32)
+            lost[f] = value - rounded
+            acc_ref[place, :] = rounded
+
+
 def write_messages(dims, pitch, acc_ref, out_ref):
     n_row, n_col, scen_local, time_block, _, own_tiles = dims
     piece = own_tiles * time_block
+    round_sums(dims, pitch, acc_ref)
     for group in range(n_row):
         for column in range(n_col):
             for j in range(scen_local):

time: 171 us -> 171 us (level)
  no operation moved by 1% of the time
where the time goes in v10:
time: 171 us
  blocking collectives  122 us (71%)
  Pallas kernels  20 us (12%)
  waiting for transfers between devices  15.7 us (9%)
  starting transfers between devices  11.9 us (7%)
    all_to_all x2, blocking collectives, per_device(): recv = lax.all_to_all(send, ('row', 'col'), 0, 0, tiled=True)  62.8 us
    all_to_all x2, blocking collectives, per_device(): probe = lax.all_to_all(send, ('row', 'col'), 0, 0, tiled=True)  59.3 us
    ppermute x8, waiting for transfers between devices, swap_chip(): lax.ppermute(value, 'col', [(i, i ^ 2 << (step + i % 2) % bits) for i in...  12.2 us
    ppermute x8, starting transfers between devices, swap_chip(): lax.ppermute(value, 'col', [(i, i ^ 2 << (step + i % 2) % bits) for i in...  10.5 us
    pallas_call x2, Pallas kernels, forward(): pl.pallas_call(functools.partial(forward_kernel, dims, pitch), in_specs=[...  7.77 us
    pallas_call x1, Pallas kernels, first_backward(): pl.pallas_call(functools.partial(first_backward_kernel, dims, pitch), in_...  4.74 us
    ppermute x8, waiting for transfers between devices, swap_core(): return lax.ppermute(value, 'col', [(i, i ^ 1) for i in range(n_col)])  3.5 us
  transfers between devices with their start and end apart: 16, of which 10 were waited for; matrix products, arithmetic and copies ran while one was open for 0% of the time, Pallas kernels for 1%

profile of v10, /device:TPU:0, one launch (start us, length us, event | category | flops | bytes accessed | tf_op | source)
XLA Modules:
  0.0 170.9 jit_solution(2221604490563675242)
XLA Ops:
  0.7 4.7 %first_backward_products.1 = (bf16[32,128,128]{2,1,0:T(8,128)(2,1)S(1)}, bf16[256,128,128]{2,1,0:T(8,128)(2,1)S(1)}) custom-call(s32[1]{0:T(128)} %bitcast.core_ref, s32[256]{0:T(256)} %bitcast.22, s32[256]{0:T(256)} %bitcast.26, f32[2,128,8,128]{3,2,1,0:T(8,128)} %bitcast.19, bf16[256,128,128]{2,1,0:T(8,128)(2,1)} %bitcast.34), custom_call_target="tpu_custom_call" | custom-call | flops 134217728 | bytes 4194304 | tf_op jit(solution)/shard_map/first_backward_products/pallas_call | solution.py:371
  5.4 33.3 %all_to_all.20.refs_0_ = bf16[32,128,128]{2,1,0:T(8,128)(2,1)S(1)} all-to-all(bf16[32,128,128]{2,1,0:T(8,128)(2,1)S(1)} %get-tuple-element.22), channel_id=1, replica_groups=mesh['row'=4,'col'=8] {'row','col'}, dimensions={0} | all-to-all | bytes 2097152 | tf_op jit(solution)/shard_map/all_to_all | solution.py:505
  38.8 0.9 primal_update.2
  39.8 29.7 %all_to_all.21.probe_ref = bf16[32,128,128]{2,1,0:T(8,128)(2,1)S(1)} all-to-all(bf16[32,128,128]{2,1,0:T(8,128)(2,1)S(1)} %get-tuple-element.23), channel_id=1, replica_groups=mesh['row'=4,'col'=8] {'row','col'}, dimensions={0} | all-to-all | bytes 2097152 | tf_op jit(solution)/shard_map/all_to_all | solution.py:508
  69.4 3.9 %forward_products.2 = (f32[2048,128]{1,0:T(8,128)S(1)}, bf16[512,128]{1,0:T(8,128)(2,1)S(1)}, bf16[512,128]{1,0:T(8,128)(2,1)S(1)}) custom-call(s32[1]{0:T(128)} %bitcast.core_ref, s32[256]{0:T(256)S(1)} %bitcast.23, s32[256]{0:T(256)S(1)} %bitcast.27, bf16[32,128,128]{2,1,0:T(8,128)(2,1)S(1)} %all_to_all.21.probe_ref, ...), custom_call_target="tpu_custom_call" | custom-call | flops 134217728 | bytes 4194304 | tf_op jit(solution)/shard_map/forward_products/pallas_call | solution.py:406
  73.3 0.1 collective-permute-start
  73.4 0.5 collective-permute-start.3
  73.9 0.8 collective-permute-done.other_ref
  74.8 1.5 collective-permute-start.1
  76.3 0.0 collective-permute-done.3.other_ref
  76.3 0.6 collective-permute-start.4
  77.0 2.8 %collective-permute-done.1.second_ref.refs_0_ = bf16[512,128]{1,0:T(8,128)(2,1)S(1)} collective-permute-done((bf16[512,128]{1,0:T(8,128)(2,1)S(1)}, bf16[512,128]{1,0:T(8,128)(2,1)S(1)}, u32[]{:S(2)}, u32[]{:S(2)}) %collective-permute-start.1) | collective-permute-done | bytes 131104 | tf_op jit(solution)/shard_map/ppermute | solution.py:437
  79.9 1.5 collective-permute-start.2
  81.4 0.0 collective-permute-done.4.second_ref.refs_0_
  81.4 1.5 collective-permute-start.5
  83.0 1.9 %collective-permute-done.2.refs_1_ = bf16[512,128]{1,0:T(8,128)(2,1)S(1)} collective-permute-done((bf16[512,128]{1,0:T(8,128)(2,1)S(1)}, bf16[512,128]{1,0:T(8,128)(2,1)S(1)}, u32[]{:S(2)}, u32[]{:S(2)}) %collective-permute-start.2) | collective-permute-done | bytes 131104 | tf_op jit(solution)/shard_map/ppermute | solution.py:437
  84.9 0.1 dual_update.4
  85.0 0.1 collective-permute-start.6
  85.1 1.4 collective-permute-done.5.refs_1_
  86.5 0.1 dual_update.5
  86.6 0.1 collective-permute-start.7
  86.7 0.0 collective-permute-done.6.refs_2_
  86.7 1.3 collective-permute-done.7.refs_3_
  88.0 3.2 %backward_products.1 = bf16[32,128,128]{2,1,0:T(8,128)(2,1)S(1)} custom-call(s32[1]{0:T(128)} %bitcast.core_ref, s32[256]{0:T(256)S(1)} %bitcast.24, s32[256]{0:T(256)S(1)} %bitcast.28, bf16[256,128,128]{2,1,0:T(8,128)(2,1)S(1)} %get-tuple-element.21.tiles_ref, bf16[512,128]{1,0:T(8,128)(2,1)S(1)} %get-tuple-element.26.refs_0_, ...), custom_call_target="tpu_custom_call" | custom-call | flops 134217728 | bytes 4194304 | tf_op jit(solution)/shard_map/backward_products/pallas_call | solution.py:394
  91.2 29.5 %all_to_all.22.refs_0_ = bf16[32,128,128]{2,1,0:T(8,128)(2,1)S(1)} all-to-all(bf16[32,128,128]{2,1,0:T(8,128)(2,1)S(1)} %backward_products.1), channel_id=1, replica_groups=mesh['row'=4,'col'=8] {'row','col'}, dimensions={0} | all-to-all | bytes 2097152 | tf_op jit(solution)/shard_map/all_to_all | solution.py:505
  120.7 0.8 primal_update.3
  121.5 29.7 %all_to_all.23.probe_ref = bf16[32,128,128]{2,1,0:T(8,128)(2,1)S(1)} all-to-all(bf16[32,128,128]{2,1,0:T(8,128)(2,1)S(1)} %get-tuple-element.32), channel_id=1, replica_groups=mesh['row'=4,'col'=8] {'row','col'}, dimensions={0} | all-to-all | bytes 2097152 | tf_op jit(solution)/shard_map/all_to_all | solution.py:508
  151.2 3.9 %forward_products.3 = (f32[2048,128]{1,0:T(8,128)S(1)}, bf16[512,128]{1,0:T(8,128)(2,1)S(1)}, bf16[512,128]{1,0:T(8,128)(2,1)S(1)}) custom-call(s32[1]{0:T(128)} %bitcast.core_ref, s32[256]{0:T(256)S(1)} %bitcast.25, s32[256]{0:T(256)S(1)} %bitcast.29, bf16[32,128,128]{2,1,0:T(8,128)(2,1)S(1)} %all_to_all.23.probe_ref, ...), custom_call_target="tpu_custom_call" | custom-call | flops 134217728 | bytes 4194304 | tf_op jit(solution)/shard_map/forward_products/pallas_call | solution.py:406
  155.0 0.1 collective-permute-start.11
  155.1 0.5 collective-permute-start.8
  155.6 0.8 collective-permute-done.11.other_ref
  156.5 1.5 collective-permute-start.12
  158.0 0.0 collective-permute-done.8.other_ref
  158.1 0.6 collective-permute-start.9
  158.7 2.8 %collective-permute-done.12.second_ref.refs_0_ = bf16[512,128]{1,0:T(8,128)(2,1)S(1)} collective-permute-done((bf16[512,128]{1,0:T(8,128)(2,1)S(1)}, bf16[512,128]{1,0:T(8,128)(2,1)S(1)}, u32[]{:S(2)}, u32[]{:S(2)}) %collective-permute-start.12) | collective-permute-done | bytes 131104 | tf_op jit(solution)/shard_map/ppermute | solution.py:437
  161.6 1.5 collective-permute-start.13
  163.1 0.0 collective-permute-done.9.second_ref.refs_0_
  163.1 1.5 collective-permute-start.10
  164.7 1.9 %collective-permute-done.13.refs_1_ = bf16[512,128]{1,0:T(8,128)(2,1)S(1)} collective-permute-done((bf16[512,128]{1,0:T(8,128)(2,1)S(1)}, bf16[512,128]{1,0:T(8,128)(2,1)S(1)}, u32[]{:S(2)}, u32[]{:S(2)}) %collective-permute-start.13) | collective-permute-done | bytes 131104 | tf_op jit(solution)/shard_map/ppermute | solution.py:437
  166.6 0.1 dual_update.7.refs_1_
  166.7 0.1 collective-permute-start.15
  166.8 1.4 collective-permute-done.10.refs_1_
  168.2 0.1 dual_update.6.refs_0_
  168.3 0.1 collective-permute-start.14
  168.4 1.0 own_results.1
  169.4 0.0 collective-permute-done.15.refs_1_
  169.4 0.5 collective-permute-done.14.refs_0_
  169.9 0.8 other_results.1
  (24 shorter events, 0.3 us)
Async XLA Ops:
  0.6 68.8 %copy-start.5 = (s32[1,1,256]{2,1,0:T(1,128)S(1)}, s32[1,1,256]{2,1,0:T(1,128)}, u32[]{:S(2)}) copy-start(s32[1,1,256]{2,1,0:T(1,128)} %param.11) | copy-start | bytes 3076
  0.6 68.8 %copy-start.4 = (s32[1,1,256]{2,1,0:T(1,128)S(1)}, s32[1,1,256]{2,1,0:T(1,128)}, u32[]{:S(2)}) copy-start(s32[1,1,256]{2,1,0:T(1,128)} %param.10) | copy-start | bytes 3076
  0.7 38.1 %copy-start.3 = (f32[128,256]{1,0:T(8,128)S(1)}, f32[128,256]{1,0:T(8,128)}, u32[]{:S(2)}) copy-start(f32[128,256]{1,0:T(8,128)} %refs_3_.1) | copy-start | bytes 393220
  0.7 38.1 %copy-start.7 = (s32[256]{0:T(256)S(1)}, s32[256]{0:T(256)}, u32[]{:S(2)}) copy-start(s32[256]{0:T(256)} %param.16) | copy-start | bytes 3076
  0.7 38.1 %copy-start.6 = (s32[256]{0:T(256)S(1)}, s32[256]{0:T(256)}, u32[]{:S(2)}) copy-start(s32[256]{0:T(256)} %param.15) | copy-start | bytes 3076
  0.7 38.1 %copy-start.2 = (f32[4,128,256]{2,1,0:T(8,128)S(1)}, f32[4,128,256]{2,1,0:T(8,128)}, u32[]{:S(2)}) copy-start(f32[4,128,256]{2,1,0:T(8,128)} %refs_1_.1) | copy-start | bytes 1572868
  38.8 46.1 %copy-start = (s32[16,16384]{1,0:T(8,128)S(1)}, s32[16,16384]{1,0:T(8,128)}, u32[]{:S(2)}) copy-start(s32[16,16384]{1,0:T(8,128)} %param.17) | copy-start | bytes 3145732
  38.8 46.1 %copy-start.1 = (f32[16,16384]{1,0:T(8,128)S(1)}, f32[16,16384]{1,0:T(8,128)}, u32[]{:S(2)}) copy-start(f32[16,16384]{1,0:T(8,128)} %param.13) | copy-start | bytes 3145732
  73.3 1.4 collective-permute-start
  73.4 2.9 %collective-permute-start.3 = (bf16[512,128]{1,0:T(8,128)(2,1)S(1)}, bf16[512,128]{1,0:T(8,128)(2,1)S(1)}, u32[]{:S(2)}, u32[]{:S(2)}) collective-permute-start(bf16[512,128]{1,0:T(8,128)(2,1)S(1)} %get-tuple-element.27), channel_id=1, source_target_pairs={{0,1},{1,0},{2,3},{3,2},{4,5},{5,4},{6,7},{7,6},{8,9},{9,8},{10,11... | collective-permute-start | bytes 393224 | tf_op jit(solution)/shard_map/ppermute | solution.py:432
  74.8 5.0 %collective-permute-start.1 = (bf16[512,128]{1,0:T(8,128)(2,1)S(1)}, bf16[512,128]{1,0:T(8,128)(2,1)S(1)}, u32[]{:S(2)}, u32[]{:S(2)}) collective-permute-start(bf16[512,128]{1,0:T(8,128)(2,1)S(1)} %core_pair_sum.4.first_ref), channel_id=1, source_target_pairs={{0,2},{1,5},{2,0},{3,7},{4,6},{5,1},{6,4},{7,3},{8,10},{9,13},{10,... | collective-permute-start | bytes 393224 | tf_op jit(solution)/shard_map/ppermute | solution.py:437
  76.3 5.1 %collective-permute-start.4 = (bf16[512,128]{1,0:T(8,128)(2,1)S(1)}, bf16[512,128]{1,0:T(8,128)(2,1)S(1)}, u32[]{:S(2)}, u32[]{:S(2)}) collective-permute-start(bf16[512,128]{1,0:T(8,128)(2,1)S(1)} %core_pair_sum.5.first_ref), channel_id=1, source_target_pairs={{0,2},{1,5},{2,0},{3,7},{4,6},{5,1},{6,4},{7,3},{8,10},{9,13},{10,... | collective-permute-start | bytes 393224 | tf_op jit(solution)/shard_map/ppermute | solution.py:437
  79.9 5.0 %collective-permute-start.2 = (bf16[512,128]{1,0:T(8,128)(2,1)S(1)}, bf16[512,128]{1,0:T(8,128)(2,1)S(1)}, u32[]{:S(2)}, u32[]{:S(2)}) collective-permute-start(bf16[512,128]{1,0:T(8,128)(2,1)S(1)} %chip_sum.4), channel_id=1, source_target_pairs={{0,4},{1,3},{2,6},{3,1},{4,0},{5,7},{6,2},{7,5},{8,12},{9,11},{10,... | collective-permute-start | bytes 393224 | tf_op jit(solution)/shard_map/ppermute | solution.py:437
  81.4 5.0 %collective-permute-start.5 = (bf16[512,128]{1,0:T(8,128)(2,1)S(1)}, bf16[512,128]{1,0:T(8,128)(2,1)S(1)}, u32[]{:S(2)}, u32[]{:S(2)}) collective-permute-start(bf16[512,128]{1,0:T(8,128)(2,1)S(1)} %chip_sum.5), channel_id=1, source_target_pairs={{0,4},{1,3},{2,6},{3,1},{4,0},{5,7},{6,2},{7,5},{8,12},{9,11},{10,... | collective-permute-start | bytes 393224 | tf_op jit(solution)/shard_map/ppermute | solution.py:437
  85.0 1.6 collective-permute-start.6
  86.6 1.4 collective-permute-start.7
  155.0 1.4 collective-permute-start.11
  155.1 2.9 %collective-permute-start.8 = (bf16[512,128]{1,0:T(8,128)(2,1)S(1)}, bf16[512,128]{1,0:T(8,128)(2,1)S(1)}, u32[]{:S(2)}, u32[]{:S(2)}) collective-permute-start(bf16[512,128]{1,0:T(8,128)(2,1)S(1)} %get-tuple-element.34), channel_id=1, source_target_pairs={{0,1},{1,0},{2,3},{3,2},{4,5},{5,4},{6,7},{7,6},{8,9},{9,8},{10,11... | collective-permute-start | bytes 393224 | tf_op jit(solution)/shard_map/ppermute | solution.py:432
  156.5 5.0 %collective-permute-start.12 = (bf16[512,128]{1,0:T(8,128)(2,1)S(1)}, bf16[512,128]{1,0:T(8,128)(2,1)S(1)}, u32[]{:S(2)}, u32[]{:S(2)}) collective-permute-start(bf16[512,128]{1,0:T(8,128)(2,1)S(1)} %core_pair_sum.7.first_ref), channel_id=1, source_target_pairs={{0,2},{1,5},{2,0},{3,7},{4,6},{5,1},{6,4},{7,3},{8,10},{9,13},{10,... | collective-permute-start | bytes 393224 | tf_op jit(solution)/shard_map/ppermute | solution.py:437
  158.1 5.1 %collective-permute-start.9 = (bf16[512,128]{1,0:T(8,128)(2,1)S(1)}, bf16[512,128]{1,0:T(8,128)(2,1)S(1)}, u32[]{:S(2)}, u32[]{:S(2)}) collective-permute-start(bf16[512,128]{1,0:T(8,128)(2,1)S(1)} %core_pair_sum.6.first_ref), channel_id=1, source_target_pairs={{0,2},{1,5},{2,0},{3,7},{4,6},{5,1},{6,4},{7,3},{8,10},{9,13},{10,... | collective-permute-start | bytes 393224 | tf_op jit(solution)/shard_map/ppermute | solution.py:437
  161.6 5.0 %collective-permute-start.13 = (bf16[512,128]{1,0:T(8,128)(2,1)S(1)}, bf16[512,128]{1,0:T(8,128)(2,1)S(1)}, u32[]{:S(2)}, u32[]{:S(2)}) collective-permute-start(bf16[512,128]{1,0:T(8,128)(2,1)S(1)} %chip_sum.7), channel_id=1, source_target_pairs={{0,4},{1,3},{2,6},{3,1},{4,0},{5,7},{6,2},{7,5},{8,12},{9,11},{10,... | collective-permute-start | bytes 393224 | tf_op jit(solution)/shard_map/ppermute | solution.py:437
  163.1 5.0 %collective-permute-start.10 = (bf16[512,128]{1,0:T(8,128)(2,1)S(1)}, bf16[512,128]{1,0:T(8,128)(2,1)S(1)}, u32[]{:S(2)}, u32[]{:S(2)}) collective-permute-start(bf16[512,128]{1,0:T(8,128)(2,1)S(1)} %chip_sum.6), channel_id=1, source_target_pairs={{0,4},{1,3},{2,6},{3,1},{4,0},{5,7},{6,2},{7,5},{8,12},{9,11},{10,... | collective-permute-start | bytes 393224 | tf_op jit(solution)/shard_map/ppermute | solution.py:437
  166.7 2.7 %collective-permute-start.15 = (f32[2,32,8,128]{3,2,1,0:T(8,128)S(1)}, f32[2,32,8,128]{3,2,1,0:T(8,128)S(1)}, u32[]{:S(2)}, u32[]{:S(2)}) collective-permute-start(f32[2,32,8,128]{3,2,1,0:T(8,128)S(1)} %dual_update.7.refs_1_), channel_id=1, source_target_pairs={{0,1},{1,0},{2,3},{3,2},{4,5},{5,4},{6,7},{7,6},{8,9},{9,8},{10,11... | collective-permute-start | bytes 786440 | tf_op jit(solution)/shard_map/ppermute | solution.py:432
  168.3 1.6 collective-permute-start.14

commit v11 on v10

--- a/solution.py
+++ b/solution.py
@@ -141,17 +141,18 @@
     return ref[pl.ds(pl.multiple_of(row_part(core, part, size), size), size), :]
 
 
-def backward_kernel(dims, pitch, core_ref, rows_ref, cols_ref, tiles_ref, *refs):
-    pieces, (out_ref, duals_ref, acc_ref) = refs[: 2 * PARTS], refs[2 * PARTS :]
+def clear_kernel(scen, pitch, acc_ref):
+    for row in range(0, acc_ref.shape[0], pitch):
+        acc_ref[pl.ds(row, scen), :] = jnp.zeros((scen, acc_ref.shape[1]), jnp.float32)
+
+
+def backward_kernel(dims, pitch, core_ref, rows_ref, cols_ref, tiles_ref, _, *refs):
+    pieces, (out_ref, acc_ref, duals_ref) = refs[: 2 * PARTS], refs[2 * PARTS :]
     for i, piece in enumerate(pieces):
         core = core_ref[0] if i < PARTS else 1 - core_ref[0]
         scen, side = duals_ref.shape[1:]
         rows = piece.shape[0] // scen
         duals_ref[pl.ds(row_part(core, i % PARTS, rows), rows)] = piece[...].reshape(rows, scen, side)
-    scen = duals_ref.shape[1]
-    for row in range(0, acc_ref.shape[0], pitch):
-        acc_ref[pl.ds(row, scen), :] = jnp.zeros((scen, acc_ref.shape[1]), jnp.float32)
-
     width = min(UNROLL, tiles_ref.shape[0])
 
     def body(index, _):
@@ -304,33 +305,34 @@
         refs[-1][...] = fresh.astype(jnp.bfloat16)
 
 
-def part_copies(core, parts, out_ref, sems):
+def part_copies(core, parts, out_ref, sems, used=0):
     copies = []
-    for i, ref in enumerate(parts):
+    for i, ref in parts:
         bands, rows = ref.shape[:2]
         for a in range(bands):
             place = out_ref.at[a, pl.ds(row_part(core, i, rows), rows)]
-            copies.append(pltpu.make_async_copy(ref.at[a], place, sems.at[len(copies)]))
+            copies.append(pltpu.make_async_copy(ref.at[a], place, sems.at[used + len(copies)]))
     return copies
 
 
-def own_results_kernel(core_ref, primal_ref, *refs):
-    parts, (primal_out, duals_out, sems) = refs[:PARTS], refs[PARTS:]
-    copies = part_copies(core_ref[0], parts, duals_out, sems)
-    copies.append(pltpu.make_async_copy(primal_ref, primal_out, sems.at[len(copies)]))
+def finish(copies):
     for copy in copies:
         copy.start()
     for copy in copies:
         copy.wait()
 
 
+def own_results_kernel(core_ref, primal_ref, *refs):
+    (*own, other), (primal_out, duals_out, sems) = refs[: PARTS + 1], refs[PARTS + 1 :]
+    copies = part_copies(core_ref[0], list(enumerate(own)), duals_out, sems)
+    copies += part_copies(1 - core_ref[0], [(0, other)], duals_out, sems, len(copies))
+    copies.append(pltpu.make_async_copy(primal_ref, primal_out, sems.at[len(copies)]))
+    finish(copies)
+
+
 def other_results_kernel(core_ref, _, *refs):
-    parts, (duals_out, sems) = refs[:PARTS], refs[PARTS:]
-    copies = part_copies(1 - core_ref[0], parts, duals_out, sems)
-    for copy in copies:
-        copy.start()
-    for copy in copies:
-        copy.wait()
+    parts, (duals_out, sems) = refs[: PARTS - 1], refs[PARTS - 1 :]
+    finish(part_copies(1 - core_ref[0], list(enumerate(parts, 1)), duals_out, sems))
 
 
 def per_device(
@@ -391,16 +393,24 @@
 
     def backward(rounded, tiles):
         pieces = [*rounded, *map(swap_core, rounded)]
+        cleared = pl.pallas_call(
+            functools.partial(clear_kernel, scen, pitch),
+            out_specs=whole(),
+            out_shape=acc_cols,
+            compiler_params=params(),
+            name="clear_sums",
+        )()
         return pl.pallas_call(
             functools.partial(backward_kernel, dims, pitch),
-            in_specs=[scalars()] * 3 + [whole()] * (1 + len(pieces)),
-            out_specs=whole(),
-            out_shape=messages,
-            scratch_shapes=[picked_duals, acc_cols],
+            in_specs=[scalars()] * 3 + [whole()] * (2 + len(pieces)),
+            out_specs=[whole()] * 2,
+            out_shape=[messages, acc_cols],
+            input_output_aliases={4: 1},
+            scratch_shapes=[picked_duals],
             compiler_params=params(),
             cost_estimate=cost,
             name="backward_products",
-        )(core, rows, cols, in_vmem(tiles), *pieces)
+        )(core, rows, cols, in_vmem(tiles), in_vmem(cleared), *pieces)[0]
 
     def forward(probe, tiles):
         return pl.pallas_call(
@@ -474,26 +484,27 @@
     def results(primal, owned):
         duals_shape = jax.ShapeDtypeStruct((scen // band, row_tiles, band, side), jnp.float32)
         hbm = pl.BlockSpec(memory_space=pltpu.HBM)
-        copies = PARTS * (scen // band)
+        copies = scen // band
+        others = [swap_core(part) for part in owned]
         primal_out, duals_out = pl.pallas_call(
             own_results_kernel,
-            in_specs=[scalars()] + [whole()] * (1 + PARTS),
+            in_specs=[scalars()] + [whole()] * (2 + PARTS),
             out_specs=[hbm, hbm],
             out_shape=[jax.ShapeDtypeStruct(primal.shape, jnp.float32), duals_shape],
-            scratch_shapes=[pltpu.SemaphoreType.DMA((copies + 1,))],
+            scratch_shapes=[pltpu.SemaphoreType.DMA(((PARTS + 1) * copies + 1,))],
             compiler_params=params(),
             name="own_results",
-        )(core, in_vmem(primal), *owned)
+        )(core, in_vmem(primal), *owned, others[0])
         duals_out = pl.pallas_call(
             other_results_kernel,
-            in_specs=[scalars(), hbm] + [whole()] * PARTS,
+            in_specs=[scalars(), hbm] + [whole()] * (PARTS - 1),
             out_specs=hbm,
             out_shape=duals_shape,
             input_output_aliases={1: 0},
-            scratch_shapes=[pltpu.SemaphoreType.DMA((copies,))],
+            scratch_shapes=[pltpu.SemaphoreType.DMA(((PARTS - 1) * copies,))],
             compiler_params=params(),
             name="other_results",
-        )(core, duals_out, *map(swap_core, owned))
+        )(core, duals_out, *others[1:])
         return primal_out, duals_out.transpose(0, 2, 1, 3).reshape(scen, row_length)
 
     send, tiles = first_backward(banded(dual_vars))

time: 171 us -> 171 us (level)
  no operation moved by 1% of the time
where the time goes in v11:
time: 171 us
  blocking collectives  122 us (71%)
  Pallas kernels  20.1 us (12%)
  waiting for transfers between devices  15.5 us (9%)
  starting transfers between devices  11.9 us (7%)
    all_to_all x2, blocking collectives, per_device(): recv = lax.all_to_all(send, ('row', 'col'), 0, 0, tiled=True)  62.8 us
    all_to_all x2, blocking collectives, per_device(): probe = lax.all_to_all(send, ('row', 'col'), 0, 0, tiled=True)  59.3 us
    ppermute x8, waiting for transfers between devices, swap_chip(): lax.ppermute(value, 'col', [(i, i ^ 2 << (step + i % 2) % bits) for i in...  12.2 us
    ppermute x8, starting transfers between devices, swap_chip(): lax.ppermute(value, 'col', [(i, i ^ 2 << (step + i % 2) % bits) for i in...  10.5 us
    pallas_call x2, Pallas kernels, forward(): pl.pallas_call(functools.partial(forward_kernel, dims, pitch), in_specs=[...  7.76 us
    pallas_call x1, Pallas kernels, first_backward(): pl.pallas_call(functools.partial(first_backward_kernel, dims, pitch), in_...  4.74 us
  transfers between devices with their start and end apart: 16, of which 10 were waited for; matrix products, arithmetic and copies ran while one was open for 0% of the time, Pallas kernels for 1%

profile of v11, /device:TPU:0, one launch (start us, length us, event | category | flops | bytes accessed | tf_op | source)
XLA Modules:
  0.0 170.7 jit_solution(15239262170314838722)
XLA Ops:
  0.7 4.7 %first_backward_products.1 = (bf16[32,128,128]{2,1,0:T(8,128)(2,1)S(1)}, bf16[256,128,128]{2,1,0:T(8,128)(2,1)S(1)}) custom-call(s32[1]{0:T(128)} %bitcast.core_ref, s32[256]{0:T(256)} %bitcast.22, s32[256]{0:T(256)} %bitcast.26, f32[2,128,8,128]{3,2,1,0:T(8,128)} %bitcast.19, bf16[256,128,128]{2,1,0:T(8,128)(2,1)} %bitcast.34), custom_call_target="tpu_custom_call" | custom-call | flops 134217728 | bytes 4194304 | tf_op jit(solution)/shard_map/first_backward_products/pallas_call | solution.py:373
  5.4 33.3 %all_to_all.20.refs_0_ = bf16[32,128,128]{2,1,0:T(8,128)(2,1)S(1)} all-to-all(bf16[32,128,128]{2,1,0:T(8,128)(2,1)S(1)} %get-tuple-element.23), channel_id=1, replica_groups=mesh['row'=4,'col'=8] {'row','col'}, dimensions={0} | all-to-all | bytes 2097152 | tf_op jit(solution)/shard_map/all_to_all | solution.py:516
  38.8 0.9 primal_update.2
  39.8 29.7 %all_to_all.21.probe_ref = bf16[32,128,128]{2,1,0:T(8,128)(2,1)S(1)} all-to-all(bf16[32,128,128]{2,1,0:T(8,128)(2,1)S(1)} %get-tuple-element.24), channel_id=1, replica_groups=mesh['row'=4,'col'=8] {'row','col'}, dimensions={0} | all-to-all | bytes 2097152 | tf_op jit(solution)/shard_map/all_to_all | solution.py:519
  69.4 3.9 %forward_products.2 = (f32[2048,128]{1,0:T(8,128)S(1)}, bf16[512,128]{1,0:T(8,128)(2,1)S(1)}, bf16[512,128]{1,0:T(8,128)(2,1)S(1)}) custom-call(s32[1]{0:T(128)} %bitcast.core_ref, s32[256]{0:T(256)S(1)} %bitcast.23, s32[256]{0:T(256)S(1)} %bitcast.27, bf16[32,128,128]{2,1,0:T(8,128)(2,1)S(1)} %all_to_all.21.probe_ref, ...), custom_call_target="tpu_custom_call" | custom-call | flops 134217728 | bytes 4194304 | tf_op jit(solution)/shard_map/forward_products/pallas_call | solution.py:416
  73.3 0.1 collective-permute-start
  73.4 0.5 collective-permute-start.3
  73.9 0.8 collective-permute-done.other_ref
  74.8 1.5 collective-permute-start.1
  76.3 0.0 collective-permute-done.3.other_ref
  76.3 0.6 collective-permute-start.4
  77.0 2.8 %collective-permute-done.1.second_ref.refs_0_ = bf16[512,128]{1,0:T(8,128)(2,1)S(1)} collective-permute-done((bf16[512,128]{1,0:T(8,128)(2,1)S(1)}, bf16[512,128]{1,0:T(8,128)(2,1)S(1)}, u32[]{:S(2)}, u32[]{:S(2)}) %collective-permute-start.1) | collective-permute-done | bytes 131104 | tf_op jit(solution)/shard_map/ppermute | solution.py:447
  79.8 1.5 collective-permute-start.2
  81.4 0.0 collective-permute-done.4.second_ref.refs_0_
  81.4 1.5 collective-permute-start.5
  83.0 1.9 %collective-permute-done.2.refs_1_ = bf16[512,128]{1,0:T(8,128)(2,1)S(1)} collective-permute-done((bf16[512,128]{1,0:T(8,128)(2,1)S(1)}, bf16[512,128]{1,0:T(8,128)(2,1)S(1)}, u32[]{:S(2)}, u32[]{:S(2)}) %collective-permute-start.2) | collective-permute-done | bytes 131104 | tf_op jit(solution)/shard_map/ppermute | solution.py:447
  84.9 0.1 dual_update.4
  85.0 0.1 collective-permute-start.6
  85.1 1.4 collective-permute-done.5.refs_1_
  86.4 0.1 dual_update.5
  86.6 0.1 collective-permute-start.7
  86.7 0.1 clear_sums.1._
  86.8 0.0 collective-permute-done.6.refs_2_
  86.8 1.2 collective-permute-done.7.refs_3_
  88.0 3.1 %backward_products.1 = (bf16[32,128,128]{2,1,0:T(8,128)(2,1)S(1)}, f32[6144,128]{1,0:T(8,128)S(1)}) custom-call(s32[1]{0:T(128)} %bitcast.core_ref, s32[256]{0:T(256)S(1)} %bitcast.24, s32[256]{0:T(256)S(1)} %bitcast.28, bf16[256,128,128]{2,1,0:T(8,128)(2,1)S(1)} %get-tuple-element.22.tiles_ref, ...), custom_call_target="tpu_custom_call", output_to_operand_aliasing={{1}: (4, {})} | custom-call | flops 134217728 | bytes 4194304 | tf_op jit(solution)/shard_map/backward_products/pallas_call | solution.py:403
  91.1 29.5 %all_to_all.22.refs_0_ = bf16[32,128,128]{2,1,0:T(8,128)(2,1)S(1)} all-to-all(bf16[32,128,128]{2,1,0:T(8,128)(2,1)S(1)} %get-tuple-element.30), channel_id=1, replica_groups=mesh['row'=4,'col'=8] {'row','col'}, dimensions={0} | all-to-all | bytes 2097152 | tf_op jit(solution)/shard_map/all_to_all | solution.py:516
  120.6 0.8 primal_update.3
  121.4 29.7 %all_to_all.23.probe_ref = bf16[32,128,128]{2,1,0:T(8,128)(2,1)S(1)} all-to-all(bf16[32,128,128]{2,1,0:T(8,128)(2,1)S(1)} %get-tuple-element.34), channel_id=1, replica_groups=mesh['row'=4,'col'=8] {'row','col'}, dimensions={0} | all-to-all | bytes 2097152 | tf_op jit(solution)/shard_map/all_to_all | solution.py:519
  151.1 3.9 %forward_products.3 = (f32[2048,128]{1,0:T(8,128)S(1)}, bf16[512,128]{1,0:T(8,128)(2,1)S(1)}, bf16[512,128]{1,0:T(8,128)(2,1)S(1)}) custom-call(s32[1]{0:T(128)} %bitcast.core_ref, s32[256]{0:T(256)S(1)} %bitcast.25, s32[256]{0:T(256)S(1)} %bitcast.29, bf16[32,128,128]{2,1,0:T(8,128)(2,1)S(1)} %all_to_all.23.probe_ref, ...), custom_call_target="tpu_custom_call" | custom-call | flops 134217728 | bytes 4194304 | tf_op jit(solution)/shard_map/forward_products/pallas_call | solution.py:416
  155.0 0.1 collective-permute-start.8
  155.1 0.5 collective-permute-start.11
  155.6 0.8 collective-permute-done.8.other_ref
  156.4 1.5 collective-permute-start.9
  158.0 0.0 collective-permute-done.11.other_ref
  158.0 0.6 collective-permute-start.12
  158.6 2.8 %collective-permute-done.9.second_ref.refs_0_ = bf16[512,128]{1,0:T(8,128)(2,1)S(1)} collective-permute-done((bf16[512,128]{1,0:T(8,128)(2,1)S(1)}, bf16[512,128]{1,0:T(8,128)(2,1)S(1)}, u32[]{:S(2)}, u32[]{:S(2)}) %collective-permute-start.9) | collective-permute-done | bytes 131104 | tf_op jit(solution)/shard_map/ppermute | solution.py:447
  161.5 1.5 collective-permute-start.10
  163.0 0.0 collective-permute-done.12.second_ref.refs_0_
  163.1 1.5 collective-permute-start.13
  164.6 1.9 %collective-permute-done.10.refs_1_ = bf16[512,128]{1,0:T(8,128)(2,1)S(1)} collective-permute-done((bf16[512,128]{1,0:T(8,128)(2,1)S(1)}, bf16[512,128]{1,0:T(8,128)(2,1)S(1)}, u32[]{:S(2)}, u32[]{:S(2)}) %collective-permute-start.10) | collective-permute-done | bytes 131104 | tf_op jit(solution)/shard_map/ppermute | solution.py:447
  166.5 0.1 dual_update.6.refs_0_
  166.7 0.1 collective-permute-start.14
  166.7 1.4 collective-permute-done.13.refs_1_
  168.1 0.1 dual_update.7.refs_1_
  168.3 0.1 collective-permute-start.15
  168.3 1.1 own_results.1
  169.5 0.4 collective-permute-done.15.refs_0_
  169.9 0.7 other_results.1
  (25 shorter events, 0.3 us)
Async XLA Ops:
  0.6 68.8 %copy-start.5 = (s32[1,1,256]{2,1,0:T(1,128)S(1)}, s32[1,1,256]{2,1,0:T(1,128)}, u32[]{:S(2)}) copy-start(s32[1,1,256]{2,1,0:T(1,128)} %param.11) | copy-start | bytes 3076
  0.6 68.8 %copy-start.4 = (s32[1,1,256]{2,1,0:T(1,128)S(1)}, s32[1,1,256]{2,1,0:T(1,128)}, u32[]{:S(2)}) copy-start(s32[1,1,256]{2,1,0:T(1,128)} %param.10) | copy-start | bytes 3076
  0.7 38.1 %copy-start.3 = (f32[128,256]{1,0:T(8,128)S(1)}, f32[128,256]{1,0:T(8,128)}, u32[]{:S(2)}) copy-start(f32[128,256]{1,0:T(8,128)} %refs_3_.1) | copy-start | bytes 393220
  0.7 38.1 %copy-start.7 = (s32[256]{0:T(256)S(1)}, s32[256]{0:T(256)}, u32[]{:S(2)}) copy-start(s32[256]{0:T(256)} %param.16) | copy-start | bytes 3076
  0.7 38.1 %copy-start.6 = (s32[256]{0:T(256)S(1)}, s32[256]{0:T(256)}, u32[]{:S(2)}) copy-start(s32[256]{0:T(256)} %param.15) | copy-start | bytes 3076
  0.7 38.1 %copy-start.2 = (f32[4,128,256]{2,1,0:T(8,128)S(1)}, f32[4,128,256]{2,1,0:T(8,128)}, u32[]{:S(2)}) copy-start(f32[4,128,256]{2,1,0:T(8,128)} %refs_1_.1) | copy-start | bytes 1572868
  38.8 46.1 %copy-start = (s32[16,16384]{1,0:T(8,128)S(1)}, s32[16,16384]{1,0:T(8,128)}, u32[]{:S(2)}) copy-start(s32[16,16384]{1,0:T(8,128)} %param.17) | copy-start | bytes 3145732
  38.8 46.1 %copy-start.1 = (f32[16,16384]{1,0:T(8,128)S(1)}, f32[16,16384]{1,0:T(8,128)}, u32[]{:S(2)}) copy-start(f32[16,16384]{1,0:T(8,128)} %param.13) | copy-start | bytes 3145732
  73.3 1.4 collective-permute-start
  73.4 2.9 %collective-permute-start.3 = (bf16[512,128]{1,0:T(8,128)(2,1)S(1)}, bf16[512,128]{1,0:T(8,128)(2,1)S(1)}, u32[]{:S(2)}, u32[]{:S(2)}) collective-permute-start(bf16[512,128]{1,0:T(8,128)(2,1)S(1)} %get-tuple-element.28), channel_id=1, source_target_pairs={{0,1},{1,0},{2,3},{3,2},{4,5},{5,4},{6,7},{7,6},{8,9},{9,8},{10,11... | collective-permute-start | bytes 393224 | tf_op jit(solution)/shard_map/ppermute | solution.py:442
  74.8 5.0 %collective-permute-start.1 = (bf16[512,128]{1,0:T(8,128)(2,1)S(1)}, bf16[512,128]{1,0:T(8,128)(2,1)S(1)}, u32[]{:S(2)}, u32[]{:S(2)}) collective-permute-start(bf16[512,128]{1,0:T(8,128)(2,1)S(1)} %core_pair_sum.4.first_ref), channel_id=1, source_target_pairs={{0,2},{1,5},{2,0},{3,7},{4,6},{5,1},{6,4},{7,3},{8,10},{9,13},{10,... | collective-permute-start | bytes 393224 | tf_op jit(solution)/shard_map/ppermute | solution.py:447
  76.3 5.0 %collective-permute-start.4 = (bf16[512,128]{1,0:T(8,128)(2,1)S(1)}, bf16[512,128]{1,0:T(8,128)(2,1)S(1)}, u32[]{:S(2)}, u32[]{:S(2)}) collective-permute-start(bf16[512,128]{1,0:T(8,128)(2,1)S(1)} %core_pair_sum.5.first_ref), channel_id=1, source_target_pairs={{0,2},{1,5},{2,0},{3,7},{4,6},{5,1},{6,4},{7,3},{8,10},{9,13},{10,... | collective-permute-start | bytes 393224 | tf_op jit(solution)/shard_map/ppermute | solution.py:447
  79.8 5.0 %collective-permute-start.2 = (bf16[512,128]{1,0:T(8,128)(2,1)S(1)}, bf16[512,128]{1,0:T(8,128)(2,1)S(1)}, u32[]{:S(2)}, u32[]{:S(2)}) collective-permute-start(bf16[512,128]{1,0:T(8,128)(2,1)S(1)} %chip_sum.4), channel_id=1, source_target_pairs={{0,4},{1,3},{2,6},{3,1},{4,0},{5,7},{6,2},{7,5},{8,12},{9,11},{10,... | collective-permute-start | bytes 393224 | tf_op jit(solution)/shard_map/ppermute | solution.py:447
  81.4 5.0 %collective-permute-start.5 = (bf16[512,128]{1,0:T(8,128)(2,1)S(1)}, bf16[512,128]{1,0:T(8,128)(2,1)S(1)}, u32[]{:S(2)}, u32[]{:S(2)}) collective-permute-start(bf16[512,128]{1,0:T(8,128)(2,1)S(1)} %chip_sum.5), channel_id=1, source_target_pairs={{0,4},{1,3},{2,6},{3,1},{4,0},{5,7},{6,2},{7,5},{8,12},{9,11},{10,... | collective-permute-start | bytes 393224 | tf_op jit(solution)/shard_map/ppermute | solution.py:447
  85.0 1.8 %collective-permute-start.6 = (bf16[512,128]{1,0:T(8,128)(2,1)S(1)}, bf16[512,128]{1,0:T(8,128)(2,1)S(1)}, u32[]{:S(2)}, u32[]{:S(2)}) collective-permute-start(bf16[512,128]{1,0:T(8,128)(2,1)S(1)} %get-tuple-element.27.refs_0_), channel_id=1, source_target_pairs={{0,1},{1,0},{2,3},{3,2},{4,5},{5,4},{6,7},{7,6},{8,9},{9,8},{10,11... | collective-permute-start | bytes 393224 | tf_op jit(solution)/shard_map/ppermute | solution.py:442
  86.6 1.4 collective-permute-start.7
  155.0 1.4 collective-permute-start.8
  155.1 2.9 %collective-permute-start.11 = (bf16[512,128]{1,0:T(8,128)(2,1)S(1)}, bf16[512,128]{1,0:T(8,128)(2,1)S(1)}, u32[]{:S(2)}, u32[]{:S(2)}) collective-permute-start(bf16[512,128]{1,0:T(8,128)(2,1)S(1)} %get-tuple-element.38), channel_id=1, source_target_pairs={{0,1},{1,0},{2,3},{3,2},{4,5},{5,4},{6,7},{7,6},{8,9},{9,8},{10,11... | collective-permute-start | bytes 393224 | tf_op jit(solution)/shard_map/ppermute | solution.py:442
  156.4 5.0 %collective-permute-start.9 = (bf16[512,128]{1,0:T(8,128)(2,1)S(1)}, bf16[512,128]{1,0:T(8,128)(2,1)S(1)}, u32[]{:S(2)}, u32[]{:S(2)}) collective-permute-start(bf16[512,128]{1,0:T(8,128)(2,1)S(1)} %core_pair_sum.6.first_ref), channel_id=1, source_target_pairs={{0,2},{1,5},{2,0},{3,7},{4,6},{5,1},{6,4},{7,3},{8,10},{9,13},{10,... | collective-permute-start | bytes 393224 | tf_op jit(solution)/shard_map/ppermute | solution.py:447
  158.0 5.1 %collective-permute-start.12 = (bf16[512,128]{1,0:T(8,128)(2,1)S(1)}, bf16[512,128]{1,0:T(8,128)(2,1)S(1)}, u32[]{:S(2)}, u32[]{:S(2)}) collective-permute-start(bf16[512,128]{1,0:T(8,128)(2,1)S(1)} %core_pair_sum.7.first_ref), channel_id=1, source_target_pairs={{0,2},{1,5},{2,0},{3,7},{4,6},{5,1},{6,4},{7,3},{8,10},{9,13},{10,... | collective-permute-start | bytes 393224 | tf_op jit(solution)/shard_map/ppermute | solution.py:447
  161.5 5.0 %collective-permute-start.10 = (bf16[512,128]{1,0:T(8,128)(2,1)S(1)}, bf16[512,128]{1,0:T(8,128)(2,1)S(1)}, u32[]{:S(2)}, u32[]{:S(2)}) collective-permute-start(bf16[512,128]{1,0:T(8,128)(2,1)S(1)} %chip_sum.6), channel_id=1, source_target_pairs={{0,4},{1,3},{2,6},{3,1},{4,0},{5,7},{6,2},{7,5},{8,12},{9,11},{10,... | collective-permute-start | bytes 393224 | tf_op jit(solution)/shard_map/ppermute | solution.py:447
  163.1 5.0 %collective-permute-start.13 = (bf16[512,128]{1,0:T(8,128)(2,1)S(1)}, bf16[512,128]{1,0:T(8,128)(2,1)S(1)}, u32[]{:S(2)}, u32[]{:S(2)}) collective-permute-start(bf16[512,128]{1,0:T(8,128)(2,1)S(1)} %chip_sum.7), channel_id=1, source_target_pairs={{0,4},{1,3},{2,6},{3,1},{4,0},{5,7},{6,2},{7,5},{8,12},{9,11},{10,... | collective-permute-start | bytes 393224 | tf_op jit(solution)/shard_map/ppermute | solution.py:447
  166.7 1.7 collective-permute-start.14
  168.3 1.6 collective-permute-start.15

commit v12 on v11

--- a/solution.py
+++ b/solution.py
@@ -43,10 +43,10 @@
     return pl.multiple_of((column % flight_tiles * time_block + column // flight_tiles) * pitch, 8)
 
 
-def trailing_adds(width, products, add):
+def trailing_adds(width, group, products, add):
     waiting = []
-    for u in range(0, width, 2):
-        waiting += zip((u, u + 1), products(u))
+    for u in range(0, width, group):
+        waiting += zip(range(u, u + group), products(u))
         while len(waiting) > TRAIL:
             add(*waiting.pop(0))
     for item in waiting:
@@ -66,7 +66,7 @@
         place = column_place(dims, cols_ref[start + u], pitch)
         acc_ref[pl.ds(place, scen), :] += product
 
-    trailing_adds(width, products, add)
+    trailing_adds(width, 2, products, add)
 
 
 def round_sums(dims, pitch, acc_ref):
@@ -188,20 +188,25 @@
         start = index * width
 
         def products(u):
-            both = jnp.concatenate([tiles_ref[start + u], tiles_ref[start + u + 1]], axis=1)
+            first, second, third, fourth = (picked(start + u + i) for i in range(4))
+            zero = jnp.zeros_like(first)
+            left = jnp.concatenate([first, second, zero, zero], axis=0)
+            right = jnp.concatenate([zero, zero, third, fourth], axis=0)
+            sides = [tiles_ref[pl.ds(start + u + i, 2)] for i in (0, 2)]
+            both = jnp.concatenate([two.reshape(-1, two.shape[2]) for two in sides], axis=1)
             result = lax.dot_general(
-                stacked_pair(picked(start + u), picked(start + u + 1)),
-                both,
-                TRANSPOSED,
-                preferred_element_type=jnp.float32,
+                jnp.concatenate([left, right], axis=1), both, TRANSPOSED, preferred_element_type=jnp.float32
             )
-            return result[:scen], result[scen:]
+            side = tiles_ref.shape[1]
+            return [
+                result[i * scen : (i + 1) * scen, i % 2 * side : (i % 2 + 1) * side] for i in range(4)
+            ]
 
         def add(u, product):
             place = pl.multiple_of(rows_ref[start + u] * scen, scen)
             acc_ref[pl.ds(place, scen), :] += product
 
-        trailing_adds(width, products, add)
+        trailing_adds(width, 4, products, add)
         return 0
 
     lax.fori_loop(0, tiles_ref.shape[0] // width, body, 0)

time: 171 us -> 170 us (level)
  no operation moved by 1% of the time
where the time goes in v12:
time: 170 us
  blocking collectives  122 us (72%)
  Pallas kernels  19.5 us (11%)
  waiting for transfers between devices  15.5 us (9%)
  starting transfers between devices  11.9 us (7%)
    all_to_all x2, blocking collectives, per_device(): recv = lax.all_to_all(send, ('row', 'col'), 0, 0, tiled=True)  62.8 us
    all_to_all x2, blocking collectives, per_device(): probe = lax.all_to_all(send, ('row', 'col'), 0, 0, tiled=True)  59.3 us
    ppermute x8, waiting for transfers between devices, swap_chip(): lax.ppermute(value, 'col', [(i, i ^ 2 << (step + i % 2) % bits) for i in...  12.3 us
    ppermute x8, starting transfers between devices, swap_chip(): lax.ppermute(value, 'col', [(i, i ^ 2 << (step + i % 2) % bits) for i in...  10.5 us
    pallas_call x2, Pallas kernels, forward(): pl.pallas_call(functools.partial(forward_kernel, dims, pitch), in_specs=[...  7.13 us
    pallas_call x1, Pallas kernels, first_backward(): pl.pallas_call(functools.partial(first_backward_kernel, dims, pitch), in_...  4.74 us
  transfers between devices with their start and end apart: 16, of which 10 were waited for; matrix products, arithmetic and copies ran while one was open for 0% of the time, Pallas kernels for 1%

profile of v12, /device:TPU:0, one launch (start us, length us, event | category | flops | bytes accessed | tf_op | source)
XLA Modules:
  0.0 170.1 jit_solution(6067255970683202353)
XLA Ops:
  0.7 4.7 %first_backward_products.1 = (bf16[32,128,128]{2,1,0:T(8,128)(2,1)S(1)}, bf16[256,128,128]{2,1,0:T(8,128)(2,1)S(1)}) custom-call(s32[1]{0:T(128)} %bitcast.core_ref, s32[256]{0:T(256)} %bitcast.22, s32[256]{0:T(256)} %bitcast.26, f32[2,128,8,128]{3,2,1,0:T(8,128)} %bitcast.19, bf16[256,128,128]{2,1,0:T(8,128)(2,1)} %bitcast.34), custom_call_target="tpu_custom_call" | custom-call | flops 134217728 | bytes 4194304 | tf_op jit(solution)/shard_map/first_backward_products/pallas_call | solution.py:378
  5.4 33.3 %all_to_all.20.refs_0_ = bf16[32,128,128]{2,1,0:T(8,128)(2,1)S(1)} all-to-all(bf16[32,128,128]{2,1,0:T(8,128)(2,1)S(1)} %get-tuple-element.23), channel_id=1, replica_groups=mesh['row'=4,'col'=8] {'row','col'}, dimensions={0} | all-to-all | bytes 2097152 | tf_op jit(solution)/shard_map/all_to_all | solution.py:521
  38.8 0.9 primal_update.2
  39.8 29.7 %all_to_all.21.probe_ref = bf16[32,128,128]{2,1,0:T(8,128)(2,1)S(1)} all-to-all(bf16[32,128,128]{2,1,0:T(8,128)(2,1)S(1)} %get-tuple-element.24), channel_id=1, replica_groups=mesh['row'=4,'col'=8] {'row','col'}, dimensions={0} | all-to-all | bytes 2097152 | tf_op jit(solution)/shard_map/all_to_all | solution.py:524
  69.4 3.6 %forward_products.2 = (f32[2048,128]{1,0:T(8,128)S(1)}, bf16[512,128]{1,0:T(8,128)(2,1)S(1)}, bf16[512,128]{1,0:T(8,128)(2,1)S(1)}) custom-call(s32[1]{0:T(128)} %bitcast.core_ref, s32[256]{0:T(256)S(1)} %bitcast.23, s32[256]{0:T(256)S(1)} %bitcast.27, bf16[32,128,128]{2,1,0:T(8,128)(2,1)S(1)} %all_to_all.21.probe_ref, ...), custom_call_target="tpu_custom_call" | custom-call | flops 134217728 | bytes 4194304 | tf_op jit(solution)/shard_map/forward_products/pallas_call | solution.py:421
  73.0 0.1 collective-permute-start
  73.1 0.5 collective-permute-start.3
  73.6 0.8 collective-permute-done.other_ref
  74.5 1.5 collective-permute-start.1
  76.0 0.0 collective-permute-done.3.other_ref
  76.0 0.6 collective-permute-start.4
  76.6 2.8 %collective-permute-done.1.second_ref.refs_0_ = bf16[512,128]{1,0:T(8,128)(2,1)S(1)} collective-permute-done((bf16[512,128]{1,0:T(8,128)(2,1)S(1)}, bf16[512,128]{1,0:T(8,128)(2,1)S(1)}, u32[]{:S(2)}, u32[]{:S(2)}) %collective-permute-start.1) | collective-permute-done | bytes 131104 | tf_op jit(solution)/shard_map/ppermute | solution.py:452
  79.5 1.5 collective-permute-start.2
  81.1 0.0 collective-permute-done.4.second_ref.refs_0_
  81.1 1.5 collective-permute-start.5
  82.6 1.9 %collective-permute-done.2.refs_1_ = bf16[512,128]{1,0:T(8,128)(2,1)S(1)} collective-permute-done((bf16[512,128]{1,0:T(8,128)(2,1)S(1)}, bf16[512,128]{1,0:T(8,128)(2,1)S(1)}, u32[]{:S(2)}, u32[]{:S(2)}) %collective-permute-start.2) | collective-permute-done | bytes 131104 | tf_op jit(solution)/shard_map/ppermute | solution.py:452
  84.6 0.1 dual_update.4
  84.7 0.1 collective-permute-start.6
  84.8 1.4 collective-permute-done.5.refs_1_
  86.1 0.1 dual_update.5
  86.3 0.1 collective-permute-start.7
  86.3 0.1 clear_sums.1._
  86.5 0.0 collective-permute-done.6.refs_2_
  86.5 1.2 collective-permute-done.7.refs_3_
  87.7 3.1 %backward_products.1 = (bf16[32,128,128]{2,1,0:T(8,128)(2,1)S(1)}, f32[6144,128]{1,0:T(8,128)S(1)}) custom-call(s32[1]{0:T(128)} %bitcast.core_ref, s32[256]{0:T(256)S(1)} %bitcast.24, s32[256]{0:T(256)S(1)} %bitcast.28, bf16[256,128,128]{2,1,0:T(8,128)(2,1)S(1)} %get-tuple-element.22.tiles_ref, ...), custom_call_target="tpu_custom_call", output_to_operand_aliasing={{1}: (4, {})} | custom-call | flops 134217728 | bytes 4194304 | tf_op jit(solution)/shard_map/backward_products/pallas_call | solution.py:408
  90.8 29.5 %all_to_all.22.refs_0_ = bf16[32,128,128]{2,1,0:T(8,128)(2,1)S(1)} all-to-all(bf16[32,128,128]{2,1,0:T(8,128)(2,1)S(1)} %get-tuple-element.30), channel_id=1, replica_groups=mesh['row'=4,'col'=8] {'row','col'}, dimensions={0} | all-to-all | bytes 2097152 | tf_op jit(solution)/shard_map/all_to_all | solution.py:521
  120.3 0.8 primal_update.3
  121.1 29.7 %all_to_all.23.probe_ref = bf16[32,128,128]{2,1,0:T(8,128)(2,1)S(1)} all-to-all(bf16[32,128,128]{2,1,0:T(8,128)(2,1)S(1)} %get-tuple-element.34), channel_id=1, replica_groups=mesh['row'=4,'col'=8] {'row','col'}, dimensions={0} | all-to-all | bytes 2097152 | tf_op jit(solution)/shard_map/all_to_all | solution.py:524
  150.8 3.6 %forward_products.3 = (f32[2048,128]{1,0:T(8,128)S(1)}, bf16[512,128]{1,0:T(8,128)(2,1)S(1)}, bf16[512,128]{1,0:T(8,128)(2,1)S(1)}) custom-call(s32[1]{0:T(128)} %bitcast.core_ref, s32[256]{0:T(256)S(1)} %bitcast.25, s32[256]{0:T(256)S(1)} %bitcast.29, bf16[32,128,128]{2,1,0:T(8,128)(2,1)S(1)} %all_to_all.23.probe_ref, ...), custom_call_target="tpu_custom_call" | custom-call | flops 134217728 | bytes 4194304 | tf_op jit(solution)/shard_map/forward_products/pallas_call | solution.py:421
  154.4 0.1 collective-permute-start.8
  154.4 0.5 collective-permute-start.11
  154.9 0.8 collective-permute-done.8.other_ref
  155.8 1.5 collective-permute-start.9
  157.3 0.0 collective-permute-done.11.other_ref
  157.4 0.6 collective-permute-start.12
  158.0 2.8 %collective-permute-done.9.second_ref.refs_0_ = bf16[512,128]{1,0:T(8,128)(2,1)S(1)} collective-permute-done((bf16[512,128]{1,0:T(8,128)(2,1)S(1)}, bf16[512,128]{1,0:T(8,128)(2,1)S(1)}, u32[]{:S(2)}, u32[]{:S(2)}) %collective-permute-start.9) | collective-permute-done | bytes 131104 | tf_op jit(solution)/shard_map/ppermute | solution.py:452
  160.9 1.6 collective-permute-start.10
  162.5 1.5 collective-permute-start.13
  164.0 1.9 %collective-permute-done.10.refs_1_ = bf16[512,128]{1,0:T(8,128)(2,1)S(1)} collective-permute-done((bf16[512,128]{1,0:T(8,128)(2,1)S(1)}, bf16[512,128]{1,0:T(8,128)(2,1)S(1)}, u32[]{:S(2)}, u32[]{:S(2)}) %collective-permute-start.10) | collective-permute-done | bytes 131104 | tf_op jit(solution)/shard_map/ppermute | solution.py:452
  165.9 0.1 dual_update.6.refs_0_
  166.0 0.1 collective-permute-start.14
  166.1 1.4 collective-permute-done.13.refs_1_
  167.5 0.1 dual_update.7.refs_1_
  167.6 0.1 collective-permute-start.15
  167.7 0.0 collective-permute-done.14.refs_2_
  167.7 1.1 own_results.1
  168.8 0.4 collective-permute-done.15.refs_0_
  169.2 0.7 other_results.1
  (25 shorter events, 0.3 us)
Async XLA Ops:
  0.6 68.8 %copy-start.5 = (s32[1,1,256]{2,1,0:T(1,128)S(1)}, s32[1,1,256]{2,1,0:T(1,128)}, u32[]{:S(2)}) copy-start(s32[1,1,256]{2,1,0:T(1,128)} %param.11) | copy-start | bytes 3076
  0.6 68.8 %copy-start.4 = (s32[1,1,256]{2,1,0:T(1,128)S(1)}, s32[1,1,256]{2,1,0:T(1,128)}, u32[]{:S(2)}) copy-start(s32[1,1,256]{2,1,0:T(1,128)} %param.10) | copy-start | bytes 3076
  0.7 38.1 %copy-start.3 = (f32[128,256]{1,0:T(8,128)S(1)}, f32[128,256]{1,0:T(8,128)}, u32[]{:S(2)}) copy-start(f32[128,256]{1,0:T(8,128)} %refs_3_.1) | copy-start | bytes 393220
  0.7 38.1 %copy-start.7 = (s32[256]{0:T(256)S(1)}, s32[256]{0:T(256)}, u32[]{:S(2)}) copy-start(s32[256]{0:T(256)} %param.16) | copy-start | bytes 3076
  0.7 38.1 %copy-start.6 = (s32[256]{0:T(256)S(1)}, s32[256]{0:T(256)}, u32[]{:S(2)}) copy-start(s32[256]{0:T(256)} %param.15) | copy-start | bytes 3076
  0.7 38.1 %copy-start.2 = (f32[4,128,256]{2,1,0:T(8,128)S(1)}, f32[4,128,256]{2,1,0:T(8,128)}, u32[]{:S(2)}) copy-start(f32[4,128,256]{2,1,0:T(8,128)} %refs_1_.1) | copy-start | bytes 1572868
  38.8 45.8 %copy-start = (s32[16,16384]{1,0:T(8,128)S(1)}, s32[16,16384]{1,0:T(8,128)}, u32[]{:S(2)}) copy-start(s32[16,16384]{1,0:T(8,128)} %param.17) | copy-start | bytes 3145732
  38.8 45.8 %copy-start.1 = (f32[16,16384]{1,0:T(8,128)S(1)}, f32[16,16384]{1,0:T(8,128)}, u32[]{:S(2)}) copy-start(f32[16,16384]{1,0:T(8,128)} %param.13) | copy-start | bytes 3145732
  73.0 1.4 collective-permute-start
  73.1 2.9 %collective-permute-start.3 = (bf16[512,128]{1,0:T(8,128)(2,1)S(1)}, bf16[512,128]{1,0:T(8,128)(2,1)S(1)}, u32[]{:S(2)}, u32[]{:S(2)}) collective-permute-start(bf16[512,128]{1,0:T(8,128)(2,1)S(1)} %get-tuple-element.28), channel_id=1, source_target_pairs={{0,1},{1,0},{2,3},{3,2},{4,5},{5,4},{6,7},{7,6},{8,9},{9,8},{10,11... | collective-permute-start | bytes 393224 | tf_op jit(solution)/shard_map/ppermute | solution.py:447
  74.5 5.0 %collective-permute-start.1 = (bf16[512,128]{1,0:T(8,128)(2,1)S(1)}, bf16[512,128]{1,0:T(8,128)(2,1)S(1)}, u32[]{:S(2)}, u32[]{:S(2)}) collective-permute-start(bf16[512,128]{1,0:T(8,128)(2,1)S(1)} %core_pair_sum.4.first_ref), channel_id=1, source_target_pairs={{0,2},{1,5},{2,0},{3,7},{4,6},{5,1},{6,4},{7,3},{8,10},{9,13},{10,... | collective-permute-start | bytes 393224 | tf_op jit(solution)/shard_map/ppermute | solution.py:452
  76.0 5.1 %collective-permute-start.4 = (bf16[512,128]{1,0:T(8,128)(2,1)S(1)}, bf16[512,128]{1,0:T(8,128)(2,1)S(1)}, u32[]{:S(2)}, u32[]{:S(2)}) collective-permute-start(bf16[512,128]{1,0:T(8,128)(2,1)S(1)} %core_pair_sum.5.first_ref), channel_id=1, source_target_pairs={{0,2},{1,5},{2,0},{3,7},{4,6},{5,1},{6,4},{7,3},{8,10},{9,13},{10,... | collective-permute-start | bytes 393224 | tf_op jit(solution)/shard_map/ppermute | solution.py:452
  79.5 5.0 %collective-permute-start.2 = (bf16[512,128]{1,0:T(8,128)(2,1)S(1)}, bf16[512,128]{1,0:T(8,128)(2,1)S(1)}, u32[]{:S(2)}, u32[]{:S(2)}) collective-permute-start(bf16[512,128]{1,0:T(8,128)(2,1)S(1)} %chip_sum.4), channel_id=1, source_target_pairs={{0,4},{1,3},{2,6},{3,1},{4,0},{5,7},{6,2},{7,5},{8,12},{9,11},{10,... | collective-permute-start | bytes 393224 | tf_op jit(solution)/shard_map/ppermute | solution.py:452
  81.1 5.0 %collective-permute-start.5 = (bf16[512,128]{1,0:T(8,128)(2,1)S(1)}, bf16[512,128]{1,0:T(8,128)(2,1)S(1)}, u32[]{:S(2)}, u32[]{:S(2)}) collective-permute-start(bf16[512,128]{1,0:T(8,128)(2,1)S(1)} %chip_sum.5), channel_id=1, source_target_pairs={{0,4},{1,3},{2,6},{3,1},{4,0},{5,7},{6,2},{7,5},{8,12},{9,11},{10,... | collective-permute-start | bytes 393224 | tf_op jit(solution)/shard_map/ppermute | solution.py:452
  84.7 1.8 %collective-permute-start.6 = (bf16[512,128]{1,0:T(8,128)(2,1)S(1)}, bf16[512,128]{1,0:T(8,128)(2,1)S(1)}, u32[]{:S(2)}, u32[]{:S(2)}) collective-permute-start(bf16[512,128]{1,0:T(8,128)(2,1)S(1)} %get-tuple-element.27.refs_0_), channel_id=1, source_target_pairs={{0,1},{1,0},{2,3},{3,2},{4,5},{5,4},{6,7},{7,6},{8,9},{9,8},{10,11... | collective-permute-start | bytes 393224 | tf_op jit(solution)/shard_map/ppermute | solution.py:447
  86.3 1.4 collective-permute-start.7
  154.4 1.4 collective-permute-start.8
  154.4 2.9 %collective-permute-start.11 = (bf16[512,128]{1,0:T(8,128)(2,1)S(1)}, bf16[512,128]{1,0:T(8,128)(2,1)S(1)}, u32[]{:S(2)}, u32[]{:S(2)}) collective-permute-start(bf16[512,128]{1,0:T(8,128)(2,1)S(1)} %get-tuple-element.38), channel_id=1, source_target_pairs={{0,1},{1,0},{2,3},{3,2},{4,5},{5,4},{6,7},{7,6},{8,9},{9,8},{10,11... | collective-permute-start | bytes 393224 | tf_op jit(solution)/shard_map/ppermute | solution.py:447
  155.8 5.0 %collective-permute-start.9 = (bf16[512,128]{1,0:T(8,128)(2,1)S(1)}, bf16[512,128]{1,0:T(8,128)(2,1)S(1)}, u32[]{:S(2)}, u32[]{:S(2)}) collective-permute-start(bf16[512,128]{1,0:T(8,128)(2,1)S(1)} %core_pair_sum.6.first_ref), channel_id=1, source_target_pairs={{0,2},{1,5},{2,0},{3,7},{4,6},{5,1},{6,4},{7,3},{8,10},{9,13},{10,... | collective-permute-start | bytes 393224 | tf_op jit(solution)/shard_map/ppermute | solution.py:452
  157.4 5.1 %collective-permute-start.12 = (bf16[512,128]{1,0:T(8,128)(2,1)S(1)}, bf16[512,128]{1,0:T(8,128)(2,1)S(1)}, u32[]{:S(2)}, u32[]{:S(2)}) collective-permute-start(bf16[512,128]{1,0:T(8,128)(2,1)S(1)} %core_pair_sum.7.first_ref), channel_id=1, source_target_pairs={{0,2},{1,5},{2,0},{3,7},{4,6},{5,1},{6,4},{7,3},{8,10},{9,13},{10,... | collective-permute-start | bytes 393224 | tf_op jit(solution)/shard_map/ppermute | solution.py:452
  160.9 5.0 %collective-permute-start.10 = (bf16[512,128]{1,0:T(8,128)(2,1)S(1)}, bf16[512,128]{1,0:T(8,128)(2,1)S(1)}, u32[]{:S(2)}, u32[]{:S(2)}) collective-permute-start(bf16[512,128]{1,0:T(8,128)(2,1)S(1)} %chip_sum.6), channel_id=1, source_target_pairs={{0,4},{1,3},{2,6},{3,1},{4,0},{5,7},{6,2},{7,5},{8,12},{9,11},{10,... | collective-permute-start | bytes 393224 | tf_op jit(solution)/shard_map/ppermute | solution.py:452
  162.5 5.0 %collective-permute-start.13 = (bf16[512,128]{1,0:T(8,128)(2,1)S(1)}, bf16[512,128]{1,0:T(8,128)(2,1)S(1)}, u32[]{:S(2)}, u32[]{:S(2)}) collective-permute-start(bf16[512,128]{1,0:T(8,128)(2,1)S(1)} %chip_sum.7), channel_id=1, source_target_pairs={{0,4},{1,3},{2,6},{3,1},{4,0},{5,7},{6,2},{7,5},{8,12},{9,11},{10,... | collective-permute-start | bytes 393224 | tf_op jit(solution)/shard_map/ppermute | solution.py:452
  166.0 1.7 collective-permute-start.14
  167.6 1.6 collective-permute-start.15

commit v13 on v12

--- a/solution.py
+++ b/solution.py
@@ -12,7 +12,7 @@
 SIGMA_STEP = 0.2
 PARTS = 2
 UNROLL = 256
-FIRST_UNROLL = 32
+FIRST_LOAD = 16
 TRAIL = 16
 PITCH_PAD = 8
 VMEM_BYTES = 24 * 1024 * 1024
@@ -53,10 +53,12 @@
         add(*item)
 
 
-def backward_blocks(dims, pitch, width, rows_ref, cols_ref, duals_ref, tiles_ref, acc_ref, start):
+def backward_blocks(dims, pitch, width, rows_ref, cols_ref, duals_ref, tiles_ref, acc_ref, start, ready=None):
     scen = dims[0] * dims[2]
 
     def products(u):
+        if ready is not None:
+            ready(u)
         pair = stacked_pair(duals_ref[rows_ref[start + u]], duals_ref[rows_ref[start + u + 1]])
         both = tiles_ref[pl.ds(start + u, 2)]
         result = jnp.dot(pair, both.reshape(-1, both.shape[2]), preferred_element_type=jnp.float32)
@@ -121,15 +123,11 @@
     bands = [bands_ref[a].astype(jnp.bfloat16) for a in range(bands_ref.shape[0])]
     duals_ref[...] = jnp.concatenate(bands, axis=1)
 
-    def body(index, _):
-        backward_blocks(
-            dims, pitch, FIRST_UNROLL, rows_ref, cols_ref, duals_ref, tiles_ref, acc_ref, index * FIRST_UNROLL
-        )
-        return 0
-
-    for i, copy in enumerate(copies):
-        copy.wait()
-        lax.fori_loop(i * chunk // FIRST_UNROLL, (i + 1) * chunk // FIRST_UNROLL, body, 0)
+    def ready(u):
+        if u % chunk == 0:
+            copies[u // chunk].wait()
+
+    backward_blocks(dims, pitch, count, rows_ref, cols_ref, duals_ref, tiles_ref, acc_ref, 0, ready)
     write_messages(dims, pitch, acc_ref, out_ref)
 
 
@@ -386,7 +384,7 @@
                 pltpu.VMEM(duals.shape, jnp.float32),
                 picked_duals,
                 acc_cols,
-                pltpu.SemaphoreType.DMA((count // FIRST_UNROLL + 3,)),
+                pltpu.SemaphoreType.DMA((count // FIRST_LOAD + 3,)),
             ],
             compiler_params=params(),
             cost_estimate=cost,

time: 170 us -> 172 us (1.012)
  Pallas kernels: 19.5 us -> 21.3 us
    pallas_call x1, Pallas kernels: 4.74 us -> 6.62 us  [first_backward(): pl.pallas_call(functools.partial(first_backward_kernel, dims, pitch), in_...]
where the time goes in v13:
time: 172 us
  blocking collectives  122 us (71%)
  Pallas kernels  21.3 us (12%)
  waiting for transfers between devices  15.5 us (9%)
  starting transfers between devices  11.9 us (7%)
    all_to_all x2, blocking collectives, per_device(): recv = lax.all_to_all(send, ('row', 'col'), 0, 0, tiled=True)  62.8 us
    all_to_all x2, blocking collectives, per_device(): probe = lax.all_to_all(send, ('row', 'col'), 0, 0, tiled=True)  59.3 us
    ppermute x8, waiting for transfers between devices, swap_chip(): lax.ppermute(value, 'col', [(i, i ^ 2 << (step + i % 2) % bits) for i in...  12.2 us
    ppermute x8, starting transfers between devices, swap_chip(): lax.ppermute(value, 'col', [(i, i ^ 2 << (step + i % 2) % bits) for i in...  10.5 us
    pallas_call x2, Pallas kernels, forward(): pl.pallas_call(functools.partial(forward_kernel, dims, pitch), in_specs=[...  7.12 us
    pallas_call x1, Pallas kernels, first_backward(): pl.pallas_call(functools.partial(first_backward_kernel, dims, pitch), in_...  6.62 us
  transfers between devices with their start and end apart: 16, of which 10 were waited for; matrix products, arithmetic and copies ran while one was open for 0% of the time, Pallas kernels for 1%

profile of v13, /device:TPU:0, one launch (start us, length us, event | category | flops | bytes accessed | tf_op | source)
XLA Modules:
  0.0 172.0 jit_solution(12226163423024055662)
XLA Ops:
  0.7 6.6 %first_backward_products.1 = (bf16[32,128,128]{2,1,0:T(8,128)(2,1)S(1)}, bf16[256,128,128]{2,1,0:T(8,128)(2,1)S(1)}) custom-call(s32[1]{0:T(128)} %bitcast.core_ref, s32[256]{0:T(256)} %bitcast.22, s32[256]{0:T(256)} %bitcast.26, f32[2,128,8,128]{3,2,1,0:T(8,128)} %bitcast.19, bf16[256,128,128]{2,1,0:T(8,128)(2,1)} %bitcast.34), custom_call_target="tpu_custom_call" | custom-call | flops 134217728 | bytes 4194304 | tf_op jit(solution)/shard_map/first_backward_products/pallas_call | solution.py:376
  7.3 33.3 %all_to_all.20.refs_0_ = bf16[32,128,128]{2,1,0:T(8,128)(2,1)S(1)} all-to-all(bf16[32,128,128]{2,1,0:T(8,128)(2,1)S(1)} %get-tuple-element.23), channel_id=1, replica_groups=mesh['row'=4,'col'=8] {'row','col'}, dimensions={0} | all-to-all | bytes 2097152 | tf_op jit(solution)/shard_map/all_to_all | solution.py:519
  40.7 0.9 primal_update.2
  41.6 29.7 %all_to_all.21.probe_ref = bf16[32,128,128]{2,1,0:T(8,128)(2,1)S(1)} all-to-all(bf16[32,128,128]{2,1,0:T(8,128)(2,1)S(1)} %get-tuple-element.24), channel_id=1, replica_groups=mesh['row'=4,'col'=8] {'row','col'}, dimensions={0} | all-to-all | bytes 2097152 | tf_op jit(solution)/shard_map/all_to_all | solution.py:522
  71.3 3.6 %forward_products.2 = (f32[2048,128]{1,0:T(8,128)S(1)}, bf16[512,128]{1,0:T(8,128)(2,1)S(1)}, bf16[512,128]{1,0:T(8,128)(2,1)S(1)}) custom-call(s32[1]{0:T(128)} %bitcast.core_ref, s32[256]{0:T(256)S(1)} %bitcast.23, s32[256]{0:T(256)S(1)} %bitcast.27, bf16[32,128,128]{2,1,0:T(8,128)(2,1)S(1)} %all_to_all.21.probe_ref, ...), custom_call_target="tpu_custom_call" | custom-call | flops 134217728 | bytes 4194304 | tf_op jit(solution)/shard_map/forward_products/pallas_call | solution.py:419
  74.9 0.1 collective-permute-start
  75.0 0.5 collective-permute-start.3
  75.5 0.8 collective-permute-done.other_ref
  76.3 1.5 collective-permute-start.1
  77.9 0.0 collective-permute-done.3.other_ref
  77.9 0.6 collective-permute-start.4
  78.5 2.8 %collective-permute-done.1.second_ref.refs_0_ = bf16[512,128]{1,0:T(8,128)(2,1)S(1)} collective-permute-done((bf16[512,128]{1,0:T(8,128)(2,1)S(1)}, bf16[512,128]{1,0:T(8,128)(2,1)S(1)}, u32[]{:S(2)}, u32[]{:S(2)}) %collective-permute-start.1) | collective-permute-done | bytes 131104 | tf_op jit(solution)/shard_map/ppermute | solution.py:450
  81.4 1.5 collective-permute-start.2
  82.9 0.0 collective-permute-done.4.second_ref.refs_0_
  83.0 1.5 collective-permute-start.5
  84.5 1.9 %collective-permute-done.2.refs_1_ = bf16[512,128]{1,0:T(8,128)(2,1)S(1)} collective-permute-done((bf16[512,128]{1,0:T(8,128)(2,1)S(1)}, bf16[512,128]{1,0:T(8,128)(2,1)S(1)}, u32[]{:S(2)}, u32[]{:S(2)}) %collective-permute-start.2) | collective-permute-done | bytes 131104 | tf_op jit(solution)/shard_map/ppermute | solution.py:450
  86.4 0.1 dual_update.4
  86.6 0.1 collective-permute-start.6
  86.6 1.4 collective-permute-done.5.refs_1_
  88.0 0.1 dual_update.5
  88.1 0.1 collective-permute-start.7
  88.2 0.1 clear_sums.1._
  88.4 0.0 collective-permute-done.6.refs_2_
  88.4 1.2 collective-permute-done.7.refs_3_
  89.6 3.1 %backward_products.1 = (bf16[32,128,128]{2,1,0:T(8,128)(2,1)S(1)}, f32[6144,128]{1,0:T(8,128)S(1)}) custom-call(s32[1]{0:T(128)} %bitcast.core_ref, s32[256]{0:T(256)S(1)} %bitcast.24, s32[256]{0:T(256)S(1)} %bitcast.28, bf16[256,128,128]{2,1,0:T(8,128)(2,1)S(1)} %get-tuple-element.22.tiles_ref, ...), custom_call_target="tpu_custom_call", output_to_operand_aliasing={{1}: (4, {})} | custom-call | flops 134217728 | bytes 4194304 | tf_op jit(solution)/shard_map/backward_products/pallas_call | solution.py:406
  92.7 29.5 %all_to_all.22.refs_0_ = bf16[32,128,128]{2,1,0:T(8,128)(2,1)S(1)} all-to-all(bf16[32,128,128]{2,1,0:T(8,128)(2,1)S(1)} %get-tuple-element.30), channel_id=1, replica_groups=mesh['row'=4,'col'=8] {'row','col'}, dimensions={0} | all-to-all | bytes 2097152 | tf_op jit(solution)/shard_map/all_to_all | solution.py:519
  122.2 0.8 primal_update.3
  123.0 29.7 %all_to_all.23.probe_ref = bf16[32,128,128]{2,1,0:T(8,128)(2,1)S(1)} all-to-all(bf16[32,128,128]{2,1,0:T(8,128)(2,1)S(1)} %get-tuple-element.34), channel_id=1, replica_groups=mesh['row'=4,'col'=8] {'row','col'}, dimensions={0} | all-to-all | bytes 2097152 | tf_op jit(solution)/shard_map/all_to_all | solution.py:522
  152.7 3.6 %forward_products.3 = (f32[2048,128]{1,0:T(8,128)S(1)}, bf16[512,128]{1,0:T(8,128)(2,1)S(1)}, bf16[512,128]{1,0:T(8,128)(2,1)S(1)}) custom-call(s32[1]{0:T(128)} %bitcast.core_ref, s32[256]{0:T(256)S(1)} %bitcast.25, s32[256]{0:T(256)S(1)} %bitcast.29, bf16[32,128,128]{2,1,0:T(8,128)(2,1)S(1)} %all_to_all.23.probe_ref, ...), custom_call_target="tpu_custom_call" | custom-call | flops 134217728 | bytes 4194304 | tf_op jit(solution)/shard_map/forward_products/pallas_call | solution.py:419
  156.2 0.1 collective-permute-start.8
  156.3 0.5 collective-permute-start.11
  156.8 0.8 collective-permute-done.8.other_ref
  157.7 1.5 collective-permute-start.9
  159.2 0.0 collective-permute-done.11.other_ref
  159.2 0.6 collective-permute-start.12
  159.9 2.8 %collective-permute-done.9.second_ref.refs_0_ = bf16[512,128]{1,0:T(8,128)(2,1)S(1)} collective-permute-done((bf16[512,128]{1,0:T(8,128)(2,1)S(1)}, bf16[512,128]{1,0:T(8,128)(2,1)S(1)}, u32[]{:S(2)}, u32[]{:S(2)}) %collective-permute-start.9) | collective-permute-done | bytes 131104 | tf_op jit(solution)/shard_map/ppermute | solution.py:450
  162.8 1.5 collective-permute-start.10
  164.3 1.5 collective-permute-start.13
  165.9 1.9 %collective-permute-done.10.refs_1_ = bf16[512,128]{1,0:T(8,128)(2,1)S(1)} collective-permute-done((bf16[512,128]{1,0:T(8,128)(2,1)S(1)}, bf16[512,128]{1,0:T(8,128)(2,1)S(1)}, u32[]{:S(2)}, u32[]{:S(2)}) %collective-permute-start.10) | collective-permute-done | bytes 131104 | tf_op jit(solution)/shard_map/ppermute | solution.py:450
  167.8 0.1 dual_update.6.refs_0_
  167.9 0.1 collective-permute-start.14
  168.0 1.4 collective-permute-done.13.refs_1_
  169.4 0.1 dual_update.7.refs_1_
  169.5 0.1 collective-permute-start.15
  169.6 0.0 collective-permute-done.14.refs_2_
  169.6 1.1 own_results.1
  170.7 0.4 collective-permute-done.15.refs_0_
  171.1 0.7 other_results.1
  (25 shorter events, 0.3 us)
Async XLA Ops:
  0.6 70.7 %copy-start.5 = (s32[1,1,256]{2,1,0:T(1,128)S(1)}, s32[1,1,256]{2,1,0:T(1,128)}, u32[]{:S(2)}) copy-start(s32[1,1,256]{2,1,0:T(1,128)} %param.11) | copy-start | bytes 3076
  0.6 70.7 %copy-start.4 = (s32[1,1,256]{2,1,0:T(1,128)S(1)}, s32[1,1,256]{2,1,0:T(1,128)}, u32[]{:S(2)}) copy-start(s32[1,1,256]{2,1,0:T(1,128)} %param.10) | copy-start | bytes 3076
  0.7 40.0 %copy-start.3 = (f32[128,256]{1,0:T(8,128)S(1)}, f32[128,256]{1,0:T(8,128)}, u32[]{:S(2)}) copy-start(f32[128,256]{1,0:T(8,128)} %refs_3_.1) | copy-start | bytes 393220
  0.7 40.0 %copy-start.7 = (s32[256]{0:T(256)S(1)}, s32[256]{0:T(256)}, u32[]{:S(2)}) copy-start(s32[256]{0:T(256)} %param.16) | copy-start | bytes 3076
  0.7 40.0 %copy-start.6 = (s32[256]{0:T(256)S(1)}, s32[256]{0:T(256)}, u32[]{:S(2)}) copy-start(s32[256]{0:T(256)} %param.15) | copy-start | bytes 3076
  0.7 40.0 %copy-start.2 = (f32[4,128,256]{2,1,0:T(8,128)S(1)}, f32[4,128,256]{2,1,0:T(8,128)}, u32[]{:S(2)}) copy-start(f32[4,128,256]{2,1,0:T(8,128)} %refs_1_.1) | copy-start | bytes 1572868
  40.7 45.8 %copy-start = (s32[16,16384]{1,0:T(8,128)S(1)}, s32[16,16384]{1,0:T(8,128)}, u32[]{:S(2)}) copy-start(s32[16,16384]{1,0:T(8,128)} %param.17) | copy-start | bytes 3145732
  40.7 45.8 %copy-start.1 = (f32[16,16384]{1,0:T(8,128)S(1)}, f32[16,16384]{1,0:T(8,128)}, u32[]{:S(2)}) copy-start(f32[16,16384]{1,0:T(8,128)} %param.13) | copy-start | bytes 3145732
  74.9 1.4 collective-permute-start
  75.0 2.9 %collective-permute-start.3 = (bf16[512,128]{1,0:T(8,128)(2,1)S(1)}, bf16[512,128]{1,0:T(8,128)(2,1)S(1)}, u32[]{:S(2)}, u32[]{:S(2)}) collective-permute-start(bf16[512,128]{1,0:T(8,128)(2,1)S(1)} %get-tuple-element.28), channel_id=1, source_target_pairs={{0,1},{1,0},{2,3},{3,2},{4,5},{5,4},{6,7},{7,6},{8,9},{9,8},{10,11... | collective-permute-start | bytes 393224 | tf_op jit(solution)/shard_map/ppermute | solution.py:445
  76.3 5.0 %collective-permute-start.1 = (bf16[512,128]{1,0:T(8,128)(2,1)S(1)}, bf16[512,128]{1,0:T(8,128)(2,1)S(1)}, u32[]{:S(2)}, u32[]{:S(2)}) collective-permute-start(bf16[512,128]{1,0:T(8,128)(2,1)S(1)} %core_pair_sum.4.first_ref), channel_id=1, source_target_pairs={{0,2},{1,5},{2,0},{3,7},{4,6},{5,1},{6,4},{7,3},{8,10},{9,13},{10,... | collective-permute-start | bytes 393224 | tf_op jit(solution)/shard_map/ppermute | solution.py:450
  77.9 5.1 %collective-permute-start.4 = (bf16[512,128]{1,0:T(8,128)(2,1)S(1)}, bf16[512,128]{1,0:T(8,128)(2,1)S(1)}, u32[]{:S(2)}, u32[]{:S(2)}) collective-permute-start(bf16[512,128]{1,0:T(8,128)(2,1)S(1)} %core_pair_sum.5.first_ref), channel_id=1, source_target_pairs={{0,2},{1,5},{2,0},{3,7},{4,6},{5,1},{6,4},{7,3},{8,10},{9,13},{10,... | collective-permute-start | bytes 393224 | tf_op jit(solution)/shard_map/ppermute | solution.py:450
  81.4 5.0 %collective-permute-start.2 = (bf16[512,128]{1,0:T(8,128)(2,1)S(1)}, bf16[512,128]{1,0:T(8,128)(2,1)S(1)}, u32[]{:S(2)}, u32[]{:S(2)}) collective-permute-start(bf16[512,128]{1,0:T(8,128)(2,1)S(1)} %chip_sum.4), channel_id=1, source_target_pairs={{0,4},{1,3},{2,6},{3,1},{4,0},{5,7},{6,2},{7,5},{8,12},{9,11},{10,... | collective-permute-start | bytes 393224 | tf_op jit(solution)/shard_map/ppermute | solution.py:450
  83.0 5.0 %collective-permute-start.5 = (bf16[512,128]{1,0:T(8,128)(2,1)S(1)}, bf16[512,128]{1,0:T(8,128)(2,1)S(1)}, u32[]{:S(2)}, u32[]{:S(2)}) collective-permute-start(bf16[512,128]{1,0:T(8,128)(2,1)S(1)} %chip_sum.5), channel_id=1, source_target_pairs={{0,4},{1,3},{2,6},{3,1},{4,0},{5,7},{6,2},{7,5},{8,12},{9,11},{10,... | collective-permute-start | bytes 393224 | tf_op jit(solution)/shard_map/ppermute | solution.py:450
  86.6 1.8 %collective-permute-start.6 = (bf16[512,128]{1,0:T(8,128)(2,1)S(1)}, bf16[512,128]{1,0:T(8,128)(2,1)S(1)}, u32[]{:S(2)}, u32[]{:S(2)}) collective-permute-start(bf16[512,128]{1,0:T(8,128)(2,1)S(1)} %get-tuple-element.27.refs_0_), channel_id=1, source_target_pairs={{0,1},{1,0},{2,3},{3,2},{4,5},{5,4},{6,7},{7,6},{8,9},{9,8},{10,11... | collective-permute-start | bytes 393224 | tf_op jit(solution)/shard_map/ppermute | solution.py:445
  88.1 1.4 collective-permute-start.7
  156.2 1.4 collective-permute-start.8
  156.3 2.9 %collective-permute-start.11 = (bf16[512,128]{1,0:T(8,128)(2,1)S(1)}, bf16[512,128]{1,0:T(8,128)(2,1)S(1)}, u32[]{:S(2)}, u32[]{:S(2)}) collective-permute-start(bf16[512,128]{1,0:T(8,128)(2,1)S(1)} %get-tuple-element.38), channel_id=1, source_target_pairs={{0,1},{1,0},{2,3},{3,2},{4,5},{5,4},{6,7},{7,6},{8,9},{9,8},{10,11... | collective-permute-start | bytes 393224 | tf_op jit(solution)/shard_map/ppermute | solution.py:445
  157.7 5.0 %collective-permute-start.9 = (bf16[512,128]{1,0:T(8,128)(2,1)S(1)}, bf16[512,128]{1,0:T(8,128)(2,1)S(1)}, u32[]{:S(2)}, u32[]{:S(2)}) collective-permute-start(bf16[512,128]{1,0:T(8,128)(2,1)S(1)} %core_pair_sum.6.first_ref), channel_id=1, source_target_pairs={{0,2},{1,5},{2,0},{3,7},{4,6},{5,1},{6,4},{7,3},{8,10},{9,13},{10,... | collective-permute-start | bytes 393224 | tf_op jit(solution)/shard_map/ppermute | solution.py:450
  159.2 5.0 %collective-permute-start.12 = (bf16[512,128]{1,0:T(8,128)(2,1)S(1)}, bf16[512,128]{1,0:T(8,128)(2,1)S(1)}, u32[]{:S(2)}, u32[]{:S(2)}) collective-permute-start(bf16[512,128]{1,0:T(8,128)(2,1)S(1)} %core_pair_sum.7.first_ref), channel_id=1, source_target_pairs={{0,2},{1,5},{2,0},{3,7},{4,6},{5,1},{6,4},{7,3},{8,10},{9,13},{10,... | collective-permute-start | bytes 393224 | tf_op jit(solution)/shard_map/ppermute | solution.py:450
  162.8 5.0 %collective-permute-start.10 = (bf16[512,128]{1,0:T(8,128)(2,1)S(1)}, bf16[512,128]{1,0:T(8,128)(2,1)S(1)}, u32[]{:S(2)}, u32[]{:S(2)}) collective-permute-start(bf16[512,128]{1,0:T(8,128)(2,1)S(1)} %chip_sum.6), channel_id=1, source_target_pairs={{0,4},{1,3},{2,6},{3,1},{4,0},{5,7},{6,2},{7,5},{8,12},{9,11},{10,... | collective-permute-start | bytes 393224 | tf_op jit(solution)/shard_map/ppermute | solution.py:450
  164.3 5.0 %collective-permute-start.13 = (bf16[512,128]{1,0:T(8,128)(2,1)S(1)}, bf16[512,128]{1,0:T(8,128)(2,1)S(1)}, u32[]{:S(2)}, u32[]{:S(2)}) collective-permute-start(bf16[512,128]{1,0:T(8,128)(2,1)S(1)} %chip_sum.7), channel_id=1, source_target_pairs={{0,4},{1,3},{2,6},{3,1},{4,0},{5,7},{6,2},{7,5},{8,12},{9,11},{10,... | collective-permute-start | bytes 393224 | tf_op jit(solution)/shard_map/ppermute | solution.py:450
  167.9 1.7 collective-permute-start.14
  169.5 1.6 collective-permute-start.15

commit v14 on v12

--- a/solution.py
+++ b/solution.py
@@ -71,24 +71,30 @@
 
 def round_sums(dims, pitch, acc_ref):
     scen, time_block, flight_tiles = dims[0] * dims[2], dims[3], dims[4]
-    lost = [jnp.zeros((scen, acc_ref.shape[1]), jnp.float32)] * flight_tiles
-    for minute in reversed(range(time_block)):
+
+    def body(index, lost):
+        minute, kept = time_block - 1 - index, []
         for f in range(flight_tiles):
-            place = pl.ds((f * time_block + minute) * pitch, scen)
+            place = pl.ds(pl.multiple_of((f * time_block + minute) * pitch, 8), scen)
             value = acc_ref[place, :] + lost[f]
             rounded = value.astype(jnp.bfloat16).astype(jnp.float32)
-            lost[f] = value - rounded
+            kept.append(value - rounded)
             acc_ref[place, :] = rounded
+        return tuple(kept)
+
+    nothing = jnp.zeros((scen, acc_ref.shape[1]), jnp.float32)
+    lax.fori_loop(0, time_block, body, (nothing,) * flight_tiles)
 
 
 def write_messages(dims, pitch, acc_ref, out_ref):
     n_row, n_col, scen_local, time_block, _, own_tiles = dims
     piece = own_tiles * time_block
     round_sums(dims, pitch, acc_ref)
-    for group in range(n_row):
-        for column in range(n_col):
+
+    def body(column, _):
+        for group in range(n_row):
             for j in range(scen_local):
-                base = column * own_tiles * time_block * pitch + group * scen_local + j
+                base = column * (own_tiles * time_block * pitch) + group * scen_local + j
                 parts = [
                     acc_ref[pl.ds(base + f * time_block * pitch, time_block, stride=pitch), :]
                     for f in range(own_tiles)
@@ -96,6 +102,9 @@
                 out_ref[group * n_col + column, pl.ds(j * piece, piece), :] = jnp.concatenate(
                     parts, axis=0
                 ).astype(jnp.bfloat16)
+        return 0
+
+    lax.fori_loop(0, n_col, body, 0)
 
 
 def first_backward_kernel(

time: 170 us -> 172 us (1.012)
  no operation moved by 1% of the time
where the time goes in v14:
time: 172 us
  blocking collectives  122 us (71%)
  Pallas kernels  21.2 us (12%)
  waiting for transfers between devices  15.5 us (9%)
  starting transfers between devices  11.9 us (7%)
    all_to_all x2, blocking collectives, per_device(): recv = lax.all_to_all(send, ('row', 'col'), 0, 0, tiled=True)  62.8 us
    all_to_all x2, blocking collectives, per_device(): probe = lax.all_to_all(send, ('row', 'col'), 0, 0, tiled=True)  59.3 us
    ppermute x8, waiting for transfers between devices, swap_chip(): lax.ppermute(value, 'col', [(i, i ^ 2 << (step + i % 2) % bits) for i in...  12.3 us
    ppermute x8, starting transfers between devices, swap_chip(): lax.ppermute(value, 'col', [(i, i ^ 2 << (step + i % 2) % bits) for i in...  10.5 us
    pallas_call x2, Pallas kernels, forward(): pl.pallas_call(functools.partial(forward_kernel, dims, pitch), in_specs=[...  7.12 us
    pallas_call x1, Pallas kernels, first_backward(): pl.pallas_call(functools.partial(first_backward_kernel, dims, pitch), in_...  5.63 us
    pallas_call x1, Pallas kernels, backward(): pl.pallas_call(functools.partial(backward_kernel, dims, pitch), in_specs=...  4.02 us
  transfers between devices with their start and end apart: 16, of which 10 were waited for; matrix products, arithmetic and copies ran while one was open for 0% of the time, Pallas kernels for 1%

profile of v14, /device:TPU:0, one launch (start us, length us, event | category | flops | bytes accessed | tf_op | source)
XLA Modules:
  0.0 171.9 jit_solution(18139651635695140489)
XLA Ops:
  0.7 5.6 %first_backward_products.1 = (bf16[32,128,128]{2,1,0:T(8,128)(2,1)S(1)}, bf16[256,128,128]{2,1,0:T(8,128)(2,1)S(1)}) custom-call(s32[1]{0:T(128)} %bitcast.core_ref, s32[256]{0:T(256)} %bitcast.22, s32[256]{0:T(256)} %bitcast.26, f32[2,128,8,128]{3,2,1,0:T(8,128)} %bitcast.19, bf16[256,128,128]{2,1,0:T(8,128)(2,1)} %bitcast.34), custom_call_target="tpu_custom_call" | custom-call | flops 134217728 | bytes 4194304 | tf_op jit(solution)/shard_map/first_backward_products/pallas_call | solution.py:387
  6.3 33.3 %all_to_all.20.refs_0_ = bf16[32,128,128]{2,1,0:T(8,128)(2,1)S(1)} all-to-all(bf16[32,128,128]{2,1,0:T(8,128)(2,1)S(1)} %get-tuple-element.23), channel_id=1, replica_groups=mesh['row'=4,'col'=8] {'row','col'}, dimensions={0} | all-to-all | bytes 2097152 | tf_op jit(solution)/shard_map/all_to_all | solution.py:530
  39.7 0.9 primal_update.2
  40.7 29.7 %all_to_all.21.probe_ref = bf16[32,128,128]{2,1,0:T(8,128)(2,1)S(1)} all-to-all(bf16[32,128,128]{2,1,0:T(8,128)(2,1)S(1)} %get-tuple-element.24), channel_id=1, replica_groups=mesh['row'=4,'col'=8] {'row','col'}, dimensions={0} | all-to-all | bytes 2097152 | tf_op jit(solution)/shard_map/all_to_all | solution.py:533
  70.3 3.6 %forward_products.2 = (f32[2048,128]{1,0:T(8,128)S(1)}, bf16[512,128]{1,0:T(8,128)(2,1)S(1)}, bf16[512,128]{1,0:T(8,128)(2,1)S(1)}) custom-call(s32[1]{0:T(128)} %bitcast.core_ref, s32[256]{0:T(256)S(1)} %bitcast.23, s32[256]{0:T(256)S(1)} %bitcast.27, bf16[32,128,128]{2,1,0:T(8,128)(2,1)S(1)} %all_to_all.21.probe_ref, ...), custom_call_target="tpu_custom_call" | custom-call | flops 134217728 | bytes 4194304 | tf_op jit(solution)/shard_map/forward_products/pallas_call | solution.py:430
  73.9 0.1 collective-permute-start
  74.0 0.5 collective-permute-start.3
  74.5 0.8 collective-permute-done.other_ref
  75.3 1.5 collective-permute-start.1
  76.9 0.0 collective-permute-done.3.other_ref
  76.9 0.6 collective-permute-start.4
  77.5 2.8 %collective-permute-done.1.second_ref.refs_0_ = bf16[512,128]{1,0:T(8,128)(2,1)S(1)} collective-permute-done((bf16[512,128]{1,0:T(8,128)(2,1)S(1)}, bf16[512,128]{1,0:T(8,128)(2,1)S(1)}, u32[]{:S(2)}, u32[]{:S(2)}) %collective-permute-start.1) | collective-permute-done | bytes 131104 | tf_op jit(solution)/shard_map/ppermute | solution.py:461
  80.4 1.5 collective-permute-start.2
  82.0 0.0 collective-permute-done.4.second_ref.refs_0_
  82.0 1.5 collective-permute-start.5
  83.5 1.9 %collective-permute-done.2.refs_1_ = bf16[512,128]{1,0:T(8,128)(2,1)S(1)} collective-permute-done((bf16[512,128]{1,0:T(8,128)(2,1)S(1)}, bf16[512,128]{1,0:T(8,128)(2,1)S(1)}, u32[]{:S(2)}, u32[]{:S(2)}) %collective-permute-start.2) | collective-permute-done | bytes 131104 | tf_op jit(solution)/shard_map/ppermute | solution.py:461
  85.5 0.1 dual_update.4
  85.6 0.1 collective-permute-start.6
  85.7 1.4 collective-permute-done.5.refs_1_
  87.0 0.1 dual_update.5
  87.2 0.1 collective-permute-start.7
  87.2 0.1 clear_sums.1._
  87.4 0.0 collective-permute-done.6.refs_2_
  87.4 1.2 collective-permute-done.7.refs_3_
  88.6 4.0 %backward_products.1 = (bf16[32,128,128]{2,1,0:T(8,128)(2,1)S(1)}, f32[6144,128]{1,0:T(8,128)S(1)}) custom-call(s32[1]{0:T(128)} %bitcast.core_ref, s32[256]{0:T(256)S(1)} %bitcast.24, s32[256]{0:T(256)S(1)} %bitcast.28, bf16[256,128,128]{2,1,0:T(8,128)(2,1)S(1)} %get-tuple-element.22.tiles_ref, ...), custom_call_target="tpu_custom_call", output_to_operand_aliasing={{1}: (4, {})} | custom-call | flops 134217728 | bytes 4194304 | tf_op jit(solution)/shard_map/backward_products/pallas_call | solution.py:417
  92.6 29.5 %all_to_all.22.refs_0_ = bf16[32,128,128]{2,1,0:T(8,128)(2,1)S(1)} all-to-all(bf16[32,128,128]{2,1,0:T(8,128)(2,1)S(1)} %get-tuple-element.30), channel_id=1, replica_groups=mesh['row'=4,'col'=8] {'row','col'}, dimensions={0} | all-to-all | bytes 2097152 | tf_op jit(solution)/shard_map/all_to_all | solution.py:530
  122.1 0.8 primal_update.3
  122.9 29.7 %all_to_all.23.probe_ref = bf16[32,128,128]{2,1,0:T(8,128)(2,1)S(1)} all-to-all(bf16[32,128,128]{2,1,0:T(8,128)(2,1)S(1)} %get-tuple-element.34), channel_id=1, replica_groups=mesh['row'=4,'col'=8] {'row','col'}, dimensions={0} | all-to-all | bytes 2097152 | tf_op jit(solution)/shard_map/all_to_all | solution.py:533
  152.6 3.6 %forward_products.3 = (f32[2048,128]{1,0:T(8,128)S(1)}, bf16[512,128]{1,0:T(8,128)(2,1)S(1)}, bf16[512,128]{1,0:T(8,128)(2,1)S(1)}) custom-call(s32[1]{0:T(128)} %bitcast.core_ref, s32[256]{0:T(256)S(1)} %bitcast.25, s32[256]{0:T(256)S(1)} %bitcast.29, bf16[32,128,128]{2,1,0:T(8,128)(2,1)S(1)} %all_to_all.23.probe_ref, ...), custom_call_target="tpu_custom_call" | custom-call | flops 134217728 | bytes 4194304 | tf_op jit(solution)/shard_map/forward_products/pallas_call | solution.py:430
  156.1 0.1 collective-permute-start.8
  156.2 0.5 collective-permute-start.11
  156.7 0.8 collective-permute-done.8.other_ref
  157.6 1.5 collective-permute-start.9
  159.1 0.0 collective-permute-done.11.other_ref
  159.1 0.6 collective-permute-start.12
  159.8 2.8 %collective-permute-done.9.second_ref.refs_0_ = bf16[512,128]{1,0:T(8,128)(2,1)S(1)} collective-permute-done((bf16[512,128]{1,0:T(8,128)(2,1)S(1)}, bf16[512,128]{1,0:T(8,128)(2,1)S(1)}, u32[]{:S(2)}, u32[]{:S(2)}) %collective-permute-start.9) | collective-permute-done | bytes 131104 | tf_op jit(solution)/shard_map/ppermute | solution.py:461
  162.7 1.5 collective-permute-start.10
  164.2 0.0 collective-permute-done.12.second_ref.refs_0_
  164.2 1.5 collective-permute-start.13
  165.8 1.9 %collective-permute-done.10.refs_1_ = bf16[512,128]{1,0:T(8,128)(2,1)S(1)} collective-permute-done((bf16[512,128]{1,0:T(8,128)(2,1)S(1)}, bf16[512,128]{1,0:T(8,128)(2,1)S(1)}, u32[]{:S(2)}, u32[]{:S(2)}) %collective-permute-start.10) | collective-permute-done | bytes 131104 | tf_op jit(solution)/shard_map/ppermute | solution.py:461
  167.7 0.1 dual_update.6.refs_0_
  167.8 0.1 collective-permute-start.14
  167.9 1.4 collective-permute-done.13.refs_1_
  169.3 0.1 dual_update.7.refs_1_
  169.4 0.1 collective-permute-start.15
  169.5 1.1 own_results.1
  170.6 0.4 collective-permute-done.15.refs_0_
  171.0 0.7 other_results.1
  (25 shorter events, 0.3 us)
Async XLA Ops:
  0.6 69.7 %copy-start.5 = (s32[1,1,256]{2,1,0:T(1,128)S(1)}, s32[1,1,256]{2,1,0:T(1,128)}, u32[]{:S(2)}) copy-start(s32[1,1,256]{2,1,0:T(1,128)} %param.11) | copy-start | bytes 3076
  0.6 69.7 %copy-start.4 = (s32[1,1,256]{2,1,0:T(1,128)S(1)}, s32[1,1,256]{2,1,0:T(1,128)}, u32[]{:S(2)}) copy-start(s32[1,1,256]{2,1,0:T(1,128)} %param.10) | copy-start | bytes 3076
  0.7 39.0 %copy-start.3 = (f32[128,256]{1,0:T(8,128)S(1)}, f32[128,256]{1,0:T(8,128)}, u32[]{:S(2)}) copy-start(f32[128,256]{1,0:T(8,128)} %refs_3_.1) | copy-start | bytes 393220
  0.7 39.0 %copy-start.7 = (s32[256]{0:T(256)S(1)}, s32[256]{0:T(256)}, u32[]{:S(2)}) copy-start(s32[256]{0:T(256)} %param.16) | copy-start | bytes 3076
  0.7 39.0 %copy-start.6 = (s32[256]{0:T(256)S(1)}, s32[256]{0:T(256)}, u32[]{:S(2)}) copy-start(s32[256]{0:T(256)} %param.15) | copy-start | bytes 3076
  0.7 39.0 %copy-start.2 = (f32[4,128,256]{2,1,0:T(8,128)S(1)}, f32[4,128,256]{2,1,0:T(8,128)}, u32[]{:S(2)}) copy-start(f32[4,128,256]{2,1,0:T(8,128)} %refs_1_.1) | copy-start | bytes 1572868
  39.7 45.8 %copy-start = (s32[16,16384]{1,0:T(8,128)S(1)}, s32[16,16384]{1,0:T(8,128)}, u32[]{:S(2)}) copy-start(s32[16,16384]{1,0:T(8,128)} %param.17) | copy-start | bytes 3145732
  39.7 45.8 %copy-start.1 = (f32[16,16384]{1,0:T(8,128)S(1)}, f32[16,16384]{1,0:T(8,128)}, u32[]{:S(2)}) copy-start(f32[16,16384]{1,0:T(8,128)} %param.13) | copy-start | bytes 3145732
  73.9 1.4 collective-permute-start
  74.0 2.9 %collective-permute-start.3 = (bf16[512,128]{1,0:T(8,128)(2,1)S(1)}, bf16[512,128]{1,0:T(8,128)(2,1)S(1)}, u32[]{:S(2)}, u32[]{:S(2)}) collective-permute-start(bf16[512,128]{1,0:T(8,128)(2,1)S(1)} %get-tuple-element.28), channel_id=1, source_target_pairs={{0,1},{1,0},{2,3},{3,2},{4,5},{5,4},{6,7},{7,6},{8,9},{9,8},{10,11... | collective-permute-start | bytes 393224 | tf_op jit(solution)/shard_map/ppermute | solution.py:456
  75.3 5.0 %collective-permute-start.1 = (bf16[512,128]{1,0:T(8,128)(2,1)S(1)}, bf16[512,128]{1,0:T(8,128)(2,1)S(1)}, u32[]{:S(2)}, u32[]{:S(2)}) collective-permute-start(bf16[512,128]{1,0:T(8,128)(2,1)S(1)} %core_pair_sum.4.first_ref), channel_id=1, source_target_pairs={{0,2},{1,5},{2,0},{3,7},{4,6},{5,1},{6,4},{7,3},{8,10},{9,13},{10,... | collective-permute-start | bytes 393224 | tf_op jit(solution)/shard_map/ppermute | solution.py:461
  76.9 5.0 %collective-permute-start.4 = (bf16[512,128]{1,0:T(8,128)(2,1)S(1)}, bf16[512,128]{1,0:T(8,128)(2,1)S(1)}, u32[]{:S(2)}, u32[]{:S(2)}) collective-permute-start(bf16[512,128]{1,0:T(8,128)(2,1)S(1)} %core_pair_sum.5.first_ref), channel_id=1, source_target_pairs={{0,2},{1,5},{2,0},{3,7},{4,6},{5,1},{6,4},{7,3},{8,10},{9,13},{10,... | collective-permute-start | bytes 393224 | tf_op jit(solution)/shard_map/ppermute | solution.py:461
  80.4 5.0 %collective-permute-start.2 = (bf16[512,128]{1,0:T(8,128)(2,1)S(1)}, bf16[512,128]{1,0:T(8,128)(2,1)S(1)}, u32[]{:S(2)}, u32[]{:S(2)}) collective-permute-start(bf16[512,128]{1,0:T(8,128)(2,1)S(1)} %chip_sum.4), channel_id=1, source_target_pairs={{0,4},{1,3},{2,6},{3,1},{4,0},{5,7},{6,2},{7,5},{8,12},{9,11},{10,... | collective-permute-start | bytes 393224 | tf_op jit(solution)/shard_map/ppermute | solution.py:461
  82.0 5.0 %collective-permute-start.5 = (bf16[512,128]{1,0:T(8,128)(2,1)S(1)}, bf16[512,128]{1,0:T(8,128)(2,1)S(1)}, u32[]{:S(2)}, u32[]{:S(2)}) collective-permute-start(bf16[512,128]{1,0:T(8,128)(2,1)S(1)} %chip_sum.5), channel_id=1, source_target_pairs={{0,4},{1,3},{2,6},{3,1},{4,0},{5,7},{6,2},{7,5},{8,12},{9,11},{10,... | collective-permute-start | bytes 393224 | tf_op jit(solution)/shard_map/ppermute | solution.py:461
  85.6 1.8 %collective-permute-start.6 = (bf16[512,128]{1,0:T(8,128)(2,1)S(1)}, bf16[512,128]{1,0:T(8,128)(2,1)S(1)}, u32[]{:S(2)}, u32[]{:S(2)}) collective-permute-start(bf16[512,128]{1,0:T(8,128)(2,1)S(1)} %get-tuple-element.27.refs_0_), channel_id=1, source_target_pairs={{0,1},{1,0},{2,3},{3,2},{4,5},{5,4},{6,7},{7,6},{8,9},{9,8},{10,11... | collective-permute-start | bytes 393224 | tf_op jit(solution)/shard_map/ppermute | solution.py:456
  87.2 1.4 collective-permute-start.7
  156.1 1.4 collective-permute-start.8
  156.2 2.9 %collective-permute-start.11 = (bf16[512,128]{1,0:T(8,128)(2,1)S(1)}, bf16[512,128]{1,0:T(8,128)(2,1)S(1)}, u32[]{:S(2)}, u32[]{:S(2)}) collective-permute-start(bf16[512,128]{1,0:T(8,128)(2,1)S(1)} %get-tuple-element.38), channel_id=1, source_target_pairs={{0,1},{1,0},{2,3},{3,2},{4,5},{5,4},{6,7},{7,6},{8,9},{9,8},{10,11... | collective-permute-start | bytes 393224 | tf_op jit(solution)/shard_map/ppermute | solution.py:456
  157.6 5.0 %collective-permute-start.9 = (bf16[512,128]{1,0:T(8,128)(2,1)S(1)}, bf16[512,128]{1,0:T(8,128)(2,1)S(1)}, u32[]{:S(2)}, u32[]{:S(2)}) collective-permute-start(bf16[512,128]{1,0:T(8,128)(2,1)S(1)} %core_pair_sum.6.first_ref), channel_id=1, source_target_pairs={{0,2},{1,5},{2,0},{3,7},{4,6},{5,1},{6,4},{7,3},{8,10},{9,13},{10,... | collective-permute-start | bytes 393224 | tf_op jit(solution)/shard_map/ppermute | solution.py:461
  159.1 5.1 %collective-permute-start.12 = (bf16[512,128]{1,0:T(8,128)(2,1)S(1)}, bf16[512,128]{1,0:T(8,128)(2,1)S(1)}, u32[]{:S(2)}, u32[]{:S(2)}) collective-permute-start(bf16[512,128]{1,0:T(8,128)(2,1)S(1)} %core_pair_sum.7.first_ref), channel_id=1, source_target_pairs={{0,2},{1,5},{2,0},{3,7},{4,6},{5,1},{6,4},{7,3},{8,10},{9,13},{10,... | collective-permute-start | bytes 393224 | tf_op jit(solution)/shard_map/ppermute | solution.py:461
  162.7 5.0 %collective-permute-start.10 = (bf16[512,128]{1,0:T(8,128)(2,1)S(1)}, bf16[512,128]{1,0:T(8,128)(2,1)S(1)}, u32[]{:S(2)}, u32[]{:S(2)}) collective-permute-start(bf16[512,128]{1,0:T(8,128)(2,1)S(1)} %chip_sum.6), channel_id=1, source_target_pairs={{0,4},{1,3},{2,6},{3,1},{4,0},{5,7},{6,2},{7,5},{8,12},{9,11},{10,... | collective-permute-start | bytes 393224 | tf_op jit(solution)/shard_map/ppermute | solution.py:461
  164.2 5.0 %collective-permute-start.13 = (bf16[512,128]{1,0:T(8,128)(2,1)S(1)}, bf16[512,128]{1,0:T(8,128)(2,1)S(1)}, u32[]{:S(2)}, u32[]{:S(2)}) collective-permute-start(bf16[512,128]{1,0:T(8,128)(2,1)S(1)} %chip_sum.7), channel_id=1, source_target_pairs={{0,4},{1,3},{2,6},{3,1},{4,0},{5,7},{6,2},{7,5},{8,12},{9,11},{10,... | collective-permute-start | bytes 393224 | tf_op jit(solution)/shard_map/ppermute | solution.py:461
  167.8 1.7 collective-permute-start.14
  169.4 1.6 collective-permute-start.15

commit v15 on v12

--- a/solution.py
+++ b/solution.py
@@ -256,11 +256,11 @@
     gradient = running(jnp.concatenate(slopes, axis=1), True, 2)
     old = jnp.concatenate([inc_ref[j] for j in range(scen_local)], axis=1)
     if first:
-        old_sum = running(old, False, 3)
+        old_sum = running(old, False, 2)
     else:
         old_sum = jnp.concatenate([cum_ref[j] for j in range(scen_local)], axis=1)
     fresh = jnp.clip(old - tau_step * gradient, 0.0, jnp.concatenate([upper] * scen_local, axis=1))
-    fresh_sum = running(fresh, False, 3)
+    fresh_sum = running(fresh, False, 2)
     probe = (2.0 * fresh_sum - old_sum).astype(jnp.bfloat16)
     for j in range(scen_local):
         lanes = slice(j * flight_local, (j + 1) * flight_local)

time: 170 us -> 170 us (level)
  no operation moved by 1% of the time
where the time goes in v15:
time: 170 us
  blocking collectives  122 us (72%)
  Pallas kernels  19.3 us (11%)
  waiting for transfers between devices  15.5 us (9%)
  starting transfers between devices  11.9 us (7%)
    all_to_all x2, blocking collectives, per_device(): recv = lax.all_to_all(send, ('row', 'col'), 0, 0, tiled=True)  62.8 us
    all_to_all x2, blocking collectives, per_device(): probe = lax.all_to_all(send, ('row', 'col'), 0, 0, tiled=True)  59.3 us
    ppermute x8, waiting for transfers between devices, swap_chip(): lax.ppermute(value, 'col', [(i, i ^ 2 << (step + i % 2) % bits) for i in...  12.2 us
    ppermute x8, starting transfers between devices, swap_chip(): lax.ppermute(value, 'col', [(i, i ^ 2 << (step + i % 2) % bits) for i in...  10.5 us
    pallas_call x2, Pallas kernels, forward(): pl.pallas_call(functools.partial(forward_kernel, dims, pitch), in_specs=[...  7.12 us
    pallas_call x1, Pallas kernels, first_backward(): pl.pallas_call(functools.partial(first_backward_kernel, dims, pitch), in_...  4.74 us
  transfers between devices with their start and end apart: 16, of which 10 were waited for; matrix products, arithmetic and copies ran while one was open for 0% of the time, Pallas kernels for 1%

profile of v15, /device:TPU:0, one launch (start us, length us, event | category | flops | bytes accessed | tf_op | source)
XLA Modules:
  0.0 169.9 jit_solution(7586178301794759607)
XLA Ops:
  0.7 4.7 %first_backward_products.1 = (bf16[32,128,128]{2,1,0:T(8,128)(2,1)S(1)}, bf16[256,128,128]{2,1,0:T(8,128)(2,1)S(1)}) custom-call(s32[1]{0:T(128)} %bitcast.core_ref, s32[256]{0:T(256)} %bitcast.22, s32[256]{0:T(256)} %bitcast.26, f32[2,128,8,128]{3,2,1,0:T(8,128)} %bitcast.19, bf16[256,128,128]{2,1,0:T(8,128)(2,1)} %bitcast.34), custom_call_target="tpu_custom_call" | custom-call | flops 134217728 | bytes 4194304 | tf_op jit(solution)/shard_map/first_backward_products/pallas_call | solution.py:378
  5.4 33.3 %all_to_all.20.refs_0_ = bf16[32,128,128]{2,1,0:T(8,128)(2,1)S(1)} all-to-all(bf16[32,128,128]{2,1,0:T(8,128)(2,1)S(1)} %get-tuple-element.23), channel_id=1, replica_groups=mesh['row'=4,'col'=8] {'row','col'}, dimensions={0} | all-to-all | bytes 2097152 | tf_op jit(solution)/shard_map/all_to_all | solution.py:521
  38.8 0.8 primal_update.2
  39.6 29.7 %all_to_all.21.probe_ref = bf16[32,128,128]{2,1,0:T(8,128)(2,1)S(1)} all-to-all(bf16[32,128,128]{2,1,0:T(8,128)(2,1)S(1)} %get-tuple-element.24), channel_id=1, replica_groups=mesh['row'=4,'col'=8] {'row','col'}, dimensions={0} | all-to-all | bytes 2097152 | tf_op jit(solution)/shard_map/all_to_all | solution.py:524
  69.3 3.6 %forward_products.2 = (f32[2048,128]{1,0:T(8,128)S(1)}, bf16[512,128]{1,0:T(8,128)(2,1)S(1)}, bf16[512,128]{1,0:T(8,128)(2,1)S(1)}) custom-call(s32[1]{0:T(128)} %bitcast.core_ref, s32[256]{0:T(256)S(1)} %bitcast.23, s32[256]{0:T(256)S(1)} %bitcast.27, bf16[32,128,128]{2,1,0:T(8,128)(2,1)S(1)} %all_to_all.21.probe_ref, ...), custom_call_target="tpu_custom_call" | custom-call | flops 134217728 | bytes 4194304 | tf_op jit(solution)/shard_map/forward_products/pallas_call | solution.py:421
  72.9 0.1 collective-permute-start
  73.0 0.5 collective-permute-start.3
  73.5 0.8 collective-permute-done.other_ref
  74.3 1.5 collective-permute-start.1
  75.9 0.0 collective-permute-done.3.other_ref
  75.9 0.6 collective-permute-start.4
  76.5 2.8 %collective-permute-done.1.second_ref.refs_0_ = bf16[512,128]{1,0:T(8,128)(2,1)S(1)} collective-permute-done((bf16[512,128]{1,0:T(8,128)(2,1)S(1)}, bf16[512,128]{1,0:T(8,128)(2,1)S(1)}, u32[]{:S(2)}, u32[]{:S(2)}) %collective-permute-start.1) | collective-permute-done | bytes 131104 | tf_op jit(solution)/shard_map/ppermute | solution.py:452
  79.4 1.5 collective-permute-start.2
  80.9 0.0 collective-permute-done.4.second_ref.refs_0_
  81.0 1.5 collective-permute-start.5
  82.5 1.9 %collective-permute-done.2.refs_1_ = bf16[512,128]{1,0:T(8,128)(2,1)S(1)} collective-permute-done((bf16[512,128]{1,0:T(8,128)(2,1)S(1)}, bf16[512,128]{1,0:T(8,128)(2,1)S(1)}, u32[]{:S(2)}, u32[]{:S(2)}) %collective-permute-start.2) | collective-permute-done | bytes 131104 | tf_op jit(solution)/shard_map/ppermute | solution.py:452
  84.4 0.1 dual_update.4
  84.6 0.1 collective-permute-start.6
  84.6 1.4 collective-permute-done.5.refs_1_
  86.0 0.1 dual_update.5
  86.1 0.1 collective-permute-start.7
  86.2 0.1 clear_sums.1._
  86.4 0.0 collective-permute-done.6.refs_2_
  86.4 1.2 collective-permute-done.7.refs_3_
  87.6 3.1 %backward_products.1 = (bf16[32,128,128]{2,1,0:T(8,128)(2,1)S(1)}, f32[6144,128]{1,0:T(8,128)S(1)}) custom-call(s32[1]{0:T(128)} %bitcast.core_ref, s32[256]{0:T(256)S(1)} %bitcast.24, s32[256]{0:T(256)S(1)} %bitcast.28, bf16[256,128,128]{2,1,0:T(8,128)(2,1)S(1)} %get-tuple-element.22.tiles_ref, ...), custom_call_target="tpu_custom_call", output_to_operand_aliasing={{1}: (4, {})} | custom-call | flops 134217728 | bytes 4194304 | tf_op jit(solution)/shard_map/backward_products/pallas_call | solution.py:408
  90.7 29.5 %all_to_all.22.refs_0_ = bf16[32,128,128]{2,1,0:T(8,128)(2,1)S(1)} all-to-all(bf16[32,128,128]{2,1,0:T(8,128)(2,1)S(1)} %get-tuple-element.30), channel_id=1, replica_groups=mesh['row'=4,'col'=8] {'row','col'}, dimensions={0} | all-to-all | bytes 2097152 | tf_op jit(solution)/shard_map/all_to_all | solution.py:521
  120.2 0.7 primal_update.3
  120.9 29.7 %all_to_all.23.probe_ref = bf16[32,128,128]{2,1,0:T(8,128)(2,1)S(1)} all-to-all(bf16[32,128,128]{2,1,0:T(8,128)(2,1)S(1)} %get-tuple-element.34), channel_id=1, replica_groups=mesh['row'=4,'col'=8] {'row','col'}, dimensions={0} | all-to-all | bytes 2097152 | tf_op jit(solution)/shard_map/all_to_all | solution.py:524
  150.6 3.6 %forward_products.3 = (f32[2048,128]{1,0:T(8,128)S(1)}, bf16[512,128]{1,0:T(8,128)(2,1)S(1)}, bf16[512,128]{1,0:T(8,128)(2,1)S(1)}) custom-call(s32[1]{0:T(128)} %bitcast.core_ref, s32[256]{0:T(256)S(1)} %bitcast.25, s32[256]{0:T(256)S(1)} %bitcast.29, bf16[32,128,128]{2,1,0:T(8,128)(2,1)S(1)} %all_to_all.23.probe_ref, ...), custom_call_target="tpu_custom_call" | custom-call | flops 134217728 | bytes 4194304 | tf_op jit(solution)/shard_map/forward_products/pallas_call | solution.py:421
  154.2 0.1 collective-permute-start.8
  154.2 0.5 collective-permute-start.11
  154.7 0.8 collective-permute-done.8.other_ref
  155.6 1.5 collective-permute-start.9
  157.1 0.0 collective-permute-done.11.other_ref
  157.2 0.6 collective-permute-start.12
  157.8 2.8 %collective-permute-done.9.second_ref.refs_0_ = bf16[512,128]{1,0:T(8,128)(2,1)S(1)} collective-permute-done((bf16[512,128]{1,0:T(8,128)(2,1)S(1)}, bf16[512,128]{1,0:T(8,128)(2,1)S(1)}, u32[]{:S(2)}, u32[]{:S(2)}) %collective-permute-start.9) | collective-permute-done | bytes 131104 | tf_op jit(solution)/shard_map/ppermute | solution.py:452
  160.7 1.5 collective-permute-start.10
  162.2 0.0 collective-permute-done.12.second_ref.refs_0_
  162.3 1.5 collective-permute-start.13
  163.8 1.9 %collective-permute-done.10.refs_1_ = bf16[512,128]{1,0:T(8,128)(2,1)S(1)} collective-permute-done((bf16[512,128]{1,0:T(8,128)(2,1)S(1)}, bf16[512,128]{1,0:T(8,128)(2,1)S(1)}, u32[]{:S(2)}, u32[]{:S(2)}) %collective-permute-start.10) | collective-permute-done | bytes 131104 | tf_op jit(solution)/shard_map/ppermute | solution.py:452
  165.7 0.1 dual_update.6.refs_0_
  165.8 0.1 collective-permute-start.14
  165.9 1.4 collective-permute-done.13.refs_1_
  167.3 0.1 dual_update.7.refs_1_
  167.4 0.1 collective-permute-start.15
  167.5 1.1 own_results.1
  168.6 0.4 collective-permute-done.15.refs_0_
  169.0 0.7 other_results.1
  (25 shorter events, 0.3 us)
Async XLA Ops:
  0.6 68.7 %copy-start.5 = (s32[1,1,256]{2,1,0:T(1,128)S(1)}, s32[1,1,256]{2,1,0:T(1,128)}, u32[]{:S(2)}) copy-start(s32[1,1,256]{2,1,0:T(1,128)} %param.11) | copy-start | bytes 3076
  0.6 68.7 %copy-start.4 = (s32[1,1,256]{2,1,0:T(1,128)S(1)}, s32[1,1,256]{2,1,0:T(1,128)}, u32[]{:S(2)}) copy-start(s32[1,1,256]{2,1,0:T(1,128)} %param.10) | copy-start | bytes 3076
  0.7 38.1 %copy-start.3 = (f32[128,256]{1,0:T(8,128)S(1)}, f32[128,256]{1,0:T(8,128)}, u32[]{:S(2)}) copy-start(f32[128,256]{1,0:T(8,128)} %refs_3_.1) | copy-start | bytes 393220
  0.7 38.1 %copy-start.7 = (s32[256]{0:T(256)S(1)}, s32[256]{0:T(256)}, u32[]{:S(2)}) copy-start(s32[256]{0:T(256)} %param.16) | copy-start | bytes 3076
  0.7 38.1 %copy-start.6 = (s32[256]{0:T(256)S(1)}, s32[256]{0:T(256)}, u32[]{:S(2)}) copy-start(s32[256]{0:T(256)} %param.15) | copy-start | bytes 3076
  0.7 38.1 %copy-start.2 = (f32[4,128,256]{2,1,0:T(8,128)S(1)}, f32[4,128,256]{2,1,0:T(8,128)}, u32[]{:S(2)}) copy-start(f32[4,128,256]{2,1,0:T(8,128)} %refs_1_.1) | copy-start | bytes 1572868
  38.8 45.6 %copy-start = (s32[16,16384]{1,0:T(8,128)S(1)}, s32[16,16384]{1,0:T(8,128)}, u32[]{:S(2)}) copy-start(s32[16,16384]{1,0:T(8,128)} %param.17) | copy-start | bytes 3145732
  38.8 45.6 %copy-start.1 = (f32[16,16384]{1,0:T(8,128)S(1)}, f32[16,16384]{1,0:T(8,128)}, u32[]{:S(2)}) copy-start(f32[16,16384]{1,0:T(8,128)} %param.13) | copy-start | bytes 3145732
  72.9 1.4 collective-permute-start
  73.0 2.9 %collective-permute-start.3 = (bf16[512,128]{1,0:T(8,128)(2,1)S(1)}, bf16[512,128]{1,0:T(8,128)(2,1)S(1)}, u32[]{:S(2)}, u32[]{:S(2)}) collective-permute-start(bf16[512,128]{1,0:T(8,128)(2,1)S(1)} %get-tuple-element.28), channel_id=1, source_target_pairs={{0,1},{1,0},{2,3},{3,2},{4,5},{5,4},{6,7},{7,6},{8,9},{9,8},{10,11... | collective-permute-start | bytes 393224 | tf_op jit(solution)/shard_map/ppermute | solution.py:447
  74.3 5.0 %collective-permute-start.1 = (bf16[512,128]{1,0:T(8,128)(2,1)S(1)}, bf16[512,128]{1,0:T(8,128)(2,1)S(1)}, u32[]{:S(2)}, u32[]{:S(2)}) collective-permute-start(bf16[512,128]{1,0:T(8,128)(2,1)S(1)} %core_pair_sum.4.first_ref), channel_id=1, source_target_pairs={{0,2},{1,5},{2,0},{3,7},{4,6},{5,1},{6,4},{7,3},{8,10},{9,13},{10,... | collective-permute-start | bytes 393224 | tf_op jit(solution)/shard_map/ppermute | solution.py:452
  75.9 5.0 %collective-permute-start.4 = (bf16[512,128]{1,0:T(8,128)(2,1)S(1)}, bf16[512,128]{1,0:T(8,128)(2,1)S(1)}, u32[]{:S(2)}, u32[]{:S(2)}) collective-permute-start(bf16[512,128]{1,0:T(8,128)(2,1)S(1)} %core_pair_sum.5.first_ref), channel_id=1, source_target_pairs={{0,2},{1,5},{2,0},{3,7},{4,6},{5,1},{6,4},{7,3},{8,10},{9,13},{10,... | collective-permute-start | bytes 393224 | tf_op jit(solution)/shard_map/ppermute | solution.py:452
  79.4 5.0 %collective-permute-start.2 = (bf16[512,128]{1,0:T(8,128)(2,1)S(1)}, bf16[512,128]{1,0:T(8,128)(2,1)S(1)}, u32[]{:S(2)}, u32[]{:S(2)}) collective-permute-start(bf16[512,128]{1,0:T(8,128)(2,1)S(1)} %chip_sum.4), channel_id=1, source_target_pairs={{0,4},{1,3},{2,6},{3,1},{4,0},{5,7},{6,2},{7,5},{8,12},{9,11},{10,... | collective-permute-start | bytes 393224 | tf_op jit(solution)/shard_map/ppermute | solution.py:452
  81.0 5.0 %collective-permute-start.5 = (bf16[512,128]{1,0:T(8,128)(2,1)S(1)}, bf16[512,128]{1,0:T(8,128)(2,1)S(1)}, u32[]{:S(2)}, u32[]{:S(2)}) collective-permute-start(bf16[512,128]{1,0:T(8,128)(2,1)S(1)} %chip_sum.5), channel_id=1, source_target_pairs={{0,4},{1,3},{2,6},{3,1},{4,0},{5,7},{6,2},{7,5},{8,12},{9,11},{10,... | collective-permute-start | bytes 393224 | tf_op jit(solution)/shard_map/ppermute | solution.py:452
  84.6 1.8 %collective-permute-start.6 = (bf16[512,128]{1,0:T(8,128)(2,1)S(1)}, bf16[512,128]{1,0:T(8,128)(2,1)S(1)}, u32[]{:S(2)}, u32[]{:S(2)}) collective-permute-start(bf16[512,128]{1,0:T(8,128)(2,1)S(1)} %get-tuple-element.27.refs_0_), channel_id=1, source_target_pairs={{0,1},{1,0},{2,3},{3,2},{4,5},{5,4},{6,7},{7,6},{8,9},{9,8},{10,11... | collective-permute-start | bytes 393224 | tf_op jit(solution)/shard_map/ppermute | solution.py:447
  86.1 1.4 collective-permute-start.7
  154.2 1.4 collective-permute-start.8
  154.2 2.9 %collective-permute-start.11 = (bf16[512,128]{1,0:T(8,128)(2,1)S(1)}, bf16[512,128]{1,0:T(8,128)(2,1)S(1)}, u32[]{:S(2)}, u32[]{:S(2)}) collective-permute-start(bf16[512,128]{1,0:T(8,128)(2,1)S(1)} %get-tuple-element.38), channel_id=1, source_target_pairs={{0,1},{1,0},{2,3},{3,2},{4,5},{5,4},{6,7},{7,6},{8,9},{9,8},{10,11... | collective-permute-start | bytes 393224 | tf_op jit(solution)/shard_map/ppermute | solution.py:447
  155.6 5.0 %collective-permute-start.9 = (bf16[512,128]{1,0:T(8,128)(2,1)S(1)}, bf16[512,128]{1,0:T(8,128)(2,1)S(1)}, u32[]{:S(2)}, u32[]{:S(2)}) collective-permute-start(bf16[512,128]{1,0:T(8,128)(2,1)S(1)} %core_pair_sum.6.first_ref), channel_id=1, source_target_pairs={{0,2},{1,5},{2,0},{3,7},{4,6},{5,1},{6,4},{7,3},{8,10},{9,13},{10,... | collective-permute-start | bytes 393224 | tf_op jit(solution)/shard_map/ppermute | solution.py:452
  157.2 5.1 %collective-permute-start.12 = (bf16[512,128]{1,0:T(8,128)(2,1)S(1)}, bf16[512,128]{1,0:T(8,128)(2,1)S(1)}, u32[]{:S(2)}, u32[]{:S(2)}) collective-permute-start(bf16[512,128]{1,0:T(8,128)(2,1)S(1)} %core_pair_sum.7.first_ref), channel_id=1, source_target_pairs={{0,2},{1,5},{2,0},{3,7},{4,6},{5,1},{6,4},{7,3},{8,10},{9,13},{10,... | collective-permute-start | bytes 393224 | tf_op jit(solution)/shard_map/ppermute | solution.py:452
  160.7 5.0 %collective-permute-start.10 = (bf16[512,128]{1,0:T(8,128)(2,1)S(1)}, bf16[512,128]{1,0:T(8,128)(2,1)S(1)}, u32[]{:S(2)}, u32[]{:S(2)}) collective-permute-start(bf16[512,128]{1,0:T(8,128)(2,1)S(1)} %chip_sum.6), channel_id=1, source_target_pairs={{0,4},{1,3},{2,6},{3,1},{4,0},{5,7},{6,2},{7,5},{8,12},{9,11},{10,... | collective-permute-start | bytes 393224 | tf_op jit(solution)/shard_map/ppermute | solution.py:452
  162.3 5.0 %collective-permute-start.13 = (bf16[512,128]{1,0:T(8,128)(2,1)S(1)}, bf16[512,128]{1,0:T(8,128)(2,1)S(1)}, u32[]{:S(2)}, u32[]{:S(2)}) collective-permute-start(bf16[512,128]{1,0:T(8,128)(2,1)S(1)} %chip_sum.7), channel_id=1, source_target_pairs={{0,4},{1,3},{2,6},{3,1},{4,0},{5,7},{6,2},{7,5},{8,12},{9,11},{10,... | collective-permute-start | bytes 393224 | tf_op jit(solution)/shard_map/ppermute | solution.py:452
  165.8 1.7 collective-permute-start.14
  167.4 1.6 collective-permute-start.15
